TPU v7x, 32 devices: a whole 2x2x4 slice. The times are simulated.
32 devices in a mesh: scene: 2 (over y), blk: 8 (over z, x), head: 2 (over core).
Axes of the slice: x: 2, y: 2, z: 4, core: 2. Of those that a mesh axis runs over, the one named last changes fastest.
Arguments:
- patch_rows: bfloat16 [32, 192, 1024], P(('scene', 'blk'), None, 'head'), parts along dimension 0
- special_rows: bfloat16 [32, 5, 1024], P(('scene', 'blk'), None, 'head'), parts along dimension 0, may hold values from -6 to 6
- role_first: bfloat16 [5, 1024], replicated, may hold values from -3 to 3
- role_rest: bfloat16 [5, 1024], replicated, may hold values from -3 to 3
- frame_order: int32 [32], P(('scene', 'blk')), parts along dimension 0, may hold values from 0 to 15, each once
- covisible: int32 [32, 16], P(('scene', 'blk')), parts along dimension 0, may hold values from 0 to 1, as said below
- w_qkv: bfloat16 [3, 1024, 1024], P(None, None, 'head')
- w_out: bfloat16 [1024, 1024], P('head'), may hold values from -0.1875 to 0.1875
Outputs:
- patch_out: bfloat16 [32, 192, 1024], P(('scene', 'blk'), None, 'head'), parts along dimension 0
- special_out: bfloat16 [32, 5, 1024], P(('scene', 'blk'), None, 'head'), parts along dimension 0
There are 2 independent parts, one for each index of `scene`. A program takes and returns all parts, laid end to end along the dimension named above; an argument that names none is the same for every part. Nothing has to cross between parts.
Inputs may be any that keep to these rules, and one draw needn't show every extreme that they name: Image a sits on index a // 2 of blk. covisible[a, b] = covisible[b, a]; covisible[a, a] = 1; covisible[a, b] is 0 whenever the owners of a and b are more than 1 indices apart around the loop of blk, and that distance 1 is reached. `frame_order`: each capture index appears once.
All inputs are finite; a program needn't handle non-finite values.
Results may differ from a plain program's by a relative error of at most 0.012.
The roundings to bfloat16 on the way count: a program that leaves them out, or rounds other values in their place, can miss the bound.
Values may be sent and summed in bfloat16 or wider, within the bound.
No kernel may reach another device: no remote copies, remote signals or barrier semaphores. Data moves between devices by JAX's collectives and lax.ppermute only.
A program may use at most 128 MiB of HBM per device.

v0:
```python
import jax
import jax.numpy as jnp
from jax import lax
from jax.sharding import PartitionSpec as P

HEAD_DIM = 64


def shifted(block, axis, distance):
    devices = range(lax.axis_size(axis))
    route = [((i - distance) % len(devices), i) for i in devices]
    return lax.ppermute(block, axis, route)


def attend(softmax_state, queries, key_value, allowed):
    head_count = queries.shape[1]
    keys_part = key_value[0].reshape(key_value.shape[1], head_count, -1)
    values_part = key_value[1].reshape(key_value.shape[1], head_count, -1)
    scores = jnp.einsum("rhd,khd->hrk", queries, keys_part, preferred_element_type=jnp.float32)
    scores = scores * queries.shape[2] ** (-0.5)
    if allowed is not None:
        scores = jnp.where(allowed[None], scores, -jnp.inf)
    running, denominator, numerator = softmax_state
    newest = jnp.maximum(running, jnp.max(scores, axis=2))
    factor = jnp.exp(running - newest)
    weights = jnp.exp(scores - newest[:, :, None])
    denominator = denominator * factor + jnp.sum(weights, axis=2)
    numerator = numerator * factor[:, :, None] + jnp.einsum(
        "hrk,khd->hrd",
        weights.astype(jnp.bfloat16),
        values_part,
        preferred_element_type=jnp.float32,
    )
    return (newest, denominator, numerator)


def per_device(
    patch_rows, special_rows, role_first, role_rest, frame_order, covisible, w_qkv, w_out
):
    images_here = patch_rows.shape[0]
    patch_count = patch_rows.shape[1]
    special_count = special_rows.shape[1]
    per_image = special_count + patch_count
    dev_rows = images_here * per_image
    patches, specials = (
        lax.all_gather(patch_rows, "head", axis=2, tiled=True),
        lax.all_gather(special_rows, "head", axis=2, tiled=True),
    )
    width = patches.shape[2]
    reference_frame = (frame_order == 0)[:, None, None]
    role_added = jnp.where(
        reference_frame, role_first.astype(jnp.float32)[None], role_rest.astype(jnp.float32)[None]
    )
    specials = (specials.astype(jnp.float32) + role_added).astype(jnp.bfloat16)
    all_rows = jnp.concatenate([specials, patches], axis=1).reshape(dev_rows, width)
    local_width = w_qkv.shape[2]
    head_count = local_width // HEAD_DIM
    queries = jnp.dot(all_rows, w_qkv[0], preferred_element_type=jnp.float32).astype(jnp.bfloat16)
    keys_here = jnp.dot(all_rows, w_qkv[1], preferred_element_type=jnp.float32).astype(jnp.bfloat16)
    values_here = jnp.dot(all_rows, w_qkv[2], preferred_element_type=jnp.float32).astype(
        jnp.bfloat16
    )
    queries = queries.reshape(dev_rows, head_count, HEAD_DIM)
    keys_images = keys_here.reshape(images_here, per_image, local_width)
    values_images = values_here.reshape(images_here, per_image, local_width)
    special_pair = jnp.stack(
        [
            keys_images[:, :special_count].reshape(-1, local_width),
            values_images[:, :special_count].reshape(-1, local_width),
        ]
    )
    own_pair = jnp.stack(
        [
            keys_images[:, special_count:].reshape(-1, local_width),
            values_images[:, special_count:].reshape(-1, local_width),
        ]
    )
    softmax_state = (
        jnp.full((head_count, dev_rows), -1e30, jnp.float32),
        jnp.zeros((head_count, dev_rows), jnp.float32),
        jnp.zeros((head_count, dev_rows, HEAD_DIM), jnp.float32),
    )
    softmax_state = attend(
        softmax_state, queries, lax.all_gather(special_pair, "blk", axis=1, tiled=True), None
    )
    owner_count = lax.axis_size("blk")
    my_index = lax.axis_index("blk")
    reach_span = max(1, owner_count // 64)

    def process(carry, key_value, offset):
        source_device = (my_index + offset) % owner_count
        columns = lax.dynamic_slice_in_dim(covisible, source_device * images_here, images_here, 1)
        allowed = jnp.repeat(jnp.repeat(columns > 0, per_image, 0), patch_count, 1)
        return attend(carry, queries, key_value, allowed)

    travel = shifted(own_pair, "blk", reach_span)
    softmax_state = process(softmax_state, travel, -reach_span)

    def one_turn(turn_index, carry):
        moving, inner_state = carry
        moving = shifted(moving, "blk", -1)
        return (moving, process(inner_state, moving, turn_index - reach_span))

    travel, softmax_state = lax.fori_loop(1, 2 * reach_span + 1, one_turn, (travel, softmax_state))
    running, denominator, numerator = softmax_state
    attended = (numerator / denominator[:, :, None]).astype(jnp.bfloat16)
    attended = jnp.transpose(attended, (1, 0, 2)).reshape(dev_rows, local_width)
    partial_out = jnp.dot(attended, w_out, preferred_element_type=jnp.float32).reshape(
        images_here, per_image, width
    )
    special_sum, patch_sum = (
        lax.psum_scatter(
            partial_out[:, :special_count].astype(jnp.bfloat16),
            "head",
            scatter_dimension=2,
            tiled=True,
        ).astype(jnp.float32),
        lax.psum_scatter(
            partial_out[:, special_count:].astype(jnp.bfloat16),
            "head",
            scatter_dimension=2,
            tiled=True,
        ).astype(jnp.float32),
    )
    return (patch_sum.astype(jnp.bfloat16), special_sum.astype(jnp.bfloat16))


def solution(mesh):
    in_specs = (
        P(("scene", "blk"), None, "head"),
        P(("scene", "blk"), None, "head"),
        P(),
        P(),
        P(("scene", "blk")),
        P(("scene", "blk"), None),
        P(None, None, "head"),
        P("head", None),
    )
    out_specs = (P(("scene", "blk"), None, "head"), P(("scene", "blk"), None, "head"))
    return jax.shard_map(
        per_device, mesh=mesh, in_specs=in_specs, out_specs=out_specs, check_vma=False
    )
```

profile of v0, /device:TPU:0, one launch (start us, length us, event | category | flops | bytes accessed | tf_op | source)
XLA Modules:
  0.0 151.4 jit_solution(5894837340517497049)
XLA Ops:
  7.2 2.8 %all_gather.10 = bf16[2,192,1024]{2,1,0:T(8,128)(2,1)S(1)} all-gather(bf16[2,192,512]{2,1,0:T(8,128)(2,1)} %param.10), channel_id=1, replica_groups=mesh['scene'=2,'blk'=8,'head'=2] {'head'}, dimensions={2}, use_global_device_ids=true | all-gather | bytes 1179648 | tf_op jit(solution)/shard_map/all_gather | solution.py:46
  11.5 2.2 %all_gather.9 = bf16[2,5,1024]{2,0,1:T(2,128)(2,1)S(1)} all-gather(bf16[2,5,512]{2,0,1:T(2,128)(2,1)} %param.11), channel_id=1, replica_groups=mesh['scene'=2,'blk'=8,'head'=2] {'head'}, dimensions={2}, use_global_device_ids=true | all-gather | bytes 30720 | tf_op jit(solution)/shard_map/all_gather | solution.py:47
  14.8 2.1 %convolution_convert_fusion.3 = bf16[394,512]{1,0:T(8,128)(2,1)S(1)} fusion(bf16[394,1024]{1,0:T(8,128)(2,1)S(1)} %reshape.65, bf16[3,1024,512]{2,1,0:T(8,128)(2,1)} %param.16), kind=kOutput, calls=%fused_computation.29 | convolution fusion | flops 413340672 | bytes 2258944 | tf_op jit(solution)/shard_map/dot_general | solution.py:59
  16.9 1.8 %convolution_convert_fusion.2 = bf16[394,512]{1,0:T(8,128)(2,1)S(1)} fusion(bf16[394,1024]{1,0:T(8,128)(2,1)S(1)} %reshape.65, bf16[3,1024,512]{2,1,0:T(8,128)(2,1)} %param.16), kind=kOutput, calls=%fused_computation.28 | convolution fusion | flops 413340672 | bytes 2258944 | tf_op jit(solution)/shard_map/dot_general | solution.py:60
  19.1 1.0 pad_maximum_fusion.1
  20.1 2.8 %collective-permute-start.1 = (bf16[2,384,512]{2,1,0:T(8,128)(2,1)}, bf16[2,384,512]{2,1,0:T(8,128)(2,1)S(1)}, u32[]{:S(2)}, u32[]{:S(2)}) collective-permute-start(bf16[2,384,512]{2,1,0:T(8,128)(2,1)} %pad_maximum_fusion.1), channel_id=1, source_target_pairs={{14,0},{0,2},{2,4},{4,6},{6,8},{8,10},{10,12},{12,14},{15,1},{1,3}... | collective-permute-start | bytes 2359304 | tf_op jit(solution)/shard_map/ppermute | solution.py:12
  22.9 2.1 %convolution_convert_fusion.1 = bf16[394,512]{1,0:T(8,128)(2,1)S(1)} fusion(bf16[394,1024]{1,0:T(8,128)(2,1)} %copy-done.5, bf16[3,1024,512]{2,1,0:T(8,128)(2,1)} %param.16), kind=kOutput, calls=%fused_computation.27 | convolution fusion | flops 413340672 | bytes 2271232 | tf_op jit(solution)/shard_map/dot_general | solution.py:58
  25.5 0.9 copy.39
  26.7 41.5 %all_gather.11 = bf16[2,80,512]{2,0,1:T(2,128)(2,1)S(1)} all-gather(bf16[2,10,512]{2,0,1:T(2,128)(2,1)S(1)} %copy.36), channel_id=1, replica_groups=mesh['scene'=2,'blk'=8,'head'=2] {'blk'}, dimensions={1}, use_global_device_ids=true | all-gather | bytes 184320 | tf_op jit(solution)/shard_map/all_gather | solution.py:84
  69.4 2.0 %fusion.40 = (f32[8,394]{1,0:T(8,128)}, f32[8,394,80]{1,2,0:T(8,128)}) fusion(bf16[394,8,64]{0,2,1:T(8,128)(2,1)S(1)} %bitcast.56, bf16[80,8,64]{0,2,1:T(8,128)(2,1)S(1)} %bitcast.66), kind=kOutput, calls=%fused_computation.59 | convolution fusion | flops 32777648 | bytes 1506624 | tf_op jit(solution)/shard_map/rhd,khd->hrk/dot_general | solution.py:19
  71.7 0.9 copy.42
  72.6 2.1 %fusion.11 = (f32[8,394]{1,0:T(8,128)S(1)}, f32[8,394,384]{2,1,0:T(8,128)S(1)}) fusion(pred[394,384]{1,0:T(8,128)(4,1)} %copy.39, bf16[394,8,64]{0,2,1:T(8,128)(2,1)S(1)} %bitcast.57, bf16[384,8,64]{0,2,1:T(8,128)(2,1)S(1)} %bitcast.61), kind=kOutput, calls=%fused_computation.16 | convolution fusion | flops 158555056 | bytes 5802048 | tf_op jit(solution)/shard_map/rhd,khd->hrk/dot_general | solution.py:19
  75.1 1.8 %fusion.13 = f32[8,394]{1,0:T(8,128)S(1)} fusion(f32[8,394,384]{2,1,0:T(8,128)S(1)} %get-tuple-element.328, f32[8,394]{1,0:T(8,128)S(1)} %get-tuple-element.392, pred[394,384]{1,0:T(8,128)(4,1)S(1)} %copy-done.2), kind=kLoop, calls=%fused_computation.18 | loop fusion | flops 4838320 | bytes 5017984 | tf_op jit(solution)/shard_map/reduce_sum | solution.py:27
  77.2 2.4 %fusion.18 = f32[8,394,64]{1,2,0:T(8,128)} fusion(f32[8,394,64]{1,2,0:T(8,128)S(1)} %fusion.17, bf16[384,8,64]{0,2,1:T(8,128)(2,1)S(1)} %bitcast.67, f32[8,394,384]{2,1,0:T(8,128)S(1)} %get-tuple-element.328, f32[8,394]{1,0:T(8,128)S(1)} %get-tuple-element.392, pred[394,384]{1,0:T(8,128)(4,1)S(1)} %copy-done.2), kind=kOutput, calls=%fused_computation.25 | convolution fusion | flops 159970304 | bytes 7012416 | tf_op jit(solution)/shard_map/hrk,khd->hrd/dot_general | solution.py:28
  80.1 39.8 %while.23 = (s32[]{:T(128)}, bf16[2,384,512]{1,2,0:T(8,128)(2,1)S(1)}, f32[8,394]{1,0:T(8,128)S(1)}, f32[8,394]{1,0:T(8,128)S(1)}, f32[8,394,64]{1,2,0:T(8,128)}...) while((s32[]{:T(128)}, ...), condition=%wide.region_7.8_spmd, body=%wide.region_4.7_spmd.sunk | while | flops 323578048 | bytes 31188024 | solution.py:104
  80.1 1.7 %collective-permute-start = (bf16[2,384,512]{1,2,0:T(8,128)(2,1)S(1)}, bf16[2,384,512]{1,2,0:T(8,128)(2,1)S(1)}, u32[]{:S(2)}, u32[]{:S(2)}) collective-permute-start(bf16[2,384,512]{1,2,0:T(8,128)(2,1)S(1)} %get-tuple-element.405), channel_id=1, source_target_pairs={{2,0},{4,2},{6,4},{8,6},{10,8},{12,10},{14,12},{0,14},{3,1},{5,3},... | collective-permute-start | bytes 2359304 | tf_op jit(solution)/shard_map/while/body/eval_jaxpr/ppermute | solution.py:12
  82.5 11.8 %collective-permute-done = bf16[2,384,512]{1,2,0:T(8,128)(2,1)S(1)} collective-permute-done((bf16[2,384,512]{1,2,0:T(8,128)(2,1)S(1)}, bf16[2,384,512]{1,2,0:T(8,128)(2,1)S(1)}, u32[]{:S(2)}, u32[]{:S(2)}) %collective-permute-start) | collective-permute-done | bytes 786464 | tf_op jit(solution)/shard_map/while/body/eval_jaxpr/ppermute | solution.py:12
  94.3 1.1 fusion.66
  95.5 1.8 %fusion.67 = f32[8,394]{1,0:T(8,128)S(1)} fusion(f32[8,394,384]{2,1,0:T(8,128)S(1)} %get-tuple-element.386, f32[8,394]{1,0:T(8,128)S(1)} %max.29, pred[394,384]{1,0:T(8,128)(4,1)S(1)} %copy.53), kind=kLoop, calls=%fused_computation.4.clone.1 | loop fusion | flops 4838320 | bytes 5017984 | tf_op jit(solution)/shard_map/while/body/eval_jaxpr/reduce_sum | solution.py:27
  97.3 1.6 %fusion.68 = f32[8,394,64]{1,2,0:T(8,128)S(1)} fusion(bf16[384,8,64]{0,2,1:T(8,128)(2,1)S(1)} %bitcast.60, f32[8,394,384]{2,1,0:T(8,128)S(1)} %get-tuple-element.386, f32[8,394]{1,0:T(8,128)S(1)} %max.29, pred[394,384]{1,0:T(8,128)(4,1)S(1)} %copy.53, f32[8,394,64]{1,2,0:T(8,128)S(1)} %copy-done.3, f32[8,394]{1,0:T(8,128)S(1)} %get-tuple-element.389), kind=kOutput, calls=%fused_computation.7.clone.1 | convolution fusion | flops 160172032 | bytes 7025024 | tf_op jit(solution)/shard_map/while/body/eval_jaxpr/hrk,khd->hrd/dot_general | solution.py:28
  99.0 0.9 copy-done.4
  99.9 4.0 %collective-permute-start = (bf16[2,384,512]{1,2,0:T(8,128)(2,1)S(1)}, bf16[2,384,512]{1,2,0:T(8,128)(2,1)S(1)}, u32[]{:S(2)}, u32[]{:S(2)}) collective-permute-start(bf16[2,384,512]{1,2,0:T(8,128)(2,1)S(1)} %get-tuple-element.405), channel_id=1, source_target_pairs={{2,0},{4,2},{6,4},{8,6},{10,8},{12,10},{14,12},{0,14},{3,1},{5,3},... | collective-permute-start | bytes 2359304 | tf_op jit(solution)/shard_map/while/body/eval_jaxpr/ppermute | solution.py:12
  104.6 9.7 %collective-permute-done = bf16[2,384,512]{1,2,0:T(8,128)(2,1)S(1)} collective-permute-done((bf16[2,384,512]{1,2,0:T(8,128)(2,1)S(1)}, bf16[2,384,512]{1,2,0:T(8,128)(2,1)S(1)}, u32[]{:S(2)}, u32[]{:S(2)}) %collective-permute-start) | collective-permute-done | bytes 786464 | tf_op jit(solution)/shard_map/while/body/eval_jaxpr/ppermute | solution.py:12
  114.4 1.1 fusion.66
  115.5 1.8 %fusion.67 = f32[8,394]{1,0:T(8,128)S(1)} fusion(f32[8,394,384]{2,1,0:T(8,128)S(1)} %get-tuple-element.386, f32[8,394]{1,0:T(8,128)S(1)} %max.29, pred[394,384]{1,0:T(8,128)(4,1)S(1)} %copy.53), kind=kLoop, calls=%fused_computation.4.clone.1 | loop fusion | flops 4838320 | bytes 5017984 | tf_op jit(solution)/shard_map/while/body/eval_jaxpr/reduce_sum | solution.py:27
  117.3 1.6 %fusion.68 = f32[8,394,64]{1,2,0:T(8,128)S(1)} fusion(bf16[384,8,64]{0,2,1:T(8,128)(2,1)S(1)} %bitcast.60, f32[8,394,384]{2,1,0:T(8,128)S(1)} %get-tuple-element.386, f32[8,394]{1,0:T(8,128)S(1)} %max.29, pred[394,384]{1,0:T(8,128)(4,1)S(1)} %copy.53, f32[8,394,64]{1,2,0:T(8,128)S(1)} %copy-done.3, f32[8,394]{1,0:T(8,128)S(1)} %get-tuple-element.389), kind=kOutput, calls=%fused_computation.7.clone.1 | convolution fusion | flops 160172032 | bytes 7025024 | tf_op jit(solution)/shard_map/while/body/eval_jaxpr/hrk,khd->hrd/dot_general | solution.py:28
  119.0 0.9 copy-done.4
  119.9 1.3 fusion.33
  122.9 1.1 slice.90
  124.0 8.3 %reduce-scatter.5.cloned.1.call-done = bf16[2,5,512]{2,1,0:T(8,128)(2,1)} async-done(((bf16[2,5,1024]{2,1,0:T(8,128)(2,1)}), bf16[2,5,512]{2,1,0:T(8,128)(2,1)}) %reduce-scatter.5.cloned.1.call-update) | async-done | bytes 10256 | tf_op jit(solution)/shard_map/reduce_scatter | solution.py:112
  132.3 1.3 copy.46
  133.7 10.9 %reduce-scatter.3.cloned.1.call-done = bf16[2,192,512]{2,1,0:T(8,128)(2,1)} async-done(((bf16[2,192,1024]{2,1,0:T(8,128)(2,1)}), bf16[2,192,512]{2,1,0:T(8,128)(2,1)}) %reduce-scatter.3.cloned.1.call-update) | async-done | bytes 393232 | tf_op jit(solution)/shard_map/reduce_scatter | solution.py:118
  (89 shorter events, 9.5 us)
Async XLA Ops:
  7.2 114.4 %copy-start = (bf16[512,1024]{1,0:T(8,128)(2,1)S(1)}, bf16[512,1024]{1,0:T(8,128)(2,1)}, u32[]{:S(2)}) copy-start(bf16[512,1024]{1,0:T(8,128)(2,1)} %param.17) | copy-start | bytes 3145732
  7.2 125.2 %reduce-scatter.5.cloned.1.call-start = ((), (), s32[]{:S(2)}) async-start(), calls=%async_computation.3 | async-start | bytes 49152 | tf_op jit(solution)/shard_map/reduce_scatter | solution.py:112
  14.8 4.1 %copy-start.5 = (bf16[394,1024]{1,0:T(8,128)(2,1)}, bf16[394,1024]{1,0:T(8,128)(2,1)S(1)}, u32[]{:S(2)}) copy-start(bf16[394,1024]{1,0:T(8,128)(2,1)S(1)} %reshape.65) | copy-start | bytes 2420740
  16.9 8.1 %copy-start.9 = (s32[2,16]{1,0:T(2,128)S(1)}, s32[2,16]{1,0:T(2,128)}, u32[]{:S(2)}) copy-start(s32[2,16]{1,0:T(2,128)} %param.15) | copy-start | bytes 388
  20.1 51.3 %collective-permute-start.1 = (bf16[2,384,512]{2,1,0:T(8,128)(2,1)}, bf16[2,384,512]{2,1,0:T(8,128)(2,1)S(1)}, u32[]{:S(2)}, u32[]{:S(2)}) collective-permute-start(bf16[2,384,512]{2,1,0:T(8,128)(2,1)} %pad_maximum_fusion.1), channel_id=1, source_target_pairs={{14,0},{0,2},{2,4},{4,6},{6,8},{8,10},{10,12},{12,14},{15,1},{1,3}... | collective-permute-start | bytes 2359304 | tf_op jit(solution)/shard_map/ppermute | solution.py:12
  71.7 3.1 %copy-start.8 = (f32[8,394]{1,0:T(8,128)S(1)}, f32[8,394]{1,0:T(8,128)}, u32[]{:S(2)}) copy-start(f32[8,394]{1,0:T(8,128)} %get-tuple-element.325) | copy-start | bytes 37828
  71.7 3.4 %copy-start.2 = (pred[394,384]{1,0:T(8,128)(4,1)S(1)}, pred[394,384]{1,0:T(8,128)(4,1)}, u32[]{:S(2)}) copy-start(pred[394,384]{1,0:T(8,128)(4,1)} %copy.39) | copy-start | bytes 453892
  72.6 2.2 %copy-start.1 = (f32[8,394,80]{1,2,0:T(8,128)S(1)}, f32[8,394,80]{1,2,0:T(8,128)}, u32[]{:S(2)}) copy-start(f32[8,394,80]{1,2,0:T(8,128)} %get-tuple-element.326) | copy-start | bytes 3025924
  72.6 4.2 %copy-start.6 = (bf16[1,80,512]{1,2,0:T(8,128)(2,1)S(1)}, bf16[1,80,512]{1,2,0:T(8,128)(2,1)}, u32[]{:S(2)}) copy-start(bf16[1,80,512]{1,2,0:T(8,128)(2,1)} %copy.41) | copy-start | bytes 245764
  74.8 2.5 %copy-start.7 = (bf16[1,384,512]{1,2,0:T(8,128)(2,1)S(1)}, bf16[1,384,512]{1,2,0:T(8,128)(2,1)}, u32[]{:S(2)}) copy-start(bf16[1,384,512]{1,2,0:T(8,128)(2,1)} %copy.42) | copy-start | bytes 1179652
  77.2 2.8 %copy-start.10 = (s32[2,16]{1,0:T(2,128)S(1)}, s32[2,16]{1,0:T(2,128)}, u32[]{:S(2)}) copy-start(s32[2,16]{1,0:T(2,128)} %param.15) | copy-start | bytes 388
  80.1 14.2 %collective-permute-start = (bf16[2,384,512]{1,2,0:T(8,128)(2,1)S(1)}, bf16[2,384,512]{1,2,0:T(8,128)(2,1)S(1)}, u32[]{:S(2)}, u32[]{:S(2)}) collective-permute-start(bf16[2,384,512]{1,2,0:T(8,128)(2,1)S(1)} %get-tuple-element.405), channel_id=1, source_target_pairs={{2,0},{4,2},{6,4},{8,6},{10,8},{12,10},{14,12},{0,14},{3,1},{5,3},... | collective-permute-start | bytes 2359304 | tf_op jit(solution)/shard_map/while/body/eval_jaxpr/ppermute | solution.py:12
  94.3 3.0 %copy-start.3 = (f32[8,394,64]{1,2,0:T(8,128)S(1)}, f32[8,394,64]{1,2,0:T(8,128)}, u32[]{:S(2)}) copy-start(f32[8,394,64]{1,2,0:T(8,128)} %get-tuple-element.408) | copy-start | bytes 2420740 | tf_op jit(solution)/shard_map/while
  98.9 1.0 copy-start.4
  99.9 14.4 %collective-permute-start = (bf16[2,384,512]{1,2,0:T(8,128)(2,1)S(1)}, bf16[2,384,512]{1,2,0:T(8,128)(2,1)S(1)}, u32[]{:S(2)}, u32[]{:S(2)}) collective-permute-start(bf16[2,384,512]{1,2,0:T(8,128)(2,1)S(1)} %get-tuple-element.405), channel_id=1, source_target_pairs={{2,0},{4,2},{6,4},{8,6},{10,8},{12,10},{14,12},{0,14},{3,1},{5,3},... | collective-permute-start | bytes 2359304 | tf_op jit(solution)/shard_map/while/body/eval_jaxpr/ppermute | solution.py:12
  114.3 3.0 %copy-start.3 = (f32[8,394,64]{1,2,0:T(8,128)S(1)}, f32[8,394,64]{1,2,0:T(8,128)}, u32[]{:S(2)}) copy-start(f32[8,394,64]{1,2,0:T(8,128)} %get-tuple-element.408) | copy-start | bytes 2420740 | tf_op jit(solution)/shard_map/while
  118.9 1.0 copy-start.4
  122.8 21.8 %reduce-scatter.3.cloned.1.call-start = ((), (), s32[]{:S(2)}) async-start(), calls=%async_computation.2 | async-start | bytes 1179648 | tf_op jit(solution)/shard_map/reduce_scatter | solution.py:118
Sparse Core Ops, SparseCore 0:
  123.0 9.3 reduce-scatter.4
  135.2 9.4 reduce-scatter.2
where the time goes:
time: 152 us; the launch traced here: 151 us
  blocking collectives  46.4 us (31%)
  waiting for transfers between devices  40.7 us (27%)
  matrix products  19.1 us (13%)
  between operations  14.4 us (9%)
  local copies, waits for them, and re-layouts  11.6 us (8%)
  other arithmetic  10.4 us (7%)
  starting transfers between devices  8.61 us (6%)
    all_gather x1, blocking collectives, per_device(): lax.all_gather(special_pair, 'blk', axis=1, tiled=True)  41.5 us
    ppermute x3, waiting for transfers between devices, shifted(): return lax.ppermute(block, axis, route)  21.4 us
    reduce_scatter x1, waiting for transfers between devices, per_device(): lax.psum_scatter(partial_out[:, special_count:].astype(jnp.bfloat16), 'he...  10.9 us
    ppermute x3, starting transfers between devices, shifted(): return lax.ppermute(block, axis, route)  8.53 us
    reduce_scatter x1, waiting for transfers between devices, per_device(): lax.psum_scatter(partial_out[:, :special_count].astype(jnp.bfloat16), 'he...  8.32 us
    dot_general x4, matrix products, attend(): jnp.einsum('rhd,khd->hrk', queries, keys_part, preferred_element_type=jnp...  6.48 us
    dot_general x4, matrix products, attend(): jnp.einsum('hrk,khd->hrd', weights.astype(jnp.bfloat16), values_part, pre...  6 us
    reduce_sum x4, other arithmetic, attend(): denominator = denominator * factor + jnp.sum(weights, axis=2)  5.5 us
  transfers between devices with their start and end apart: 5, of which 4 were waited for; matrix products, arithmetic and copies ran while one was open for 7% of the time, Pallas kernels for 0%

commit v1 on v0

v1 whole, which is shorter than its diff:
```python
import functools

import jax
import jax.numpy as jnp
from jax import lax
from jax.experimental import pallas as pl
from jax.experimental.pallas import tpu as pltpu
from jax.sharding import PartitionSpec as P

HEAD_DIM = 64
PAIR = 2 * HEAD_DIM
TILE_ROWS = 16
BLOCKED = -(2.0**127)
VMEM_BYTES = 32 * 1024 * 1024


def shifted(block, axis, distance):
    count = lax.axis_size(axis)
    route = [((i - distance) % count, i) for i in range(count)]
    return lax.ppermute(block, axis, route)


def swapped(block, axis, bit):
    count = lax.axis_size(axis)
    return lax.ppermute(block, axis, [(i ^ bit, i) for i in range(count)])


def project(own, other, w_ref, which, half):
    depth = own.shape[1]
    mine = pl.ds(pl.multiple_of(half * depth, depth), depth)
    theirs = pl.ds(pl.multiple_of((1 - half) * depth, depth), depth)
    return jnp.dot(own, w_ref[which, mine, :], preferred_element_type=jnp.float32) + jnp.dot(
        other, w_ref[which, theirs, :], preferred_element_type=jnp.float32
    )


def lanes_of(sub):
    lane = lax.broadcasted_iota(jnp.int32, (1, PAIR), 1)
    in_head = (lane >= sub * HEAD_DIM) & (lane < (sub + 1) * HEAD_DIM)
    return in_head, lane - (1 - sub) * HEAD_DIM


def image_bias(covisible, owner, images, sub):
    spare = lanes_of(sub)[1]
    rows = []
    for b in range(images):
        row = jnp.zeros((1, PAIR), jnp.float32)
        for a in range(images):
            seen = covisible[a, owner * images + b] > 0
            row = jnp.where(spare == a, jnp.where(seen, 0.0, BLOCKED), row)
        rows.append(row)
    return rows


def patch_key_head(keys_pair, covisible, owner, images, sub):
    in_head = lanes_of(sub)[0]
    per_image = keys_pair.shape[0] // images
    rows = image_bias(covisible, owner, images, sub)
    return jnp.concatenate(
        [
            jnp.where(in_head, keys_pair[b * per_image : (b + 1) * per_image], rows[b])
            for b in range(images)
        ],
        axis=0,
    ).astype(jnp.bfloat16)


def special_key_head(keys_pair, real_rows, images, sub):
    in_head, spare = lanes_of(sub)
    row = lax.broadcasted_iota(jnp.int32, keys_pair.shape, 0) % TILE_ROWS
    blocked = (row >= real_rows) & (spare >= 0) & (spare < images)
    return jnp.where(in_head, keys_pair, jnp.where(blocked, BLOCKED, 0.0)).astype(jnp.bfloat16)


def value_head(values_pair, sub):
    return jnp.where(lanes_of(sub)[0], values_pair, 1.0).astype(jnp.bfloat16)


def score(queries, keys):
    return lax.dot_general(
        queries, keys, (((1,), (1,)), ((), ())), preferred_element_type=jnp.float32
    )


def attend(queries, keys, values, state):
    scores = score(queries, keys)
    largest = jnp.max(scores, axis=1, keepdims=True)
    if state is not None:
        before, total = state
        largest = jnp.maximum(before[:, :1], largest)
    weights = jnp.exp(scores - largest).astype(jnp.bfloat16)
    added = jnp.dot(weights, values, preferred_element_type=jnp.float32)
    if state is not None:
        added = added + total * jnp.exp(before - largest)
    return largest, added


def first_kernel(
    images, special_count, covisible, own, other, own_special, other_special, w_qkv,
    queries_out, largest_out, total_out,
):
    half = lax.axis_index("head")
    owner = lax.axis_index("blk")
    patch_total = own.shape[0]
    per_image = patch_total // images
    own_rows = jnp.concatenate([own[...], own_special[...]], axis=0)
    other_rows = jnp.concatenate([other[...], other_special[...]], axis=0)
    queries = project(own_rows, other_rows, w_qkv, 0, half) * HEAD_DIM ** (-0.5)
    keys = project(own[...], other[...], w_qkv, 1, half)
    values = project(own[...], other[...], w_qkv, 2, half)
    rows = queries.shape[0]
    row = lax.broadcasted_iota(jnp.int32, (rows, PAIR), 0)
    image = jnp.where(
        row < patch_total, row // per_image, jnp.minimum((row - patch_total) // special_count, images - 1)
    )
    for pair in range(queries.shape[1] // PAIR):
        cols = slice(pair * PAIR, (pair + 1) * PAIR)
        for sub in range(2):
            head = 2 * pair + sub
            in_head, spare = lanes_of(sub)
            mark = jnp.where(spare == image, 1.0, 0.0)
            query_head = jnp.where(in_head, queries[:, cols], mark).astype(jnp.bfloat16)
            queries_out[head] = query_head
            largest, total = attend(
                query_head,
                patch_key_head(keys[:, cols], covisible, owner, images, sub),
                value_head(values[:, cols], sub),
                None,
            )
            largest_out[head] = jnp.broadcast_to(largest, total.shape)
            total_out[head] = total


def neighbour_kernel(
    images, offset, covisible, own, other, w_qkv, queries, largest_in, total_in,
    largest_out, total_out,
):
    half = lax.axis_index("head")
    count = lax.axis_size("blk")
    owner = lax.rem(lax.axis_index("blk") + offset + count, count)
    keys = project(own[...], other[...], w_qkv, 1, half)
    values = project(own[...], other[...], w_qkv, 2, half)
    for head in range(queries.shape[0]):
        pair, sub = head // 2, head % 2
        cols = slice(pair * PAIR, (pair + 1) * PAIR)
        largest, total = attend(
            queries[head],
            patch_key_head(keys[:, cols], covisible, owner, images, sub),
            value_head(values[:, cols], sub),
            (largest_in[head], total_in[head]),
        )
        largest_out[head] = jnp.broadcast_to(largest, total.shape)
        total_out[head] = total


def last_kernel(
    images, offset, real_rows, covisible, own, other, own_special, other_special, w_qkv, w_out,
    queries, largest_in, total_in, kept_out, sent_out,
):
    half = lax.axis_index("head")
    count = lax.axis_size("blk")
    owner = lax.rem(lax.axis_index("blk") + offset + count, count)
    patch_total = own.shape[0]
    own_rows = jnp.concatenate([own[...], own_special[...]], axis=0)
    other_rows = jnp.concatenate([other[...], other_special[...]], axis=0)
    keys = project(own_rows, other_rows, w_qkv, 1, half)
    values = project(own_rows, other_rows, w_qkv, 2, half)
    lane = lax.broadcasted_iota(jnp.int32, (1, PAIR), 1)
    attended = []
    for pair in range(queries.shape[0] // 2):
        cols = slice(pair * PAIR, (pair + 1) * PAIR)
        totals = []
        for sub in range(2):
            head = 2 * pair + sub
            key_head = jnp.concatenate(
                [
                    patch_key_head(keys[:patch_total, cols], covisible, owner, images, sub),
                    special_key_head(keys[patch_total:, cols], real_rows, images, sub),
                ],
                axis=0,
            )
            totals.append(
                attend(
                    queries[head],
                    key_head,
                    value_head(values[:, cols], sub),
                    (largest_in[head], total_in[head]),
                )[1]
            )
        numerator = jnp.where(lane < HEAD_DIM, totals[0], totals[1])
        denominator = pltpu.roll(jnp.where(lane < HEAD_DIM, totals[1], totals[0]), HEAD_DIM, 1)
        attended.append((numerator / denominator).astype(jnp.bfloat16))
    attended = jnp.concatenate(attended, axis=1)
    width = kept_out.shape[1]
    mine = pl.ds(pl.multiple_of(half * width, width), width)
    theirs = pl.ds(pl.multiple_of((1 - half) * width, width), width)
    sent_out[...] = jnp.dot(
        attended, w_out[:, theirs], preferred_element_type=jnp.float32
    ).astype(jnp.bfloat16)
    kept_out[...] = jnp.dot(attended, w_out[:, mine], preferred_element_type=jnp.float32)


def call(kernel, out_shape, *operands):
    smem = pl.BlockSpec(memory_space=pltpu.SMEM)
    vmem = pl.BlockSpec(memory_space=pltpu.VMEM)
    return pl.pallas_call(
        kernel,
        out_shape=out_shape,
        in_specs=[smem] + [vmem] * (len(operands) - 1),
        out_specs=[vmem] * len(out_shape),
        compiler_params=pltpu.CompilerParams(vmem_limit_bytes=VMEM_BYTES),
    )(*operands)


def gathered(block, axis):
    count = lax.axis_size(axis)
    if count & (count - 1):
        return lax.all_gather(block, axis, axis=0, tiled=True)
    bit = 1
    while bit < count:
        block = jnp.concatenate([block, swapped(block, axis, bit)], axis=0)
        bit *= 2
    return block


def per_device(
    patch_rows, special_rows, role_first, role_rest, frame_order, covisible, w_qkv, w_out
):
    images, patch_count, width = patch_rows.shape
    special_count = special_rows.shape[1]
    real_rows = images * special_count
    padding = -real_rows % TILE_ROWS
    half = lax.axis_index("head")
    owner_count = lax.axis_size("blk")
    reach = max(1, owner_count // 64)

    own = patch_rows.reshape(images * patch_count, width)
    other = swapped(own, "head", 1)
    role = jnp.where(
        (frame_order == 0)[:, None, None],
        lax.dynamic_slice_in_dim(role_first, half * width, width, 1)[None],
        lax.dynamic_slice_in_dim(role_rest, half * width, width, 1)[None],
    )
    specials = special_rows.astype(jnp.float32) + role.astype(jnp.float32)
    specials = specials.astype(jnp.bfloat16).reshape(real_rows, width)
    specials = jnp.pad(specials, ((0, padding), (0, 0)))
    other_specials = swapped(specials, "head", 1)
    all_specials = gathered(specials, "blk")
    all_other_specials = swapped(all_specials, "head", 1)

    near = []
    for distance in range(1, reach + 1):
        for offset in (-distance, distance):
            near_own = shifted(own, "blk", -offset)
            near.append((offset, near_own, swapped(near_own, "head", 1)))

    head_count = width // HEAD_DIM
    rows = images * patch_count + real_rows + padding
    wide = jax.ShapeDtypeStruct((head_count, rows, PAIR), jnp.float32)
    queries, largest, total = call(
        functools.partial(first_kernel, images, special_count),
        [jax.ShapeDtypeStruct((head_count, rows, PAIR), jnp.bfloat16), wide, wide],
        covisible, own, other, specials, other_specials, w_qkv,
    )
    for offset, near_own, near_other in near[:-1]:
        largest, total = call(
            functools.partial(neighbour_kernel, images, offset),
            [wide, wide],
            covisible, near_own, near_other, w_qkv, queries, largest, total,
        )
    offset, near_own, near_other = near[-1]
    kept, sent = call(
        functools.partial(last_kernel, images, offset, real_rows),
        [
            jax.ShapeDtypeStruct((rows, width), jnp.float32),
            jax.ShapeDtypeStruct((rows, width), jnp.bfloat16),
        ],
        covisible, near_own, near_other, all_specials, all_other_specials, w_qkv, w_out,
        queries, largest, total,
    )
    received = swapped(sent, "head", 1)
    out = (kept + received.astype(jnp.float32)).astype(jnp.bfloat16)
    patch_total = images * patch_count
    return (
        out[:patch_total].reshape(images, patch_count, width),
        out[patch_total : patch_total + real_rows].reshape(images, special_count, width),
    )


def solution(mesh):
    in_specs = (
        P(("scene", "blk"), None, "head"),
        P(("scene", "blk"), None, "head"),
        P(),
        P(),
        P(("scene", "blk")),
        P(("scene", "blk"), None),
        P(None, None, "head"),
        P("head", None),
    )
    out_specs = (P(("scene", "blk"), None, "head"), P(("scene", "blk"), None, "head"))
    return jax.shard_map(
        per_device, mesh=mesh, in_specs=in_specs, out_specs=out_specs, check_vma=False
    )
```

time: 152 us -> 55.5 us (0.37)
  blocking collectives: 46.4 us -> 0 us
  waiting for transfers between devices: 40.7 us -> 21.4 us
  matrix products: 19.1 us -> 0 us
  Pallas kernels: 0 us -> 14.5 us
  between operations: 14.4 us -> 0.76 us
  other arithmetic: 10.4 us -> 1.6 us
  local copies, waits for them, and re-layouts: 11.6 us -> 5.71 us
  starting transfers between devices: 8.61 us -> 11.2 us
    all_gather x3 -> x0, blocking collectives: 46.4 us -> none  [the longest x1 41.5 us: per_device(): lax.all_gather(special_pair, 'blk', axis=1, tiled=True)]
    ppermute x3 -> x2, waiting for transfers between devices: 21.4 us -> 0.01 us  [shifted(): return lax.ppermute(block, axis, route)]
    ppermute x0 -> x9, waiting for transfers between devices: none -> 21.4 us  [swapped(): return lax.ppermute(block, axis, [(i ^ bit, i) for i in range(count)])]
    reduce_scatter x2 -> x0, waiting for transfers between devices: 19.3 us -> none  [the longest x1 10.9 us: per_device(): lax.psum_scatter(partial_out[:, special_count:].astype(jnp.bfloat16), 'he...]
    dot_general x12 -> x0, matrix products: 19.1 us -> none  [the longest x4 6.48 us: attend(): jnp.einsum('rhd,khd->hrk', queries, keys_part, preferred_element_type=jnp...]
    pallas_call x0 -> x3, Pallas kernels: none -> 14.5 us  [call(): pl.pallas_call(kernel, out_shape=out_shape, in_specs=[smem] + [vmem] * (l...]
    reduce_sum x4 -> x0, other arithmetic: 5.5 us -> none  [attend(): denominator = denominator * factor + jnp.sum(weights, axis=2)]
    ppermute x0 -> x9, starting transfers between devices: none -> 5.15 us  [swapped(): return lax.ppermute(block, axis, [(i ^ bit, i) for i in range(count)])]
  transfers between devices with their start and end apart: 5 -> 11, of which waited for: 4 -> 5; matrix products, arithmetic and copies ran while one was open for 7% -> 4% of each run, Pallas kernels for 0% -> 16%
where the time goes in v1:
time: 55.5 us; the launch traced here: 55.2 us
  waiting for transfers between devices  21.4 us (39%)
  Pallas kernels  14.5 us (26%)
  starting transfers between devices  11.2 us (20%)
  local copies, waits for them, and re-layouts  5.71 us (10%)
  other arithmetic  1.6 us (3%)
  between operations  0.76 us (1%)
    ppermute x9, waiting for transfers between devices, swapped(): return lax.ppermute(block, axis, [(i ^ bit, i) for i in range(count)])  21.4 us
    pallas_call x3, Pallas kernels, call(): pl.pallas_call(kernel, out_shape=out_shape, in_specs=[smem] + [vmem] * (l...  14.5 us
    ppermute x2, starting transfers between devices, shifted(): return lax.ppermute(block, axis, route)  6.1 us
    ppermute x9, starting transfers between devices, swapped(): return lax.ppermute(block, axis, [(i ^ bit, i) for i in range(count)])  5.15 us
    unnamed x11, local copies, waits for them, and re-layouts  4.18 us
  transfers between devices with their start and end apart: 11, of which 5 were waited for; matrix products, arithmetic and copies ran while one was open for 4% of the time, Pallas kernels for 16%

profile of v1, /device:TPU:0, one launch (start us, length us, event | category | flops | bytes accessed | tf_op | source)
XLA Modules:
  0.0 55.2 jit_solution(10336081257730835333)
XLA Ops:
  0.6 3.0 %collective-permute-start.8 = (bf16[384,512]{1,0:T(8,128)(2,1)}, bf16[384,512]{1,0:T(8,128)(2,1)S(1)}, u32[]{:S(2)}, u32[]{:S(2)}) collective-permute-start(bf16[384,512]{1,0:T(8,128)(2,1)} %bitcast.2), channel_id=1, source_target_pairs={{14,0},{0,2},{2,4},{4,6},{6,8},{8,10},{10,12},{12,14},{15,1},{1,3}... | collective-permute-start | bytes 1179656 | tf_op jit(solution)/shard_map/ppermute | solution.py:20
  3.6 3.1 %collective-permute-start = (bf16[384,512]{1,0:T(8,128)(2,1)}, bf16[384,512]{1,0:T(8,128)(2,1)S(1)}, u32[]{:S(2)}, u32[]{:S(2)}) collective-permute-start(bf16[384,512]{1,0:T(8,128)(2,1)} %bitcast.3), channel_id=1, source_target_pairs={{2,0},{4,2},{6,4},{8,6},{10,8},{12,10},{14,12},{0,14},{3,1},{5,3},... | collective-permute-start | bytes 1179656 | tf_op jit(solution)/shard_map/ppermute | solution.py:20
  6.7 0.7 %broadcast_compare_fusion = pred[2]{0:T(512)(128)(4,1)S(1)} fusion(s32[2]{0:T(128)} %param.12), kind=kLoop, calls=%fused_computation.8 | loop fusion | flops 2 | bytes 10 | tf_op jit(solution)/shard_map/eq | solution.py:240
  7.4 0.7 %constant_dynamic-slice_fusion = (bf16[5,512]{1,0:T(8,128)(2,1)S(1)}, bf16[5,512]{1,0:T(8,128)(2,1)S(1)}) fusion(bf16[5,1024]{1,0:T(8,128)(2,1)} %param.11, s32[]{:T(128)S(6)} %select_n.8, bf16[5,1024]{1,0:T(8,128)(2,1)} %param.10), kind=kLoop, calls=%fused_computation.6 | loop fusion | bytes 20484 | tf_op jit(solution)/shard_map/dynamic_slice | solution.py:242
  8.1 0.8 %add_convert_fusion.1 = bf16[2,5,512]{2,0,1:T(2,128)(2,1)S(1)} fusion(bf16[2,5,512]{2,0,1:T(2,128)(2,1)} %param.9, pred[2]{0:T(512)(128)(4,1)S(1)} %broadcast_compare_fusion, bf16[5,512]{1,0:T(8,128)(2,1)S(1)} %get-tuple-element.20, bf16[5,512]{1,0:T(8,128)(2,1)S(1)} %get-tuple-element.21), kind=kLoop, calls=%fused_computation.4 | loop fusion | flops 25600 | bytes 30722 | tf_op jit(solution)/shard_map/convert_element_type | solution.py:245
  8.9 0.1 collective-permute-start.2
  9.0 14.2 %collective-permute-done.2 = bf16[16,512]{1,0:T(8,128)(2,1)S(1)} collective-permute-done((bf16[16,512]{1,0:T(8,128)(2,1)S(1)}, bf16[16,512]{1,0:T(8,128)(2,1)S(1)}, u32[]{:S(2)}, u32[]{:S(2)}) %collective-permute-start.2) | collective-permute-done | bytes 16416 | tf_op jit(solution)/shard_map/ppermute | solution.py:25
  23.2 1.3 %collective-permute-start.3 = (bf16[32,512]{1,0:T(8,128)(2,1)S(1)}, bf16[32,512]{1,0:T(8,128)(2,1)S(1)}, u32[]{:S(2)}, u32[]{:S(2)}) collective-permute-start(bf16[32,512]{1,0:T(8,128)(2,1)S(1)} %pad_maximum_fusion.2), channel_id=1, source_target_pairs={{4,0},{6,2},{0,4},{2,6},{12,8},{14,10},{8,12},{10,14},{5,1},{7,3},... | collective-permute-start | bytes 98312 | tf_op jit(solution)/shard_map/ppermute | solution.py:25
  24.5 0.0 collective-permute-start.6
  24.5 0.0 collective-permute-done.8.own
  24.5 0.5 collective-permute-start.9
  25.0 0.0 collective-permute-done.own
  25.0 0.1 collective-permute-start.1
  25.0 2.1 %collective-permute-done.3 = bf16[32,512]{1,0:T(8,128)(2,1)S(1)} collective-permute-done((bf16[32,512]{1,0:T(8,128)(2,1)S(1)}, bf16[32,512]{1,0:T(8,128)(2,1)S(1)}, u32[]{:S(2)}, u32[]{:S(2)}) %collective-permute-start.3) | collective-permute-done | bytes 32800 | tf_op jit(solution)/shard_map/ppermute | solution.py:25
  27.1 2.3 %collective-permute-start.4 = (bf16[64,512]{1,0:T(8,128)(2,1)S(1)}, bf16[64,512]{1,0:T(8,128)(2,1)S(1)}, u32[]{:S(2)}, u32[]{:S(2)}) collective-permute-start(bf16[64,512]{1,0:T(8,128)(2,1)S(1)} %pad_maximum_fusion.1), channel_id=1, source_target_pairs={{8,0},{10,2},{12,4},{14,6},{0,8},{2,10},{4,12},{6,14},{9,1},{11,3}... | collective-permute-start | bytes 196616 | tf_op jit(solution)/shard_map/ppermute | solution.py:25
  29.4 2.9 %collective-permute-done.4 = bf16[64,512]{1,0:T(8,128)(2,1)S(1)} collective-permute-done((bf16[64,512]{1,0:T(8,128)(2,1)S(1)}, bf16[64,512]{1,0:T(8,128)(2,1)S(1)}, u32[]{:S(2)}, u32[]{:S(2)}) %collective-permute-start.4) | collective-permute-done | bytes 65568 | tf_op jit(solution)/shard_map/ppermute | solution.py:25
  32.3 0.1 collective-permute-start.5
  32.4 0.5 collective-permute-start.7
  32.9 0.9 %collective-permute-done.7.other_special = bf16[16,512]{1,0:T(8,128)(2,1)S(1)} collective-permute-done((bf16[16,512]{1,0:T(8,128)(2,1)S(1)}, bf16[16,512]{1,0:T(8,128)(2,1)S(1)}, u32[]{:S(2)}, u32[]{:S(2)}) %collective-permute-start.7) | collective-permute-done | bytes 16416 | tf_op jit(solution)/shard_map/ppermute | solution.py:25
  33.7 1.9 %copy-done = bf16[3,1024,512]{2,1,0:T(8,128)(2,1)S(1)} copy-done((bf16[3,1024,512]{2,1,0:T(8,128)(2,1)S(1)}, bf16[3,1024,512]{2,1,0:T(8,128)(2,1)}, u32[]{:S(2)}) %copy-start) | copy-done | bytes 3145752
  35.6 1.0 %copy-done.3 = bf16[2,192,512]{2,1,0:T(8,128)(2,1)S(1)} copy-done((bf16[2,192,512]{2,1,0:T(8,128)(2,1)S(1)}, bf16[2,192,512]{2,1,0:T(8,128)(2,1)}, u32[]{:S(2)}) %copy-start.3) | copy-done | bytes 393240
  36.6 0.7 %copy-done.4 = s32[2,16]{1,0:T(2,128)S(1)} copy-done((s32[2,16]{1,0:T(2,128)S(1)}, s32[2,16]{1,0:T(2,128)}, u32[]{:S(2)}) %copy-start.4) | copy-done | bytes 152
  37.3 4.0 %shard_map.95 = (bf16[8,400,128]{2,1,0:T(8,128)(2,1)S(1)}, f32[8,400,128]{2,1,0:T(8,128)S(1)}, f32[8,400,128]{2,1,0:T(8,128)S(1)}) custom-call(s32[2,16]{1,0:T(2,128)S(1)} %copy-done.4, bf16[384,512]{1,0:T(8,128)(2,1)S(1)} %bitcast.5, bf16[384,512]{1,0:T(8,128)(2,1)S(1)} %collective-permute-done.6.other, bf16[16,512]{1,0:T(8,128)(2,1)S(1)} %pad.4.own_special, ...), custom_call_target="tpu_custom_call" | custom-call | tf_op jit(solution)/shard_map/pallas_call | solution.py:206
  41.3 0.0 collective-permute-done.9.other
  41.4 0.0 copy-start.2
  41.4 4.7 %shard_map.96 = (f32[8,400,128]{2,1,0:T(8,128)S(1)}, f32[8,400,128]{2,1,0:T(8,128)S(1)}) custom-call(s32[2,16]{1,0:T(2,128)S(1)} %copy-done.4, bf16[384,512]{1,0:T(8,128)(2,1)S(1)} %collective-permute-done.8.own, bf16[384,512]{1,0:T(8,128)(2,1)S(1)} %collective-permute-done.9.other, bf16[3,1024,512]{2,1,0:T(8,128)(2,1)S(1)} %copy-done.1, ...), custom_call_target="tpu_custom_call" | custom-call | tf_op jit(solution)/shard_map/pallas_call | solution.py:206
  46.1 5.7 %shard_map.97 = (f32[400,512]{1,0:T(8,128)S(1)}, bf16[400,512]{1,0:T(8,128)(2,1)S(1)}) custom-call(s32[2,16]{1,0:T(2,128)S(1)} %copy-done.4, bf16[384,512]{1,0:T(8,128)(2,1)S(1)} %collective-permute-done.own, bf16[384,512]{1,0:T(8,128)(2,1)S(1)} %collective-permute-done.1.other, bf16[128,512]{1,0:T(8,128)(2,1)S(1)} %pad_maximum_fusion.own_special, ...), custom_call_target="tpu_custom_call" | custom-call | tf_op jit(solution)/shard_map/pallas_call | solution.py:206
  51.8 0.4 collective-permute-start.10
  52.2 1.4 %collective-permute-done.10 = bf16[400,512]{1,0:T(8,128)(2,1)S(1)} collective-permute-done((bf16[400,512]{1,0:T(8,128)(2,1)S(1)}, bf16[400,512]{1,0:T(8,128)(2,1)S(1)}, u32[]{:S(2)}, u32[]{:S(2)}) %collective-permute-start.10) | collective-permute-done | bytes 409632 | tf_op jit(solution)/shard_map/ppermute | solution.py:25
  53.6 0.1 add_convert_fusion
  53.8 0.8 %slice.8 = bf16[384,512]{1,0:T(8,128)(2,1)} slice(bf16[400,512]{1,0:T(8,128)(2,1)S(1)} %add_convert_fusion), slice={[0:384], [0:512]} | slice | bytes 786432 | tf_op jit(solution)/shard_map/slice | solution.py:285
  54.6 0.6 %copy.13 = bf16[2,5,512]{2,0,1:T(2,128)(2,1)} copy(bf16[2,5,512]{2,1,0:T(8,128)(2,1)S(1)} %reshape.22) | data formatting | bytes 20480
  (17 shorter events, 0.1 us)
Async XLA Ops:
  0.6 23.8 %collective-permute-start.8 = (bf16[384,512]{1,0:T(8,128)(2,1)}, bf16[384,512]{1,0:T(8,128)(2,1)S(1)}, u32[]{:S(2)}, u32[]{:S(2)}) collective-permute-start(bf16[384,512]{1,0:T(8,128)(2,1)} %bitcast.2), channel_id=1, source_target_pairs={{14,0},{0,2},{2,4},{4,6},{6,8},{8,10},{10,12},{12,14},{15,1},{1,3}... | collective-permute-start | bytes 1179656 | tf_op jit(solution)/shard_map/ppermute | solution.py:20
  3.6 21.3 %collective-permute-start = (bf16[384,512]{1,0:T(8,128)(2,1)}, bf16[384,512]{1,0:T(8,128)(2,1)S(1)}, u32[]{:S(2)}, u32[]{:S(2)}) collective-permute-start(bf16[384,512]{1,0:T(8,128)(2,1)} %bitcast.3), channel_id=1, source_target_pairs={{2,0},{4,2},{6,4},{8,6},{10,8},{12,10},{14,12},{0,14},{3,1},{5,3},... | collective-permute-start | bytes 1179656 | tf_op jit(solution)/shard_map/ppermute | solution.py:20
  8.9 14.2 %collective-permute-start.2 = (bf16[16,512]{1,0:T(8,128)(2,1)S(1)}, bf16[16,512]{1,0:T(8,128)(2,1)S(1)}, u32[]{:S(2)}, u32[]{:S(2)}) collective-permute-start(bf16[16,512]{1,0:T(8,128)(2,1)S(1)} %pad.4.own_special), channel_id=1, source_target_pairs={{2,0},{0,2},{6,4},{4,6},{10,8},{8,10},{14,12},{12,14},{3,1},{1,3},... | collective-permute-start | bytes 49160 | tf_op jit(solution)/shard_map/ppermute | solution.py:25
  23.2 3.9 %collective-permute-start.3 = (bf16[32,512]{1,0:T(8,128)(2,1)S(1)}, bf16[32,512]{1,0:T(8,128)(2,1)S(1)}, u32[]{:S(2)}, u32[]{:S(2)}) collective-permute-start(bf16[32,512]{1,0:T(8,128)(2,1)S(1)} %pad_maximum_fusion.2), channel_id=1, source_target_pairs={{4,0},{6,2},{0,4},{2,6},{12,8},{14,10},{8,12},{10,14},{5,1},{7,3},... | collective-permute-start | bytes 98312 | tf_op jit(solution)/shard_map/ppermute | solution.py:25
  24.5 9.3 %collective-permute-start.6 = (bf16[384,512]{1,0:T(8,128)(2,1)}, bf16[384,512]{1,0:T(8,128)(2,1)S(1)}, u32[]{:S(2)}, u32[]{:S(2)}) collective-permute-start(bf16[384,512]{1,0:T(8,128)(2,1)} %bitcast.4), channel_id=1, source_target_pairs={{1,0},{0,1},{3,2},{2,3},{5,4},{4,5},{7,6},{6,7},{9,8},{8,9},{11,10... | collective-permute-start | bytes 1179656 | tf_op jit(solution)/shard_map/ppermute | solution.py:25
  24.5 16.9 %collective-permute-start.9 = (bf16[384,512]{1,0:T(8,128)(2,1)S(1)}, bf16[384,512]{1,0:T(8,128)(2,1)S(1)}, u32[]{:S(2)}, u32[]{:S(2)}) collective-permute-start(bf16[384,512]{1,0:T(8,128)(2,1)S(1)} %collective-permute-done.8.own), channel_id=1, source_target_pairs={{1,0},{0,1},{3,2},{2,3},{5,4},{4,5},{7,6},{6,7},{9,8},{8,9},{11,10... | collective-permute-start | bytes 1179656 | tf_op jit(solution)/shard_map/ppermute | solution.py:25
  25.0 21.1 %collective-permute-start.1 = (bf16[384,512]{1,0:T(8,128)(2,1)S(1)}, bf16[384,512]{1,0:T(8,128)(2,1)S(1)}, u32[]{:S(2)}, u32[]{:S(2)}) collective-permute-start(bf16[384,512]{1,0:T(8,128)(2,1)S(1)} %collective-permute-done.own), channel_id=1, source_target_pairs={{1,0},{0,1},{3,2},{2,3},{5,4},{4,5},{7,6},{6,7},{9,8},{8,9},{11,10... | collective-permute-start | bytes 1179656 | tf_op jit(solution)/shard_map/ppermute | solution.py:25
  27.1 5.2 %collective-permute-start.4 = (bf16[64,512]{1,0:T(8,128)(2,1)S(1)}, bf16[64,512]{1,0:T(8,128)(2,1)S(1)}, u32[]{:S(2)}, u32[]{:S(2)}) collective-permute-start(bf16[64,512]{1,0:T(8,128)(2,1)S(1)} %pad_maximum_fusion.1), channel_id=1, source_target_pairs={{8,0},{10,2},{12,4},{14,6},{0,8},{2,10},{4,12},{6,14},{9,1},{11,3}... | collective-permute-start | bytes 196616 | tf_op jit(solution)/shard_map/ppermute | solution.py:25
  32.3 13.8 %collective-permute-start.5 = (bf16[128,512]{1,0:T(8,128)(2,1)S(1)}, bf16[128,512]{1,0:T(8,128)(2,1)S(1)}, u32[]{:S(2)}, u32[]{:S(2)}) collective-permute-start(bf16[128,512]{1,0:T(8,128)(2,1)S(1)} %pad_maximum_fusion.own_special), channel_id=1, source_target_pairs={{1,0},{0,1},{3,2},{2,3},{5,4},{4,5},{7,6},{6,7},{9,8},{8,9},{11,10... | collective-permute-start | bytes 393224 | tf_op jit(solution)/shard_map/ppermute | solution.py:25
  32.4 1.4 %collective-permute-start.7 = (bf16[16,512]{1,0:T(8,128)(2,1)S(1)}, bf16[16,512]{1,0:T(8,128)(2,1)S(1)}, u32[]{:S(2)}, u32[]{:S(2)}) collective-permute-start(bf16[16,512]{1,0:T(8,128)(2,1)S(1)} %pad.4.own_special), channel_id=1, source_target_pairs={{1,0},{0,1},{3,2},{2,3},{5,4},{4,5},{7,6},{6,7},{9,8},{8,9},{11,10... | collective-permute-start | bytes 49160 | tf_op jit(solution)/shard_map/ppermute | solution.py:25
  33.7 1.9 %copy-start = (bf16[3,1024,512]{2,1,0:T(8,128)(2,1)S(1)}, bf16[3,1024,512]{2,1,0:T(8,128)(2,1)}, u32[]{:S(2)}) copy-start(bf16[3,1024,512]{2,1,0:T(8,128)(2,1)} %w_qkv.5) | copy-start | bytes 9437188
  35.6 1.0 %copy-start.3 = (bf16[2,192,512]{2,1,0:T(8,128)(2,1)S(1)}, bf16[2,192,512]{2,1,0:T(8,128)(2,1)}, u32[]{:S(2)}) copy-start(bf16[2,192,512]{2,1,0:T(8,128)(2,1)} %param.8) | copy-start | bytes 1179652
  36.6 0.7 %copy-start.4 = (s32[2,16]{1,0:T(2,128)S(1)}, s32[2,16]{1,0:T(2,128)}, u32[]{:S(2)}) copy-start(s32[2,16]{1,0:T(2,128)} %covisible.5) | copy-start | bytes 388
  37.3 4.1 %copy-start.1 = (bf16[3,1024,512]{2,1,0:T(8,128)(2,1)S(1)}, bf16[3,1024,512]{2,1,0:T(8,128)(2,1)}, u32[]{:S(2)}) copy-start(bf16[3,1024,512]{2,1,0:T(8,128)(2,1)} %w_qkv.5) | copy-start | bytes 9437188
  41.4 4.7 %copy-start.2 = (bf16[512,1024]{1,0:T(8,128)(2,1)S(1)}, bf16[512,1024]{1,0:T(8,128)(2,1)}, u32[]{:S(2)}) copy-start(bf16[512,1024]{1,0:T(8,128)(2,1)} %w_out.1) | copy-start | bytes 3145732
  51.8 1.8 %collective-permute-start.10 = (bf16[400,512]{1,0:T(8,128)(2,1)S(1)}, bf16[400,512]{1,0:T(8,128)(2,1)S(1)}, u32[]{:S(2)}, u32[]{:S(2)}) collective-permute-start(bf16[400,512]{1,0:T(8,128)(2,1)S(1)} %get-tuple-element.15), channel_id=1, source_target_pairs={{1,0},{0,1},{3,2},{2,3},{5,4},{4,5},{7,6},{6,7},{9,8},{8,9},{11,10... | collective-permute-start | bytes 1228808 | tf_op jit(solution)/shard_map/ppermute | solution.py:25

commit v2 on v1

v2 whole, which is shorter than its diff:
```python
import functools

import jax
import jax.numpy as jnp
from jax import lax
from jax.experimental import pallas as pl
from jax.experimental.pallas import tpu as pltpu
from jax.sharding import PartitionSpec as P

HEAD_DIM = 64
PAIR = 2 * HEAD_DIM
TILE_ROWS = 16
BLOCKED = -(2.0**127)
VMEM_BYTES = 32 * 1024 * 1024


def shifted(block, axis, distance):
    count = lax.axis_size(axis)
    route = [((i - distance) % count, i) for i in range(count)]
    return lax.ppermute(block, axis, route)


def swapped(block, axis, bit):
    count = lax.axis_size(axis)
    return lax.ppermute(block, axis, [(i ^ bit, i) for i in range(count)])


def project(own, other, w_ref, which, half):
    depth = own.shape[1]
    mine = pl.ds(pl.multiple_of(half * depth, depth), depth)
    theirs = pl.ds(pl.multiple_of((1 - half) * depth, depth), depth)
    return jnp.dot(own, w_ref[which, mine, :], preferred_element_type=jnp.float32) + jnp.dot(
        other, w_ref[which, theirs, :], preferred_element_type=jnp.float32
    )


def lanes_of(sub):
    lane = lax.broadcasted_iota(jnp.int32, (1, PAIR), 1)
    in_head = (lane >= sub * HEAD_DIM) & (lane < (sub + 1) * HEAD_DIM)
    return in_head, lane - (1 - sub) * HEAD_DIM


def image_bias(covisible, source, images, sub):
    owner, b = source
    spare = lanes_of(sub)[1]
    row = jnp.zeros((1, PAIR), jnp.float32)
    for a in range(images):
        seen = covisible[a, owner * images + b] > 0
        row = jnp.where(spare == a, jnp.where(seen, 0.0, BLOCKED), row)
    return row


def patch_key_head(keys_pair, covisible, sources, images, sub):
    in_head = lanes_of(sub)[0]
    per_image = keys_pair.shape[0] // len(sources)
    return jnp.concatenate(
        [
            jnp.where(
                in_head,
                keys_pair[i * per_image : (i + 1) * per_image],
                image_bias(covisible, source, images, sub),
            )
            for i, source in enumerate(sources)
        ],
        axis=0,
    ).astype(jnp.bfloat16)


def special_key_head(keys_pair, real_rows, images, sub):
    in_head, spare = lanes_of(sub)
    row = lax.broadcasted_iota(jnp.int32, keys_pair.shape, 0) % TILE_ROWS
    blocked = (row >= real_rows) & (spare >= 0) & (spare < images)
    return jnp.where(in_head, keys_pair, jnp.where(blocked, BLOCKED, 0.0)).astype(jnp.bfloat16)


def value_head(values_pair, sub):
    return jnp.where(lanes_of(sub)[0], values_pair, 1.0).astype(jnp.bfloat16)


def score(queries, keys):
    return lax.dot_general(
        queries, keys, (((1,), (1,)), ((), ())), preferred_element_type=jnp.float32
    )


def attend(queries, keys, values, state):
    scores = score(queries, keys)
    largest = jnp.max(scores, axis=1, keepdims=True)
    if state is not None:
        before, total = state
        largest = jnp.maximum(before[:, :1], largest)
    weights = jnp.exp(scores - largest).astype(jnp.bfloat16)
    added = jnp.dot(weights, values, preferred_element_type=jnp.float32)
    if state is not None:
        added = added + total * jnp.exp(before - largest)
    return largest, added


def start_kernel(
    special_count, frame_order, patches, specials, role_first, role_rest,
    own_out, early_out, late_out, special_out, copied,
):
    images, per_image, width = patches.shape
    copies = []
    for b in range(images):
        rows = pl.ds(b * per_image, per_image)
        copies.append(pltpu.make_async_copy(patches.at[b], own_out.at[rows], copied.at[2 * b]))
        target = early_out.at[pl.ds(0, per_image)] if b == 0 else late_out
        copies.append(pltpu.make_async_copy(patches.at[b], target, copied.at[2 * b + 1]))
    for copy in copies:
        copy.start()
    half = lax.axis_index("head")
    columns = pl.ds(pl.multiple_of(half * width, width), width)
    first = role_first[:, columns].astype(jnp.float32)
    rest = role_rest[:, columns].astype(jnp.float32)
    summed = [
        specials[:, b, :].astype(jnp.float32) + jnp.where(frame_order[b] == 0, first, rest)
        for b in range(images)
    ]
    padding = special_out.shape[0] - images * special_count
    summed.append(jnp.zeros((padding, width), jnp.float32))
    block = jnp.concatenate(summed, axis=0).astype(jnp.bfloat16)
    special_out[...] = block
    own_out[images * per_image :, :] = block
    early_out[per_image:, :] = block
    for copy in copies:
        copy.wait()


def first_kernel(
    images, special_count, patch_total, covisible, own, other, w_qkv,
    queries_out, largest_out, total_out,
):
    half = lax.axis_index("head")
    owner = lax.axis_index("blk")
    per_image = patch_total // images
    queries = project(own[...], other[...], w_qkv, 0, half) * HEAD_DIM ** (-0.5)
    keys = project(own[:patch_total, :], other[:patch_total, :], w_qkv, 1, half)
    values = project(own[:patch_total, :], other[:patch_total, :], w_qkv, 2, half)
    rows = queries.shape[0]
    row = lax.broadcasted_iota(jnp.int32, (rows, PAIR), 0)
    image = jnp.where(
        row < patch_total, row // per_image, jnp.minimum((row - patch_total) // special_count, images - 1)
    )
    for pair in range(queries.shape[1] // PAIR):
        cols = slice(pair * PAIR, (pair + 1) * PAIR)
        for sub in range(2):
            head = 2 * pair + sub
            in_head, spare = lanes_of(sub)
            mark = jnp.where(spare == image, 1.0, 0.0)
            query_head = jnp.where(in_head, queries[:, cols], mark).astype(jnp.bfloat16)
            queries_out[head] = query_head
            largest, total = attend(
                query_head,
                patch_key_head(keys[:, cols], covisible, [(owner, b) for b in range(images)], images, sub),
                value_head(values[:, cols], sub),
                None,
            )
            largest_out[head] = jnp.broadcast_to(largest, total.shape)
            total_out[head] = total


def owner_at(offset):
    count = lax.axis_size("blk")
    here = lax.axis_index("blk")
    if isinstance(offset, tuple):
        offset = jnp.where(lax.rem(here, 2) == 0, offset[0], offset[1])
    return lax.rem(here + offset + count, count)


def later_kernel(images, blocks, special_count, per_image, covisible, *refs):
    inputs, refs = refs[: 2 * len(blocks)], refs[2 * len(blocks) :]
    last = special_count > 0
    if last:
        own_special, other_special, w_qkv, w_out, queries, largest_in, total_in, kept_out, sent_out = refs
    else:
        w_qkv, queries, largest_in, total_in, largest_out, total_out = refs
    half = lax.axis_index("head")
    own_rows = [ref[:per_image, :] for ref in inputs[: len(blocks)]]
    other_rows = [ref[:per_image, :] for ref in inputs[len(blocks) :]]
    if last:
        own_rows.append(own_special[...])
        other_rows.append(other_special[...])
    own_rows = jnp.concatenate(own_rows, axis=0)
    other_rows = jnp.concatenate(other_rows, axis=0)
    keys = project(own_rows, other_rows, w_qkv, 1, half)
    values = project(own_rows, other_rows, w_qkv, 2, half)
    patch_total = per_image * len(blocks)
    sources = [(owner_at(offset), b) for offset, b in blocks]
    lane = lax.broadcasted_iota(jnp.int32, (1, PAIR), 1)
    attended = []
    for pair in range(queries.shape[0] // 2):
        cols = slice(pair * PAIR, (pair + 1) * PAIR)
        totals = []
        for sub in range(2):
            head = 2 * pair + sub
            key_head = patch_key_head(keys[:patch_total, cols], covisible, sources, images, sub)
            if last:
                special = special_key_head(keys[patch_total:, cols], images * special_count, images, sub)
                key_head = jnp.concatenate([key_head, special], axis=0)
            largest, total = attend(
                queries[head], key_head, value_head(values[:, cols], sub), (largest_in[head], total_in[head])
            )
            totals.append(total)
            if not last:
                largest_out[head] = jnp.broadcast_to(largest, total.shape)
                total_out[head] = total
        if last:
            numerator = jnp.where(lane < HEAD_DIM, totals[0], totals[1])
            denominator = pltpu.roll(jnp.where(lane < HEAD_DIM, totals[1], totals[0]), HEAD_DIM, 1)
            attended.append((numerator / denominator).astype(jnp.bfloat16))
    if last:
        attended = jnp.concatenate(attended, axis=1)
        width = kept_out.shape[1]
        mine = pl.ds(pl.multiple_of(half * width, width), width)
        theirs = pl.ds(pl.multiple_of((1 - half) * width, width), width)
        sent_out[...] = jnp.dot(
            attended, w_out[:, theirs], preferred_element_type=jnp.float32
        ).astype(jnp.bfloat16)
        kept_out[...] = jnp.dot(attended, w_out[:, mine], preferred_element_type=jnp.float32)


def end_kernel(images, kept, received, patch_out, special_out):
    patch_total = patch_out.shape[0]
    special_count = special_out.shape[0]
    patch_out[...] = (kept[:patch_total, :] + received[:patch_total, :].astype(jnp.float32)).astype(
        jnp.bfloat16
    )
    rest = kept[patch_total:, :] + received[patch_total:, :].astype(jnp.float32)
    rows = [rest[b * special_count : (b + 1) * special_count][:, None, :] for b in range(images)]
    special_out[...] = jnp.concatenate(rows, axis=1).astype(jnp.bfloat16)


SMEM = pl.BlockSpec(memory_space=pltpu.SMEM)
VMEM = pl.BlockSpec(memory_space=pltpu.VMEM)
HBM = pl.BlockSpec(memory_space=pl.ANY)


def call(kernel, out_shape, operands, in_specs=None, out_specs=None, scratch=()):
    return pl.pallas_call(
        kernel,
        out_shape=out_shape,
        in_specs=in_specs or [SMEM] + [VMEM] * (len(operands) - 1),
        out_specs=out_specs or [VMEM] * len(out_shape),
        scratch_shapes=scratch,
        compiler_params=pltpu.CompilerParams(vmem_limit_bytes=VMEM_BYTES),
    )(*operands)


def gathered(block, axis, bit):
    count = lax.axis_size(axis)
    if count & (count - 1):
        return lax.all_gather(block, axis, axis=0, tiled=True)
    while bit < count:
        block = jnp.concatenate([block, swapped(block, axis, bit)], axis=0)
        bit *= 2
    return block


def after(array, *others):
    return lax.optimization_barrier((array, *others))[0]


def relayed(block, axis):
    count = lax.axis_size(axis)
    return lax.ppermute(block, axis, [(i, (i + (2 if i % 2 == 0 else -2)) % count) for i in range(count)])


def per_device(
    patch_rows, special_rows, role_first, role_rest, frame_order, covisible, w_qkv, w_out
):
    images, per_image, width = patch_rows.shape
    special_count = special_rows.shape[1]
    real_rows = images * special_count
    special_block = real_rows + -real_rows % TILE_ROWS
    owner_count = lax.axis_size("blk")
    reach = max(1, owner_count // 64)
    patch_total = images * per_image
    rows = patch_total + special_block
    head_count = width // HEAD_DIM
    narrow = lambda count: jax.ShapeDtypeStruct((count, width), jnp.bfloat16)
    wide = jax.ShapeDtypeStruct((head_count, rows, PAIR), jnp.float32)

    own, early, late, specials = call(
        functools.partial(start_kernel, special_count),
        [narrow(rows), narrow(per_image + special_block), narrow(per_image), narrow(special_block)],
        (frame_order, patch_rows, jnp.transpose(special_rows, (1, 0, 2)), role_first, role_rest),
        in_specs=[SMEM, HBM, VMEM, VMEM, VMEM],
        scratch=[pltpu.SemaphoreType.DMA((2 * images,))],
    )

    def first():
        return call(
            functools.partial(first_kernel, images, special_count, patch_total),
            [jax.ShapeDtypeStruct((head_count, rows, PAIR), jnp.bfloat16), wide, wide],
            (covisible, own, swapped(own, "head", 1), w_qkv),
        )

    def later(blocks, sources, extra, state):
        pairs = [own_half for own_half, _ in sources] + [other for _, other in sources]
        return call(
            functools.partial(
                later_kernel, images, blocks, special_count if extra else 0, per_image
            ),
            [jax.ShapeDtypeStruct((rows, width), jnp.float32), narrow(rows)] if extra else [wide, wide],
            (covisible, *pairs, *extra[:2], w_qkv, *extra[2:], *state),
        )

    if reach == 1 and owner_count % 2 == 0 and images == 2:
        next_early = swapped(early, "blk", 1)
        next_late = swapped(late, "blk", 1)
        queries, largest, total = first()
        next_early = after(next_early, queries)
        far_early = relayed(next_early, "blk")
        pair = jnp.concatenate([specials, next_early[per_image:]], axis=0)
        all_specials = gathered(pair, "blk", 2)
        next_early = (next_early, swapped(next_early, "head", 1))
        beside, beyond = (1, -1), (-1, 1)
        largest, total = later(
            [(beside, 0)], [next_early], (), (queries, largest, total)
        )
        next_late = after(next_late, largest)
        far_late = relayed(next_late, "blk")
        next_late = (next_late, swapped(next_late, "head", 1))
        far_early = (far_early, swapped(far_early, "head", 1))
        all_specials = (all_specials, swapped(all_specials, "head", 1))
        largest, total = later(
            [(beside, 1), (beyond, 0)], [next_late, far_early], (), (queries, largest, total)
        )
        far_late = (far_late, swapped(far_late, "head", 1))
        blocks, sources = [(beyond, 1)], [far_late]
    else:
        near = []
        for distance in range(1, reach + 1):
            for offset in (-distance, distance):
                parts = [shifted(part, "blk", -offset) for part in (early, late)]
                sources = [(part, swapped(part, "head", 1)) for part in parts]
                near.append(([(offset, 0), (offset, 1)], sources))
        all_specials = gathered(specials, "blk", 1)
        all_specials = (all_specials, swapped(all_specials, "head", 1))
        queries, largest, total = first()
        for blocks, sources in near[:-1]:
            largest, total = later(blocks, sources, (), (queries, largest, total))
        blocks, sources = near[-1]
    kept, sent = later(blocks, sources, (*all_specials, w_out), (queries, largest, total))
    received = swapped(sent, "head", 1)
    patch_out, special_out = call(
        functools.partial(end_kernel, images),
        [narrow(patch_total), jax.ShapeDtypeStruct((special_count, images, width), jnp.bfloat16)],
        (kept, received),
        in_specs=[VMEM, VMEM],
        out_specs=[pl.BlockSpec(), pl.BlockSpec()],
    )
    return patch_out.reshape(patch_rows.shape), jnp.transpose(special_out, (1, 0, 2))


def solution(mesh):
    in_specs = (
        P(("scene", "blk"), None, "head"),
        P(("scene", "blk"), None, "head"),
        P(),
        P(),
        P(("scene", "blk")),
        P(("scene", "blk"), None),
        P(None, None, "head"),
        P("head", None),
    )
    out_specs = (P(("scene", "blk"), None, "head"), P(("scene", "blk"), None, "head"))
    return jax.shard_map(
        per_device, mesh=mesh, in_specs=in_specs, out_specs=out_specs, check_vma=False
    )
```

time: 55.5 us -> 50.4 us (0.908)
  waiting for transfers between devices: 21.4 us -> 8.05 us
  Pallas kernels: 14.5 us -> 22.1 us
  other arithmetic: 1.6 us -> 0.02 us
  starting transfers between devices: 11.2 us -> 12.6 us
  local copies, waits for them, and re-layouts: 5.71 us -> 6.36 us
    ppermute x9 -> x11, waiting for transfers between devices: 21.4 us -> 2.75 us  [swapped(): return lax.ppermute(block, axis, [(i ^ bit, i) for i in range(count)])]
    pallas_call x3 -> x6, Pallas kernels: 14.5 us -> 22.1 us  [call(): pl.pallas_call(kernel, out_shape=out_shape, in_specs=in_specs or [SMEM] +...]
    ppermute x2, waiting for transfers between devices: 0.01 us -> 5.3 us  [relayed(): lax.ppermute(block, axis, [(i, (i + (2 if i % 2 == 0 else -2)) % count) f...]
    ppermute x9 -> x11, starting transfers between devices: 5.15 us -> 10.3 us  [swapped(): return lax.ppermute(block, axis, [(i ^ bit, i) for i in range(count)])]
    ppermute x2, starting transfers between devices: 6.1 us -> 2.26 us  [relayed(): lax.ppermute(block, axis, [(i, (i + (2 if i % 2 == 0 else -2)) % count) f...]
    unnamed x11 -> x20, local copies, waits for them, and re-layouts: 4.18 us -> 6.36 us
    convert_element_type x2 -> x0, other arithmetic: 0.93 us -> none  [the longest x1 0.78 us: per_device(): specials = specials.astype(jnp.bfloat16).reshape(real_rows, width)]
    slice x2 -> x1, local copies, waits for them, and re-layouts: 0.77 us -> 0.01 us  [per_device(): pair = jnp.concatenate([specials, next_early[per_image:]], axis=0)]
  transfers between devices with their start and end apart: 11 -> 13, of which waited for: 5 -> 3; matrix products, arithmetic and copies ran while one was open for 4% -> 0% of each run, Pallas kernels for 16% -> 29%
where the time goes in v2:
time: 50.4 us; the launch traced here: 49.9 us
  Pallas kernels  22.1 us (44%)
  starting transfers between devices  12.6 us (25%)
  waiting for transfers between devices  8.05 us (16%)
  local copies, waits for them, and re-layouts  6.36 us (13%)
  between operations  0.76 us (2%)
    pallas_call x6, Pallas kernels, call(): pl.pallas_call(kernel, out_shape=out_shape, in_specs=in_specs or [SMEM] +...  22.1 us
    ppermute x11, starting transfers between devices, swapped(): return lax.ppermute(block, axis, [(i ^ bit, i) for i in range(count)])  10.3 us
    unnamed x20, local copies, waits for them, and re-layouts  6.36 us
    ppermute x2, waiting for transfers between devices, relayed(): lax.ppermute(block, axis, [(i, (i + (2 if i % 2 == 0 else -2)) % count) f...  5.3 us
    ppermute x11, waiting for transfers between devices, swapped(): return lax.ppermute(block, axis, [(i ^ bit, i) for i in range(count)])  2.75 us
    ppermute x2, starting transfers between devices, relayed(): lax.ppermute(block, axis, [(i, (i + (2 if i % 2 == 0 else -2)) % count) f...  2.26 us
  transfers between devices with their start and end apart: 13, of which 3 were waited for; matrix products, arithmetic and copies ran while one was open for 0% of the time, Pallas kernels for 29%

profile of v2, /device:TPU:0, one launch (start us, length us, event | category | flops | bytes accessed | tf_op | source)
XLA Modules:
  0.0 49.9 jit_solution(10966033639849044087)
XLA Ops:
  0.6 1.0 %copy-done.3 = bf16[2,192,512]{2,1,0:T(8,128)(2,1)S(1)} copy-done((bf16[2,192,512]{2,1,0:T(8,128)(2,1)S(1)}, bf16[2,192,512]{2,1,0:T(8,128)(2,1)}, u32[]{:S(2)}) %copy-start.3) | copy-done | bytes 393240
  1.6 0.7 %copy-done.6 = bf16[5,1024]{1,0:T(8,128)(2,1)S(1)} copy-done((bf16[5,1024]{1,0:T(8,128)(2,1)S(1)}, bf16[5,1024]{1,0:T(8,128)(2,1)}, u32[]{:S(2)}) %copy-start.6) | copy-done | bytes 10264
  2.3 0.7 %copy-done.7 = bf16[5,1024]{1,0:T(8,128)(2,1)S(1)} copy-done((bf16[5,1024]{1,0:T(8,128)(2,1)S(1)}, bf16[5,1024]{1,0:T(8,128)(2,1)}, u32[]{:S(2)}) %copy-start.7) | copy-done | bytes 10264
  3.1 0.7 %copy-done.8 = bf16[2,5,512]{2,0,1:T(2,128)(2,1)S(1)} copy-done((bf16[2,5,512]{2,0,1:T(2,128)(2,1)S(1)}, bf16[2,5,512]{2,0,1:T(2,128)(2,1)}, u32[]{:S(2)}) %copy-start.8) | copy-done | bytes 10264
  3.8 0.7 %copy-done.9 = s32[2]{0:T(128)S(1)} copy-done((s32[2]{0:T(128)S(1)}, s32[2]{0:T(128)}, u32[]{:S(2)}) %copy-start.9) | copy-done | bytes 32
  4.4 1.6 %shard_map.95 = (bf16[400,512]{1,0:T(8,128)(2,1)S(1)}, bf16[208,512]{1,0:T(8,128)(2,1)S(1)}, bf16[192,512]{1,0:T(8,128)(2,1)S(1)}, bf16[16,512]{1,0:T(8,128)(2,1)S(1)}) custom-call(s32[2]{0:T(128)S(1)} %copy-done.9, bf16[2,192,512]{2,1,0:T(8,128)(2,1)S(1)} %copy-done.3, bf16[5,2,512]{2,1,0:T(2,128)(2,1)S(1)} %bitcast.3, bf16[5,1024]{1,0:T(8,128)(2,1)S(1)} %copy-done.6, ...), custom_call_target="tpu_custom_call" | custom-call | tf_op jit(solution)/shard_map/pallas_call | solution.py:240
  6.0 0.5 %collective-permute-start.2 = (bf16[400,512]{1,0:T(8,128)(2,1)S(1)}, bf16[400,512]{1,0:T(8,128)(2,1)S(1)}, u32[]{:S(2)}, u32[]{:S(2)}) collective-permute-start(bf16[400,512]{1,0:T(8,128)(2,1)S(1)} %get-tuple-element.21.own), channel_id=1, source_target_pairs={{1,0},{0,1},{3,2},{2,3},{5,4},{4,5},{7,6},{6,7},{9,8},{8,9},{11,10... | collective-permute-start | bytes 1228808 | tf_op jit(solution)/shard_map/ppermute | solution.py:25
  6.6 2.6 %collective-permute-start.1 = (bf16[208,512]{1,0:T(8,128)(2,1)S(1)}, bf16[208,512]{1,0:T(8,128)(2,1)S(1)}, u32[]{:S(2)}, u32[]{:S(2)}) collective-permute-start(bf16[208,512]{1,0:T(8,128)(2,1)S(1)} %get-tuple-element.20), channel_id=1, source_target_pairs={{2,0},{0,2},{6,4},{4,6},{10,8},{8,10},{14,12},{12,14},{3,1},{1,3},... | collective-permute-start | bytes 638984 | tf_op jit(solution)/shard_map/ppermute | solution.py:25
  9.1 0.0 collective-permute-done.2.other
  9.1 1.9 %copy-done = bf16[3,1024,512]{2,1,0:T(8,128)(2,1)S(1)} copy-done((bf16[3,1024,512]{2,1,0:T(8,128)(2,1)S(1)}, bf16[3,1024,512]{2,1,0:T(8,128)(2,1)}, u32[]{:S(2)}) %copy-start) | copy-done | bytes 3145752
  11.0 0.7 %copy-done.4 = s32[2,16]{1,0:T(2,128)S(1)} copy-done((s32[2,16]{1,0:T(2,128)S(1)}, s32[2,16]{1,0:T(2,128)}, u32[]{:S(2)}) %copy-start.4) | copy-done | bytes 152
  11.7 4.0 %shard_map.96 = (bf16[8,400,128]{2,1,0:T(8,128)(2,1)S(1)}, f32[8,400,128]{2,1,0:T(8,128)S(1)}, f32[8,400,128]{2,1,0:T(8,128)S(1)}) custom-call(s32[2,16]{1,0:T(2,128)S(1)} %copy-done.4, bf16[400,512]{1,0:T(8,128)(2,1)S(1)} %get-tuple-element.21.own, bf16[400,512]{1,0:T(8,128)(2,1)S(1)} %collective-permute-done.2.other, bf16[3,1024,512]{2,1,0:T(8,128)(2,1)S(1)} %copy-done), custom_call_target="tpu_custom_call" | custom-call | tf_op jit(solution)/shard_map/pallas_call | solution.py:240
  15.8 0.0 collective-permute-done.1.refs_0_
  15.8 0.2 collective-permute-start.3
  16.0 1.6 %collective-permute-start = (bf16[192,512]{1,0:T(8,128)(2,1)S(1)}, bf16[192,512]{1,0:T(8,128)(2,1)S(1)}, u32[]{:S(2)}, u32[]{:S(2)}) collective-permute-start(bf16[192,512]{1,0:T(8,128)(2,1)S(1)} %get-tuple-element.19), channel_id=1, source_target_pairs={{2,0},{0,2},{6,4},{4,6},{10,8},{8,10},{14,12},{12,14},{3,1},{1,3},... | collective-permute-start | bytes 589832 | tf_op jit(solution)/shard_map/ppermute | solution.py:25
  17.6 1.6 %collective-permute-start.9 = (bf16[208,512]{1,0:T(8,128)(2,1)S(1)}, bf16[208,512]{1,0:T(8,128)(2,1)S(1)}, u32[]{:S(2)}, u32[]{:S(2)}) collective-permute-start(bf16[208,512]{1,0:T(8,128)(2,1)S(1)} %collective-permute-done.1.refs_0_), channel_id=1, source_target_pairs={{0,4},{2,14},{4,8},{6,2},{8,12},{10,6},{12,0},{14,10},{1,5},{3,15}... | collective-permute-start | bytes 638984 | tf_op jit(solution)/shard_map/ppermute | solution.py:266
  19.2 1.6 %collective-permute-start.6 = (bf16[32,512]{1,0:T(8,128)(2,1)S(1)}, bf16[32,512]{1,0:T(8,128)(2,1)S(1)}, u32[]{:S(2)}, u32[]{:S(2)}) collective-permute-start(bf16[32,512]{1,0:T(8,128)(2,1)S(1)} %pad_maximum_fusion.2), channel_id=1, source_target_pairs={{4,0},{6,2},{0,4},{2,6},{12,8},{14,10},{8,12},{10,14},{5,1},{7,3},... | collective-permute-start | bytes 98312 | tf_op jit(solution)/shard_map/ppermute | solution.py:25
  20.8 0.0 collective-permute-done.3.refs_1_
  20.8 5.8 %shard_map.97 = (f32[8,400,128]{2,1,0:T(8,128)S(1)}, f32[8,400,128]{2,1,0:T(8,128)S(1)}) custom-call(s32[2,16]{1,0:T(2,128)S(1)} %copy-done.4, bf16[208,512]{1,0:T(8,128)(2,1)S(1)} %collective-permute-done.1.refs_0_, bf16[208,512]{1,0:T(8,128)(2,1)S(1)} %collective-permute-done.3.refs_1_, bf16[3,1024,512]{2,1,0:T(8,128)(2,1)S(1)} %copy-done.1, ...), custom_call_target="tpu_custom_call" | custom-call | tf_op jit(solution)/shard_map/pallas_call | solution.py:240
  26.7 0.0 collective-permute-done.refs_0_
  26.7 0.7 %collective-permute-start.4 = (bf16[192,512]{1,0:T(8,128)(2,1)S(1)}, bf16[192,512]{1,0:T(8,128)(2,1)S(1)}, u32[]{:S(2)}, u32[]{:S(2)}) collective-permute-start(bf16[192,512]{1,0:T(8,128)(2,1)S(1)} %collective-permute-done.refs_0_), channel_id=1, source_target_pairs={{0,4},{2,14},{4,8},{6,2},{8,12},{10,6},{12,0},{14,10},{1,5},{3,15}... | collective-permute-start | bytes 589832 | tf_op jit(solution)/shard_map/ppermute | solution.py:266
  27.4 2.6 %collective-permute-start.7 = (bf16[64,512]{1,0:T(8,128)(2,1)S(1)}, bf16[64,512]{1,0:T(8,128)(2,1)S(1)}, u32[]{:S(2)}, u32[]{:S(2)}) collective-permute-start(bf16[64,512]{1,0:T(8,128)(2,1)S(1)} %pad_maximum_fusion.1), channel_id=1, source_target_pairs={{8,0},{10,2},{12,4},{14,6},{0,8},{2,10},{4,12},{6,14},{9,1},{11,3}... | collective-permute-start | bytes 196616 | tf_op jit(solution)/shard_map/ppermute | solution.py:25
  30.0 0.5 %collective-permute-start.11 = (bf16[208,512]{1,0:T(8,128)(2,1)S(1)}, bf16[208,512]{1,0:T(8,128)(2,1)S(1)}, u32[]{:S(2)}, u32[]{:S(2)}) collective-permute-start(bf16[208,512]{1,0:T(8,128)(2,1)S(1)} %collective-permute-done.9.refs_1_), channel_id=1, source_target_pairs={{1,0},{0,1},{3,2},{2,3},{5,4},{4,5},{7,6},{6,7},{9,8},{8,9},{11,10... | collective-permute-start | bytes 638984 | tf_op jit(solution)/shard_map/ppermute | solution.py:25
  30.5 5.3 %collective-permute-done.4.refs_0_ = bf16[192,512]{1,0:T(8,128)(2,1)S(1)} collective-permute-done((bf16[192,512]{1,0:T(8,128)(2,1)S(1)}, bf16[192,512]{1,0:T(8,128)(2,1)S(1)}, u32[]{:S(2)}, u32[]{:S(2)}) %collective-permute-start.4) | collective-permute-done | bytes 196640 | tf_op jit(solution)/shard_map/ppermute | solution.py:266
  35.8 1.4 %collective-permute-done.7 = bf16[64,512]{1,0:T(8,128)(2,1)S(1)} collective-permute-done((bf16[64,512]{1,0:T(8,128)(2,1)S(1)}, bf16[64,512]{1,0:T(8,128)(2,1)S(1)}, u32[]{:S(2)}, u32[]{:S(2)}) %collective-permute-start.7) | collective-permute-done | bytes 65568 | tf_op jit(solution)/shard_map/ppermute | solution.py:25
  37.2 0.1 collective-permute-start.8
  37.3 0.0 copy-start.2
  37.3 4.7 %shard_map.98 = (f32[8,400,128]{2,1,0:T(8,128)S(1)}, f32[8,400,128]{2,1,0:T(8,128)S(1)}) custom-call(s32[2,16]{1,0:T(2,128)S(1)} %copy-done.5, bf16[192,512]{1,0:T(8,128)(2,1)S(1)} %collective-permute-done.refs_0_, bf16[208,512]{1,0:T(8,128)(2,1)S(1)} %collective-permute-done.9.refs_1_, bf16[192,512]{1,0:T(8,128)(2,1)S(1)} %collective-permute-done.10.refs_2_, ...), custom_call_target="tpu_custom_call" | custom-call | tf_op jit(solution)/shard_map/pallas_call | solution.py:240
  42.0 5.1 %shard_map.99 = (f32[400,512]{1,0:T(8,128)S(1)}, bf16[400,512]{1,0:T(8,128)(2,1)S(1)}) custom-call(s32[2,16]{1,0:T(2,128)S(1)} %copy-done.5, bf16[192,512]{1,0:T(8,128)(2,1)S(1)} %collective-permute-done.4.refs_0_, bf16[192,512]{1,0:T(8,128)(2,1)S(1)} %collective-permute-done.5.refs_1_, bf16[128,512]{1,0:T(8,128)(2,1)S(1)} %pad_maximum_fusion.refs_2_, ...), custom_call_target="tpu_custom_call" | custom-call | tf_op jit(solution)/shard_map/pallas_call | solution.py:240
  47.1 0.5 %collective-permute-start.12 = (bf16[400,512]{1,0:T(8,128)(2,1)S(1)}, bf16[400,512]{1,0:T(8,128)(2,1)S(1)}, u32[]{:S(2)}, u32[]{:S(2)}) collective-permute-start(bf16[400,512]{1,0:T(8,128)(2,1)S(1)} %get-tuple-element.33), channel_id=1, source_target_pairs={{1,0},{0,1},{3,2},{2,3},{5,4},{4,5},{7,6},{6,7},{9,8},{8,9},{11,10... | collective-permute-start | bytes 1228808 | tf_op jit(solution)/shard_map/ppermute | solution.py:25
  47.7 1.4 %collective-permute-done.12.received = bf16[400,512]{1,0:T(8,128)(2,1)S(1)} collective-permute-done((bf16[400,512]{1,0:T(8,128)(2,1)S(1)}, bf16[400,512]{1,0:T(8,128)(2,1)S(1)}, u32[]{:S(2)}, u32[]{:S(2)}) %collective-permute-start.12) | collective-permute-done | bytes 409632 | tf_op jit(solution)/shard_map/ppermute | solution.py:25
  49.1 0.8 %shard_map.100 = (bf16[384,512]{1,0:T(8,128)(2,1)}, bf16[5,2,512]{2,1,0:T(2,128)(2,1)}) custom-call(f32[400,512]{1,0:T(8,128)S(1)} %get-tuple-element.32.kept, bf16[400,512]{1,0:T(8,128)(2,1)S(1)} %collective-permute-done.12.received), custom_call_target="tpu_custom_call" | custom-call | tf_op jit(solution)/shard_map/pallas_call | solution.py:240
  (24 shorter events, 0.1 us)
Async XLA Ops:
  0.6 1.0 %copy-start.3 = (bf16[2,192,512]{2,1,0:T(8,128)(2,1)S(1)}, bf16[2,192,512]{2,1,0:T(8,128)(2,1)}, u32[]{:S(2)}) copy-start(bf16[2,192,512]{2,1,0:T(8,128)(2,1)} %patches.1) | copy-start | bytes 1179652
  1.6 0.7 %copy-start.6 = (bf16[5,1024]{1,0:T(8,128)(2,1)S(1)}, bf16[5,1024]{1,0:T(8,128)(2,1)}, u32[]{:S(2)}) copy-start(bf16[5,1024]{1,0:T(8,128)(2,1)} %role_first.1) | copy-start | bytes 30724
  2.3 0.7 %copy-start.7 = (bf16[5,1024]{1,0:T(8,128)(2,1)S(1)}, bf16[5,1024]{1,0:T(8,128)(2,1)}, u32[]{:S(2)}) copy-start(bf16[5,1024]{1,0:T(8,128)(2,1)} %role_rest.1) | copy-start | bytes 30724
  3.1 0.7 %copy-start.8 = (bf16[2,5,512]{2,0,1:T(2,128)(2,1)S(1)}, bf16[2,5,512]{2,0,1:T(2,128)(2,1)}, u32[]{:S(2)}) copy-start(bf16[2,5,512]{2,0,1:T(2,128)(2,1)} %param.9) | copy-start | bytes 30724
  3.8 0.7 %copy-start.9 = (s32[2]{0:T(128)S(1)}, s32[2]{0:T(128)}, u32[]{:S(2)}) copy-start(s32[2]{0:T(128)} %frame_order.1) | copy-start | bytes 28
  6.0 3.1 %collective-permute-start.2 = (bf16[400,512]{1,0:T(8,128)(2,1)S(1)}, bf16[400,512]{1,0:T(8,128)(2,1)S(1)}, u32[]{:S(2)}, u32[]{:S(2)}) collective-permute-start(bf16[400,512]{1,0:T(8,128)(2,1)S(1)} %get-tuple-element.21.own), channel_id=1, source_target_pairs={{1,0},{0,1},{3,2},{2,3},{5,4},{4,5},{7,6},{6,7},{9,8},{8,9},{11,10... | collective-permute-start | bytes 1228808 | tf_op jit(solution)/shard_map/ppermute | solution.py:25
  6.6 9.2 %collective-permute-start.1 = (bf16[208,512]{1,0:T(8,128)(2,1)S(1)}, bf16[208,512]{1,0:T(8,128)(2,1)S(1)}, u32[]{:S(2)}, u32[]{:S(2)}) collective-permute-start(bf16[208,512]{1,0:T(8,128)(2,1)S(1)} %get-tuple-element.20), channel_id=1, source_target_pairs={{2,0},{0,2},{6,4},{4,6},{10,8},{8,10},{14,12},{12,14},{3,1},{1,3},... | collective-permute-start | bytes 638984 | tf_op jit(solution)/shard_map/ppermute | solution.py:25
  9.1 1.9 %copy-start = (bf16[3,1024,512]{2,1,0:T(8,128)(2,1)S(1)}, bf16[3,1024,512]{2,1,0:T(8,128)(2,1)}, u32[]{:S(2)}) copy-start(bf16[3,1024,512]{2,1,0:T(8,128)(2,1)} %refs_4_.3) | copy-start | bytes 9437188
  11.0 0.7 %copy-start.4 = (s32[2,16]{1,0:T(2,128)S(1)}, s32[2,16]{1,0:T(2,128)}, u32[]{:S(2)}) copy-start(s32[2,16]{1,0:T(2,128)} %covisible.7) | copy-start | bytes 388
  11.7 9.1 %copy-start.1 = (bf16[3,1024,512]{2,1,0:T(8,128)(2,1)S(1)}, bf16[3,1024,512]{2,1,0:T(8,128)(2,1)}, u32[]{:S(2)}) copy-start(bf16[3,1024,512]{2,1,0:T(8,128)(2,1)} %refs_4_.3) | copy-start | bytes 9437188
  15.8 5.0 %collective-permute-start.3 = (bf16[208,512]{1,0:T(8,128)(2,1)S(1)}, bf16[208,512]{1,0:T(8,128)(2,1)S(1)}, u32[]{:S(2)}, u32[]{:S(2)}) collective-permute-start(bf16[208,512]{1,0:T(8,128)(2,1)S(1)} %collective-permute-done.1.refs_0_), channel_id=1, source_target_pairs={{1,0},{0,1},{3,2},{2,3},{5,4},{4,5},{7,6},{6,7},{9,8},{8,9},{11,10... | collective-permute-start | bytes 638984 | tf_op jit(solution)/shard_map/ppermute | solution.py:25
  16.0 10.7 %collective-permute-start = (bf16[192,512]{1,0:T(8,128)(2,1)S(1)}, bf16[192,512]{1,0:T(8,128)(2,1)S(1)}, u32[]{:S(2)}, u32[]{:S(2)}) collective-permute-start(bf16[192,512]{1,0:T(8,128)(2,1)S(1)} %get-tuple-element.19), channel_id=1, source_target_pairs={{2,0},{0,2},{6,4},{4,6},{10,8},{8,10},{14,12},{12,14},{3,1},{1,3},... | collective-permute-start | bytes 589832 | tf_op jit(solution)/shard_map/ppermute | solution.py:25
  17.6 12.4 %collective-permute-start.9 = (bf16[208,512]{1,0:T(8,128)(2,1)S(1)}, bf16[208,512]{1,0:T(8,128)(2,1)S(1)}, u32[]{:S(2)}, u32[]{:S(2)}) collective-permute-start(bf16[208,512]{1,0:T(8,128)(2,1)S(1)} %collective-permute-done.1.refs_0_), channel_id=1, source_target_pairs={{0,4},{2,14},{4,8},{6,2},{8,12},{10,6},{12,0},{14,10},{1,5},{3,15}... | collective-permute-start | bytes 638984 | tf_op jit(solution)/shard_map/ppermute | solution.py:266
  19.2 8.1 %collective-permute-start.6 = (bf16[32,512]{1,0:T(8,128)(2,1)S(1)}, bf16[32,512]{1,0:T(8,128)(2,1)S(1)}, u32[]{:S(2)}, u32[]{:S(2)}) collective-permute-start(bf16[32,512]{1,0:T(8,128)(2,1)S(1)} %pad_maximum_fusion.2), channel_id=1, source_target_pairs={{4,0},{6,2},{0,4},{2,6},{12,8},{14,10},{8,12},{10,14},{5,1},{7,3},... | collective-permute-start | bytes 98312 | tf_op jit(solution)/shard_map/ppermute | solution.py:25
  20.8 16.5 %copy-start.5 = (s32[2,16]{1,0:T(2,128)S(1)}, s32[2,16]{1,0:T(2,128)}, u32[]{:S(2)}) copy-start(s32[2,16]{1,0:T(2,128)} %covisible.7) | copy-start | bytes 388
  26.7 9.2 %collective-permute-start.4 = (bf16[192,512]{1,0:T(8,128)(2,1)S(1)}, bf16[192,512]{1,0:T(8,128)(2,1)S(1)}, u32[]{:S(2)}, u32[]{:S(2)}) collective-permute-start(bf16[192,512]{1,0:T(8,128)(2,1)S(1)} %collective-permute-done.refs_0_), channel_id=1, source_target_pairs={{0,4},{2,14},{4,8},{6,2},{8,12},{10,6},{12,0},{14,10},{1,5},{3,15}... | collective-permute-start | bytes 589832 | tf_op jit(solution)/shard_map/ppermute | solution.py:266
  27.4 9.8 %collective-permute-start.7 = (bf16[64,512]{1,0:T(8,128)(2,1)S(1)}, bf16[64,512]{1,0:T(8,128)(2,1)S(1)}, u32[]{:S(2)}, u32[]{:S(2)}) collective-permute-start(bf16[64,512]{1,0:T(8,128)(2,1)S(1)} %pad_maximum_fusion.1), channel_id=1, source_target_pairs={{8,0},{10,2},{12,4},{14,6},{0,8},{2,10},{4,12},{6,14},{9,1},{11,3}... | collective-permute-start | bytes 196616 | tf_op jit(solution)/shard_map/ppermute | solution.py:25
  30.0 7.3 %collective-permute-start.10 = (bf16[192,512]{1,0:T(8,128)(2,1)S(1)}, bf16[192,512]{1,0:T(8,128)(2,1)S(1)}, u32[]{:S(2)}, u32[]{:S(2)}) collective-permute-start(bf16[192,512]{1,0:T(8,128)(2,1)S(1)} %collective-permute-done.refs_0_), channel_id=1, source_target_pairs={{1,0},{0,1},{3,2},{2,3},{5,4},{4,5},{7,6},{6,7},{9,8},{8,9},{11,10... | collective-permute-start | bytes 589832 | tf_op jit(solution)/shard_map/ppermute | solution.py:25
  30.0 7.3 %collective-permute-start.11 = (bf16[208,512]{1,0:T(8,128)(2,1)S(1)}, bf16[208,512]{1,0:T(8,128)(2,1)S(1)}, u32[]{:S(2)}, u32[]{:S(2)}) collective-permute-start(bf16[208,512]{1,0:T(8,128)(2,1)S(1)} %collective-permute-done.9.refs_1_), channel_id=1, source_target_pairs={{1,0},{0,1},{3,2},{2,3},{5,4},{4,5},{7,6},{6,7},{9,8},{8,9},{11,10... | collective-permute-start | bytes 638984 | tf_op jit(solution)/shard_map/ppermute | solution.py:25
  35.8 6.2 %collective-permute-start.5 = (bf16[192,512]{1,0:T(8,128)(2,1)S(1)}, bf16[192,512]{1,0:T(8,128)(2,1)S(1)}, u32[]{:S(2)}, u32[]{:S(2)}) collective-permute-start(bf16[192,512]{1,0:T(8,128)(2,1)S(1)} %collective-permute-done.4.refs_0_), channel_id=1, source_target_pairs={{1,0},{0,1},{3,2},{2,3},{5,4},{4,5},{7,6},{6,7},{9,8},{8,9},{11,10... | collective-permute-start | bytes 589832 | tf_op jit(solution)/shard_map/ppermute | solution.py:25
  37.2 4.8 %collective-permute-start.8 = (bf16[128,512]{1,0:T(8,128)(2,1)S(1)}, bf16[128,512]{1,0:T(8,128)(2,1)S(1)}, u32[]{:S(2)}, u32[]{:S(2)}) collective-permute-start(bf16[128,512]{1,0:T(8,128)(2,1)S(1)} %pad_maximum_fusion.refs_2_), channel_id=1, source_target_pairs={{1,0},{0,1},{3,2},{2,3},{5,4},{4,5},{7,6},{6,7},{9,8},{8,9},{11,10... | collective-permute-start | bytes 393224 | tf_op jit(solution)/shard_map/ppermute | solution.py:25
  37.3 4.7 %copy-start.2 = (bf16[512,1024]{1,0:T(8,128)(2,1)S(1)}, bf16[512,1024]{1,0:T(8,128)(2,1)}, u32[]{:S(2)}) copy-start(bf16[512,1024]{1,0:T(8,128)(2,1)} %refs_5_.1) | copy-start | bytes 3145732
  47.1 1.9 %collective-permute-start.12 = (bf16[400,512]{1,0:T(8,128)(2,1)S(1)}, bf16[400,512]{1,0:T(8,128)(2,1)S(1)}, u32[]{:S(2)}, u32[]{:S(2)}) collective-permute-start(bf16[400,512]{1,0:T(8,128)(2,1)S(1)} %get-tuple-element.33), channel_id=1, source_target_pairs={{1,0},{0,1},{3,2},{2,3},{5,4},{4,5},{7,6},{6,7},{9,8},{8,9},{11,10... | collective-permute-start | bytes 1228808 | tf_op jit(solution)/shard_map/ppermute | solution.py:25

commit v3 on v0

v3 whole, which is shorter than its diff:
```python
import functools

import jax
import jax.numpy as jnp
from jax import lax
from jax.experimental import pallas as pl
from jax.experimental.pallas import tpu as pltpu
from jax.sharding import PartitionSpec as P

HEAD_DIM = 64
PAIR = 2 * HEAD_DIM
TILE_ROWS = 16
VMEM_BYTES = 32 * 1024 * 1024
SMEM = pl.BlockSpec(memory_space=pltpu.SMEM)
VMEM = pl.BlockSpec(memory_space=pltpu.VMEM)
HBM = pl.BlockSpec(memory_space=pltpu.HBM)


def shifted(block, axis, distance):
    count = lax.axis_size(axis)
    route = [((i - distance) % count, i) for i in range(count)]
    return lax.ppermute(block, axis, route)


def swapped(block, axis, bit):
    count = lax.axis_size(axis)
    return lax.ppermute(block, axis, [(i ^ bit, i) for i in range(count)])


def relayed(block, axis):
    count = lax.axis_size(axis)
    return lax.ppermute(block, axis, [(i, (i + (2 if i % 2 == 0 else -2)) % count) for i in range(count)])


def halves(width):
    half = lax.axis_index("head")
    mine = pl.ds(pl.multiple_of(half * width, width), width)
    theirs = pl.ds(pl.multiple_of((1 - half) * width, width), width)
    return mine, theirs


def product(left, right):
    return jnp.dot(left, right, preferred_element_type=jnp.float32)


def owner_at(offset):
    count = lax.axis_size("blk")
    here = lax.axis_index("blk")
    if isinstance(offset, tuple):
        offset = jnp.where(lax.rem(here, 2) == 0, offset[0], offset[1])
    return lax.rem(here + offset + count, count)


def start_kernel(
    offsets, frame_order, covisible, patches, specials, role_first, role_rest,
    own_out, pieces_out, special_out, mask_out, order, seen, special_rows, first_rows, rest_rows, copied,
):
    images, per_image, width = patches.shape
    special_count = specials.shape[0]
    patch_total = images * per_image
    small = [
        pltpu.make_async_copy(source, target, copied.at[i])
        for i, (source, target) in enumerate(
            [
                (specials, special_rows), (role_first, first_rows), (role_rest, rest_rows),
                (frame_order, order), (covisible, seen),
            ]
        )
    ]
    large = []
    for b in range(images):
        large.append((patches.at[b], pieces_out.at[b]))
        large.append((patches.at[b], own_out.at[pl.ds(b * per_image, per_image)]))
    large = [
        pltpu.make_async_copy(source, target, copied.at[len(small) + i])
        for i, (source, target) in enumerate(large)
    ]
    for copy in small + large:
        copy.start()
    for copy in small:
        copy.wait()
    mine, _ = halves(width)
    first = first_rows[:, mine].astype(jnp.float32)
    rest = rest_rows[:, mine].astype(jnp.float32)
    summed = [
        special_rows[:, b, :].astype(jnp.float32) + jnp.where(order[b] == 0, first, rest)
        for b in range(images)
    ]
    padding = special_out.shape[0] - images * special_count
    summed.append(jnp.zeros((padding, width), jnp.float32))
    block = jnp.concatenate(summed, axis=0).astype(jnp.bfloat16)
    special_out[...] = block
    own_out[patch_total:, :] = block
    lane = lax.broadcasted_iota(jnp.int32, (1, mask_out.shape[1]), 1)
    special_lane = lax.rem(lane - patch_total, special_out.shape[0])
    image = jnp.where(
        lane < patch_total, lane // per_image, jnp.minimum(special_lane // special_count, images - 1)
    )
    for i, offset in enumerate(offsets):
        for b in range(images):
            row = jnp.zeros(lane.shape, jnp.float32)
            for a in range(images):
                hidden = seen[a, owner_at(offset) * images + b] <= 0
                row = jnp.where((image == a) & hidden, -jnp.inf, row)
            mask_out[i * images + b : i * images + b + 1, :] = row
    for copy in large:
        copy.wait()


def partial_kernel(own, w_qkv, sums_out, weights_out, copied):
    width = own.shape[1]
    mine, theirs = halves(width)
    copies = [
        pltpu.make_async_copy(w_qkv.at[i, rows], weights_out.at[i, rows], copied.at[i, j])
        for j, rows in enumerate((mine, theirs))
        for i in range(3)
    ]
    for copy in copies:
        copy.start()
    for i in range(3):
        copies[i].wait()
        sums_out[i] = product(own[...], weights_out[i, mine, :])
    for i in range(3, 6):
        copies[i].wait()


def project(own, other, weights, which):
    mine, theirs = halves(own.shape[1])
    return product(own, weights[which, mine, :]) + product(other, weights[which, theirs, :])


def attend(scores, masks, state):
    largest = None if state is None else state
    start = 0
    for count, mask in masks:
        part = jnp.max(scores[start : start + count], axis=0, keepdims=True) + mask
        largest = part if largest is None else jnp.maximum(largest, part)
        start += count
    weights, start = [], 0
    for count, mask in masks:
        weights.append(jnp.exp(scores[start : start + count] - (largest - mask)).astype(jnp.bfloat16))
        start += count
    factor = None if state is None else jnp.exp(state - largest)
    return largest, factor, jnp.concatenate(weights, axis=0)


def attend_all(keys, values, masks, queries, special_queries, state, special_rows, special_real):
    pairs = queries.shape[0]
    rows = queries.shape[2] // 2
    count = keys.shape[0]
    values = jnp.transpose(values).astype(jnp.bfloat16)
    keys = keys.astype(jnp.bfloat16)
    ones = jnp.ones((TILE_ROWS, count), jnp.bfloat16)
    key_row = lax.broadcasted_iota(jnp.int32, (special_rows, 1), 0)
    real = lax.rem(key_row, TILE_ROWS) < special_real

    def scored(keys, queries):
        scores = product(keys, queries)
        if not special_rows:
            return scores
        cut = count - special_rows
        special = jnp.where(real, scores[cut:], -jnp.inf)
        return jnp.concatenate([scores[:cut], special], axis=0)

    for pair in range(pairs):
        scores = scored(keys[:, pair * PAIR : (pair + 1) * PAIR], queries[pair])
        both = [(n, jnp.concatenate([mask[:, :rows]] * 2, axis=1)) for n, mask in masks]
        largest, factor, weights = attend(scores, both, state and state.largest(pair))
        for sub in range(2):
            first = pair * PAIR + sub * HEAD_DIM
            lanes = slice(sub * rows, (sub + 1) * rows)
            left = jnp.concatenate([values[first : first + HEAD_DIM], ones], axis=0)
            added = product(left, weights[:, lanes])
            added = added[: HEAD_DIM + 1]
            if state is not None:
                before = jnp.concatenate([state.total(pair, sub), state.weight(pair, sub)], axis=0)
                added = added + before * factor[:, lanes]
            yield pair, sub, largest[:, lanes], added[:HEAD_DIM], added[HEAD_DIM:]
    only = [(n, mask[:, rows:]) for n, mask in masks]
    largest, factor, weights = attend(
        scored(keys, special_queries[...]), only, state and state.largest(pairs)
    )
    added = product(jnp.concatenate([values, ones], axis=0), weights)[: values.shape[0] + 1]
    if state is not None:
        before = jnp.concatenate([state.total(pairs, 0), state.weight(pairs, 0)], axis=0)
        added = added + before * factor
    yield pairs, 0, largest, added[:-1], added[-1:]


class State:
    def __init__(self, rows, refs):
        self.rows = rows
        self.largest_ref, self.weight_ref, self.total_ref, self.special_ref = refs

    def lanes(self, pair, sub):
        if pair == self.total_ref.shape[0]:
            return slice(0, self.special_ref.shape[1])
        return slice(sub * self.rows, (sub + 1) * self.rows)

    def largest(self, pair):
        stop = self.special_ref.shape[1] if pair == self.total_ref.shape[0] else 2 * self.rows
        return self.largest_ref[pair : pair + 1, 0:stop]

    def weight(self, pair, sub):
        return self.weight_ref[pair : pair + 1, self.lanes(pair, sub)]

    def total(self, pair, sub):
        if pair == self.total_ref.shape[0]:
            return self.special_ref[...]
        return self.total_ref[pair, :, self.lanes(pair, sub)]

    def put(self, pair, sub, largest, total, weight):
        lanes = self.lanes(pair, sub)
        self.largest_ref[pair : pair + 1, lanes] = largest
        self.weight_ref[pair : pair + 1, lanes] = weight
        if pair == self.total_ref.shape[0]:
            self.special_ref[...] = total
        else:
            self.total_ref[pair, :, lanes] = total


def first_kernel(
    images, patch_total, mask, sums, other, weights, queries_out, special_out, *state_out
):
    _, theirs = halves(other.shape[1])
    queries, keys, values = [sums[i] + product(other[...], weights[i, theirs, :]) for i in range(3)]
    queries = queries * HEAD_DIM ** (-0.5)
    columns = jnp.transpose(queries[:patch_total]).astype(jnp.bfloat16)
    zero = jnp.zeros((HEAD_DIM, patch_total), jnp.bfloat16)
    pairs = queries_out.shape[0]
    for pair in range(pairs):
        first = pair * PAIR
        upper = jnp.concatenate([columns[first : first + HEAD_DIM], zero], axis=1)
        lower = jnp.concatenate([zero, columns[first + HEAD_DIM : first + PAIR]], axis=1)
        queries_out[pair] = jnp.concatenate([upper, lower], axis=0)
    special = jnp.concatenate([queries[patch_total:]] * (2 * pairs), axis=0)
    row = lax.broadcasted_iota(jnp.int32, special.shape, 0) // (queries.shape[0] - patch_total)
    lane = lax.broadcasted_iota(jnp.int32, special.shape, 1) // HEAD_DIM
    special = jnp.where(row == lane, special, 0.0)
    special_out[...] = jnp.transpose(special).astype(jnp.bfloat16)
    per_image = patch_total // images
    masks = [(per_image, mask[b : b + 1, :]) for b in range(images)]
    state = State(patch_total, state_out)
    for result in attend_all(
        keys[:patch_total], values[:patch_total], masks, queries_out, special_out, None, 0, 0
    ):
        state.put(*result)


def later_kernel(sources, per_image, mask, *refs):
    count = len(sources)
    own = jnp.concatenate([ref[...] for ref in refs[:count]], axis=0)
    other = jnp.concatenate([ref[...] for ref in refs[count : 2 * count]], axis=0)
    weights, queries, special_queries = refs[2 * count : 2 * count + 3]
    state_in, state_out = refs[2 * count + 3 : 2 * count + 7], refs[2 * count + 7 :]
    rows = queries.shape[2] // 2
    keys = project(own, other, weights, 1)
    values = project(own, other, weights, 2)
    masks = [(per_image, mask[i : i + 1, :]) for i in sources]
    state = State(rows, state_out)
    for result in attend_all(
        keys, values, masks, queries, special_queries, State(rows, state_in), 0, 0
    ):
        state.put(*result)


def last_kernel(sources, per_image, special_real, mask, *refs):
    count = len(sources)
    own_special, other_special = refs[2 * count : 2 * count + 2]
    own = jnp.concatenate([ref[...] for ref in refs[:count]] + [own_special[...]], axis=0)
    other = jnp.concatenate([ref[...] for ref in refs[count : 2 * count]] + [other_special[...]], axis=0)
    weights, queries, special_queries = refs[2 * count + 2 : 2 * count + 5]
    state_in = refs[2 * count + 5 : 2 * count + 9]
    w_out, kept_out, sent_out, w_here, copied = refs[2 * count + 9 :]
    copy = pltpu.make_async_copy(w_out, w_here, copied)
    copy.start()
    pairs, rows = queries.shape[0], queries.shape[2] // 2
    keys = project(own, other, weights, 1)
    values = project(own, other, weights, 2)
    special_rows = own_special.shape[0]
    masks = [(per_image, mask[i : i + 1, :]) for i in sources]
    masks.append((special_rows, jnp.zeros((1, mask.shape[1]), jnp.float32)))
    columns = []
    for pair, _, _, total, weight in attend_all(
        keys, values, masks, queries, special_queries, State(rows, state_in), special_rows, special_real
    ):
        columns.append(total / weight)
    special = columns.pop()
    attended = jnp.transpose(jnp.concatenate(columns, axis=0))
    row = lax.broadcasted_iota(jnp.int32, special.shape, 0) // HEAD_DIM
    lane = lax.broadcasted_iota(jnp.int32, special.shape, 1) // TILE_ROWS
    special = jnp.transpose(jnp.where(row == lane, special, 0.0))
    special = sum(special[i * TILE_ROWS : (i + 1) * TILE_ROWS] for i in range(2 * pairs))
    attended = jnp.concatenate([attended, special], axis=0).astype(jnp.bfloat16)
    mine, theirs = halves(kept_out.shape[1])
    copy.wait()
    sent_out[...] = product(attended, w_here[:, theirs]).astype(jnp.bfloat16)
    kept_out[...] = product(attended, w_here[:, mine])


def end_kernel(images, kept, received, patch_out, special_out):
    patch_total = patch_out.shape[0]
    special_count = special_out.shape[0]
    patch_out[...] = (kept[:patch_total, :] + received[:patch_total, :].astype(jnp.float32)).astype(
        jnp.bfloat16
    )
    rest = kept[patch_total:, :] + received[patch_total:, :].astype(jnp.float32)
    rows = [rest[b * special_count : (b + 1) * special_count][:, None, :] for b in range(images)]
    special_out[...] = jnp.concatenate(rows, axis=1).astype(jnp.bfloat16)


def call(kernel, out_shape, operands, in_specs=None, out_specs=None, scratch=()):
    return pl.pallas_call(
        kernel,
        out_shape=out_shape,
        in_specs=in_specs or [VMEM] * len(operands),
        out_specs=out_specs or [VMEM] * len(out_shape),
        scratch_shapes=scratch,
        compiler_params=pltpu.CompilerParams(vmem_limit_bytes=VMEM_BYTES),
        cost_estimate=pl.CostEstimate(flops=0, transcendentals=0, bytes_accessed=0),
    )(*operands)


def gathered(block, axis):
    count = lax.axis_size(axis)
    if count & (count - 1):
        return lax.all_gather(block, axis, axis=0, tiled=True)
    bit = 1
    while bit < count:
        bit *= 2
        block = jnp.concatenate([block, swapped(block, axis, bit % count + bit // count)], axis=0)
    return block


def after(array, *others):
    return lax.optimization_barrier((array, *others))[0]


def per_device(
    patch_rows, special_rows, role_first, role_rest, frame_order, covisible, w_qkv, w_out
):
    images, per_image, width = patch_rows.shape
    special_count = special_rows.shape[1]
    real_rows = images * special_count
    special_block = real_rows + -real_rows % TILE_ROWS
    owner_count = lax.axis_size("blk")
    reach = max(1, owner_count // 64)
    patch_total = images * per_image
    rows = patch_total + special_block
    heads = width // HEAD_DIM
    pairs = heads // 2
    relay = reach == 1 and owner_count % 2 == 0

    if relay:
        offsets = [0, (1, -1), (-1, 1)]
    else:
        offsets = [0] + [sign * d for d in range(1, reach + 1) for sign in (-1, 1)]
    mask_rows = -(-len(offsets) * images // 8) * 8
    bf16 = lambda *shape: jax.ShapeDtypeStruct(shape, jnp.bfloat16)
    f32 = lambda *shape: jax.ShapeDtypeStruct(shape, jnp.float32)
    state_shape = [
        f32(8, 2 * patch_total),
        f32(8, 2 * patch_total),
        f32(pairs, HEAD_DIM, 2 * patch_total),
        f32(width, heads * special_block),
    ]

    turned = jnp.transpose(special_rows, (1, 0, 2))
    own, pieces, specials, mask = call(
        functools.partial(start_kernel, offsets),
        [
            bf16(rows, width),
            bf16(images, per_image, width),
            bf16(special_block, width),
            f32(mask_rows, patch_total + heads * special_block),
        ],
        (frame_order, covisible, patch_rows, turned, role_first, role_rest),
        in_specs=[HBM] * 6,
        scratch=[
            pltpu.SMEM(frame_order.shape, jnp.int32),
            pltpu.SMEM(covisible.shape, jnp.int32),
            pltpu.VMEM(turned.shape, jnp.bfloat16),
            pltpu.VMEM(role_first.shape, jnp.bfloat16),
            pltpu.VMEM(role_rest.shape, jnp.bfloat16),
            pltpu.SemaphoreType.DMA((5 + 2 * images,)),
        ],
    )
    pieces = [pieces[b] for b in range(images)]

    def later(sources, parts, *operands):
        halves_here = [part[0] for part in parts] + [part[1] for part in parts]
        return call(
            functools.partial(later_kernel, sources, per_image),
            state_shape,
            (mask, *halves_here, *operands),
        )

    near = [swapped(piece, "blk", 1) for piece in pieces] if relay else []
    other = swapped(own, "head", 1)
    all_specials = gathered(specials, "blk")
    sums, weights = call(
        partial_kernel,
        [f32(3, rows, width), bf16(*w_qkv.shape)],
        (own, w_qkv),
        in_specs=[VMEM, HBM],
        scratch=[pltpu.SemaphoreType.DMA((3, 2))],
    )
    queries, special_queries, *state = call(
        functools.partial(first_kernel, images, patch_total),
        [bf16(pairs, PAIR, 2 * patch_total), bf16(width, heads * special_block), *state_shape],
        (mask, sums, other, weights),
    )
    fixed = (weights, queries, special_queries)
    all_specials = (all_specials, swapped(all_specials, "head", 1))
    both = lambda part: (part, swapped(part, "head", 1))
    if relay:
        groups, far = [], []
        for b in range(images):
            near[b] = after(near[b], state[0])
            far.append(relayed(near[b], "blk"))
            if b == images - 1:
                far[:-1] = [both(part) for part in far[:-1]]
                last = later(
                    [images + b] + [2 * images + c for c in range(b)],
                    [both(near[b]), *far[:-1]], *fixed, *state,
                )
            else:
                state = later([images + b], [both(near[b])], *fixed, *state)
        state = last
        sources, parts = [3 * images - 1], [both(far[-1])]
    else:
        near = []
        for offset in offsets[1:]:
            near.append([both(shifted(piece, "blk", -offset)) for piece in pieces])
        for i, parts in enumerate(near[:-1]):
            state = later([(i + 1) * images + b for b in range(images)], parts, *fixed, *state)
        sources, parts = [len(near) * images + b for b in range(images)], near[-1]
    kept, sent = call(
        functools.partial(last_kernel, sources, per_image, real_rows),
        [f32(rows, width), bf16(rows, width)],
        (
            mask, *[part[0] for part in parts], *[part[1] for part in parts], *all_specials,
            *fixed, *state, w_out,
        ),
        in_specs=[VMEM] * (1 + 2 * len(parts) + 2 + len(fixed) + len(state)) + [HBM],
        scratch=[pltpu.VMEM(w_out.shape, jnp.bfloat16), pltpu.SemaphoreType.DMA],
    )
    received = swapped(sent, "head", 1)
    patch_out, special_out = call(
        functools.partial(end_kernel, images),
        [bf16(patch_total, width), bf16(special_count, images, width)],
        (kept, received),
        out_specs=[pl.BlockSpec(), pl.BlockSpec()],
    )
    return patch_out.reshape(patch_rows.shape), jnp.transpose(special_out, (1, 0, 2))


def solution(mesh):
    in_specs = (
        P(("scene", "blk"), None, "head"),
        P(("scene", "blk"), None, "head"),
        P(),
        P(),
        P(("scene", "blk")),
        P(("scene", "blk"), None),
        P(None, None, "head"),
        P("head", None),
    )
    out_specs = (P(("scene", "blk"), None, "head"), P(("scene", "blk"), None, "head"))
    return jax.shard_map(
        per_device, mesh=mesh, in_specs=in_specs, out_specs=out_specs, check_vma=False
    )
```

time: 152 us -> 45.7 us (0.30)
  blocking collectives: 46.4 us -> 0 us
  waiting for transfers between devices: 40.7 us -> 8.81 us
  matrix products: 19.1 us -> 0 us
  Pallas kernels: 0 us -> 17.1 us
  between operations: 14.4 us -> 0.79 us
  other arithmetic: 10.4 us -> 0.01 us
  local copies, waits for them, and re-layouts: 11.6 us -> 6.39 us
  starting transfers between devices: 8.61 us -> 12.2 us
    all_gather x3 -> x0, blocking collectives: 46.4 us -> none  [the longest x1 41.5 us: per_device(): lax.all_gather(special_pair, 'blk', axis=1, tiled=True)]
    reduce_scatter x2 -> x0, waiting for transfers between devices: 19.3 us -> none  [the longest x1 10.9 us: per_device(): lax.psum_scatter(partial_out[:, special_count:].astype(jnp.bfloat16), 'he...]
    dot_general x12 -> x0, matrix products: 19.1 us -> none  [the longest x4 6.48 us: attend(): jnp.einsum('rhd,khd->hrk', queries, keys_part, preferred_element_type=jnp...]
    pallas_call x0 -> x7, Pallas kernels: none -> 17.1 us  [call(): pl.pallas_call(kernel, out_shape=out_shape, in_specs=in_specs or [VMEM] *...]
    ppermute x3 -> x14, waiting for transfers between devices: 21.4 us -> 8.81 us  [the longest x2 7.07 us: relayed(): lax.ppermute(block, axis, [(i, (i + (2 if i % 2 == 0 else -2)) % count) f...]
    reduce_sum x4 -> x0, other arithmetic: 5.5 us -> none  [attend(): denominator = denominator * factor + jnp.sum(weights, axis=2)]
    unnamed x19, local copies, waits for them, and re-layouts: 1.37 us -> 6.36 us
    slice x14 -> x0, local copies, waits for them, and re-layouts: 4.43 us -> none  [the longest x6 2.15 us: attend(): values_part = key_value[1].reshape(key_value.shape[1], head_count, -1)]
  transfers between devices with their start and end apart: 5 -> 14, of which waited for: 4 -> 3; matrix products, arithmetic and copies ran while one was open for 7% -> 0% of each run, Pallas kernels for 0% -> 24%
where the time goes in v3:
time: 45.7 us; the launch traced here: 45.3 us
  Pallas kernels  17.1 us (37%)
  starting transfers between devices  12.2 us (27%)
  waiting for transfers between devices  8.81 us (19%)
  local copies, waits for them, and re-layouts  6.39 us (14%)
  between operations  0.79 us (2%)
    pallas_call x7, Pallas kernels, call(): pl.pallas_call(kernel, out_shape=out_shape, in_specs=in_specs or [VMEM] *...  17.1 us
    ppermute x12, starting transfers between devices, swapped(): return lax.ppermute(block, axis, [(i ^ bit, i) for i in range(count)])  11.1 us
    ppermute x2, waiting for transfers between devices, relayed(): lax.ppermute(block, axis, [(i, (i + (2 if i % 2 == 0 else -2)) % count) f...  7.07 us
    unnamed x19, local copies, waits for them, and re-layouts  6.36 us
    ppermute x12, waiting for transfers between devices, swapped(): return lax.ppermute(block, axis, [(i ^ bit, i) for i in range(count)])  1.74 us
    ppermute x2, starting transfers between devices, relayed(): lax.ppermute(block, axis, [(i, (i + (2 if i % 2 == 0 else -2)) % count) f...  1.13 us
  transfers between devices with their start and end apart: 14, of which 3 were waited for; matrix products, arithmetic and copies ran while one was open for 0% of the time, Pallas kernels for 24%

profile of v3, /device:TPU:0, one launch (start us, length us, event | category | flops | bytes accessed | tf_op | source)
XLA Modules:
  0.0 45.3 jit_solution(2643011834557789709)
XLA Ops:
  0.6 1.0 %copy-done.2 = bf16[2,192,512]{2,1,0:T(8,128)(2,1)S(1)} copy-done((bf16[2,192,512]{2,1,0:T(8,128)(2,1)S(1)}, bf16[2,192,512]{2,1,0:T(8,128)(2,1)}, u32[]{:S(2)}) %copy-start.2) | copy-done | bytes 393240
  1.6 0.7 %copy-done.3 = bf16[5,1024]{1,0:T(8,128)(2,1)S(1)} copy-done((bf16[5,1024]{1,0:T(8,128)(2,1)S(1)}, bf16[5,1024]{1,0:T(8,128)(2,1)}, u32[]{:S(2)}) %copy-start.3) | copy-done | bytes 10264
  2.3 0.7 %copy-done.4 = bf16[5,1024]{1,0:T(8,128)(2,1)S(1)} copy-done((bf16[5,1024]{1,0:T(8,128)(2,1)S(1)}, bf16[5,1024]{1,0:T(8,128)(2,1)}, u32[]{:S(2)}) %copy-start.4) | copy-done | bytes 10264
  3.1 0.7 %copy-done.5 = bf16[2,5,512]{2,0,1:T(2,128)(2,1)S(1)} copy-done((bf16[2,5,512]{2,0,1:T(2,128)(2,1)S(1)}, bf16[2,5,512]{2,0,1:T(2,128)(2,1)}, u32[]{:S(2)}) %copy-start.5) | copy-done | bytes 10264
  3.8 0.7 %copy-done.6 = s32[2,16]{1,0:T(2,128)S(1)} copy-done((s32[2,16]{1,0:T(2,128)S(1)}, s32[2,16]{1,0:T(2,128)}, u32[]{:S(2)}) %copy-start.6) | copy-done | bytes 152
  4.4 0.7 %copy-done.7 = s32[2]{0:T(128)S(1)} copy-done((s32[2]{0:T(128)S(1)}, s32[2]{0:T(128)}, u32[]{:S(2)}) %copy-start.7) | copy-done | bytes 32
  5.1 1.2 %shard_map.95 = (bf16[400,512]{1,0:T(8,128)(2,1)S(1)}, bf16[2,192,512]{2,1,0:T(8,128)(2,1)S(1)}, bf16[16,512]{1,0:T(8,128)(2,1)S(1)}, f32[8,512]{1,0:T(8,128)S(1)}) custom-call(s32[2]{0:T(128)S(1)} %copy-done.7, s32[2,16]{1,0:T(2,128)S(1)} %copy-done.6, bf16[2,192,512]{2,1,0:T(8,128)(2,1)S(1)} %copy-done.2, bf16[5,2,512]{2,1,0:T(2,128)(2,1)S(1)} %bitcast.7, ...), custom_call_target="tpu_custom_call" | custom-call | tf_op jit(solution)/shard_map/pallas_call | solution.py:313
  6.3 0.5 %collective-permute-start.2 = (bf16[400,512]{1,0:T(8,128)(2,1)S(1)}, bf16[400,512]{1,0:T(8,128)(2,1)S(1)}, u32[]{:S(2)}, u32[]{:S(2)}) collective-permute-start(bf16[400,512]{1,0:T(8,128)(2,1)S(1)} %get-tuple-element.30.own), channel_id=1, source_target_pairs={{1,0},{0,1},{3,2},{2,3},{5,4},{4,5},{7,6},{6,7},{9,8},{8,9},{11,10... | collective-permute-start | bytes 1228808 | tf_op jit(solution)/shard_map/ppermute | solution.py:27
  6.9 2.6 %collective-permute-start.1 = (bf16[192,512]{1,0:T(8,128)(2,1)S(1)}, bf16[192,512]{1,0:T(8,128)(2,1)S(1)}, u32[]{:S(2)}, u32[]{:S(2)}) collective-permute-start(bf16[192,512]{1,0:T(8,128)(2,1)S(1)} %get-tuple-element.54), channel_id=1, source_target_pairs={{2,0},{0,2},{6,4},{4,6},{10,8},{8,10},{14,12},{12,14},{3,1},{1,3},... | collective-permute-start | bytes 589832 | tf_op jit(solution)/shard_map/ppermute | solution.py:27
  9.4 0.1 collective-permute-start
  9.5 2.0 %collective-permute-start.6 = (bf16[16,512]{1,0:T(8,128)(2,1)S(1)}, bf16[16,512]{1,0:T(8,128)(2,1)S(1)}, u32[]{:S(2)}, u32[]{:S(2)}) collective-permute-start(bf16[16,512]{1,0:T(8,128)(2,1)S(1)} %get-tuple-element.42), channel_id=1, source_target_pairs={{4,0},{6,2},{0,4},{2,6},{12,8},{14,10},{8,12},{10,14},{5,1},{7,3},... | collective-permute-start | bytes 49160 | tf_op jit(solution)/shard_map/ppermute | solution.py:27
  11.5 1.9 %copy-done = bf16[3,1024,512]{2,1,0:T(8,128)(2,1)S(1)} copy-done((bf16[3,1024,512]{2,1,0:T(8,128)(2,1)S(1)}, bf16[3,1024,512]{2,1,0:T(8,128)(2,1)}, u32[]{:S(2)}) %copy-start) | copy-done | bytes 3145752
  13.4 1.4 %shard_map.96 = (f32[3,400,512]{2,1,0:T(8,128)S(1)}, bf16[3,1024,512]{2,1,0:T(8,128)(2,1)S(1)}) custom-call(bf16[400,512]{1,0:T(8,128)(2,1)S(1)} %get-tuple-element.30.own, bf16[3,1024,512]{2,1,0:T(8,128)(2,1)S(1)} %copy-done), custom_call_target="tpu_custom_call" | custom-call | tf_op jit(solution)/shard_map/pallas_call | solution.py:313
  14.8 0.0 collective-permute-done.2.other
  14.9 3.3 %shard_map.97 = (bf16[4,128,768]{2,1,0:T(8,128)(2,1)S(1)}, bf16[512,128]{1,0:T(8,128)(2,1)S(1)}, f32[8,768]{1,0:T(8,128)S(1)}, f32[8,768]{1,0:T(8,128)S(1)}, f32...) custom-call(f32[8,512]{1,0:T(8,128)S(1)} %get-tuple-element.28.mask, f32[3,400,512]{2,1,0:T(8,128)S(1)} %get-tuple-element.31.sums, ...), custom_call_target="tpu_custom_call" | custom-call | tf_op jit(solution)/shard_map/pallas_call | solution.py:313
  18.2 0.1 collective-permute-start.3
  18.2 0.0 collective-permute-done.6
  18.3 2.7 %collective-permute-start.7 = (bf16[32,512]{1,0:T(8,128)(2,1)S(1)}, bf16[32,512]{1,0:T(8,128)(2,1)S(1)}, u32[]{:S(2)}, u32[]{:S(2)}) collective-permute-start(bf16[32,512]{1,0:T(8,128)(2,1)S(1)} %pad_maximum_fusion.1), channel_id=1, source_target_pairs={{8,0},{10,2},{12,4},{14,6},{0,8},{2,10},{4,12},{6,14},{9,1},{11,3}... | collective-permute-start | bytes 98312 | tf_op jit(solution)/shard_map/ppermute | solution.py:27
  20.9 0.4 collective-permute-start.10
  21.4 2.2 %shard_map.98 = (f32[8,768]{1,0:T(8,128)S(1)}, f32[8,768]{1,0:T(8,128)S(1)}, f32[4,64,768]{2,1,0:T(8,128)S(1)}, f32[512,128]{1,0:T(8,128)S(1)}) custom-call(f32[8,512]{1,0:T(8,128)S(1)} %get-tuple-element.28.mask, bf16[192,512]{1,0:T(8,128)(2,1)S(1)} %collective-permute-done.1.refs_0_, bf16[192,512]{1,0:T(8,128)(2,1)S(1)} %collective-permute-done.3.refs_1_, ...), custom_call_target="tpu_custom_call" | custom-call | tf_op jit(solution)/shard_map/pallas_call | solution.py:313
  23.6 0.0 copy-start.1
  23.7 0.7 %collective-permute-start.4 = (bf16[192,512]{1,0:T(8,128)(2,1)S(1)}, bf16[192,512]{1,0:T(8,128)(2,1)S(1)}, u32[]{:S(2)}, u32[]{:S(2)}) collective-permute-start(bf16[192,512]{1,0:T(8,128)(2,1)S(1)} %collective-permute-done.refs_0_), channel_id=1, source_target_pairs={{0,4},{2,14},{4,8},{6,2},{8,12},{10,6},{12,0},{14,10},{1,5},{3,15}... | collective-permute-start | bytes 589832 | tf_op jit(solution)/shard_map/ppermute | solution.py:32
  24.3 0.0 collective-permute-done.7
  24.3 2.5 %collective-permute-start.8 = (bf16[64,512]{1,0:T(8,128)(2,1)S(1)}, bf16[64,512]{1,0:T(8,128)(2,1)S(1)}, u32[]{:S(2)}, u32[]{:S(2)}) collective-permute-start(bf16[64,512]{1,0:T(8,128)(2,1)S(1)} %pad_maximum_fusion), channel_id=1, source_target_pairs={{2,0},{0,2},{6,4},{4,6},{10,8},{8,10},{14,12},{12,14},{3,1},{1,3},... | collective-permute-start | bytes 196616 | tf_op jit(solution)/shard_map/ppermute | solution.py:27
  26.8 3.7 %collective-permute-done.10.refs_1_ = bf16[192,512]{1,0:T(8,128)(2,1)S(1)} collective-permute-done((bf16[192,512]{1,0:T(8,128)(2,1)S(1)}, bf16[192,512]{1,0:T(8,128)(2,1)S(1)}, u32[]{:S(2)}, u32[]{:S(2)}) %collective-permute-start.10) | collective-permute-done | bytes 196640 | tf_op jit(solution)/shard_map/ppermute | solution.py:32
  30.5 3.4 %collective-permute-done.4.refs_0_ = bf16[192,512]{1,0:T(8,128)(2,1)S(1)} collective-permute-done((bf16[192,512]{1,0:T(8,128)(2,1)S(1)}, bf16[192,512]{1,0:T(8,128)(2,1)S(1)}, u32[]{:S(2)}, u32[]{:S(2)}) %collective-permute-start.4) | collective-permute-done | bytes 196640 | tf_op jit(solution)/shard_map/ppermute | solution.py:32
  33.9 0.6 %collective-permute-start.9 = (bf16[128,512]{1,0:T(8,128)(2,1)S(1)}, bf16[128,512]{1,0:T(8,128)(2,1)S(1)}, u32[]{:S(2)}, u32[]{:S(2)}) collective-permute-start(bf16[128,512]{1,0:T(8,128)(2,1)S(1)} %constant_dynamic-update-slice_fusion.refs_2_), channel_id=1, source_target_pairs={{1,0},{0,1},{3,2},{2,3},{5,4},{4,5},{7,6},{6,7},{9,8},{8,9},{11,10... | collective-permute-start | bytes 393224 | tf_op jit(solution)/shard_map/ppermute | solution.py:27
  34.5 3.9 %shard_map.99 = (f32[8,768]{1,0:T(8,128)S(1)}, f32[8,768]{1,0:T(8,128)S(1)}, f32[4,64,768]{2,1,0:T(8,128)S(1)}, f32[512,128]{1,0:T(8,128)S(1)}) custom-call(f32[8,512]{1,0:T(8,128)S(1)} %get-tuple-element.28.mask, bf16[192,512]{1,0:T(8,128)(2,1)S(1)} %collective-permute-done.refs_0_, bf16[192,512]{1,0:T(8,128)(2,1)S(1)} %collective-permute-done.10.refs_1_, ...), custom_call_target="tpu_custom_call" | custom-call | tf_op jit(solution)/shard_map/pallas_call | solution.py:313
  38.4 4.2 %shard_map.100 = (f32[400,512]{1,0:T(8,128)S(1)}, bf16[400,512]{1,0:T(8,128)(2,1)S(1)}) custom-call(f32[8,512]{1,0:T(8,128)S(1)} %get-tuple-element.28.mask, bf16[192,512]{1,0:T(8,128)(2,1)S(1)} %collective-permute-done.4.refs_0_, bf16[192,512]{1,0:T(8,128)(2,1)S(1)} %collective-permute-done.5.refs_1_, ...), custom_call_target="tpu_custom_call" | custom-call | tf_op jit(solution)/shard_map/pallas_call | solution.py:313
  42.6 0.1 collective-permute-start.13
  42.7 1.7 %collective-permute-done.13.received = bf16[400,512]{1,0:T(8,128)(2,1)S(1)} collective-permute-done((bf16[400,512]{1,0:T(8,128)(2,1)S(1)}, bf16[400,512]{1,0:T(8,128)(2,1)S(1)}, u32[]{:S(2)}, u32[]{:S(2)}) %collective-permute-start.13) | collective-permute-done | bytes 409632 | tf_op jit(solution)/shard_map/ppermute | solution.py:27
  44.5 0.8 %shard_map.101 = (bf16[384,512]{1,0:T(8,128)(2,1)}, bf16[5,2,512]{2,1,0:T(2,128)(2,1)}) custom-call(f32[400,512]{1,0:T(8,128)S(1)} %get-tuple-element.50.kept, bf16[400,512]{1,0:T(8,128)(2,1)S(1)} %collective-permute-done.13.received), custom_call_target="tpu_custom_call" | custom-call | tf_op jit(solution)/shard_map/pallas_call | solution.py:313
  (26 shorter events, 0.1 us)
Async XLA Ops:
  0.6 1.0 %copy-start.2 = (bf16[2,192,512]{2,1,0:T(8,128)(2,1)S(1)}, bf16[2,192,512]{2,1,0:T(8,128)(2,1)}, u32[]{:S(2)}) copy-start(bf16[2,192,512]{2,1,0:T(8,128)(2,1)} %patches.1) | copy-start | bytes 1179652
  1.6 0.7 %copy-start.3 = (bf16[5,1024]{1,0:T(8,128)(2,1)S(1)}, bf16[5,1024]{1,0:T(8,128)(2,1)}, u32[]{:S(2)}) copy-start(bf16[5,1024]{1,0:T(8,128)(2,1)} %role_first.1) | copy-start | bytes 30724
  2.3 0.7 %copy-start.4 = (bf16[5,1024]{1,0:T(8,128)(2,1)S(1)}, bf16[5,1024]{1,0:T(8,128)(2,1)}, u32[]{:S(2)}) copy-start(bf16[5,1024]{1,0:T(8,128)(2,1)} %role_rest.1) | copy-start | bytes 30724
  3.1 0.7 %copy-start.5 = (bf16[2,5,512]{2,0,1:T(2,128)(2,1)S(1)}, bf16[2,5,512]{2,0,1:T(2,128)(2,1)}, u32[]{:S(2)}) copy-start(bf16[2,5,512]{2,0,1:T(2,128)(2,1)} %param.9) | copy-start | bytes 30724
  3.8 0.7 %copy-start.6 = (s32[2,16]{1,0:T(2,128)S(1)}, s32[2,16]{1,0:T(2,128)}, u32[]{:S(2)}) copy-start(s32[2,16]{1,0:T(2,128)} %covisible.1) | copy-start | bytes 388
  4.4 0.7 %copy-start.7 = (s32[2]{0:T(128)S(1)}, s32[2]{0:T(128)}, u32[]{:S(2)}) copy-start(s32[2]{0:T(128)} %frame_order.1) | copy-start | bytes 28
  6.3 8.5 %collective-permute-start.2 = (bf16[400,512]{1,0:T(8,128)(2,1)S(1)}, bf16[400,512]{1,0:T(8,128)(2,1)S(1)}, u32[]{:S(2)}, u32[]{:S(2)}) collective-permute-start(bf16[400,512]{1,0:T(8,128)(2,1)S(1)} %get-tuple-element.30.own), channel_id=1, source_target_pairs={{1,0},{0,1},{3,2},{2,3},{5,4},{4,5},{7,6},{6,7},{9,8},{8,9},{11,10... | collective-permute-start | bytes 1228808 | tf_op jit(solution)/shard_map/ppermute | solution.py:27
  6.9 11.3 %collective-permute-start.1 = (bf16[192,512]{1,0:T(8,128)(2,1)S(1)}, bf16[192,512]{1,0:T(8,128)(2,1)S(1)}, u32[]{:S(2)}, u32[]{:S(2)}) collective-permute-start(bf16[192,512]{1,0:T(8,128)(2,1)S(1)} %get-tuple-element.54), channel_id=1, source_target_pairs={{2,0},{0,2},{6,4},{4,6},{10,8},{8,10},{14,12},{12,14},{3,1},{1,3},... | collective-permute-start | bytes 589832 | tf_op jit(solution)/shard_map/ppermute | solution.py:27
  9.4 14.2 %collective-permute-start = (bf16[192,512]{1,0:T(8,128)(2,1)S(1)}, bf16[192,512]{1,0:T(8,128)(2,1)S(1)}, u32[]{:S(2)}, u32[]{:S(2)}) collective-permute-start(bf16[192,512]{1,0:T(8,128)(2,1)S(1)} %get-tuple-element.55), channel_id=1, source_target_pairs={{2,0},{0,2},{6,4},{4,6},{10,8},{8,10},{14,12},{12,14},{3,1},{1,3},... | collective-permute-start | bytes 589832 | tf_op jit(solution)/shard_map/ppermute | solution.py:27
  9.5 8.7 %collective-permute-start.6 = (bf16[16,512]{1,0:T(8,128)(2,1)S(1)}, bf16[16,512]{1,0:T(8,128)(2,1)S(1)}, u32[]{:S(2)}, u32[]{:S(2)}) collective-permute-start(bf16[16,512]{1,0:T(8,128)(2,1)S(1)} %get-tuple-element.42), channel_id=1, source_target_pairs={{4,0},{6,2},{0,4},{2,6},{12,8},{14,10},{8,12},{10,14},{5,1},{7,3},... | collective-permute-start | bytes 49160 | tf_op jit(solution)/shard_map/ppermute | solution.py:27
  11.5 1.9 %copy-start = (bf16[3,1024,512]{2,1,0:T(8,128)(2,1)S(1)}, bf16[3,1024,512]{2,1,0:T(8,128)(2,1)}, u32[]{:S(2)}) copy-start(bf16[3,1024,512]{2,1,0:T(8,128)(2,1)} %w_qkv.1) | copy-start | bytes 9437188
  18.2 3.2 %collective-permute-start.3 = (bf16[192,512]{1,0:T(8,128)(2,1)S(1)}, bf16[192,512]{1,0:T(8,128)(2,1)S(1)}, u32[]{:S(2)}, u32[]{:S(2)}) collective-permute-start(bf16[192,512]{1,0:T(8,128)(2,1)S(1)} %collective-permute-done.1.refs_0_), channel_id=1, source_target_pairs={{1,0},{0,1},{3,2},{2,3},{5,4},{4,5},{7,6},{6,7},{9,8},{8,9},{11,10... | collective-permute-start | bytes 589832 | tf_op jit(solution)/shard_map/ppermute | solution.py:27
  18.3 6.1 %collective-permute-start.7 = (bf16[32,512]{1,0:T(8,128)(2,1)S(1)}, bf16[32,512]{1,0:T(8,128)(2,1)S(1)}, u32[]{:S(2)}, u32[]{:S(2)}) collective-permute-start(bf16[32,512]{1,0:T(8,128)(2,1)S(1)} %pad_maximum_fusion.1), channel_id=1, source_target_pairs={{8,0},{10,2},{12,4},{14,6},{0,8},{2,10},{4,12},{6,14},{9,1},{11,3}... | collective-permute-start | bytes 98312 | tf_op jit(solution)/shard_map/ppermute | solution.py:27
  20.9 9.5 %collective-permute-start.10 = (bf16[192,512]{1,0:T(8,128)(2,1)S(1)}, bf16[192,512]{1,0:T(8,128)(2,1)S(1)}, u32[]{:S(2)}, u32[]{:S(2)}) collective-permute-start(bf16[192,512]{1,0:T(8,128)(2,1)S(1)} %collective-permute-done.1.refs_0_), channel_id=1, source_target_pairs={{0,4},{2,14},{4,8},{6,2},{8,12},{10,6},{12,0},{14,10},{1,5},{3,15}... | collective-permute-start | bytes 589832 | tf_op jit(solution)/shard_map/ppermute | solution.py:32
  23.6 14.8 %copy-start.1 = (bf16[512,1024]{1,0:T(8,128)(2,1)S(1)}, bf16[512,1024]{1,0:T(8,128)(2,1)}, u32[]{:S(2)}) copy-start(bf16[512,1024]{1,0:T(8,128)(2,1)} %refs_11_.1) | copy-start | bytes 3145732
  23.7 10.2 %collective-permute-start.4 = (bf16[192,512]{1,0:T(8,128)(2,1)S(1)}, bf16[192,512]{1,0:T(8,128)(2,1)S(1)}, u32[]{:S(2)}, u32[]{:S(2)}) collective-permute-start(bf16[192,512]{1,0:T(8,128)(2,1)S(1)} %collective-permute-done.refs_0_), channel_id=1, source_target_pairs={{0,4},{2,14},{4,8},{6,2},{8,12},{10,6},{12,0},{14,10},{1,5},{3,15}... | collective-permute-start | bytes 589832 | tf_op jit(solution)/shard_map/ppermute | solution.py:32
  24.3 9.6 %collective-permute-start.8 = (bf16[64,512]{1,0:T(8,128)(2,1)S(1)}, bf16[64,512]{1,0:T(8,128)(2,1)S(1)}, u32[]{:S(2)}, u32[]{:S(2)}) collective-permute-start(bf16[64,512]{1,0:T(8,128)(2,1)S(1)} %pad_maximum_fusion), channel_id=1, source_target_pairs={{2,0},{0,2},{6,4},{4,6},{10,8},{8,10},{14,12},{12,14},{3,1},{1,3},... | collective-permute-start | bytes 196616 | tf_op jit(solution)/shard_map/ppermute | solution.py:27
  26.8 7.7 %collective-permute-start.11 = (bf16[192,512]{1,0:T(8,128)(2,1)S(1)}, bf16[192,512]{1,0:T(8,128)(2,1)S(1)}, u32[]{:S(2)}, u32[]{:S(2)}) collective-permute-start(bf16[192,512]{1,0:T(8,128)(2,1)S(1)} %collective-permute-done.refs_0_), channel_id=1, source_target_pairs={{1,0},{0,1},{3,2},{2,3},{5,4},{4,5},{7,6},{6,7},{9,8},{8,9},{11,10... | collective-permute-start | bytes 589832 | tf_op jit(solution)/shard_map/ppermute | solution.py:27
  30.5 4.0 %collective-permute-start.12 = (bf16[192,512]{1,0:T(8,128)(2,1)S(1)}, bf16[192,512]{1,0:T(8,128)(2,1)S(1)}, u32[]{:S(2)}, u32[]{:S(2)}) collective-permute-start(bf16[192,512]{1,0:T(8,128)(2,1)S(1)} %collective-permute-done.10.refs_1_), channel_id=1, source_target_pairs={{1,0},{0,1},{3,2},{2,3},{5,4},{4,5},{7,6},{6,7},{9,8},{8,9},{11,10... | collective-permute-start | bytes 589832 | tf_op jit(solution)/shard_map/ppermute | solution.py:27
  33.9 4.5 %collective-permute-start.5 = (bf16[192,512]{1,0:T(8,128)(2,1)S(1)}, bf16[192,512]{1,0:T(8,128)(2,1)S(1)}, u32[]{:S(2)}, u32[]{:S(2)}) collective-permute-start(bf16[192,512]{1,0:T(8,128)(2,1)S(1)} %collective-permute-done.4.refs_0_), channel_id=1, source_target_pairs={{1,0},{0,1},{3,2},{2,3},{5,4},{4,5},{7,6},{6,7},{9,8},{8,9},{11,10... | collective-permute-start | bytes 589832 | tf_op jit(solution)/shard_map/ppermute | solution.py:27
  33.9 4.5 %collective-permute-start.9 = (bf16[128,512]{1,0:T(8,128)(2,1)S(1)}, bf16[128,512]{1,0:T(8,128)(2,1)S(1)}, u32[]{:S(2)}, u32[]{:S(2)}) collective-permute-start(bf16[128,512]{1,0:T(8,128)(2,1)S(1)} %constant_dynamic-update-slice_fusion.refs_2_), channel_id=1, source_target_pairs={{1,0},{0,1},{3,2},{2,3},{5,4},{4,5},{7,6},{6,7},{9,8},{8,9},{11,10... | collective-permute-start | bytes 393224 | tf_op jit(solution)/shard_map/ppermute | solution.py:27
  42.6 1.8 %collective-permute-start.13 = (bf16[400,512]{1,0:T(8,128)(2,1)S(1)}, bf16[400,512]{1,0:T(8,128)(2,1)S(1)}, u32[]{:S(2)}, u32[]{:S(2)}) collective-permute-start(bf16[400,512]{1,0:T(8,128)(2,1)S(1)} %get-tuple-element.51), channel_id=1, source_target_pairs={{1,0},{0,1},{3,2},{2,3},{5,4},{4,5},{7,6},{6,7},{9,8},{8,9},{11,10... | collective-permute-start | bytes 1228808 | tf_op jit(solution)/shard_map/ppermute | solution.py:27

commit v4 on v3

--- a/solution.py
+++ b/solution.py
@@ -32,6 +32,11 @@
     return lax.ppermute(block, axis, [(i, (i + (2 if i % 2 == 0 else -2)) % count) for i in range(count)])
 
 
+def crossed(block, axis):
+    count = lax.axis_size(axis)
+    return lax.ppermute(block, axis, [(i, (i + (-1 if i % 2 == 0 else 1)) % count) for i in range(count)])
+
+
 def halves(width):
     half = lax.axis_index("head")
     mine = pl.ds(pl.multiple_of(half * width, width), width)
@@ -53,9 +58,10 @@
 
 def start_kernel(
     offsets, frame_order, covisible, patches, specials, role_first, role_rest,
-    own_out, pieces_out, special_out, mask_out, order, seen, special_rows, first_rows, rest_rows, copied,
+    own_out, special_out, mask_out, *rest,
 ):
     images, per_image, width = patches.shape
+    pieces_out, (order, seen, special_rows, first_rows, rest_rows, copied) = rest[:images], rest[images:]
     special_count = specials.shape[0]
     patch_total = images * per_image
     small = [
@@ -69,7 +75,7 @@
     ]
     large = []
     for b in range(images):
-        large.append((patches.at[b], pieces_out.at[b]))
+        large.append((patches.at[b], pieces_out[b]))
         large.append((patches.at[b], own_out.at[pl.ds(b * per_image, per_image)]))
     large = [
         pltpu.make_async_copy(source, target, copied.at[len(small) + i])
@@ -310,6 +316,11 @@
 
 
 def call(kernel, out_shape, operands, in_specs=None, out_specs=None, scratch=()):
+    if in_specs:
+        operands = [
+            pltpu.with_memory_space_constraint(operand, pltpu.HBM) if spec is HBM else operand
+            for operand, spec in zip(operands, in_specs)
+        ]
     return pl.pallas_call(
         kernel,
         out_shape=out_shape,
@@ -322,14 +333,8 @@
 
 
 def gathered(block, axis):
-    count = lax.axis_size(axis)
-    if count & (count - 1):
-        return lax.all_gather(block, axis, axis=0, tiled=True)
-    bit = 1
-    while bit < count:
-        bit *= 2
-        block = jnp.concatenate([block, swapped(block, axis, bit % count + bit // count)], axis=0)
-    return block
+    copies = jnp.concatenate([block] * lax.axis_size(axis), axis=0)
+    return lax.all_to_all(copies, axis, split_axis=0, concat_axis=0, tiled=True)
 
 
 def after(array, *others):
@@ -349,7 +354,7 @@
     rows = patch_total + special_block
     heads = width // HEAD_DIM
     pairs = heads // 2
-    relay = reach == 1 and owner_count % 2 == 0
+    relay = reach == 1 and owner_count % 2 == 0 and images > 1
 
     if relay:
         offsets = [0, (1, -1), (-1, 1)]
@@ -366,13 +371,13 @@
     ]
 
     turned = jnp.transpose(special_rows, (1, 0, 2))
-    own, pieces, specials, mask = call(
+    own, specials, mask, *pieces = call(
         functools.partial(start_kernel, offsets),
         [
             bf16(rows, width),
-            bf16(images, per_image, width),
             bf16(special_block, width),
             f32(mask_rows, patch_total + heads * special_block),
+            *[bf16(per_image, width)] * images,
         ],
         (frame_order, covisible, patch_rows, turned, role_first, role_rest),
         in_specs=[HBM] * 6,
@@ -385,7 +390,6 @@
             pltpu.SemaphoreType.DMA((5 + 2 * images,)),
         ],
     )
-    pieces = [pieces[b] for b in range(images)]
 
     def later(sources, parts, *operands):
         halves_here = [part[0] for part in parts] + [part[1] for part in parts]
@@ -395,7 +399,10 @@
             (mask, *halves_here, *operands),
         )
 
-    near = [swapped(piece, "blk", 1) for piece in pieces] if relay else []
+    both = lambda part: (part, swapped(part, "head", 1))
+    if relay:
+        near = [swapped(piece, "blk", 1) for piece in pieces]
+        far = [crossed(piece, "blk") for piece in pieces[1:]]
     other = swapped(own, "head", 1)
     all_specials = gathered(specials, "blk")
     sums, weights = call(
@@ -405,30 +412,25 @@
         in_specs=[VMEM, HBM],
         scratch=[pltpu.SemaphoreType.DMA((3, 2))],
     )
+    if relay:
+        near[0] = after(near[0], sums)
+        far = [relayed(near[0], "blk"), *far]
+        near[0] = both(near[0])
     queries, special_queries, *state = call(
         functools.partial(first_kernel, images, patch_total),
         [bf16(pairs, PAIR, 2 * patch_total), bf16(width, heads * special_block), *state_shape],
         (mask, sums, other, weights),
     )
     fixed = (weights, queries, special_queries)
-    all_specials = (all_specials, swapped(all_specials, "head", 1))
-    both = lambda part: (part, swapped(part, "head", 1))
     if relay:
-        groups, far = [], []
-        for b in range(images):
-            near[b] = after(near[b], state[0])
-            far.append(relayed(near[b], "blk"))
-            if b == images - 1:
-                far[:-1] = [both(part) for part in far[:-1]]
-                last = later(
-                    [images + b] + [2 * images + c for c in range(b)],
-                    [both(near[b]), *far[:-1]], *fixed, *state,
-                )
-            else:
-                state = later([images + b], [both(near[b])], *fixed, *state)
-        state = last
-        sources, parts = [3 * images - 1], [both(far[-1])]
+        near[1:] = [both(after(part, state[0])) for part in near[1:]]
+        state = later([images], near[:1], *fixed, *state)
+        far = [both(after(part, state[0])) for part in far]
+        all_specials = both(after(all_specials, state[0]))
+        state = later([images + b for b in range(1, images)], near[1:], *fixed, *state)
+        sources, parts = [2 * images + b for b in range(images)], far
     else:
+        all_specials = both(all_specials)
         near = []
         for offset in offsets[1:]:
             near.append([both(shifted(piece, "blk", -offset)) for piece in pieces])

time: 45.7 us -> 57 us (1.25)
  Pallas kernels: 17.1 us -> 24.7 us
  local copies, waits for them, and re-layouts: 6.39 us -> 13.7 us
  waiting for transfers between devices: 8.81 us -> 2.86 us
  starting transfers between devices: 12.2 us -> 14.4 us
    pallas_call x7, Pallas kernels: 17.1 us -> 24.7 us  [call(): pl.pallas_call(kernel, out_shape=out_shape, in_specs=in_specs or [VMEM] *...]
    ppermute x2 -> x1, waiting for transfers between devices: 7.07 us -> 0.01 us  [relayed(): lax.ppermute(block, axis, [(i, (i + (2 if i % 2 == 0 else -2)) % count) f...]
    ppermute x12 -> x9, starting transfers between devices: 11.1 us -> 4.29 us  [swapped(): return lax.ppermute(block, axis, [(i ^ bit, i) for i in range(count)])]
    unnamed x19 -> x23, local copies, waits for them, and re-layouts: 6.36 us -> 13.1 us
    all_to_all x0 -> x1, starting transfers between devices: none -> 4.79 us  [gathered(): return lax.all_to_all(copies, axis, split_axis=0, concat_axis=0, tiled=True)]
    ppermute x0 -> x1, starting transfers between devices: none -> 3.57 us  [crossed(): lax.ppermute(block, axis, [(i, (i + (-1 if i % 2 == 0 else 1)) % count) f...]
    ppermute x12 -> x9, waiting for transfers between devices: 1.74 us -> 2.86 us  [swapped(): return lax.ppermute(block, axis, [(i ^ bit, i) for i in range(count)])]
    ppermute x2 -> x1, starting transfers between devices: 1.13 us -> 1.76 us  [relayed(): lax.ppermute(block, axis, [(i, (i + (2 if i % 2 == 0 else -2)) % count) f...]
  transfers between devices with their start and end apart: 14 -> 12, of which waited for: 3 -> 2; matrix products, arithmetic and copies ran while one was open for 0% -> 9% of each run, Pallas kernels for 24% -> 25%
where the time goes in v4:
time: 57 us; the launch traced here: 56.4 us
  Pallas kernels  24.7 us (43%)
  starting transfers between devices  14.4 us (25%)
  local copies, waits for them, and re-layouts  13.7 us (24%)
  waiting for transfers between devices  2.86 us (5%)
  between operations  0.77 us (1%)
    pallas_call x7, Pallas kernels, call(): pl.pallas_call(kernel, out_shape=out_shape, in_specs=in_specs or [VMEM] *...  24.7 us
    unnamed x23, local copies, waits for them, and re-layouts  13.1 us
    all_to_all x1, starting transfers between devices, gathered(): return lax.all_to_all(copies, axis, split_axis=0, concat_axis=0, tiled=True)  4.79 us
    ppermute x9, starting transfers between devices, swapped(): return lax.ppermute(block, axis, [(i ^ bit, i) for i in range(count)])  4.29 us
    ppermute x1, starting transfers between devices, crossed(): lax.ppermute(block, axis, [(i, (i + (-1 if i % 2 == 0 else 1)) % count) f...  3.57 us
    ppermute x9, waiting for transfers between devices, swapped(): return lax.ppermute(block, axis, [(i ^ bit, i) for i in range(count)])  2.86 us
    ppermute x1, starting transfers between devices, relayed(): lax.ppermute(block, axis, [(i, (i + (2 if i % 2 == 0 else -2)) % count) f...  1.76 us
  transfers between devices with their start and end apart: 12, of which 2 were waited for; matrix products, arithmetic and copies ran while one was open for 9% of the time, Pallas kernels for 25%

profile of v4, /device:TPU:0, one launch (start us, length us, event | category | flops | bytes accessed | tf_op | source)
XLA Modules:
  0.0 56.4 jit_solution(14154434155066209893)
XLA Ops:
  0.6 2.2 %shard_map.95 = (bf16[400,512]{1,0:T(8,128)(2,1)}, bf16[16,512]{1,0:T(8,128)(2,1)S(1)}, f32[8,512]{1,0:T(8,128)S(1)}, bf16[192,512]{1,0:T(8,128)(2,1)S(1)}, bf16[192,512]{1,0:T(8,128)(2,1)}) custom-call(s32[2]{0:T(128)} %frame_order.1, s32[2,16]{1,0:T(2,128)} %covisible.1, bf16[2,192,512]{2,1,0:T(8,128)(2,1)} %patches.1, bf16[5,2,512]{2,1,0:T(2,128)(2,1)} %bitcast.7, ...), custom_call_target="tpu_custom_call" | custom-call | tf_op jit(solution)/shard_map/pallas_call | solution.py:324
  2.8 3.0 %collective-permute-start.8 = (bf16[192,512]{1,0:T(8,128)(2,1)}, bf16[192,512]{1,0:T(8,128)(2,1)}, u32[]{:S(2)}, u32[]{:S(2)}) collective-permute-start(bf16[192,512]{1,0:T(8,128)(2,1)} %get-tuple-element.46), channel_id=1, source_target_pairs={{2,0},{0,2},{6,4},{4,6},{10,8},{8,10},{14,12},{12,14},{3,1},{1,3},... | collective-permute-start | bytes 589832 | tf_op jit(solution)/shard_map/ppermute | solution.py:27
  5.8 3.6 %collective-permute-start.4 = (bf16[192,512]{1,0:T(8,128)(2,1)}, bf16[192,512]{1,0:T(8,128)(2,1)}, u32[]{:S(2)}, u32[]{:S(2)}) collective-permute-start(bf16[192,512]{1,0:T(8,128)(2,1)} %get-tuple-element.46), channel_id=1, source_target_pairs={{0,14},{2,4},{4,2},{6,8},{8,6},{10,12},{12,10},{14,0},{1,15},{3,5}... | collective-permute-start | bytes 589832 | tf_op jit(solution)/shard_map/ppermute | solution.py:37
  9.4 0.6 %constant_dynamic-update-slice_fusion.7 = bf16[128,512]{1,0:T(8,128)(2,1)} fusion(bf16[16,512]{1,0:T(8,128)(2,1)S(1)} %get-tuple-element.48), kind=kLoop, calls=%fused_computation.7 | loop fusion | bytes 32768
  10.0 0.6 %constant_dynamic-update-slice_fusion.6 = bf16[128,512]{1,0:T(8,128)(2,1)} fusion(bf16[128,512]{1,0:T(8,128)(2,1)} %constant_dynamic-update-slice_fusion.7, bf16[16,512]{1,0:T(8,128)(2,1)S(1)} %get-tuple-element.48), kind=kLoop, calls=%fused_computation.6 | loop fusion | bytes 32768
  10.6 0.6 %constant_dynamic-update-slice_fusion.5 = bf16[128,512]{1,0:T(8,128)(2,1)} fusion(bf16[128,512]{1,0:T(8,128)(2,1)} %constant_dynamic-update-slice_fusion.6, bf16[16,512]{1,0:T(8,128)(2,1)S(1)} %get-tuple-element.48), kind=kLoop, calls=%fused_computation.5 | loop fusion | bytes 32768
  11.2 0.6 %constant_dynamic-update-slice_fusion.4 = bf16[128,512]{1,0:T(8,128)(2,1)} fusion(bf16[128,512]{1,0:T(8,128)(2,1)} %constant_dynamic-update-slice_fusion.5, bf16[16,512]{1,0:T(8,128)(2,1)S(1)} %get-tuple-element.48), kind=kLoop, calls=%fused_computation.4 | loop fusion | bytes 32768
  11.8 0.6 %constant_dynamic-update-slice_fusion.3 = bf16[128,512]{1,0:T(8,128)(2,1)} fusion(bf16[128,512]{1,0:T(8,128)(2,1)} %constant_dynamic-update-slice_fusion.4, bf16[16,512]{1,0:T(8,128)(2,1)S(1)} %get-tuple-element.48), kind=kLoop, calls=%fused_computation.3 | loop fusion | bytes 32768
  12.4 0.6 %constant_dynamic-update-slice_fusion.2 = bf16[128,512]{1,0:T(8,128)(2,1)} fusion(bf16[128,512]{1,0:T(8,128)(2,1)} %constant_dynamic-update-slice_fusion.3, bf16[16,512]{1,0:T(8,128)(2,1)S(1)} %get-tuple-element.48), kind=kLoop, calls=%fused_computation.2 | loop fusion | bytes 32768
  13.0 3.2 %shard_map.96 = (f32[3,400,512]{2,1,0:T(8,128)S(1)}, bf16[3,1024,512]{2,1,0:T(8,128)(2,1)S(1)}) custom-call(bf16[400,512]{1,0:T(8,128)(2,1)} %get-tuple-element.34.own, bf16[3,1024,512]{2,1,0:T(8,128)(2,1)} %w_qkv.1), custom_call_target="tpu_custom_call" | custom-call | tf_op jit(solution)/shard_map/pallas_call | solution.py:324
  16.2 1.4 %copy-done.2 = f32[3,400,512]{2,1,0:T(8,128)} copy-done((f32[3,400,512]{2,1,0:T(8,128)}, f32[3,400,512]{2,1,0:T(8,128)S(1)}, u32[]{:S(2)}) %copy-start.2) | copy-done | bytes 2457624
  17.7 0.6 %constant_dynamic-update-slice_fusion.1 = bf16[128,512]{1,0:T(8,128)(2,1)} fusion(bf16[128,512]{1,0:T(8,128)(2,1)} %constant_dynamic-update-slice_fusion.2, bf16[16,512]{1,0:T(8,128)(2,1)S(1)} %get-tuple-element.48), kind=kLoop, calls=%fused_computation.1 | loop fusion | bytes 32768
  18.3 1.2 %collective-permute-done.refs_0_ = bf16[192,512]{1,0:T(8,128)(2,1)} collective-permute-done((bf16[192,512]{1,0:T(8,128)(2,1)S(1)}, bf16[192,512]{1,0:T(8,128)(2,1)}, u32[]{:S(2)}, u32[]{:S(2)}) %collective-permute-start) | collective-permute-done | bytes 196640 | tf_op jit(solution)/shard_map/ppermute | solution.py:27
  19.5 1.8 %collective-permute-start.1 = (bf16[192,512]{1,0:T(8,128)(2,1)}, bf16[192,512]{1,0:T(8,128)(2,1)}, u32[]{:S(2)}, u32[]{:S(2)}) collective-permute-start(bf16[192,512]{1,0:T(8,128)(2,1)} %collective-permute-done.refs_0_), channel_id=1, source_target_pairs={{0,4},{2,14},{4,8},{6,2},{8,12},{10,6},{12,0},{14,10},{1,5},{3,15}... | collective-permute-start | bytes 589832 | tf_op jit(solution)/shard_map/ppermute | solution.py:32
  21.3 0.6 %constant_dynamic-update-slice_fusion = bf16[128,512]{1,0:T(8,128)(2,1)} fusion(bf16[128,512]{1,0:T(8,128)(2,1)} %constant_dynamic-update-slice_fusion.1, bf16[16,512]{1,0:T(8,128)(2,1)S(1)} %get-tuple-element.48), kind=kLoop, calls=%fused_computation | loop fusion | bytes 32768 | tf_op jit(solution)/shard_map/concatenate | solution.py:336
  21.9 4.8 %all-to-all-start = ((bf16[8,16,512]{2,1,0:T(8,128)(2,1)}), bf16[8,16,512]{2,1,0:T(8,128)(2,1)S(1)}, u32[]{:S(2)}, u32[]{:S(2)}) async-start(bf16[8,16,512]{2,1,0:T(8,128)(2,1)} %bitcast.1), calls=%async_computation | async-start | bytes 262144 | tf_op jit(solution)/shard_map/all_to_all | solution.py:337
  26.7 1.7 %copy-done.3 = f32[3,400,512]{2,1,0:T(8,128)S(1)} copy-done((f32[3,400,512]{2,1,0:T(8,128)S(1)}, f32[3,400,512]{2,1,0:T(8,128)}, u32[]{:S(2)}) %copy-start.3) | copy-done | bytes 2457624
  28.4 4.3 %shard_map.97 = (bf16[4,128,768]{2,1,0:T(8,128)(2,1)S(1)}, bf16[512,128]{1,0:T(8,128)(2,1)S(1)}, f32[8,768]{1,0:T(8,128)S(1)}, f32[8,768]{1,0:T(8,128)S(1)}, f32...) custom-call(f32[8,512]{1,0:T(8,128)S(1)} %get-tuple-element.32.mask, f32[3,400,512]{2,1,0:T(8,128)S(1)} %copy-done.3, ...), custom_call_target="tpu_custom_call" | custom-call | tf_op jit(solution)/shard_map/pallas_call | solution.py:324
  32.7 3.3 %shard_map.98 = (f32[8,768]{1,0:T(8,128)S(1)}, f32[8,768]{1,0:T(8,128)S(1)}, f32[4,64,768]{2,1,0:T(8,128)S(1)}, f32[512,128]{1,0:T(8,128)S(1)}) custom-call(f32[8,512]{1,0:T(8,128)S(1)} %get-tuple-element.32.mask, bf16[192,512]{1,0:T(8,128)(2,1)} %collective-permute-done.refs_0_, bf16[192,512]{1,0:T(8,128)(2,1)} %collective-permute-done.2.refs_1_, ...), custom_call_target="tpu_custom_call" | custom-call | tf_op jit(solution)/shard_map/pallas_call | solution.py:324
  36.0 0.9 %copy-done = bf16[4,128,768]{2,1,0:T(8,128)(2,1)} copy-done((bf16[4,128,768]{2,1,0:T(8,128)(2,1)}, bf16[4,128,768]{2,1,0:T(8,128)(2,1)S(1)}, u32[]{:S(2)}) %copy-start) | copy-done | bytes 786456
  36.9 0.9 %copy-done.4 = f32[4,64,768]{2,1,0:T(8,128)} copy-done((f32[4,64,768]{2,1,0:T(8,128)}, f32[4,64,768]{2,1,0:T(8,128)S(1)}, u32[]{:S(2)}) %copy-start.4) | copy-done | bytes 786456
  37.8 0.7 %copy-done.6 = f32[512,128]{1,0:T(8,128)} copy-done((f32[512,128]{1,0:T(8,128)}, f32[512,128]{1,0:T(8,128)S(1)}, u32[]{:S(2)}) %copy-start.6) | copy-done | bytes 262168
  38.5 0.5 collective-permute-start.6
  39.1 0.4 collective-permute-start.7
  39.5 1.1 %copy-done.1 = bf16[4,128,768]{2,1,0:T(8,128)(2,1)S(1)} copy-done((bf16[4,128,768]{2,1,0:T(8,128)(2,1)S(1)}, bf16[4,128,768]{2,1,0:T(8,128)(2,1)}, u32[]{:S(2)}) %copy-start.1) | copy-done | bytes 786456
  40.7 1.1 %copy-done.5 = f32[4,64,768]{2,1,0:T(8,128)S(1)} copy-done((f32[4,64,768]{2,1,0:T(8,128)S(1)}, f32[4,64,768]{2,1,0:T(8,128)}, u32[]{:S(2)}) %copy-start.5) | copy-done | bytes 786456
  41.8 0.9 %copy-done.7 = f32[512,128]{1,0:T(8,128)S(1)} copy-done((f32[512,128]{1,0:T(8,128)S(1)}, f32[512,128]{1,0:T(8,128)}, u32[]{:S(2)}) %copy-start.7) | copy-done | bytes 262168
  42.8 3.3 %shard_map.99 = (f32[8,768]{1,0:T(8,128)S(1)}, f32[8,768]{1,0:T(8,128)S(1)}, f32[4,64,768]{2,1,0:T(8,128)S(1)}, f32[512,128]{1,0:T(8,128)S(1)}) custom-call(f32[8,512]{1,0:T(8,128)S(1)} %get-tuple-element.32.mask, bf16[192,512]{1,0:T(8,128)(2,1)} %collective-permute-done.8.refs_0_, bf16[192,512]{1,0:T(8,128)(2,1)} %collective-permute-done.9.refs_1_, ...), custom_call_target="tpu_custom_call" | custom-call | tf_op jit(solution)/shard_map/pallas_call | solution.py:324
  46.1 7.7 %shard_map.100 = (f32[400,512]{1,0:T(8,128)S(1)}, bf16[400,512]{1,0:T(8,128)(2,1)S(1)}) custom-call(f32[8,512]{1,0:T(8,128)S(1)} %get-tuple-element.32.mask, bf16[192,512]{1,0:T(8,128)(2,1)} %collective-permute-done.1.refs_0_, bf16[192,512]{1,0:T(8,128)(2,1)} %collective-permute-done.4.refs_1_, bf16[192,512]{1,0:T(8,128)(2,1)} %collective-permute-done.5.refs_2_, ...), custom_call_target="tpu_custom_call" | custom-call | tf_op jit(solution)/shard_map/pallas_call | solution.py:324
  53.8 0.1 collective-permute-start.10
  53.9 1.7 %collective-permute-done.10.received = bf16[400,512]{1,0:T(8,128)(2,1)S(1)} collective-permute-done((bf16[400,512]{1,0:T(8,128)(2,1)S(1)}, bf16[400,512]{1,0:T(8,128)(2,1)S(1)}, u32[]{:S(2)}, u32[]{:S(2)}) %collective-permute-start.10) | collective-permute-done | bytes 409632 | tf_op jit(solution)/shard_map/ppermute | solution.py:27
  55.6 0.8 %shard_map.101 = (bf16[384,512]{1,0:T(8,128)(2,1)}, bf16[5,2,512]{2,1,0:T(2,128)(2,1)}) custom-call(f32[400,512]{1,0:T(8,128)S(1)} %get-tuple-element.58.kept, bf16[400,512]{1,0:T(8,128)(2,1)S(1)} %collective-permute-done.10.received), custom_call_target="tpu_custom_call" | custom-call | tf_op jit(solution)/shard_map/pallas_call | solution.py:324
  (23 shorter events, 0.3 us)
Async XLA Ops:
  2.8 29.8 %collective-permute-start.8 = (bf16[192,512]{1,0:T(8,128)(2,1)}, bf16[192,512]{1,0:T(8,128)(2,1)}, u32[]{:S(2)}, u32[]{:S(2)}) collective-permute-start(bf16[192,512]{1,0:T(8,128)(2,1)} %get-tuple-element.46), channel_id=1, source_target_pairs={{2,0},{0,2},{6,4},{4,6},{10,8},{8,10},{14,12},{12,14},{3,1},{1,3},... | collective-permute-start | bytes 589832 | tf_op jit(solution)/shard_map/ppermute | solution.py:27
  5.8 32.7 %collective-permute-start.4 = (bf16[192,512]{1,0:T(8,128)(2,1)}, bf16[192,512]{1,0:T(8,128)(2,1)}, u32[]{:S(2)}, u32[]{:S(2)}) collective-permute-start(bf16[192,512]{1,0:T(8,128)(2,1)} %get-tuple-element.46), channel_id=1, source_target_pairs={{0,14},{2,4},{4,2},{6,8},{8,6},{10,12},{12,10},{14,0},{1,15},{3,5}... | collective-permute-start | bytes 589832 | tf_op jit(solution)/shard_map/ppermute | solution.py:37
  9.4 17.3 %collective-permute-start.3 = (bf16[400,512]{1,0:T(8,128)(2,1)}, bf16[400,512]{1,0:T(8,128)(2,1)}, u32[]{:S(2)}, u32[]{:S(2)}) collective-permute-start(bf16[400,512]{1,0:T(8,128)(2,1)} %get-tuple-element.34.own), channel_id=1, source_target_pairs={{1,0},{0,1},{3,2},{2,3},{5,4},{4,5},{7,6},{6,7},{9,8},{8,9},{11,10... | collective-permute-start | bytes 1228808 | tf_op jit(solution)/shard_map/ppermute | solution.py:27
  9.4 10.1 %collective-permute-start = (bf16[192,512]{1,0:T(8,128)(2,1)S(1)}, bf16[192,512]{1,0:T(8,128)(2,1)}, u32[]{:S(2)}, u32[]{:S(2)}) collective-permute-start(bf16[192,512]{1,0:T(8,128)(2,1)S(1)} %get-tuple-element.33), channel_id=1, source_target_pairs={{2,0},{0,2},{6,4},{4,6},{10,8},{8,10},{14,12},{12,14},{3,1},{1,3},... | collective-permute-start | bytes 589832 | tf_op jit(solution)/shard_map/ppermute | solution.py:27
  16.2 1.4 %copy-start.2 = (f32[3,400,512]{2,1,0:T(8,128)}, f32[3,400,512]{2,1,0:T(8,128)S(1)}, u32[]{:S(2)}) copy-start(f32[3,400,512]{2,1,0:T(8,128)S(1)} %get-tuple-element.35.sums) | copy-start | bytes 7372804
  19.5 13.3 %collective-permute-start.2 = (bf16[192,512]{1,0:T(8,128)(2,1)}, bf16[192,512]{1,0:T(8,128)(2,1)}, u32[]{:S(2)}, u32[]{:S(2)}) collective-permute-start(bf16[192,512]{1,0:T(8,128)(2,1)} %collective-permute-done.refs_0_), channel_id=1, source_target_pairs={{1,0},{0,1},{3,2},{2,3},{5,4},{4,5},{7,6},{6,7},{9,8},{8,9},{11,10... | collective-permute-start | bytes 589832 | tf_op jit(solution)/shard_map/ppermute | solution.py:27
  19.5 19.5 %collective-permute-start.1 = (bf16[192,512]{1,0:T(8,128)(2,1)}, bf16[192,512]{1,0:T(8,128)(2,1)}, u32[]{:S(2)}, u32[]{:S(2)}) collective-permute-start(bf16[192,512]{1,0:T(8,128)(2,1)} %collective-permute-done.refs_0_), channel_id=1, source_target_pairs={{0,4},{2,14},{4,8},{6,2},{8,12},{10,6},{12,0},{14,10},{1,5},{3,15}... | collective-permute-start | bytes 589832 | tf_op jit(solution)/shard_map/ppermute | solution.py:32
  21.9 17.2 %all-to-all-start = ((bf16[8,16,512]{2,1,0:T(8,128)(2,1)}), bf16[8,16,512]{2,1,0:T(8,128)(2,1)S(1)}, u32[]{:S(2)}, u32[]{:S(2)}) async-start(bf16[8,16,512]{2,1,0:T(8,128)(2,1)} %bitcast.1), calls=%async_computation | async-start | bytes 262144 | tf_op jit(solution)/shard_map/all_to_all | solution.py:337
  26.7 1.7 %copy-start.3 = (f32[3,400,512]{2,1,0:T(8,128)S(1)}, f32[3,400,512]{2,1,0:T(8,128)}, u32[]{:S(2)}) copy-start(f32[3,400,512]{2,1,0:T(8,128)} %copy-done.2) | copy-start | bytes 7372804
  32.7 6.9 %collective-permute-start.9 = (bf16[192,512]{1,0:T(8,128)(2,1)}, bf16[192,512]{1,0:T(8,128)(2,1)}, u32[]{:S(2)}, u32[]{:S(2)}) collective-permute-start(bf16[192,512]{1,0:T(8,128)(2,1)} %collective-permute-done.8.refs_0_), channel_id=1, source_target_pairs={{1,0},{0,1},{3,2},{2,3},{5,4},{4,5},{7,6},{6,7},{9,8},{8,9},{11,10... | collective-permute-start | bytes 589832 | tf_op jit(solution)/shard_map/ppermute | solution.py:27
  36.0 0.9 %copy-start = (bf16[4,128,768]{2,1,0:T(8,128)(2,1)}, bf16[4,128,768]{2,1,0:T(8,128)(2,1)S(1)}, u32[]{:S(2)}) copy-start(bf16[4,128,768]{2,1,0:T(8,128)(2,1)S(1)} %get-tuple-element.38.refs_3_.refs_7_) | copy-start | bytes 2359300
  36.9 0.9 %copy-start.4 = (f32[4,64,768]{2,1,0:T(8,128)}, f32[4,64,768]{2,1,0:T(8,128)S(1)}, u32[]{:S(2)}) copy-start(f32[4,64,768]{2,1,0:T(8,128)S(1)} %get-tuple-element.52.refs_7_) | copy-start | bytes 2359300
  37.8 0.7 %copy-start.6 = (f32[512,128]{1,0:T(8,128)}, f32[512,128]{1,0:T(8,128)S(1)}, u32[]{:S(2)}) copy-start(f32[512,128]{1,0:T(8,128)S(1)} %get-tuple-element.53.refs_8_) | copy-start | bytes 786436
  38.5 7.5 %collective-permute-start.6 = (bf16[192,512]{1,0:T(8,128)(2,1)}, bf16[192,512]{1,0:T(8,128)(2,1)}, u32[]{:S(2)}, u32[]{:S(2)}) collective-permute-start(bf16[192,512]{1,0:T(8,128)(2,1)} %collective-permute-done.4.refs_1_), channel_id=1, source_target_pairs={{1,0},{0,1},{3,2},{2,3},{5,4},{4,5},{7,6},{6,7},{9,8},{8,9},{11,10... | collective-permute-start | bytes 589832 | tf_op jit(solution)/shard_map/ppermute | solution.py:27
  39.0 7.0 %collective-permute-start.5 = (bf16[192,512]{1,0:T(8,128)(2,1)}, bf16[192,512]{1,0:T(8,128)(2,1)}, u32[]{:S(2)}, u32[]{:S(2)}) collective-permute-start(bf16[192,512]{1,0:T(8,128)(2,1)} %collective-permute-done.1.refs_0_), channel_id=1, source_target_pairs={{1,0},{0,1},{3,2},{2,3},{5,4},{4,5},{7,6},{6,7},{9,8},{8,9},{11,10... | collective-permute-start | bytes 589832 | tf_op jit(solution)/shard_map/ppermute | solution.py:27
  39.1 6.9 %collective-permute-start.7 = (bf16[128,512]{1,0:T(8,128)(2,1)S(1)}, bf16[128,512]{1,0:T(8,128)(2,1)S(1)}, u32[]{:S(2)}, u32[]{:S(2)}) collective-permute-start(bf16[128,512]{1,0:T(8,128)(2,1)S(1)} %bitcast.5), channel_id=1, source_target_pairs={{1,0},{0,1},{3,2},{2,3},{5,4},{4,5},{7,6},{6,7},{9,8},{8,9},{11,10... | collective-permute-start | bytes 393224 | tf_op jit(solution)/shard_map/ppermute | solution.py:27
  39.5 1.1 %copy-start.1 = (bf16[4,128,768]{2,1,0:T(8,128)(2,1)S(1)}, bf16[4,128,768]{2,1,0:T(8,128)(2,1)}, u32[]{:S(2)}) copy-start(bf16[4,128,768]{2,1,0:T(8,128)(2,1)} %copy-done) | copy-start | bytes 2359300
  40.7 1.1 %copy-start.5 = (f32[4,64,768]{2,1,0:T(8,128)S(1)}, f32[4,64,768]{2,1,0:T(8,128)}, u32[]{:S(2)}) copy-start(f32[4,64,768]{2,1,0:T(8,128)} %copy-done.4) | copy-start | bytes 2359300
  41.8 0.9 %copy-start.7 = (f32[512,128]{1,0:T(8,128)S(1)}, f32[512,128]{1,0:T(8,128)}, u32[]{:S(2)}) copy-start(f32[512,128]{1,0:T(8,128)} %copy-done.6) | copy-start | bytes 786436
  53.8 1.8 %collective-permute-start.10 = (bf16[400,512]{1,0:T(8,128)(2,1)S(1)}, bf16[400,512]{1,0:T(8,128)(2,1)S(1)}, u32[]{:S(2)}, u32[]{:S(2)}) collective-permute-start(bf16[400,512]{1,0:T(8,128)(2,1)S(1)} %get-tuple-element.59), channel_id=1, source_target_pairs={{1,0},{0,1},{3,2},{2,3},{5,4},{4,5},{7,6},{6,7},{9,8},{8,9},{11,10... | collective-permute-start | bytes 1228808 | tf_op jit(solution)/shard_map/ppermute | solution.py:27

commit v5 on v4

v5 whole, which is shorter than its diff:
```python
import functools

import jax
import jax.numpy as jnp
from jax import lax
from jax.experimental import pallas as pl
from jax.experimental.pallas import tpu as pltpu
from jax.sharding import PartitionSpec as P

HEAD_DIM = 64
PAIR = 2 * HEAD_DIM
QUAD = 2 * PAIR
TILE_ROWS = 16
VMEM_BYTES = 32 * 1024 * 1024
SMEM = pl.BlockSpec(memory_space=pltpu.SMEM)
VMEM = pl.BlockSpec(memory_space=pltpu.VMEM)
HBM = pl.BlockSpec(memory_space=pltpu.HBM)


def shifted(block, axis, distance):
    count = lax.axis_size(axis)
    route = [((i - distance) % count, i) for i in range(count)]
    return lax.ppermute(block, axis, route)


def swapped(block, axis, bit):
    count = lax.axis_size(axis)
    return lax.ppermute(block, axis, [(i ^ bit, i) for i in range(count)])


def crossed(block, axis):
    count = lax.axis_size(axis)
    return lax.ppermute(block, axis, [(i, (i + (-1 if i % 2 == 0 else 1)) % count) for i in range(count)])


def halves(width):
    half = lax.axis_index("head")
    mine = pl.ds(pl.multiple_of(half * width, width), width)
    theirs = pl.ds(pl.multiple_of((1 - half) * width, width), width)
    return mine, theirs


def product(left, right):
    return jnp.dot(left, right, preferred_element_type=jnp.float32)


def owner_at(offset):
    count = lax.axis_size("blk")
    here = lax.axis_index("blk")
    if isinstance(offset, tuple):
        offset = jnp.where(lax.rem(here, 2) == 0, offset[0], offset[1])
    return lax.rem(here + offset + count, count)


def start_kernel(
    offsets, special_total, frame_order, covisible, patches, specials, other_specials, role_first, role_rest,
    w_qkv, own_out, special_out, mask_out, weights_out, order, seen, special_here, first_rows, rest_rows, copied,
):
    images, per_image, width = patches.shape
    special_count = specials.shape[0]
    patch_total = images * per_image
    moves = [
        (specials, special_here.at[0]), (other_specials, special_here.at[1]), (role_first, first_rows),
        (role_rest, rest_rows), (frame_order, order), (covisible, seen),
    ]
    small = len(moves)
    moves += [(patches.at[b], own_out.at[pl.ds(b * per_image, per_image)]) for b in range(images)]
    moves += [(w_qkv.at[i], weights_out.at[i]) for i in range(3)]
    copies = [
        pltpu.make_async_copy(source, target, copied.at[i]) for i, (source, target) in enumerate(moves)
    ]
    for copy in copies:
        copy.start()
    for copy in copies[:small]:
        copy.wait()
    for i, columns in enumerate(halves(width)):
        first = first_rows[:, columns].astype(jnp.float32)
        rest = rest_rows[:, columns].astype(jnp.float32)
        summed = [
            special_here[i, :, b, :].astype(jnp.float32) + jnp.where(order[b] == 0, first, rest)
            for b in range(images)
        ]
        summed.append(jnp.zeros((special_total - images * special_count, width), jnp.float32))
        special_out[i] = jnp.concatenate(summed, axis=0).astype(jnp.bfloat16)
    lane = lax.broadcasted_iota(jnp.int32, (1, mask_out.shape[1]), 1)
    special_lane = lax.rem(lane - patch_total, special_total)
    image = jnp.where(
        lane < patch_total, lane // per_image, jnp.minimum(special_lane // special_count, images - 1)
    )
    for i, offset in enumerate(offsets):
        for b in range(images):
            row = jnp.zeros(lane.shape, jnp.float32)
            for a in range(images):
                hidden = seen[a, owner_at(offset) * images + b] <= 0
                row = jnp.where((image == a) & hidden, -jnp.inf, row)
            mask_out[i * images + b : i * images + b + 1, :] = row
    for copy in copies[small:]:
        copy.wait()


def projector(own, other, weights):
    mine, theirs = halves(own.shape[1])

    def columns(which, quad):
        lanes = slice(quad * QUAD, (quad + 1) * QUAD)
        return product(own, weights[which, mine, lanes]) + product(other, weights[which, theirs, lanes])

    return columns


def attend(scores, masks, state):
    largest = state
    start = 0
    for count, mask in masks:
        part = jnp.max(scores[start : start + count], axis=0, keepdims=True)
        part = part if mask is None else part + mask
        largest = part if largest is None else jnp.maximum(largest, part)
        start += count
    weights, start = [], 0
    for count, mask in masks:
        level = largest if mask is None else largest - mask
        weights.append(jnp.exp(scores[start : start + count] - level).astype(jnp.bfloat16))
        start += count
    factor = None if state is None else jnp.exp(state - largest)
    return largest, factor, jnp.concatenate(weights, axis=0)


def attend_all(columns, masks, queries_of, special_queries, state, pairs, rows, special_real):
    keys, values = [], []

    def scored(keys, queries):
        scores = product(keys, queries)
        if all(mask is not None for _, mask in masks):
            return scores
        parts, start = [], 0
        for count, mask in masks:
            part = scores[start : start + count]
            if mask is None:
                key_row = lax.broadcasted_iota(jnp.int32, (count, 1), 0)
                part = jnp.where(lax.rem(key_row, TILE_ROWS) < special_real, part, -jnp.inf)
            parts.append(part)
            start += count
        return jnp.concatenate(parts, axis=0)

    def prepared(pair):
        if pair == pairs:
            return scored(jnp.concatenate(keys, axis=1), special_queries())
        if pair % 2 == 0:
            keys.append(columns(1, pair // 2).astype(jnp.bfloat16))
        lanes = slice((pair % 2) * PAIR, (pair % 2 + 1) * PAIR)
        return scored(keys[pair // 2][:, lanes], queries_of(pair))

    ones = jnp.ones((TILE_ROWS, sum(count for count, _ in masks)), jnp.bfloat16)
    both = [
        (count, None if mask is None else jnp.concatenate([mask[:, :rows]] * 2, axis=1))
        for count, mask in masks
    ]
    only = [(count, None if mask is None else mask[:, rows:]) for count, mask in masks]
    scores = prepared(0)
    for pair in range(pairs):
        if pair % 2 == 0:
            values.append(jnp.transpose(columns(2, pair // 2)).astype(jnp.bfloat16))
        following = prepared(pair + 1)
        largest, factor, weights = attend(scores, both, state and state.largest(pair))
        for sub in range(2):
            first = (pair % 2) * PAIR + sub * HEAD_DIM
            lanes = slice(sub * rows, (sub + 1) * rows)
            left = jnp.concatenate([values[pair // 2][first : first + HEAD_DIM], ones], axis=0)
            added = product(left, weights[:, lanes])[: HEAD_DIM + 1]
            if state is not None:
                before = jnp.concatenate([state.total(pair, sub), state.weight(pair, sub)], axis=0)
                added = added + before * factor[:, lanes]
            yield pair, sub, largest[:, lanes], added[:HEAD_DIM], added[HEAD_DIM:]
        scores = following
    largest, factor, weights = attend(scores, only, state and state.largest(pairs))
    added = product(jnp.concatenate(values + [ones], axis=0), weights)[: pairs * PAIR + 1]
    if state is not None:
        before = jnp.concatenate([state.total(pairs, 0), state.weight(pairs, 0)], axis=0)
        added = added + before * factor
    yield pairs, 0, largest, added[:-1], added[-1:]


class State:
    def __init__(self, rows, refs):
        self.rows = rows
        self.largest_ref, self.weight_ref, self.total_ref, self.special_ref = refs

    def lanes(self, pair, sub):
        if pair == self.total_ref.shape[0]:
            return slice(0, self.special_ref.shape[1])
        return slice(sub * self.rows, (sub + 1) * self.rows)

    def largest(self, pair):
        stop = self.special_ref.shape[1] if pair == self.total_ref.shape[0] else 2 * self.rows
        return self.largest_ref[pair : pair + 1, 0:stop]

    def weight(self, pair, sub):
        return self.weight_ref[pair : pair + 1, self.lanes(pair, sub)]

    def total(self, pair, sub):
        if pair == self.total_ref.shape[0]:
            return self.special_ref[...]
        return self.total_ref[pair, :, self.lanes(pair, sub)]

    def put(self, pair, sub, largest, total, weight):
        lanes = self.lanes(pair, sub)
        self.largest_ref[pair : pair + 1, lanes] = largest
        self.weight_ref[pair : pair + 1, lanes] = weight
        if pair == self.total_ref.shape[0]:
            self.special_ref[...] = total
        else:
            self.total_ref[pair, :, lanes] = total


def first_kernel(
    images, mask, own, other, special, weights, queries_out, special_out, *state_out
):
    patch_total = own.shape[0]
    columns = projector(
        jnp.concatenate([own[...], special[0]], axis=0),
        jnp.concatenate([other[...], special[1]], axis=0),
        weights,
    )
    pairs = queries_out.shape[0]
    zero = jnp.zeros((HEAD_DIM, patch_total), jnp.bfloat16)
    special_columns = []

    def patch_columns(which, quad):
        return columns(which, quad)[:patch_total]

    def queries_of(pair):
        if pair % 2 == 0:
            queries = columns(0, pair // 2) * HEAD_DIM ** (-0.5)
            special_columns.append(queries[patch_total:])
            turned = jnp.transpose(queries[:patch_total]).astype(jnp.bfloat16)
            for i in range(2):
                first = i * PAIR
                upper = jnp.concatenate([turned[first : first + HEAD_DIM], zero], axis=1)
                lower = jnp.concatenate([zero, turned[first + HEAD_DIM : first + PAIR]], axis=1)
                queries_out[pair + i] = jnp.concatenate([upper, lower], axis=0)
        return queries_out[pair]

    def special_queries():
        block = jnp.concatenate(special_columns, axis=1)
        count = block.shape[0]
        block = jnp.concatenate([block] * (2 * pairs), axis=0)
        row = lax.broadcasted_iota(jnp.int32, block.shape, 0) // count
        lane = lax.broadcasted_iota(jnp.int32, block.shape, 1) // HEAD_DIM
        block = jnp.transpose(jnp.where(row == lane, block, 0.0)).astype(jnp.bfloat16)
        special_out[...] = block
        return block

    per_image = patch_total // images
    masks = [(per_image, mask[b : b + 1, :]) for b in range(images)]
    state = State(patch_total, state_out)
    for result in attend_all(
        patch_columns, masks, queries_of, special_queries, None, pairs, patch_total, 0
    ):
        state.put(*result)


def joined(stretches, mask, refs):
    count = len(stretches)
    own = jnp.concatenate([ref[0] if len(ref.shape) > 2 else ref[...] for ref in refs[:count]], axis=0)
    other = jnp.concatenate(
        [ref[1] if len(ref.shape) > 2 else ref[...] for ref in refs[count : 2 * count]], axis=0
    )
    masks = [
        (rows, None if i is None else mask[i : i + 1, :]) for part in stretches for rows, i in part
    ]
    return own, other, masks, refs[2 * count :]


def later_kernel(stretches, special_real, mask, *refs):
    own, other, masks, refs = joined(stretches, mask, refs)
    weights, queries, special_queries = refs[:3]
    state_in, state_out = refs[3:7], refs[7:]
    pairs, rows = queries.shape[0], queries.shape[2] // 2
    state = State(rows, state_out)
    for result in attend_all(
        projector(own, other, weights), masks, lambda pair: queries[pair], lambda: special_queries[...],
        State(rows, state_in), pairs, rows, special_real,
    ):
        state.put(*result)


def last_kernel(stretches, special_real, mask, *refs):
    own, other, masks, refs = joined(stretches, mask, refs)
    weights, queries, special_queries = refs[:3]
    state_in = refs[3:7]
    w_out, kept_out, sent_out, w_here, copied = refs[7:]
    copy = pltpu.make_async_copy(w_out, w_here, copied)
    copy.start()
    pairs, rows = queries.shape[0], queries.shape[2] // 2
    columns = []
    for pair, _, _, total, weight in attend_all(
        projector(own, other, weights), masks, lambda pair: queries[pair], lambda: special_queries[...],
        State(rows, state_in), pairs, rows, special_real,
    ):
        columns.append(total / weight)
    special = columns.pop()
    attended = jnp.transpose(jnp.concatenate(columns, axis=0))
    row = lax.broadcasted_iota(jnp.int32, special.shape, 0) // HEAD_DIM
    lane = lax.broadcasted_iota(jnp.int32, special.shape, 1) // TILE_ROWS
    special = jnp.transpose(jnp.where(row == lane, special, 0.0))
    special = sum(special[i * TILE_ROWS : (i + 1) * TILE_ROWS] for i in range(2 * pairs))
    attended = jnp.concatenate([attended, special], axis=0).astype(jnp.bfloat16)
    mine, theirs = halves(kept_out.shape[1])
    copy.wait()
    sent_out[...] = product(attended, w_here[:, theirs]).astype(jnp.bfloat16)
    kept_out[...] = product(attended, w_here[:, mine])


def end_kernel(images, kept, received, patch_out, special_out):
    patch_total = patch_out.shape[0]
    special_count = special_out.shape[0]
    patch_out[...] = (kept[:patch_total, :] + received[:patch_total, :].astype(jnp.float32)).astype(
        jnp.bfloat16
    )
    rest = kept[patch_total:, :] + received[patch_total:, :].astype(jnp.float32)
    rows = [rest[b * special_count : (b + 1) * special_count][:, None, :] for b in range(images)]
    special_out[...] = jnp.concatenate(rows, axis=1).astype(jnp.bfloat16)


def call(kernel, out_shape, operands, in_specs=None, out_specs=None, scratch=(), cost=0):
    if in_specs:
        operands = [
            pltpu.with_memory_space_constraint(operand, pltpu.HBM) if spec is HBM else operand
            for operand, spec in zip(operands, in_specs)
        ]
    return pl.pallas_call(
        kernel,
        out_shape=out_shape,
        in_specs=in_specs or [VMEM] * len(operands),
        out_specs=out_specs or [VMEM] * len(out_shape),
        scratch_shapes=scratch,
        compiler_params=pltpu.CompilerParams(vmem_limit_bytes=VMEM_BYTES),
        cost_estimate=pl.CostEstimate(flops=cost, transcendentals=0, bytes_accessed=0),
    )(*operands)


def gathered(block, axis, bits):
    for bit in bits:
        block = jnp.concatenate([block, swapped(block, axis, bit)], axis=1)
    return block


def after(array, *others):
    return lax.optimization_barrier((array, *others))[0]


def per_device(
    patch_rows, special_rows, role_first, role_rest, frame_order, covisible, w_qkv, w_out
):
    images, per_image, width = patch_rows.shape
    special_count = special_rows.shape[1]
    real_rows = images * special_count
    special_block = real_rows + -real_rows % TILE_ROWS
    owner_count = lax.axis_size("blk")
    reach = max(1, owner_count // 64)
    patch_total = images * per_image
    rows = patch_total + special_block
    heads = width // HEAD_DIM
    pairs = heads // 2
    paired = reach == 1 and owner_count % 2 == 0

    if paired:
        offsets = [0, (1, -1), (-1, 1)]
    else:
        offsets = [0] + [sign * d for d in range(1, reach + 1) for sign in (-1, 1)]
    mask_rows = -(-len(offsets) * images // 8) * 8
    bf16 = lambda *shape: jax.ShapeDtypeStruct(shape, jnp.bfloat16)
    f32 = lambda *shape: jax.ShapeDtypeStruct(shape, jnp.float32)
    state_shape = [
        f32(8, 2 * patch_total),
        f32(8, 2 * patch_total),
        f32(pairs, HEAD_DIM, 2 * patch_total),
        f32(width, heads * special_block),
    ]

    both = lambda part: (part, swapped(part, "head", 1))
    patches = patch_rows.reshape(patch_total, width)
    turned = jnp.transpose(special_rows, (1, 0, 2))
    if paired:
        near = [swapped(patches, "blk", 1), crossed(patches, "blk")]
    else:
        near = [shifted(patches, "blk", -offset) for offset in offsets[1:]]
    other = swapped(patches, "head", 1)
    own, specials, mask, weights = call(
        functools.partial(start_kernel, offsets, special_block),
        [
            bf16(patch_total, width),
            bf16(2, special_block, width),
            f32(mask_rows, patch_total + heads * special_block),
            bf16(*w_qkv.shape),
        ],
        (
            frame_order, covisible, patch_rows, turned, swapped(turned, "head", 1),
            role_first, role_rest, w_qkv,
        ),
        in_specs=[HBM] * 8,
        scratch=[
            pltpu.SMEM(frame_order.shape, jnp.int32),
            pltpu.SMEM(covisible.shape, jnp.int32),
            pltpu.VMEM((2, *turned.shape), jnp.bfloat16),
            pltpu.VMEM(role_first.shape, jnp.bfloat16),
            pltpu.VMEM(role_rest.shape, jnp.bfloat16),
            pltpu.SemaphoreType.DMA((6 + images + 3,)),
        ],
    )
    if owner_count & (owner_count - 1):
        bits, everywhere = [], lax.all_gather(specials, "blk", axis=1, tiled=True)
    else:
        bits = [1 << i for i in range(1, owner_count.bit_length() - 1)] + [1]
        everywhere = gathered(specials, "blk", bits[:-1])
    queries, special_queries, *state = call(
        functools.partial(first_kernel, images),
        [bf16(pairs, PAIR, 2 * patch_total), bf16(width, heads * special_block), *state_shape],
        (mask, own, other, specials, weights),
    )
    fixed = (weights, queries, special_queries)

    def later(stretches, parts, state):
        return call(
            functools.partial(later_kernel, stretches, real_rows),
            state_shape,
            (mask, *[part[0] for part in parts], *[part[1] for part in parts], *fixed, *state),
        )

    image_rows = lambda owner: [(per_image, owner * images + b) for b in range(images)]
    for i, part in enumerate(near):
        part = after(part, state[0])
        stretches = [[image] for image in image_rows(i + 1)]
        parts = [both(part[b * per_image : (b + 1) * per_image]) for b in range(images)]
        if i < len(near) - 1:
            state = later(stretches, parts, state)
    everywhere = gathered(after(everywhere, state[0]), "blk", bits[-1:])
    stretches.append([(everywhere.shape[1], None)])
    parts.append((everywhere, everywhere))
    kept, sent = call(
        functools.partial(last_kernel, stretches, real_rows),
        [f32(rows, width), bf16(rows, width)],
        (
            mask, *[part[0] for part in parts], *[part[1] for part in parts], *fixed, *state, w_out,
        ),
        in_specs=[VMEM] * (1 + 2 * len(parts) + len(fixed) + len(state)) + [HBM],
        scratch=[pltpu.VMEM(w_out.shape, jnp.bfloat16), pltpu.SemaphoreType.DMA],
    )
    received = swapped(sent, "head", 1)
    patch_out, special_out = call(
        functools.partial(end_kernel, images),
        [bf16(patch_total, width), bf16(special_count, images, width)],
        (kept, received),
        out_specs=[pl.BlockSpec(), pl.BlockSpec()],
    )
    return patch_out.reshape(patch_rows.shape), jnp.transpose(special_out, (1, 0, 2))


def solution(mesh):
    in_specs = (
        P(("scene", "blk"), None, "head"),
        P(("scene", "blk"), None, "head"),
        P(),
        P(),
        P(("scene", "blk")),
        P(("scene", "blk"), None),
        P(None, None, "head"),
        P("head", None),
    )
    out_specs = (P(("scene", "blk"), None, "head"), P(("scene", "blk"), None, "head"))
    return jax.shard_map(
        per_device, mesh=mesh, in_specs=in_specs, out_specs=out_specs, check_vma=False
    )
```

time: 57 us -> 47.2 us (0.83)
  waiting for transfers between devices: 2.86 us -> 16.2 us
  local copies, waits for them, and re-layouts: 13.7 us -> 0.65 us
  Pallas kernels: 24.7 us -> 16.6 us
  starting transfers between devices: 14.4 us -> 12.8 us
    ppermute x9 -> x11, waiting for transfers between devices: 2.86 us -> 16.2 us  [swapped(): return lax.ppermute(block, axis, [(i ^ bit, i) for i in range(count)])]
    unnamed x23 -> x2, local copies, waits for them, and re-layouts: 13.1 us -> 0.6 us
    pallas_call x7 -> x5, Pallas kernels: 24.7 us -> 16.6 us  [call(): pl.pallas_call(kernel, out_shape=out_shape, in_specs=in_specs or [VMEM] *...]
    ppermute x9 -> x11, starting transfers between devices: 4.29 us -> 9.24 us  [swapped(): return lax.ppermute(block, axis, [(i ^ bit, i) for i in range(count)])]
    all_to_all x1 -> x0, starting transfers between devices: 4.79 us -> none  [gathered(): return lax.all_to_all(copies, axis, split_axis=0, concat_axis=0, tiled=True)]
    ppermute x1 -> x0, starting transfers between devices: 1.76 us -> none  [relayed(): lax.ppermute(block, axis, [(i, (i + (2 if i % 2 == 0 else -2)) % count) f...]
    concatenate x1 -> x0, local copies, waits for them, and re-layouts: 0.6 us -> none  [gathered(): copies = jnp.concatenate([block] * lax.axis_size(axis), axis=0)]
  transfers between devices with their start and end apart: 12 -> 12, of which waited for: 2 -> 4; matrix products, arithmetic and copies ran while one was open for 9% -> 0% of each run, Pallas kernels for 25% -> 20%
where the time goes in v5:
time: 47.2 us; the launch traced here: 47 us
  Pallas kernels  16.6 us (35%)
  waiting for transfers between devices  16.2 us (34%)
  starting transfers between devices  12.8 us (27%)
  between operations  0.76 us (2%)
  local copies, waits for them, and re-layouts  0.65 us (1%)
    pallas_call x5, Pallas kernels, call(): pl.pallas_call(kernel, out_shape=out_shape, in_specs=in_specs or [VMEM] *...  16.6 us
    ppermute x11, waiting for transfers between devices, swapped(): return lax.ppermute(block, axis, [(i ^ bit, i) for i in range(count)])  16.2 us
    ppermute x11, starting transfers between devices, swapped(): return lax.ppermute(block, axis, [(i ^ bit, i) for i in range(count)])  9.24 us
    ppermute x1, starting transfers between devices, crossed(): lax.ppermute(block, axis, [(i, (i + (-1 if i % 2 == 0 else 1)) % count) f...  3.57 us
  transfers between devices with their start and end apart: 12, of which 4 were waited for; matrix products, arithmetic and copies ran while one was open for 0% of the time, Pallas kernels for 20%

profile of v5, /device:TPU:0, one launch (start us, length us, event | category | flops | bytes accessed | tf_op | source)
XLA Modules:
  0.0 47.0 jit_solution(8429858773594831484)
XLA Ops:
  0.6 0.5 %collective-permute-start.3 = (bf16[384,512]{1,0:T(8,128)(2,1)}, bf16[384,512]{1,0:T(8,128)(2,1)S(1)}, u32[]{:S(2)}, u32[]{:S(2)}) collective-permute-start(bf16[384,512]{1,0:T(8,128)(2,1)} %bitcast.4), channel_id=1, source_target_pairs={{1,0},{0,1},{3,2},{2,3},{5,4},{4,5},{7,6},{6,7},{9,8},{8,9},{11,10... | collective-permute-start | bytes 1179656 | tf_op jit(solution)/shard_map/ppermute | solution.py:28
  1.2 2.6 %collective-permute-start.2 = (bf16[384,512]{1,0:T(8,128)(2,1)}, bf16[384,512]{1,0:T(8,128)(2,1)S(1)}, u32[]{:S(2)}, u32[]{:S(2)}) collective-permute-start(bf16[384,512]{1,0:T(8,128)(2,1)} %bitcast.5), channel_id=1, source_target_pairs={{2,0},{0,2},{6,4},{4,6},{10,8},{8,10},{14,12},{12,14},{3,1},{1,3},... | collective-permute-start | bytes 1179656 | tf_op jit(solution)/shard_map/ppermute | solution.py:28
  3.7 0.2 collective-permute-start
  3.9 3.6 %collective-permute-start.1 = (bf16[384,512]{1,0:T(8,128)(2,1)}, bf16[384,512]{1,0:T(8,128)(2,1)S(1)}, u32[]{:S(2)}, u32[]{:S(2)}) collective-permute-start(bf16[384,512]{1,0:T(8,128)(2,1)} %bitcast.6), channel_id=1, source_target_pairs={{0,14},{2,4},{4,2},{6,8},{8,6},{10,12},{12,10},{14,0},{1,15},{3,5}... | collective-permute-start | bytes 1179656 | tf_op jit(solution)/shard_map/ppermute | solution.py:33
  7.5 0.0 collective-permute-done.other_specials
  7.5 0.0 copy-start
  7.5 0.6 %copy-done = bf16[5,2,512]{2,1,0:T(2,128)(2,1)} copy-done((bf16[5,2,512]{2,1,0:T(2,128)(2,1)}, bf16[5,2,512]{2,1,0:T(2,128)(2,1)S(1)}, u32[]{:S(2)}) %copy-start) | copy-done | bytes 10264
  8.1 2.2 %shard_map.95 = (bf16[384,512]{1,0:T(8,128)(2,1)S(1)}, bf16[2,16,512]{2,1,0:T(8,128)(2,1)S(1)}, f32[8,512]{1,0:T(8,128)S(1)}, bf16[3,1024,512]{2,1,0:T(8,128)(2,1)S(1)}) custom-call(s32[2]{0:T(128)} %frame_order.1, s32[2,16]{1,0:T(2,128)} %covisible.1, bf16[2,192,512]{2,1,0:T(8,128)(2,1)} %patches.1, bf16[5,2,512]{2,1,0:T(2,128)(2,1)} %bitcast.8, ...), custom_call_target="tpu_custom_call" | custom-call | tf_op jit(solution)/shard_map/pallas_call | solution.py:331
  10.3 0.1 collective-permute-start.6
  10.4 0.0 collective-permute-done.3.other
  10.4 3.6 %shard_map.96 = (bf16[4,128,768]{2,1,0:T(8,128)(2,1)S(1)}, bf16[512,128]{1,0:T(8,128)(2,1)S(1)}, f32[8,768]{1,0:T(8,128)S(1)}, f32[8,768]{1,0:T(8,128)S(1)}, f32...) custom-call(f32[8,512]{1,0:T(8,128)S(1)} %get-tuple-element.23.mask, bf16[384,512]{1,0:T(8,128)(2,1)S(1)} %get-tuple-element.24.own, ...), custom_call_target="tpu_custom_call" | custom-call | tf_op jit(solution)/shard_map/pallas_call | solution.py:331
  14.0 8.1 %collective-permute-done.2 = bf16[384,512]{1,0:T(8,128)(2,1)S(1)} collective-permute-done((bf16[384,512]{1,0:T(8,128)(2,1)}, bf16[384,512]{1,0:T(8,128)(2,1)S(1)}, u32[]{:S(2)}, u32[]{:S(2)}) %collective-permute-start.2) | collective-permute-done | bytes 393248 | tf_op jit(solution)/shard_map/ppermute | solution.py:28
  22.1 0.1 collective-permute-start.4
  22.2 0.5 %collective-permute-start.5 = (bf16[192,512]{1,0:T(8,128)(2,1)S(1)}, bf16[192,512]{1,0:T(8,128)(2,1)S(1)}, u32[]{:S(2)}, u32[]{:S(2)}) collective-permute-start(bf16[192,512]{1,0:T(8,128)(2,1)S(1)} %get-tuple-element.46.refs_1_), channel_id=1, source_target_pairs={{1,0},{0,1},{3,2},{2,3},{5,4},{4,5},{7,6},{6,7},{9,8},{8,9},{11,10... | collective-permute-start | bytes 589832 | tf_op jit(solution)/shard_map/ppermute | solution.py:28
  22.7 0.0 collective-permute-done.6
  22.7 2.9 %collective-permute-start.7 = (bf16[2,32,512]{2,1,0:T(8,128)(2,1)S(1)}, bf16[2,32,512]{2,1,0:T(8,128)(2,1)S(1)}, u32[]{:S(2)}, u32[]{:S(2)}) collective-permute-start(bf16[2,32,512]{2,1,0:T(8,128)(2,1)S(1)} %pad_maximum_fusion.2), channel_id=1, source_target_pairs={{8,0},{10,2},{12,4},{14,6},{0,8},{2,10},{4,12},{6,14},{9,1},{11,3}... | collective-permute-start | bytes 196616 | tf_op jit(solution)/shard_map/ppermute | solution.py:28
  25.6 3.7 %collective-permute-done.7 = bf16[2,32,512]{2,1,0:T(8,128)(2,1)S(1)} collective-permute-done((bf16[2,32,512]{2,1,0:T(8,128)(2,1)S(1)}, bf16[2,32,512]{2,1,0:T(8,128)(2,1)S(1)}, u32[]{:S(2)}, u32[]{:S(2)}) %collective-permute-start.7) | collective-permute-done | bytes 65568 | tf_op jit(solution)/shard_map/ppermute | solution.py:28
  29.4 0.0 collective-permute-done.4.refs_2_
  29.4 0.0 collective-permute-done.5.refs_3_
  29.4 3.7 %shard_map.97 = (f32[8,768]{1,0:T(8,128)S(1)}, f32[8,768]{1,0:T(8,128)S(1)}, f32[4,64,768]{2,1,0:T(8,128)S(1)}, f32[512,128]{1,0:T(8,128)S(1)}) custom-call(f32[8,512]{1,0:T(8,128)S(1)} %get-tuple-element.23.mask, bf16[192,512]{1,0:T(8,128)(2,1)S(1)} %get-tuple-element.47.refs_0_, bf16[192,512]{1,0:T(8,128)(2,1)S(1)} %get-tuple-element.46.refs_1_, ...), custom_call_target="tpu_custom_call" | custom-call | tf_op jit(solution)/shard_map/pallas_call | solution.py:331
  33.1 1.8 %collective-permute-start.8 = (bf16[2,64,512]{2,1,0:T(8,128)(2,1)S(1)}, bf16[2,64,512]{2,1,0:T(8,128)(2,1)S(1)}, u32[]{:S(2)}, u32[]{:S(2)}) collective-permute-start(bf16[2,64,512]{2,1,0:T(8,128)(2,1)S(1)} %pad_maximum_fusion.1), channel_id=1, source_target_pairs={{2,0},{0,2},{6,4},{4,6},{10,8},{8,10},{14,12},{12,14},{3,1},{1,3},... | collective-permute-start | bytes 393224 | tf_op jit(solution)/shard_map/ppermute | solution.py:28
  34.9 0.0 collective-permute-done.1
  34.9 0.1 collective-permute-start.10
  35.0 0.5 %collective-permute-start.9 = (bf16[192,512]{1,0:T(8,128)(2,1)S(1)}, bf16[192,512]{1,0:T(8,128)(2,1)S(1)}, u32[]{:S(2)}, u32[]{:S(2)}) collective-permute-start(bf16[192,512]{1,0:T(8,128)(2,1)S(1)} %get-tuple-element.45.refs_0_), channel_id=1, source_target_pairs={{1,0},{0,1},{3,2},{2,3},{5,4},{4,5},{7,6},{6,7},{9,8},{8,9},{11,10... | collective-permute-start | bytes 589832 | tf_op jit(solution)/shard_map/ppermute | solution.py:28
  35.5 2.6 %collective-permute-done.8 = bf16[2,64,512]{2,1,0:T(8,128)(2,1)S(1)} collective-permute-done((bf16[2,64,512]{2,1,0:T(8,128)(2,1)S(1)}, bf16[2,64,512]{2,1,0:T(8,128)(2,1)S(1)}, u32[]{:S(2)}, u32[]{:S(2)}) %collective-permute-start.8) | collective-permute-done | bytes 131104 | tf_op jit(solution)/shard_map/ppermute | solution.py:28
  38.1 0.0 collective-permute-done.10.refs_4_
  38.1 0.0 collective-permute-done.9.refs_3_
  38.2 6.2 %shard_map.98 = (f32[400,512]{1,0:T(8,128)S(1)}, bf16[400,512]{1,0:T(8,128)(2,1)S(1)}) custom-call(f32[8,512]{1,0:T(8,128)S(1)} %get-tuple-element.23.mask, bf16[192,512]{1,0:T(8,128)(2,1)S(1)} %get-tuple-element.45.refs_0_, bf16[192,512]{1,0:T(8,128)(2,1)S(1)} %get-tuple-element.44.refs_1_, bf16[2,128,512]{2,1,0:T(8,128)(2,1)S(1)} %pad_maximum_fusion.refs_2_.refs_5_, ...), custom_call_target="tpu_custom_call" | custom-call | tf_op jit(solution)/shard_map/pallas_call | solution.py:331
  44.4 0.1 collective-permute-start.11
  44.5 1.7 %collective-permute-done.11.received = bf16[400,512]{1,0:T(8,128)(2,1)S(1)} collective-permute-done((bf16[400,512]{1,0:T(8,128)(2,1)S(1)}, bf16[400,512]{1,0:T(8,128)(2,1)S(1)}, u32[]{:S(2)}, u32[]{:S(2)}) %collective-permute-start.11) | collective-permute-done | bytes 409632 | tf_op jit(solution)/shard_map/ppermute | solution.py:28
  46.2 0.8 %shard_map.99 = (bf16[384,512]{1,0:T(8,128)(2,1)}, bf16[5,2,512]{2,1,0:T(2,128)(2,1)}) custom-call(f32[400,512]{1,0:T(8,128)S(1)} %get-tuple-element.40.kept, bf16[400,512]{1,0:T(8,128)(2,1)S(1)} %collective-permute-done.11.received), custom_call_target="tpu_custom_call" | custom-call | tf_op jit(solution)/shard_map/pallas_call | solution.py:331
  (5 shorter events, 0.1 us)
Async XLA Ops:
  0.6 9.7 %collective-permute-start.3 = (bf16[384,512]{1,0:T(8,128)(2,1)}, bf16[384,512]{1,0:T(8,128)(2,1)S(1)}, u32[]{:S(2)}, u32[]{:S(2)}) collective-permute-start(bf16[384,512]{1,0:T(8,128)(2,1)} %bitcast.4), channel_id=1, source_target_pairs={{1,0},{0,1},{3,2},{2,3},{5,4},{4,5},{7,6},{6,7},{9,8},{8,9},{11,10... | collective-permute-start | bytes 1179656 | tf_op jit(solution)/shard_map/ppermute | solution.py:28
  1.2 20.9 %collective-permute-start.2 = (bf16[384,512]{1,0:T(8,128)(2,1)}, bf16[384,512]{1,0:T(8,128)(2,1)S(1)}, u32[]{:S(2)}, u32[]{:S(2)}) collective-permute-start(bf16[384,512]{1,0:T(8,128)(2,1)} %bitcast.5), channel_id=1, source_target_pairs={{2,0},{0,2},{6,4},{4,6},{10,8},{8,10},{14,12},{12,14},{3,1},{1,3},... | collective-permute-start | bytes 1179656 | tf_op jit(solution)/shard_map/ppermute | solution.py:28
  3.7 3.7 %collective-permute-start = (bf16[5,2,512]{2,1,0:T(2,128)(2,1)}, bf16[5,2,512]{2,1,0:T(2,128)(2,1)S(1)}, u32[]{:S(2)}, u32[]{:S(2)}) collective-permute-start(bf16[5,2,512]{2,1,0:T(2,128)(2,1)} %bitcast.7), channel_id=1, source_target_pairs={{1,0},{0,1},{3,2},{2,3},{5,4},{4,5},{7,6},{6,7},{9,8},{8,9},{11,10... | collective-permute-start | bytes 30728 | tf_op jit(solution)/shard_map/ppermute | solution.py:28
  3.9 31.0 %collective-permute-start.1 = (bf16[384,512]{1,0:T(8,128)(2,1)}, bf16[384,512]{1,0:T(8,128)(2,1)S(1)}, u32[]{:S(2)}, u32[]{:S(2)}) collective-permute-start(bf16[384,512]{1,0:T(8,128)(2,1)} %bitcast.6), channel_id=1, source_target_pairs={{0,14},{2,4},{4,2},{6,8},{8,6},{10,12},{12,10},{14,0},{1,15},{3,5}... | collective-permute-start | bytes 1179656 | tf_op jit(solution)/shard_map/ppermute | solution.py:33
  7.5 0.6 %copy-start = (bf16[5,2,512]{2,1,0:T(2,128)(2,1)}, bf16[5,2,512]{2,1,0:T(2,128)(2,1)S(1)}, u32[]{:S(2)}) copy-start(bf16[5,2,512]{2,1,0:T(2,128)(2,1)S(1)} %collective-permute-done.other_specials) | copy-start | bytes 30724
  10.3 12.4 %collective-permute-start.6 = (bf16[2,16,512]{2,1,0:T(8,128)(2,1)S(1)}, bf16[2,16,512]{2,1,0:T(8,128)(2,1)S(1)}, u32[]{:S(2)}, u32[]{:S(2)}) collective-permute-start(bf16[2,16,512]{2,1,0:T(8,128)(2,1)S(1)} %get-tuple-element.25.special), channel_id=1, source_target_pairs={{4,0},{6,2},{0,4},{2,6},{12,8},{14,10},{8,12},{10,14},{5,1},{7,3},... | collective-permute-start | bytes 98312 | tf_op jit(solution)/shard_map/ppermute | solution.py:28
  22.1 7.3 %collective-permute-start.4 = (bf16[192,512]{1,0:T(8,128)(2,1)S(1)}, bf16[192,512]{1,0:T(8,128)(2,1)S(1)}, u32[]{:S(2)}, u32[]{:S(2)}) collective-permute-start(bf16[192,512]{1,0:T(8,128)(2,1)S(1)} %get-tuple-element.47.refs_0_), channel_id=1, source_target_pairs={{1,0},{0,1},{3,2},{2,3},{5,4},{4,5},{7,6},{6,7},{9,8},{8,9},{11,10... | collective-permute-start | bytes 589832 | tf_op jit(solution)/shard_map/ppermute | solution.py:28
  22.2 7.2 %collective-permute-start.5 = (bf16[192,512]{1,0:T(8,128)(2,1)S(1)}, bf16[192,512]{1,0:T(8,128)(2,1)S(1)}, u32[]{:S(2)}, u32[]{:S(2)}) collective-permute-start(bf16[192,512]{1,0:T(8,128)(2,1)S(1)} %get-tuple-element.46.refs_1_), channel_id=1, source_target_pairs={{1,0},{0,1},{3,2},{2,3},{5,4},{4,5},{7,6},{6,7},{9,8},{8,9},{11,10... | collective-permute-start | bytes 589832 | tf_op jit(solution)/shard_map/ppermute | solution.py:28
  22.7 6.7 %collective-permute-start.7 = (bf16[2,32,512]{2,1,0:T(8,128)(2,1)S(1)}, bf16[2,32,512]{2,1,0:T(8,128)(2,1)S(1)}, u32[]{:S(2)}, u32[]{:S(2)}) collective-permute-start(bf16[2,32,512]{2,1,0:T(8,128)(2,1)S(1)} %pad_maximum_fusion.2), channel_id=1, source_target_pairs={{8,0},{10,2},{12,4},{14,6},{0,8},{2,10},{4,12},{6,14},{9,1},{11,3}... | collective-permute-start | bytes 196616 | tf_op jit(solution)/shard_map/ppermute | solution.py:28
  33.1 5.0 %collective-permute-start.8 = (bf16[2,64,512]{2,1,0:T(8,128)(2,1)S(1)}, bf16[2,64,512]{2,1,0:T(8,128)(2,1)S(1)}, u32[]{:S(2)}, u32[]{:S(2)}) collective-permute-start(bf16[2,64,512]{2,1,0:T(8,128)(2,1)S(1)} %pad_maximum_fusion.1), channel_id=1, source_target_pairs={{2,0},{0,2},{6,4},{4,6},{10,8},{8,10},{14,12},{12,14},{3,1},{1,3},... | collective-permute-start | bytes 393224 | tf_op jit(solution)/shard_map/ppermute | solution.py:28
  34.9 3.2 %collective-permute-start.10 = (bf16[192,512]{1,0:T(8,128)(2,1)S(1)}, bf16[192,512]{1,0:T(8,128)(2,1)S(1)}, u32[]{:S(2)}, u32[]{:S(2)}) collective-permute-start(bf16[192,512]{1,0:T(8,128)(2,1)S(1)} %get-tuple-element.44.refs_1_), channel_id=1, source_target_pairs={{1,0},{0,1},{3,2},{2,3},{5,4},{4,5},{7,6},{6,7},{9,8},{8,9},{11,10... | collective-permute-start | bytes 589832 | tf_op jit(solution)/shard_map/ppermute | solution.py:28
  35.0 3.2 %collective-permute-start.9 = (bf16[192,512]{1,0:T(8,128)(2,1)S(1)}, bf16[192,512]{1,0:T(8,128)(2,1)S(1)}, u32[]{:S(2)}, u32[]{:S(2)}) collective-permute-start(bf16[192,512]{1,0:T(8,128)(2,1)S(1)} %get-tuple-element.45.refs_0_), channel_id=1, source_target_pairs={{1,0},{0,1},{3,2},{2,3},{5,4},{4,5},{7,6},{6,7},{9,8},{8,9},{11,10... | collective-permute-start | bytes 589832 | tf_op jit(solution)/shard_map/ppermute | solution.py:28
  44.4 1.8 %collective-permute-start.11 = (bf16[400,512]{1,0:T(8,128)(2,1)S(1)}, bf16[400,512]{1,0:T(8,128)(2,1)S(1)}, u32[]{:S(2)}, u32[]{:S(2)}) collective-permute-start(bf16[400,512]{1,0:T(8,128)(2,1)S(1)} %get-tuple-element.41), channel_id=1, source_target_pairs={{1,0},{0,1},{3,2},{2,3},{5,4},{4,5},{7,6},{6,7},{9,8},{8,9},{11,10... | collective-permute-start | bytes 1228808 | tf_op jit(solution)/shard_map/ppermute | solution.py:28

commit v6 on v5

--- a/solution.py
+++ b/solution.py
@@ -398,7 +398,7 @@
             frame_order, covisible, patch_rows, turned, swapped(turned, "head", 1),
             role_first, role_rest, w_qkv,
         ),
-        in_specs=[HBM] * 8,
+        in_specs=[HBM] * 4 + [VMEM] + [HBM] * 3,
         scratch=[
             pltpu.SMEM(frame_order.shape, jnp.int32),
             pltpu.SMEM(covisible.shape, jnp.int32),
@@ -408,11 +408,9 @@
             pltpu.SemaphoreType.DMA((6 + images + 3,)),
         ],
     )
-    if owner_count & (owner_count - 1):
-        bits, everywhere = [], lax.all_gather(specials, "blk", axis=1, tiled=True)
-    else:
-        bits = [1 << i for i in range(1, owner_count.bit_length() - 1)] + [1]
-        everywhere = gathered(specials, "blk", bits[:-1])
+    power = owner_count & (owner_count - 1) == 0
+    bits = [1 << i for i in range(1, owner_count.bit_length() - 1)] + [1] if power else []
+    everywhere = gathered(specials, "blk", bits[:1])
     queries, special_queries, *state = call(
         functools.partial(first_kernel, images),
         [bf16(pairs, PAIR, 2 * patch_total), bf16(width, heads * special_block), *state_shape],
@@ -428,15 +426,19 @@
         )
 
     image_rows = lambda owner: [(per_image, owner * images + b) for b in range(images)]
+    if power:
+        everywhere = gathered(after(everywhere, state[0]), "blk", bits[1:])
+    else:
+        everywhere = lax.all_gather(specials, "blk", axis=1, tiled=True)
     for i, part in enumerate(near):
         part = after(part, state[0])
         stretches = [[image] for image in image_rows(i + 1)]
         parts = [both(part[b * per_image : (b + 1) * per_image]) for b in range(images)]
+        if i == 0:
+            stretches.append([(everywhere.shape[1], None)])
+            parts.append((everywhere, everywhere))
         if i < len(near) - 1:
             state = later(stretches, parts, state)
-    everywhere = gathered(after(everywhere, state[0]), "blk", bits[-1:])
-    stretches.append([(everywhere.shape[1], None)])
-    parts.append((everywhere, everywhere))
     kept, sent = call(
         functools.partial(last_kernel, stretches, real_rows),
         [f32(rows, width), bf16(rows, width)],

time: 47.2 us -> 47.6 us (level)
  the two profiles are of different devices: /device:TPU:0 before, /device:TPU:25 now
where the time goes in v6:
time: 47.6 us; the launch traced here: 47.4 us
  waiting for transfers between devices  24 us (50%)
  Pallas kernels  16.5 us (35%)
  starting transfers between devices  6.09 us (13%)
  between operations  0.73 us (2%)
    ppermute x11, waiting for transfers between devices, swapped(): return lax.ppermute(block, axis, [(i ^ bit, i) for i in range(count)])  24 us
    pallas_call x5, Pallas kernels, call(): pl.pallas_call(kernel, out_shape=out_shape, in_specs=in_specs or [VMEM] *...  16.5 us
    ppermute x11, starting transfers between devices, swapped(): return lax.ppermute(block, axis, [(i ^ bit, i) for i in range(count)])  5.92 us
  transfers between devices with their start and end apart: 12, of which 7 were waited for; matrix products, arithmetic and copies ran while one was open for 0% of the time, Pallas kernels for 21%

profile of v6, /device:TPU:25, one launch (start us, length us, event | category | flops | bytes accessed | tf_op | source)
XLA Modules:
  0.0 47.4 jit_solution(5150057273732990446)
XLA Ops:
  0.6 0.7 %collective-permute-start.3 = (bf16[384,512]{1,0:T(8,128)(2,1)}, bf16[384,512]{1,0:T(8,128)(2,1)S(1)}, u32[]{:S(2)}, u32[]{:S(2)}) collective-permute-start(bf16[384,512]{1,0:T(8,128)(2,1)} %bitcast.4), channel_id=1, source_target_pairs={{1,0},{0,1},{3,2},{2,3},{5,4},{4,5},{7,6},{6,7},{9,8},{8,9},{11,10... | collective-permute-start | bytes 1179656 | tf_op jit(solution)/shard_map/ppermute | solution.py:28
  1.4 1.2 %collective-permute-start.2 = (bf16[384,512]{1,0:T(8,128)(2,1)}, bf16[384,512]{1,0:T(8,128)(2,1)S(1)}, u32[]{:S(2)}, u32[]{:S(2)}) collective-permute-start(bf16[384,512]{1,0:T(8,128)(2,1)} %bitcast.5), channel_id=1, source_target_pairs={{2,0},{0,2},{6,4},{4,6},{10,8},{8,10},{14,12},{12,14},{3,1},{1,3},... | collective-permute-start | bytes 1179656 | tf_op jit(solution)/shard_map/ppermute | solution.py:28
  2.6 0.0 copy-start
  2.6 0.3 collective-permute-start
  2.9 1.0 %collective-permute-done.other_specials = bf16[5,2,512]{2,1,0:T(2,128)(2,1)S(1)} collective-permute-done((bf16[5,2,512]{2,1,0:T(2,128)(2,1)}, bf16[5,2,512]{2,1,0:T(2,128)(2,1)S(1)}, u32[]{:S(2)}, u32[]{:S(2)}) %collective-permute-start) | collective-permute-done | bytes 10272 | tf_op jit(solution)/shard_map/ppermute | solution.py:28
  4.0 2.2 %shard_map.95 = (bf16[384,512]{1,0:T(8,128)(2,1)S(1)}, bf16[2,16,512]{2,1,0:T(8,128)(2,1)S(1)}, f32[8,512]{1,0:T(8,128)S(1)}, bf16[3,1024,512]{2,1,0:T(8,128)(2,1)S(1)}) custom-call(s32[2]{0:T(128)} %frame_order.1, s32[2,16]{1,0:T(2,128)} %covisible.1, bf16[2,192,512]{2,1,0:T(8,128)(2,1)} %patches.1, bf16[5,2,512]{2,1,0:T(2,128)(2,1)} %bitcast.8, ...), custom_call_target="tpu_custom_call" | custom-call | tf_op jit(solution)/shard_map/pallas_call | solution.py:331
  6.2 0.2 collective-permute-start.4
  6.4 2.9 %collective-permute-done.4 = bf16[2,16,512]{2,1,0:T(8,128)(2,1)S(1)} collective-permute-done((bf16[2,16,512]{2,1,0:T(8,128)(2,1)S(1)}, bf16[2,16,512]{2,1,0:T(8,128)(2,1)S(1)}, u32[]{:S(2)}, u32[]{:S(2)}) %collective-permute-start.4) | collective-permute-done | bytes 32800 | tf_op jit(solution)/shard_map/ppermute | solution.py:28
  9.3 0.0 collective-permute-done.3.other
  9.3 3.6 %shard_map.96 = (bf16[4,128,768]{2,1,0:T(8,128)(2,1)S(1)}, bf16[512,128]{1,0:T(8,128)(2,1)S(1)}, f32[8,768]{1,0:T(8,128)S(1)}, f32[8,768]{1,0:T(8,128)S(1)}, f32...) custom-call(f32[8,512]{1,0:T(8,128)S(1)} %get-tuple-element.23.mask, bf16[384,512]{1,0:T(8,128)(2,1)S(1)} %get-tuple-element.24.own, ...), custom_call_target="tpu_custom_call" | custom-call | tf_op jit(solution)/shard_map/pallas_call | solution.py:331
  13.0 0.1 collective-permute-start.5
  13.1 0.0 copy-done
  13.1 0.2 collective-permute-start.1
  13.3 0.0 collective-permute-done.2
  13.3 14.1 %collective-permute-done.5 = bf16[2,32,512]{2,1,0:T(8,128)(2,1)S(1)} collective-permute-done((bf16[2,32,512]{2,1,0:T(8,128)(2,1)S(1)}, bf16[2,32,512]{2,1,0:T(8,128)(2,1)S(1)}, u32[]{:S(2)}, u32[]{:S(2)}) %collective-permute-start.5) | collective-permute-done | bytes 65568 | tf_op jit(solution)/shard_map/ppermute | solution.py:28
  27.3 0.1 collective-permute-start.6
  27.4 0.9 %collective-permute-start.7 = (bf16[192,512]{1,0:T(8,128)(2,1)S(1)}, bf16[192,512]{1,0:T(8,128)(2,1)S(1)}, u32[]{:S(2)}, u32[]{:S(2)}) collective-permute-start(bf16[192,512]{1,0:T(8,128)(2,1)S(1)} %get-tuple-element.47.refs_0_), channel_id=1, source_target_pairs={{1,0},{0,1},{3,2},{2,3},{5,4},{4,5},{7,6},{6,7},{9,8},{8,9},{11,10... | collective-permute-start | bytes 589832 | tf_op jit(solution)/shard_map/ppermute | solution.py:28
  28.3 0.1 collective-permute-start.8
  28.4 3.2 %collective-permute-done.6 = bf16[2,64,512]{2,1,0:T(8,128)(2,1)S(1)} collective-permute-done((bf16[2,64,512]{2,1,0:T(8,128)(2,1)S(1)}, bf16[2,64,512]{2,1,0:T(8,128)(2,1)S(1)}, u32[]{:S(2)}, u32[]{:S(2)}) %collective-permute-start.6) | collective-permute-done | bytes 131104 | tf_op jit(solution)/shard_map/ppermute | solution.py:28
  31.6 0.0 collective-permute-done.7.refs_3_
  31.6 0.0 collective-permute-done.8.refs_4_
  31.6 4.4 %shard_map.97 = (f32[8,768]{1,0:T(8,128)S(1)}, f32[8,768]{1,0:T(8,128)S(1)}, f32[4,64,768]{2,1,0:T(8,128)S(1)}, f32[512,128]{1,0:T(8,128)S(1)}) custom-call(f32[8,512]{1,0:T(8,128)S(1)} %get-tuple-element.23.mask, bf16[192,512]{1,0:T(8,128)(2,1)S(1)} %get-tuple-element.47.refs_0_, bf16[192,512]{1,0:T(8,128)(2,1)S(1)} %get-tuple-element.46.refs_1_, ...), custom_call_target="tpu_custom_call" | custom-call | tf_op jit(solution)/shard_map/pallas_call | solution.py:331
  36.0 0.0 collective-permute-done.1
  36.0 1.8 %collective-permute-start.10 = (bf16[192,512]{1,0:T(8,128)(2,1)S(1)}, bf16[192,512]{1,0:T(8,128)(2,1)S(1)}, u32[]{:S(2)}, u32[]{:S(2)}) collective-permute-start(bf16[192,512]{1,0:T(8,128)(2,1)S(1)} %get-tuple-element.44.refs_1_), channel_id=1, source_target_pairs={{1,0},{0,1},{3,2},{2,3},{5,4},{4,5},{7,6},{6,7},{9,8},{8,9},{11,10... | collective-permute-start | bytes 589832 | tf_op jit(solution)/shard_map/ppermute | solution.py:28
  37.8 0.1 collective-permute-start.9
  37.9 1.0 %collective-permute-done.10.refs_3_ = bf16[192,512]{1,0:T(8,128)(2,1)S(1)} collective-permute-done((bf16[192,512]{1,0:T(8,128)(2,1)S(1)}, bf16[192,512]{1,0:T(8,128)(2,1)S(1)}, u32[]{:S(2)}, u32[]{:S(2)}) %collective-permute-start.10) | collective-permute-done | bytes 196640 | tf_op jit(solution)/shard_map/ppermute | solution.py:28
  38.9 0.4 collective-permute-done.9.refs_2_
  39.3 5.5 %shard_map.98 = (f32[400,512]{1,0:T(8,128)S(1)}, bf16[400,512]{1,0:T(8,128)(2,1)S(1)}) custom-call(f32[8,512]{1,0:T(8,128)S(1)} %get-tuple-element.23.mask, bf16[192,512]{1,0:T(8,128)(2,1)S(1)} %get-tuple-element.45.refs_0_, bf16[192,512]{1,0:T(8,128)(2,1)S(1)} %get-tuple-element.44.refs_1_, bf16[192,512]{1,0:T(8,128)(2,1)S(1)} %collective-permute-done.9.refs_2_, ...), custom_call_target="tpu_custom_call" | custom-call | tf_op jit(solution)/shard_map/pallas_call | solution.py:331
  44.8 0.3 collective-permute-start.11
  45.2 1.5 %collective-permute-done.11.received = bf16[400,512]{1,0:T(8,128)(2,1)S(1)} collective-permute-done((bf16[400,512]{1,0:T(8,128)(2,1)S(1)}, bf16[400,512]{1,0:T(8,128)(2,1)S(1)}, u32[]{:S(2)}, u32[]{:S(2)}) %collective-permute-start.11) | collective-permute-done | bytes 409632 | tf_op jit(solution)/shard_map/ppermute | solution.py:28
  46.6 0.8 %shard_map.99 = (bf16[384,512]{1,0:T(8,128)(2,1)}, bf16[5,2,512]{2,1,0:T(2,128)(2,1)}) custom-call(f32[400,512]{1,0:T(8,128)S(1)} %get-tuple-element.40.kept, bf16[400,512]{1,0:T(8,128)(2,1)S(1)} %collective-permute-done.11.received), custom_call_target="tpu_custom_call" | custom-call | tf_op jit(solution)/shard_map/pallas_call | solution.py:331
  (5 shorter events, 0.1 us)
Async XLA Ops:
  0.6 8.7 %collective-permute-start.3 = (bf16[384,512]{1,0:T(8,128)(2,1)}, bf16[384,512]{1,0:T(8,128)(2,1)S(1)}, u32[]{:S(2)}, u32[]{:S(2)}) collective-permute-start(bf16[384,512]{1,0:T(8,128)(2,1)} %bitcast.4), channel_id=1, source_target_pairs={{1,0},{0,1},{3,2},{2,3},{5,4},{4,5},{7,6},{6,7},{9,8},{8,9},{11,10... | collective-permute-start | bytes 1179656 | tf_op jit(solution)/shard_map/ppermute | solution.py:28
  1.4 11.9 %collective-permute-start.2 = (bf16[384,512]{1,0:T(8,128)(2,1)}, bf16[384,512]{1,0:T(8,128)(2,1)S(1)}, u32[]{:S(2)}, u32[]{:S(2)}) collective-permute-start(bf16[384,512]{1,0:T(8,128)(2,1)} %bitcast.5), channel_id=1, source_target_pairs={{2,0},{0,2},{6,4},{4,6},{10,8},{8,10},{14,12},{12,14},{3,1},{1,3},... | collective-permute-start | bytes 1179656 | tf_op jit(solution)/shard_map/ppermute | solution.py:28
  2.6 10.5 %copy-start = (bf16[2,192,512]{2,1,0:T(8,128)(2,1)S(1)}, bf16[2,192,512]{2,1,0:T(8,128)(2,1)}, u32[]{:S(2)}) copy-start(bf16[2,192,512]{2,1,0:T(8,128)(2,1)} %patches.1) | copy-start | bytes 1179652
  2.6 1.4 %collective-permute-start = (bf16[5,2,512]{2,1,0:T(2,128)(2,1)}, bf16[5,2,512]{2,1,0:T(2,128)(2,1)S(1)}, u32[]{:S(2)}, u32[]{:S(2)}) collective-permute-start(bf16[5,2,512]{2,1,0:T(2,128)(2,1)} %bitcast.7), channel_id=1, source_target_pairs={{1,0},{0,1},{3,2},{2,3},{5,4},{4,5},{7,6},{6,7},{9,8},{8,9},{11,10... | collective-permute-start | bytes 30728 | tf_op jit(solution)/shard_map/ppermute | solution.py:28
  6.2 3.1 %collective-permute-start.4 = (bf16[2,16,512]{2,1,0:T(8,128)(2,1)S(1)}, bf16[2,16,512]{2,1,0:T(8,128)(2,1)S(1)}, u32[]{:S(2)}, u32[]{:S(2)}) collective-permute-start(bf16[2,16,512]{2,1,0:T(8,128)(2,1)S(1)} %get-tuple-element.25.special), channel_id=1, source_target_pairs={{4,0},{6,2},{0,4},{2,6},{12,8},{14,10},{8,12},{10,14},{5,1},{7,3},... | collective-permute-start | bytes 98312 | tf_op jit(solution)/shard_map/ppermute | solution.py:28
  13.0 14.4 %collective-permute-start.5 = (bf16[2,32,512]{2,1,0:T(8,128)(2,1)S(1)}, bf16[2,32,512]{2,1,0:T(8,128)(2,1)S(1)}, u32[]{:S(2)}, u32[]{:S(2)}) collective-permute-start(bf16[2,32,512]{2,1,0:T(8,128)(2,1)S(1)} %pad_maximum_fusion.2), channel_id=1, source_target_pairs={{8,0},{10,2},{12,4},{14,6},{0,8},{2,10},{4,12},{6,14},{9,1},{11,3}... | collective-permute-start | bytes 196616 | tf_op jit(solution)/shard_map/ppermute | solution.py:28
  13.1 22.9 %collective-permute-start.1 = (bf16[384,512]{1,0:T(8,128)(2,1)S(1)}, bf16[384,512]{1,0:T(8,128)(2,1)S(1)}, u32[]{:S(2)}, u32[]{:S(2)}) collective-permute-start(bf16[384,512]{1,0:T(8,128)(2,1)S(1)} %bitcast.6), channel_id=1, source_target_pairs={{0,14},{2,4},{4,2},{6,8},{8,6},{10,12},{12,10},{14,0},{1,15},{3,5}... | collective-permute-start | bytes 1179656 | tf_op jit(solution)/shard_map/ppermute | solution.py:33
  27.3 4.2 %collective-permute-start.6 = (bf16[2,64,512]{2,1,0:T(8,128)(2,1)S(1)}, bf16[2,64,512]{2,1,0:T(8,128)(2,1)S(1)}, u32[]{:S(2)}, u32[]{:S(2)}) collective-permute-start(bf16[2,64,512]{2,1,0:T(8,128)(2,1)S(1)} %pad_maximum_fusion.1), channel_id=1, source_target_pairs={{2,0},{0,2},{6,4},{4,6},{10,8},{8,10},{14,12},{12,14},{3,1},{1,3},... | collective-permute-start | bytes 393224 | tf_op jit(solution)/shard_map/ppermute | solution.py:28
  27.4 4.2 %collective-permute-start.7 = (bf16[192,512]{1,0:T(8,128)(2,1)S(1)}, bf16[192,512]{1,0:T(8,128)(2,1)S(1)}, u32[]{:S(2)}, u32[]{:S(2)}) collective-permute-start(bf16[192,512]{1,0:T(8,128)(2,1)S(1)} %get-tuple-element.47.refs_0_), channel_id=1, source_target_pairs={{1,0},{0,1},{3,2},{2,3},{5,4},{4,5},{7,6},{6,7},{9,8},{8,9},{11,10... | collective-permute-start | bytes 589832 | tf_op jit(solution)/shard_map/ppermute | solution.py:28
  28.3 3.3 %collective-permute-start.8 = (bf16[192,512]{1,0:T(8,128)(2,1)S(1)}, bf16[192,512]{1,0:T(8,128)(2,1)S(1)}, u32[]{:S(2)}, u32[]{:S(2)}) collective-permute-start(bf16[192,512]{1,0:T(8,128)(2,1)S(1)} %get-tuple-element.46.refs_1_), channel_id=1, source_target_pairs={{1,0},{0,1},{3,2},{2,3},{5,4},{4,5},{7,6},{6,7},{9,8},{8,9},{11,10... | collective-permute-start | bytes 589832 | tf_op jit(solution)/shard_map/ppermute | solution.py:28
  36.0 2.9 %collective-permute-start.10 = (bf16[192,512]{1,0:T(8,128)(2,1)S(1)}, bf16[192,512]{1,0:T(8,128)(2,1)S(1)}, u32[]{:S(2)}, u32[]{:S(2)}) collective-permute-start(bf16[192,512]{1,0:T(8,128)(2,1)S(1)} %get-tuple-element.44.refs_1_), channel_id=1, source_target_pairs={{1,0},{0,1},{3,2},{2,3},{5,4},{4,5},{7,6},{6,7},{9,8},{8,9},{11,10... | collective-permute-start | bytes 589832 | tf_op jit(solution)/shard_map/ppermute | solution.py:28
  37.8 1.4 %collective-permute-start.9 = (bf16[192,512]{1,0:T(8,128)(2,1)S(1)}, bf16[192,512]{1,0:T(8,128)(2,1)S(1)}, u32[]{:S(2)}, u32[]{:S(2)}) collective-permute-start(bf16[192,512]{1,0:T(8,128)(2,1)S(1)} %get-tuple-element.45.refs_0_), channel_id=1, source_target_pairs={{1,0},{0,1},{3,2},{2,3},{5,4},{4,5},{7,6},{6,7},{9,8},{8,9},{11,10... | collective-permute-start | bytes 589832 | tf_op jit(solution)/shard_map/ppermute | solution.py:28
  44.8 1.8 %collective-permute-start.11 = (bf16[400,512]{1,0:T(8,128)(2,1)S(1)}, bf16[400,512]{1,0:T(8,128)(2,1)S(1)}, u32[]{:S(2)}, u32[]{:S(2)}) collective-permute-start(bf16[400,512]{1,0:T(8,128)(2,1)S(1)} %get-tuple-element.41), channel_id=1, source_target_pairs={{1,0},{0,1},{3,2},{2,3},{5,4},{4,5},{7,6},{6,7},{9,8},{8,9},{11,10... | collective-permute-start | bytes 1228808 | tf_op jit(solution)/shard_map/ppermute | solution.py:28

commit v7 on v5

--- a/solution.py
+++ b/solution.py
@@ -11,6 +11,8 @@
 PAIR = 2 * HEAD_DIM
 QUAD = 2 * PAIR
 TILE_ROWS = 16
+LOG2_E = 1.4426950408889634
+FIRST = 20_000_000_000
 VMEM_BYTES = 32 * 1024 * 1024
 SMEM = pl.BlockSpec(memory_space=pltpu.SMEM)
 VMEM = pl.BlockSpec(memory_space=pltpu.VMEM)
@@ -52,18 +54,32 @@
     return lax.rem(here + offset + count, count)
 
 
+def special_kernel(frame_order, specials, role_first, role_rest, special_out, order, here, first_rows, rest_rows, copied):
+    special_count, images, width = specials.shape
+    moves = [(specials, here), (role_first, first_rows), (role_rest, rest_rows), (frame_order, order)]
+    copies = [
+        pltpu.make_async_copy(source, target, copied.at[i]) for i, (source, target) in enumerate(moves)
+    ]
+    for copy in copies:
+        copy.start()
+    for copy in copies:
+        copy.wait()
+    mine, _ = halves(width)
+    first = first_rows[:, mine].astype(jnp.float32)
+    rest = rest_rows[:, mine].astype(jnp.float32)
+    summed = [
+        here[:, b, :].astype(jnp.float32) + jnp.where(order[b] == 0, first, rest) for b in range(images)
+    ]
+    summed.append(jnp.zeros((special_out.shape[0] - images * special_count, width), jnp.float32))
+    special_out[...] = jnp.concatenate(summed, axis=0).astype(jnp.bfloat16)
+
+
 def start_kernel(
-    offsets, special_total, frame_order, covisible, patches, specials, other_specials, role_first, role_rest,
-    w_qkv, own_out, special_out, mask_out, weights_out, order, seen, special_here, first_rows, rest_rows, copied,
+    offsets, special_count, special_total, covisible, patches, w_qkv, own_out, mask_out, weights_out, seen, copied
 ):
     images, per_image, width = patches.shape
-    special_count = specials.shape[0]
     patch_total = images * per_image
-    moves = [
-        (specials, special_here.at[0]), (other_specials, special_here.at[1]), (role_first, first_rows),
-        (role_rest, rest_rows), (frame_order, order), (covisible, seen),
-    ]
-    small = len(moves)
+    moves = [(covisible, seen)]
     moves += [(patches.at[b], own_out.at[pl.ds(b * per_image, per_image)]) for b in range(images)]
     moves += [(w_qkv.at[i], weights_out.at[i]) for i in range(3)]
     copies = [
@@ -71,17 +87,7 @@
     ]
     for copy in copies:
         copy.start()
-    for copy in copies[:small]:
-        copy.wait()
-    for i, columns in enumerate(halves(width)):
-        first = first_rows[:, columns].astype(jnp.float32)
-        rest = rest_rows[:, columns].astype(jnp.float32)
-        summed = [
-            special_here[i, :, b, :].astype(jnp.float32) + jnp.where(order[b] == 0, first, rest)
-            for b in range(images)
-        ]
-        summed.append(jnp.zeros((special_total - images * special_count, width), jnp.float32))
-        special_out[i] = jnp.concatenate(summed, axis=0).astype(jnp.bfloat16)
+    copies[0].wait()
     lane = lax.broadcasted_iota(jnp.int32, (1, mask_out.shape[1]), 1)
     special_lane = lax.rem(lane - patch_total, special_total)
     image = jnp.where(
@@ -94,7 +100,7 @@
                 hidden = seen[a, owner_at(offset) * images + b] <= 0
                 row = jnp.where((image == a) & hidden, -jnp.inf, row)
             mask_out[i * images + b : i * images + b + 1, :] = row
-    for copy in copies[small:]:
+    for copy in copies[1:]:
         copy.wait()
 
 
@@ -119,17 +125,34 @@
     weights, start = [], 0
     for count, mask in masks:
         level = largest if mask is None else largest - mask
-        weights.append(jnp.exp(scores[start : start + count] - level).astype(jnp.bfloat16))
+        weights.append(jnp.exp2((scores[start : start + count] - level).astype(jnp.bfloat16)))
         start += count
-    factor = None if state is None else jnp.exp(state - largest)
+    factor = None if state is None else jnp.exp2(state - largest)
     return largest, factor, jnp.concatenate(weights, axis=0)
 
 
 def attend_all(columns, masks, queries_of, special_queries, state, pairs, rows, special_real):
-    keys, values = [], []
-
-    def scored(keys, queries):
-        scores = product(keys, queries)
+    keys, values = {}, {}
+    quads = pairs // 2
+
+    def keys_of(quad):
+        if quad not in keys:
+            keys[quad] = columns(1, quad).astype(jnp.bfloat16)
+        return keys[quad]
+
+    def values_of(quad):
+        if quad not in values:
+            values[quad] = jnp.transpose(columns(2, quad)).astype(jnp.bfloat16)
+        return values[quad]
+
+    def prepared(pair):
+        if pair == pairs:
+            scores = product(
+                jnp.concatenate([keys_of(quad) for quad in range(quads)], axis=1), special_queries()
+            )
+        else:
+            lanes = slice((pair % 2) * PAIR, (pair % 2 + 1) * PAIR)
+            scores = product(keys_of(pair // 2)[:, lanes], queries_of(pair))
         if all(mask is not None for _, mask in masks):
             return scores
         parts, start = [], 0
@@ -142,42 +165,37 @@
             start += count
         return jnp.concatenate(parts, axis=0)
 
-    def prepared(pair):
-        if pair == pairs:
-            return scored(jnp.concatenate(keys, axis=1), special_queries())
-        if pair % 2 == 0:
-            keys.append(columns(1, pair // 2).astype(jnp.bfloat16))
-        lanes = slice((pair % 2) * PAIR, (pair % 2 + 1) * PAIR)
-        return scored(keys[pair // 2][:, lanes], queries_of(pair))
-
     ones = jnp.ones((TILE_ROWS, sum(count for count, _ in masks)), jnp.bfloat16)
     both = [
         (count, None if mask is None else jnp.concatenate([mask[:, :rows]] * 2, axis=1))
         for count, mask in masks
     ]
     only = [(count, None if mask is None else mask[:, rows:]) for count, mask in masks]
-    scores = prepared(0)
-    for pair in range(pairs):
-        if pair % 2 == 0:
-            values.append(jnp.transpose(columns(2, pair // 2)).astype(jnp.bfloat16))
-        following = prepared(pair + 1)
-        largest, factor, weights = attend(scores, both, state and state.largest(pair))
-        for sub in range(2):
-            first = (pair % 2) * PAIR + sub * HEAD_DIM
-            lanes = slice(sub * rows, (sub + 1) * rows)
-            left = jnp.concatenate([values[pair // 2][first : first + HEAD_DIM], ones], axis=0)
-            added = product(left, weights[:, lanes])[: HEAD_DIM + 1]
+    order = list(range(pairs))
+    order.insert(pairs - 2, pairs)
+    scores = prepared(order[0])
+    for step, pair in enumerate(order):
+        if pair < pairs:
+            left = [
+                values_of(pair // 2)[first : first + HEAD_DIM]
+                for first in ((pair % 2) * PAIR, (pair % 2) * PAIR + HEAD_DIM)
+            ]
+        else:
+            left = [jnp.concatenate([values_of(quad) for quad in range(quads)], axis=0)]
+        following = prepared(order[step + 1]) if step < pairs else None
+        largest, factor, weights = attend(
+            scores, both if pair < pairs else only, state and state.largest(pair)
+        )
+        width = scores.shape[1] // len(left)
+        for sub, part in enumerate(left):
+            lanes = slice(sub * width, (sub + 1) * width)
+            added = product(jnp.concatenate([part, ones], axis=0), weights[:, lanes])
+            total, weight = added[: part.shape[0]], added[part.shape[0] : part.shape[0] + 1]
             if state is not None:
-                before = jnp.concatenate([state.total(pair, sub), state.weight(pair, sub)], axis=0)
-                added = added + before * factor[:, lanes]
-            yield pair, sub, largest[:, lanes], added[:HEAD_DIM], added[HEAD_DIM:]
+                total = total + state.total(pair, sub) * factor[:, lanes]
+                weight = weight + state.weight(pair, sub) * factor[:, lanes]
+            yield pair, sub, largest[:, lanes], total, weight
         scores = following
-    largest, factor, weights = attend(scores, only, state and state.largest(pairs))
-    added = product(jnp.concatenate(values + [ones], axis=0), weights)[: pairs * PAIR + 1]
-    if state is not None:
-        before = jnp.concatenate([state.total(pairs, 0), state.weight(pairs, 0)], axis=0)
-        added = added + before * factor
-    yield pairs, 0, largest, added[:-1], added[-1:]
 
 
 class State:
@@ -213,35 +231,39 @@
 
 
 def first_kernel(
-    images, mask, own, other, special, weights, queries_out, special_out, *state_out
+    images, mask, own, other, special, other_special, weights, queries_out, special_out, *state_out
 ):
     patch_total = own.shape[0]
     columns = projector(
-        jnp.concatenate([own[...], special[0]], axis=0),
-        jnp.concatenate([other[...], special[1]], axis=0),
+        jnp.concatenate([own[...], special[...]], axis=0),
+        jnp.concatenate([other[...], other_special[...]], axis=0),
         weights,
     )
     pairs = queries_out.shape[0]
     zero = jnp.zeros((HEAD_DIM, patch_total), jnp.bfloat16)
-    special_columns = []
+    made = {}
 
     def patch_columns(which, quad):
         return columns(which, quad)[:patch_total]
 
-    def queries_of(pair):
-        if pair % 2 == 0:
-            queries = columns(0, pair // 2) * HEAD_DIM ** (-0.5)
-            special_columns.append(queries[patch_total:])
+    def columns_of(quad):
+        if quad not in made:
+            queries = columns(0, quad) * (HEAD_DIM ** (-0.5) * LOG2_E)
+            made[quad] = queries[patch_total:]
             turned = jnp.transpose(queries[:patch_total]).astype(jnp.bfloat16)
             for i in range(2):
                 first = i * PAIR
                 upper = jnp.concatenate([turned[first : first + HEAD_DIM], zero], axis=1)
                 lower = jnp.concatenate([zero, turned[first + HEAD_DIM : first + PAIR]], axis=1)
-                queries_out[pair + i] = jnp.concatenate([upper, lower], axis=0)
+                queries_out[2 * quad + i] = jnp.concatenate([upper, lower], axis=0)
+        return made[quad]
+
+    def queries_of(pair):
+        columns_of(pair // 2)
         return queries_out[pair]
 
     def special_queries():
-        block = jnp.concatenate(special_columns, axis=1)
+        block = jnp.concatenate([columns_of(quad) for quad in range(pairs // 2)], axis=1)
         count = block.shape[0]
         block = jnp.concatenate([block] * (2 * pairs), axis=0)
         row = lax.broadcasted_iota(jnp.int32, block.shape, 0) // count
@@ -261,10 +283,8 @@
 
 def joined(stretches, mask, refs):
     count = len(stretches)
-    own = jnp.concatenate([ref[0] if len(ref.shape) > 2 else ref[...] for ref in refs[:count]], axis=0)
-    other = jnp.concatenate(
-        [ref[1] if len(ref.shape) > 2 else ref[...] for ref in refs[count : 2 * count]], axis=0
-    )
+    own = jnp.concatenate([ref[...] for ref in refs[:count]], axis=0)
+    other = jnp.concatenate([ref[...] for ref in refs[count : 2 * count]], axis=0)
     masks = [
         (rows, None if i is None else mask[i : i + 1, :]) for part in stretches for rows, i in part
     ]
@@ -292,23 +312,37 @@
     copy = pltpu.make_async_copy(w_out, w_here, copied)
     copy.start()
     pairs, rows = queries.shape[0], queries.shape[2] // 2
-    columns = []
-    for pair, _, _, total, weight in attend_all(
+    columns, out, special = [], None, None
+    for pair, sub, _, total, weight in attend_all(
         projector(own, other, weights), masks, lambda pair: queries[pair], lambda: special_queries[...],
         State(rows, state_in), pairs, rows, special_real,
     ):
+        if pair == 0 and sub == 0:
+            copy.wait()
+        if pair == pairs:
+            special = total / weight
+            row = lax.broadcasted_iota(jnp.int32, special.shape, 0) // HEAD_DIM
+            lane = lax.broadcasted_iota(jnp.int32, special.shape, 1) // TILE_ROWS
+            special = jnp.transpose(jnp.where(row == lane, special, 0.0))
+            special = sum(special[i * TILE_ROWS : (i + 1) * TILE_ROWS] for i in range(2 * pairs))
+            special = product(special.astype(jnp.bfloat16), w_here[...])
+            continue
         columns.append(total / weight)
-    special = columns.pop()
-    attended = jnp.transpose(jnp.concatenate(columns, axis=0))
-    row = lax.broadcasted_iota(jnp.int32, special.shape, 0) // HEAD_DIM
-    lane = lax.broadcasted_iota(jnp.int32, special.shape, 1) // TILE_ROWS
-    special = jnp.transpose(jnp.where(row == lane, special, 0.0))
-    special = sum(special[i * TILE_ROWS : (i + 1) * TILE_ROWS] for i in range(2 * pairs))
-    attended = jnp.concatenate([attended, special], axis=0).astype(jnp.bfloat16)
-    mine, theirs = halves(kept_out.shape[1])
-    copy.wait()
-    sent_out[...] = product(attended, w_here[:, theirs]).astype(jnp.bfloat16)
-    kept_out[...] = product(attended, w_here[:, mine])
+        if pair % 2 == 1 and sub == 1:
+            quad = jnp.transpose(jnp.concatenate(columns, axis=0)).astype(jnp.bfloat16)
+            added = product(quad, w_here[(pair // 2) * QUAD : (pair // 2 + 1) * QUAD, :])
+            out = added if out is None else out + added
+            columns = []
+    half = lax.axis_index("head")
+    width = kept_out.shape[1]
+
+    def put(place, values):
+        left, right = values[:, :width], values[:, width:]
+        kept_out[place, :] = jnp.where(half == 0, left, right)
+        sent_out[place, :] = jnp.where(half == 0, right, left).astype(jnp.bfloat16)
+
+    put(slice(0, rows), out)
+    put(slice(rows, kept_out.shape[0]), special)
 
 
 def end_kernel(images, kept, received, patch_out, special_out):
@@ -322,7 +356,7 @@
     special_out[...] = jnp.concatenate(rows, axis=1).astype(jnp.bfloat16)
 
 
-def call(kernel, out_shape, operands, in_specs=None, out_specs=None, scratch=(), cost=0):
+def call(kernel, out_shape, operands, in_specs=None, out_specs=None, scratch=(), flops=0):
     if in_specs:
         operands = [
             pltpu.with_memory_space_constraint(operand, pltpu.HBM) if spec is HBM else operand
@@ -335,13 +369,20 @@
         out_specs=out_specs or [VMEM] * len(out_shape),
         scratch_shapes=scratch,
         compiler_params=pltpu.CompilerParams(vmem_limit_bytes=VMEM_BYTES),
-        cost_estimate=pl.CostEstimate(flops=cost, transcendentals=0, bytes_accessed=0),
+        cost_estimate=pl.CostEstimate(flops=flops, transcendentals=0, bytes_accessed=0),
     )(*operands)
 
 
-def gathered(block, axis, bits):
+def stack_kernel(first, second, out):
+    count = first.shape[0]
+    out[:count, :] = first[...]
+    out[count:, :] = second[...]
+
+
+def gathered(block, axis, bits, flops=0):
     for bit in bits:
-        block = jnp.concatenate([block, swapped(block, axis, bit)], axis=1)
+        shape = jax.ShapeDtypeStruct((2 * block.shape[0], block.shape[1]), block.dtype)
+        (block,) = call(stack_kernel, [shape], (block, swapped(block, axis, bit)), flops=flops)
     return block
 
 
@@ -381,42 +422,41 @@
     both = lambda part: (part, swapped(part, "head", 1))
     patches = patch_rows.reshape(patch_total, width)
     turned = jnp.transpose(special_rows, (1, 0, 2))
-    if paired:
-        near = [swapped(patches, "blk", 1), crossed(patches, "blk")]
-    else:
-        near = [shifted(patches, "blk", -offset) for offset in offsets[1:]]
-    other = swapped(patches, "head", 1)
-    own, specials, mask, weights = call(
-        functools.partial(start_kernel, offsets, special_block),
+    power = owner_count & (owner_count - 1) == 0
+    (specials,) = call(
+        special_kernel,
+        [bf16(special_block, width)],
+        (frame_order, turned, role_first, role_rest),
+        in_specs=[HBM] * 4,
+        scratch=[
+            pltpu.SMEM(frame_order.shape, jnp.int32),
+            pltpu.VMEM(turned.shape, jnp.bfloat16),
+            pltpu.VMEM(role_first.shape, jnp.bfloat16),
+            pltpu.VMEM(role_rest.shape, jnp.bfloat16),
+            pltpu.SemaphoreType.DMA((4,)),
+        ],
+    )
+    bits = [1 << i for i in range(owner_count.bit_length() - 1)] if power else []
+    everywhere = gathered(gathered(specials, "blk", bits[:1], FIRST), "blk", bits[1:2])
+    own, mask, weights = call(
+        functools.partial(start_kernel, offsets, special_count, special_block),
         [
             bf16(patch_total, width),
-            bf16(2, special_block, width),
             f32(mask_rows, patch_total + heads * special_block),
             bf16(*w_qkv.shape),
         ],
-        (
-            frame_order, covisible, patch_rows, turned, swapped(turned, "head", 1),
-            role_first, role_rest, w_qkv,
-        ),
-        in_specs=[HBM] * 8,
-        scratch=[
-            pltpu.SMEM(frame_order.shape, jnp.int32),
-            pltpu.SMEM(covisible.shape, jnp.int32),
-            pltpu.VMEM((2, *turned.shape), jnp.bfloat16),
-            pltpu.VMEM(role_first.shape, jnp.bfloat16),
-            pltpu.VMEM(role_rest.shape, jnp.bfloat16),
-            pltpu.SemaphoreType.DMA((6 + images + 3,)),
-        ],
-    )
-    if owner_count & (owner_count - 1):
-        bits, everywhere = [], lax.all_gather(specials, "blk", axis=1, tiled=True)
+        (covisible, patch_rows, w_qkv),
+        in_specs=[HBM] * 3,
+        scratch=[pltpu.SMEM(covisible.shape, jnp.int32), pltpu.SemaphoreType.DMA((1 + images + 3,))],
+    )
+    if paired:
+        near = [swapped(patches, "blk", 1), crossed(after(patches, everywhere, mask), "blk")]
     else:
-        bits = [1 << i for i in range(1, owner_count.bit_length() - 1)] + [1]
-        everywhere = gathered(specials, "blk", bits[:-1])
+        near = [shifted(patches, "blk", -offset) for offset in offsets[1:]]
     queries, special_queries, *state = call(
         functools.partial(first_kernel, images),
         [bf16(pairs, PAIR, 2 * patch_total), bf16(width, heads * special_block), *state_shape],
-        (mask, own, other, specials, weights),
+        (mask, own, swapped(patches, "head", 1), *both(specials), weights),
     )
     fixed = (weights, queries, special_queries)
 
@@ -430,13 +470,17 @@
     image_rows = lambda owner: [(per_image, owner * images + b) for b in range(images)]
     for i, part in enumerate(near):
         part = after(part, state[0])
+        if i == 0:
+            if power:
+                everywhere = gathered(after(everywhere, part), "blk", bits[2:])
+            else:
+                everywhere = lax.all_gather(specials, "blk", axis=0, tiled=True)
         stretches = [[image] for image in image_rows(i + 1)]
         parts = [both(part[b * per_image : (b + 1) * per_image]) for b in range(images)]
         if i < len(near) - 1:
             state = later(stretches, parts, state)
-    everywhere = gathered(after(everywhere, state[0]), "blk", bits[-1:])
-    stretches.append([(everywhere.shape[1], None)])
-    parts.append((everywhere, everywhere))
+    stretches.append([(everywhere.shape[0], None)])
+    parts.append(both(after(everywhere, state[0])))
     kept, sent = call(
         functools.partial(last_kernel, stretches, real_rows),
         [f32(rows, width), bf16(rows, width)],

time: 47.2 us -> 42.6 us (0.903)
  waiting for transfers between devices: 16.2 us -> 8.45 us
  starting transfers between devices: 12.8 us -> 16.1 us
  local copies, waits for them, and re-layouts: 0.65 us -> 0.06 us
    ppermute x11 -> x12, waiting for transfers between devices: 16.2 us -> 8.45 us  [swapped(): return lax.ppermute(block, axis, [(i ^ bit, i) for i in range(count)])]
    ppermute x11 -> x12, starting transfers between devices: 9.24 us -> 11.3 us  [swapped(): return lax.ppermute(block, axis, [(i ^ bit, i) for i in range(count)])]
    ppermute x1, starting transfers between devices: 3.57 us -> 4.78 us  [crossed(): lax.ppermute(block, axis, [(i, (i + (-1 if i % 2 == 0 else 1)) % count) f...]
    unnamed x2, local copies, waits for them, and re-layouts: 0.6 us -> 0.01 us
    pallas_call x5 -> x9, Pallas kernels: 16.6 us -> 17 us  [call(): pl.pallas_call(kernel, out_shape=out_shape, in_specs=in_specs or [VMEM] *...]
  transfers between devices with their start and end apart: 12 -> 13, of which waited for: 4 -> 4; matrix products, arithmetic and copies ran while one was open for 0% -> 0% of each run, Pallas kernels for 20% -> 21%
where the time goes in v7:
time: 42.6 us; the launch traced here: 42.3 us
  Pallas kernels  17 us (40%)
  starting transfers between devices  16.1 us (38%)
  waiting for transfers between devices  8.45 us (20%)
  between operations  0.74 us (2%)
    pallas_call x9, Pallas kernels, call(): pl.pallas_call(kernel, out_shape=out_shape, in_specs=in_specs or [VMEM] *...  17 us
    ppermute x12, starting transfers between devices, swapped(): return lax.ppermute(block, axis, [(i ^ bit, i) for i in range(count)])  11.3 us
    ppermute x12, waiting for transfers between devices, swapped(): return lax.ppermute(block, axis, [(i ^ bit, i) for i in range(count)])  8.45 us
    ppermute x1, starting transfers between devices, crossed(): lax.ppermute(block, axis, [(i, (i + (-1 if i % 2 == 0 else 1)) % count) f...  4.78 us
  transfers between devices with their start and end apart: 13, of which 4 were waited for; matrix products, arithmetic and copies ran while one was open for 0% of the time, Pallas kernels for 21%

profile of v7, /device:TPU:0, one launch (start us, length us, event | category | flops | bytes accessed | tf_op | source)
XLA Modules:
  0.0 42.3 jit_solution(1966973710199522871)
XLA Ops:
  0.6 0.9 %shard_map.96.first.special = bf16[16,512]{1,0:T(8,128)(2,1)S(1)} custom-call(s32[2]{0:T(128)} %frame_order.1, bf16[5,2,512]{2,1,0:T(2,128)(2,1)} %bitcast.7, bf16[5,1024]{1,0:T(8,128)(2,1)} %role_first.1, bf16[5,1024]{1,0:T(8,128)(2,1)} %role_rest.1), custom_call_target="tpu_custom_call" | custom-call | tf_op jit(solution)/shard_map/pallas_call | solution.py:365
  1.5 3.0 %collective-permute-start = (bf16[16,512]{1,0:T(8,128)(2,1)S(1)}, bf16[16,512]{1,0:T(8,128)(2,1)S(1)}, u32[]{:S(2)}, u32[]{:S(2)}) collective-permute-start(bf16[16,512]{1,0:T(8,128)(2,1)S(1)} %shard_map.96.first.special), channel_id=1, source_target_pairs={{2,0},{0,2},{6,4},{4,6},{10,8},{8,10},{14,12},{12,14},{3,1},{1,3},... | collective-permute-start | bytes 49160 | tf_op jit(solution)/shard_map/ppermute | solution.py:30
  4.5 0.0 collective-permute-start.4
  4.5 0.2 collective-permute-start.3
  4.7 1.6 %collective-permute-done.second = bf16[16,512]{1,0:T(8,128)(2,1)S(1)} collective-permute-done((bf16[16,512]{1,0:T(8,128)(2,1)S(1)}, bf16[16,512]{1,0:T(8,128)(2,1)S(1)}, u32[]{:S(2)}, u32[]{:S(2)}) %collective-permute-start) | collective-permute-done | bytes 16416 | tf_op jit(solution)/shard_map/ppermute | solution.py:30
  6.2 2.1 %collective-permute-start.1 = (bf16[32,512]{1,0:T(8,128)(2,1)S(1)}, bf16[32,512]{1,0:T(8,128)(2,1)S(1)}, u32[]{:S(2)}, u32[]{:S(2)}) collective-permute-start(bf16[32,512]{1,0:T(8,128)(2,1)S(1)} %shard_map.97.first), channel_id=1, source_target_pairs={{4,0},{6,2},{0,4},{2,6},{12,8},{14,10},{8,12},{10,14},{5,1},{7,3},... | collective-permute-start | bytes 98312 | tf_op jit(solution)/shard_map/ppermute | solution.py:30
  8.3 0.0 collective-permute-start.5
  8.3 2.1 %shard_map.95 = (bf16[384,512]{1,0:T(8,128)(2,1)S(1)}, f32[8,512]{1,0:T(8,128)S(1)}, bf16[3,1024,512]{2,1,0:T(8,128)(2,1)S(1)}) custom-call(s32[2,16]{1,0:T(2,128)} %covisible.1, bf16[2,192,512]{2,1,0:T(8,128)(2,1)} %patches.1, bf16[3,1024,512]{2,1,0:T(8,128)(2,1)} %w_qkv.1), custom_call_target="tpu_custom_call" | custom-call | tf_op jit(solution)/shard_map/pallas_call | solution.py:365
  10.4 0.0 collective-permute-done.1.second
  10.5 4.8 %collective-permute-start.2 = (bf16[384,512]{1,0:T(8,128)(2,1)S(1)}, bf16[384,512]{1,0:T(8,128)(2,1)S(1)}, u32[]{:S(2)}, u32[]{:S(2)}) collective-permute-start(bf16[384,512]{1,0:T(8,128)(2,1)S(1)} %bitcast.6), channel_id=1, source_target_pairs={{0,14},{2,4},{4,2},{6,8},{8,6},{10,12},{12,10},{14,0},{1,15},{3,5}... | collective-permute-start | bytes 1179656 | tf_op jit(solution)/shard_map/ppermute | solution.py:35
  15.3 0.0 collective-permute-done.5.other_special
  15.3 0.0 collective-permute-done.4.other
  15.3 3.4 %shard_map.99 = (bf16[4,128,768]{2,1,0:T(8,128)(2,1)S(1)}, bf16[512,128]{1,0:T(8,128)(2,1)S(1)}, f32[8,768]{1,0:T(8,128)S(1)}, f32[8,768]{1,0:T(8,128)S(1)}, f32...) custom-call(f32[8,512]{1,0:T(8,128)S(1)} %get-tuple-element.24.mask, bf16[384,512]{1,0:T(8,128)(2,1)S(1)} %get-tuple-element.26.own, ...), custom_call_target="tpu_custom_call" | custom-call | tf_op jit(solution)/shard_map/pallas_call | solution.py:365
  18.7 4.1 %collective-permute-done.3 = bf16[384,512]{1,0:T(8,128)(2,1)S(1)} collective-permute-done((bf16[384,512]{1,0:T(8,128)(2,1)}, bf16[384,512]{1,0:T(8,128)(2,1)S(1)}, u32[]{:S(2)}, u32[]{:S(2)}) %collective-permute-start.3) | collective-permute-done | bytes 393248 | tf_op jit(solution)/shard_map/ppermute | solution.py:30
  22.8 0.1 collective-permute-start.6
  22.9 0.5 %collective-permute-start.7 = (bf16[192,512]{1,0:T(8,128)(2,1)S(1)}, bf16[192,512]{1,0:T(8,128)(2,1)S(1)}, u32[]{:S(2)}, u32[]{:S(2)}) collective-permute-start(bf16[192,512]{1,0:T(8,128)(2,1)S(1)} %get-tuple-element.48.refs_1_), channel_id=1, source_target_pairs={{1,0},{0,1},{3,2},{2,3},{5,4},{4,5},{7,6},{6,7},{9,8},{8,9},{11,10... | collective-permute-start | bytes 589832 | tf_op jit(solution)/shard_map/ppermute | solution.py:30
  23.3 4.5 %collective-permute-start.8 = (bf16[64,512]{1,0:T(8,128)(2,1)S(1)}, bf16[64,512]{1,0:T(8,128)(2,1)S(1)}, u32[]{:S(2)}, u32[]{:S(2)}) collective-permute-start(bf16[64,512]{1,0:T(8,128)(2,1)S(1)} %shard_map.98.first), channel_id=1, source_target_pairs={{8,0},{10,2},{12,4},{14,6},{0,8},{2,10},{4,12},{6,14},{9,1},{11,3}... | collective-permute-start | bytes 196616 | tf_op jit(solution)/shard_map/ppermute | solution.py:30
  27.9 0.0 collective-permute-done.6.refs_2_
  27.9 0.0 collective-permute-done.7.refs_3_
  27.9 3.5 %shard_map.100 = (f32[8,768]{1,0:T(8,128)S(1)}, f32[8,768]{1,0:T(8,128)S(1)}, f32[4,64,768]{2,1,0:T(8,128)S(1)}, f32[512,128]{1,0:T(8,128)S(1)}) custom-call(f32[8,512]{1,0:T(8,128)S(1)} %get-tuple-element.24.mask, bf16[192,512]{1,0:T(8,128)(2,1)S(1)} %get-tuple-element.49.refs_0_, bf16[192,512]{1,0:T(8,128)(2,1)S(1)} %get-tuple-element.48.refs_1_, ...), custom_call_target="tpu_custom_call" | custom-call | tf_op jit(solution)/shard_map/pallas_call | solution.py:365
  31.4 0.0 collective-permute-done.2
  31.4 0.1 collective-permute-start.10
  31.5 0.5 %collective-permute-start.9 = (bf16[192,512]{1,0:T(8,128)(2,1)S(1)}, bf16[192,512]{1,0:T(8,128)(2,1)S(1)}, u32[]{:S(2)}, u32[]{:S(2)}) collective-permute-start(bf16[192,512]{1,0:T(8,128)(2,1)S(1)} %get-tuple-element.47.refs_0_), channel_id=1, source_target_pairs={{1,0},{0,1},{3,2},{2,3},{5,4},{4,5},{7,6},{6,7},{9,8},{8,9},{11,10... | collective-permute-start | bytes 589832 | tf_op jit(solution)/shard_map/ppermute | solution.py:30
  32.0 0.0 collective-permute-done.8.second
  32.0 0.1 collective-permute-start.11
  32.2 1.3 %collective-permute-done.11.refs_5_ = bf16[128,512]{1,0:T(8,128)(2,1)S(1)} collective-permute-done((bf16[128,512]{1,0:T(8,128)(2,1)S(1)}, bf16[128,512]{1,0:T(8,128)(2,1)S(1)}, u32[]{:S(2)}, u32[]{:S(2)}) %collective-permute-start.11) | collective-permute-done | bytes 131104 | tf_op jit(solution)/shard_map/ppermute | solution.py:30
  33.4 0.0 collective-permute-done.10.refs_4_
  33.4 0.0 collective-permute-done.9.refs_3_
  33.4 6.3 %shard_map.102 = (f32[400,512]{1,0:T(8,128)S(1)}, bf16[400,512]{1,0:T(8,128)(2,1)S(1)}) custom-call(f32[8,512]{1,0:T(8,128)S(1)} %get-tuple-element.24.mask, bf16[192,512]{1,0:T(8,128)(2,1)S(1)} %get-tuple-element.47.refs_0_, bf16[192,512]{1,0:T(8,128)(2,1)S(1)} %get-tuple-element.46.refs_1_, bf16[128,512]{1,0:T(8,128)(2,1)S(1)} %shard_map.101.refs_2_, ...), custom_call_target="tpu_custom_call" | custom-call | tf_op jit(solution)/shard_map/pallas_call | solution.py:365
  39.7 0.3 collective-permute-start.12
  40.0 1.5 %collective-permute-done.12.received = bf16[400,512]{1,0:T(8,128)(2,1)S(1)} collective-permute-done((bf16[400,512]{1,0:T(8,128)(2,1)S(1)}, bf16[400,512]{1,0:T(8,128)(2,1)S(1)}, u32[]{:S(2)}, u32[]{:S(2)}) %collective-permute-start.12) | collective-permute-done | bytes 409632 | tf_op jit(solution)/shard_map/ppermute | solution.py:30
  41.5 0.8 %shard_map.103 = (bf16[384,512]{1,0:T(8,128)(2,1)}, bf16[5,2,512]{2,1,0:T(2,128)(2,1)}) custom-call(f32[400,512]{1,0:T(8,128)S(1)} %get-tuple-element.42.kept, bf16[400,512]{1,0:T(8,128)(2,1)S(1)} %collective-permute-done.12.received), custom_call_target="tpu_custom_call" | custom-call | tf_op jit(solution)/shard_map/pallas_call | solution.py:365
  (7 shorter events, 0.1 us)
Async XLA Ops:
  1.5 4.7 %collective-permute-start = (bf16[16,512]{1,0:T(8,128)(2,1)S(1)}, bf16[16,512]{1,0:T(8,128)(2,1)S(1)}, u32[]{:S(2)}, u32[]{:S(2)}) collective-permute-start(bf16[16,512]{1,0:T(8,128)(2,1)S(1)} %shard_map.96.first.special), channel_id=1, source_target_pairs={{2,0},{0,2},{6,4},{4,6},{10,8},{8,10},{14,12},{12,14},{3,1},{1,3},... | collective-permute-start | bytes 49160 | tf_op jit(solution)/shard_map/ppermute | solution.py:30
  4.5 10.8 %collective-permute-start.4 = (bf16[384,512]{1,0:T(8,128)(2,1)}, bf16[384,512]{1,0:T(8,128)(2,1)S(1)}, u32[]{:S(2)}, u32[]{:S(2)}) collective-permute-start(bf16[384,512]{1,0:T(8,128)(2,1)} %bitcast.4), channel_id=1, source_target_pairs={{1,0},{0,1},{3,2},{2,3},{5,4},{4,5},{7,6},{6,7},{9,8},{8,9},{11,10... | collective-permute-start | bytes 1179656 | tf_op jit(solution)/shard_map/ppermute | solution.py:30
  4.5 18.2 %collective-permute-start.3 = (bf16[384,512]{1,0:T(8,128)(2,1)}, bf16[384,512]{1,0:T(8,128)(2,1)S(1)}, u32[]{:S(2)}, u32[]{:S(2)}) collective-permute-start(bf16[384,512]{1,0:T(8,128)(2,1)} %bitcast.5), channel_id=1, source_target_pairs={{2,0},{0,2},{6,4},{4,6},{10,8},{8,10},{14,12},{12,14},{3,1},{1,3},... | collective-permute-start | bytes 1179656 | tf_op jit(solution)/shard_map/ppermute | solution.py:30
  6.2 4.3 %copy-start = (bf16[2,192,512]{2,1,0:T(8,128)(2,1)S(1)}, bf16[2,192,512]{2,1,0:T(8,128)(2,1)}, u32[]{:S(2)}) copy-start(bf16[2,192,512]{2,1,0:T(8,128)(2,1)} %patches.1) | copy-start | bytes 1179652
  6.2 4.2 %collective-permute-start.1 = (bf16[32,512]{1,0:T(8,128)(2,1)S(1)}, bf16[32,512]{1,0:T(8,128)(2,1)S(1)}, u32[]{:S(2)}, u32[]{:S(2)}) collective-permute-start(bf16[32,512]{1,0:T(8,128)(2,1)S(1)} %shard_map.97.first), channel_id=1, source_target_pairs={{4,0},{6,2},{0,4},{2,6},{12,8},{14,10},{8,12},{10,14},{5,1},{7,3},... | collective-permute-start | bytes 98312 | tf_op jit(solution)/shard_map/ppermute | solution.py:30
  8.3 6.9 %collective-permute-start.5 = (bf16[16,512]{1,0:T(8,128)(2,1)S(1)}, bf16[16,512]{1,0:T(8,128)(2,1)S(1)}, u32[]{:S(2)}, u32[]{:S(2)}) collective-permute-start(bf16[16,512]{1,0:T(8,128)(2,1)S(1)} %shard_map.96.first.special), channel_id=1, source_target_pairs={{1,0},{0,1},{3,2},{2,3},{5,4},{4,5},{7,6},{6,7},{9,8},{8,9},{11,10... | collective-permute-start | bytes 49160 | tf_op jit(solution)/shard_map/ppermute | solution.py:30
  10.5 20.9 %collective-permute-start.2 = (bf16[384,512]{1,0:T(8,128)(2,1)S(1)}, bf16[384,512]{1,0:T(8,128)(2,1)S(1)}, u32[]{:S(2)}, u32[]{:S(2)}) collective-permute-start(bf16[384,512]{1,0:T(8,128)(2,1)S(1)} %bitcast.6), channel_id=1, source_target_pairs={{0,14},{2,4},{4,2},{6,8},{8,6},{10,12},{12,10},{14,0},{1,15},{3,5}... | collective-permute-start | bytes 1179656 | tf_op jit(solution)/shard_map/ppermute | solution.py:35
  22.8 5.1 %collective-permute-start.6 = (bf16[192,512]{1,0:T(8,128)(2,1)S(1)}, bf16[192,512]{1,0:T(8,128)(2,1)S(1)}, u32[]{:S(2)}, u32[]{:S(2)}) collective-permute-start(bf16[192,512]{1,0:T(8,128)(2,1)S(1)} %get-tuple-element.49.refs_0_), channel_id=1, source_target_pairs={{1,0},{0,1},{3,2},{2,3},{5,4},{4,5},{7,6},{6,7},{9,8},{8,9},{11,10... | collective-permute-start | bytes 589832 | tf_op jit(solution)/shard_map/ppermute | solution.py:30
  22.9 5.0 %collective-permute-start.7 = (bf16[192,512]{1,0:T(8,128)(2,1)S(1)}, bf16[192,512]{1,0:T(8,128)(2,1)S(1)}, u32[]{:S(2)}, u32[]{:S(2)}) collective-permute-start(bf16[192,512]{1,0:T(8,128)(2,1)S(1)} %get-tuple-element.48.refs_1_), channel_id=1, source_target_pairs={{1,0},{0,1},{3,2},{2,3},{5,4},{4,5},{7,6},{6,7},{9,8},{8,9},{11,10... | collective-permute-start | bytes 589832 | tf_op jit(solution)/shard_map/ppermute | solution.py:30
  23.3 8.7 %collective-permute-start.8 = (bf16[64,512]{1,0:T(8,128)(2,1)S(1)}, bf16[64,512]{1,0:T(8,128)(2,1)S(1)}, u32[]{:S(2)}, u32[]{:S(2)}) collective-permute-start(bf16[64,512]{1,0:T(8,128)(2,1)S(1)} %shard_map.98.first), channel_id=1, source_target_pairs={{8,0},{10,2},{12,4},{14,6},{0,8},{2,10},{4,12},{6,14},{9,1},{11,3}... | collective-permute-start | bytes 196616 | tf_op jit(solution)/shard_map/ppermute | solution.py:30
  31.4 2.0 %collective-permute-start.10 = (bf16[192,512]{1,0:T(8,128)(2,1)S(1)}, bf16[192,512]{1,0:T(8,128)(2,1)S(1)}, u32[]{:S(2)}, u32[]{:S(2)}) collective-permute-start(bf16[192,512]{1,0:T(8,128)(2,1)S(1)} %get-tuple-element.46.refs_1_), channel_id=1, source_target_pairs={{1,0},{0,1},{3,2},{2,3},{5,4},{4,5},{7,6},{6,7},{9,8},{8,9},{11,10... | collective-permute-start | bytes 589832 | tf_op jit(solution)/shard_map/ppermute | solution.py:30
  31.5 1.9 %collective-permute-start.9 = (bf16[192,512]{1,0:T(8,128)(2,1)S(1)}, bf16[192,512]{1,0:T(8,128)(2,1)S(1)}, u32[]{:S(2)}, u32[]{:S(2)}) collective-permute-start(bf16[192,512]{1,0:T(8,128)(2,1)S(1)} %get-tuple-element.47.refs_0_), channel_id=1, source_target_pairs={{1,0},{0,1},{3,2},{2,3},{5,4},{4,5},{7,6},{6,7},{9,8},{8,9},{11,10... | collective-permute-start | bytes 589832 | tf_op jit(solution)/shard_map/ppermute | solution.py:30
  32.0 1.4 %collective-permute-start.11 = (bf16[128,512]{1,0:T(8,128)(2,1)S(1)}, bf16[128,512]{1,0:T(8,128)(2,1)S(1)}, u32[]{:S(2)}, u32[]{:S(2)}) collective-permute-start(bf16[128,512]{1,0:T(8,128)(2,1)S(1)} %shard_map.101.refs_2_), channel_id=1, source_target_pairs={{1,0},{0,1},{3,2},{2,3},{5,4},{4,5},{7,6},{6,7},{9,8},{8,9},{11,10... | collective-permute-start | bytes 393224 | tf_op jit(solution)/shard_map/ppermute | solution.py:30
  39.7 1.8 %collective-permute-start.12 = (bf16[400,512]{1,0:T(8,128)(2,1)S(1)}, bf16[400,512]{1,0:T(8,128)(2,1)S(1)}, u32[]{:S(2)}, u32[]{:S(2)}) collective-permute-start(bf16[400,512]{1,0:T(8,128)(2,1)S(1)} %get-tuple-element.43), channel_id=1, source_target_pairs={{1,0},{0,1},{3,2},{2,3},{5,4},{4,5},{7,6},{6,7},{9,8},{8,9},{11,10... | collective-permute-start | bytes 1228808 | tf_op jit(solution)/shard_map/ppermute | solution.py:30

commit v8 on v7

--- a/solution.py
+++ b/solution.py
@@ -54,15 +54,19 @@
     return lax.rem(here + offset + count, count)
 
 
-def special_kernel(frame_order, specials, role_first, role_rest, special_out, order, here, first_rows, rest_rows, copied):
+def rows_kernel(
+    frame_order, specials, role_first, role_rest, patches,
+    special_out, patches_out, order, here, first_rows, rest_rows, copied,
+):
     special_count, images, width = specials.shape
     moves = [(specials, here), (role_first, first_rows), (role_rest, rest_rows), (frame_order, order)]
+    moves.append((patches, patches_out))
     copies = [
         pltpu.make_async_copy(source, target, copied.at[i]) for i, (source, target) in enumerate(moves)
     ]
     for copy in copies:
         copy.start()
-    for copy in copies:
+    for copy in copies[:-1]:
         copy.wait()
     mine, _ = halves(width)
     first = first_rows[:, mine].astype(jnp.float32)
@@ -72,15 +76,15 @@
     ]
     summed.append(jnp.zeros((special_out.shape[0] - images * special_count, width), jnp.float32))
     special_out[...] = jnp.concatenate(summed, axis=0).astype(jnp.bfloat16)
+    copies[-1].wait()
 
 
 def start_kernel(
-    offsets, special_count, special_total, covisible, patches, w_qkv, own_out, mask_out, weights_out, seen, copied
+    offsets, per_image, special_count, special_total, covisible, w_qkv, mask_out, weights_out, seen, copied
 ):
-    images, per_image, width = patches.shape
+    images = covisible.shape[0]
     patch_total = images * per_image
     moves = [(covisible, seen)]
-    moves += [(patches.at[b], own_out.at[pl.ds(b * per_image, per_image)]) for b in range(images)]
     moves += [(w_qkv.at[i], weights_out.at[i]) for i in range(3)]
     copies = [
         pltpu.make_async_copy(source, target, copied.at[i]) for i, (source, target) in enumerate(moves)
@@ -313,36 +317,31 @@
     copy.start()
     pairs, rows = queries.shape[0], queries.shape[2] // 2
     columns, out, special = [], None, None
+    sides = halves(kept_out.shape[1])
     for pair, sub, _, total, weight in attend_all(
         projector(own, other, weights), masks, lambda pair: queries[pair], lambda: special_queries[...],
         State(rows, state_in), pairs, rows, special_real,
     ):
         if pair == 0 and sub == 0:
             copy.wait()
+        share = total * (1.0 / weight)
         if pair == pairs:
-            special = total / weight
-            row = lax.broadcasted_iota(jnp.int32, special.shape, 0) // HEAD_DIM
-            lane = lax.broadcasted_iota(jnp.int32, special.shape, 1) // TILE_ROWS
-            special = jnp.transpose(jnp.where(row == lane, special, 0.0))
-            special = sum(special[i * TILE_ROWS : (i + 1) * TILE_ROWS] for i in range(2 * pairs))
-            special = product(special.astype(jnp.bfloat16), w_here[...])
+            row = lax.broadcasted_iota(jnp.int32, share.shape, 0) // HEAD_DIM
+            lane = lax.broadcasted_iota(jnp.int32, share.shape, 1) // TILE_ROWS
+            share = jnp.transpose(jnp.where(row == lane, share, 0.0))
+            share = sum(share[i * TILE_ROWS : (i + 1) * TILE_ROWS] for i in range(2 * pairs))
+            special = [product(share.astype(jnp.bfloat16), w_here[:, side]) for side in sides]
             continue
-        columns.append(total / weight)
+        columns.append(share)
         if pair % 2 == 1 and sub == 1:
             quad = jnp.transpose(jnp.concatenate(columns, axis=0)).astype(jnp.bfloat16)
-            added = product(quad, w_here[(pair // 2) * QUAD : (pair // 2 + 1) * QUAD, :])
-            out = added if out is None else out + added
+            features = slice((pair // 2) * QUAD, (pair // 2 + 1) * QUAD)
+            added = [product(quad, w_here[features, side]) for side in sides]
+            out = added if out is None else [before + more for before, more in zip(out, added)]
             columns = []
-    half = lax.axis_index("head")
-    width = kept_out.shape[1]
-
-    def put(place, values):
-        left, right = values[:, :width], values[:, width:]
-        kept_out[place, :] = jnp.where(half == 0, left, right)
-        sent_out[place, :] = jnp.where(half == 0, right, left).astype(jnp.bfloat16)
-
-    put(slice(0, rows), out)
-    put(slice(rows, kept_out.shape[0]), special)
+    for place, values in ((slice(0, rows), out), (slice(rows, kept_out.shape[0]), special)):
+        sent_out[place, :] = values[1].astype(jnp.bfloat16)
+        kept_out[place, :] = values[0]
 
 
 def end_kernel(images, kept, received, patch_out, special_out):
@@ -423,40 +422,39 @@
     patches = patch_rows.reshape(patch_total, width)
     turned = jnp.transpose(special_rows, (1, 0, 2))
     power = owner_count & (owner_count - 1) == 0
-    (specials,) = call(
-        special_kernel,
-        [bf16(special_block, width)],
-        (frame_order, turned, role_first, role_rest),
-        in_specs=[HBM] * 4,
+    specials, own = call(
+        rows_kernel,
+        [bf16(special_block, width), bf16(patch_total, width)],
+        (frame_order, turned, role_first, role_rest, patches),
+        in_specs=[HBM] * 5,
         scratch=[
             pltpu.SMEM(frame_order.shape, jnp.int32),
             pltpu.VMEM(turned.shape, jnp.bfloat16),
             pltpu.VMEM(role_first.shape, jnp.bfloat16),
             pltpu.VMEM(role_rest.shape, jnp.bfloat16),
-            pltpu.SemaphoreType.DMA((4,)),
+            pltpu.SemaphoreType.DMA((5,)),
         ],
     )
     bits = [1 << i for i in range(owner_count.bit_length() - 1)] if power else []
     everywhere = gathered(gathered(specials, "blk", bits[:1], FIRST), "blk", bits[1:2])
-    own, mask, weights = call(
-        functools.partial(start_kernel, offsets, special_count, special_block),
+    mask, weights = call(
+        functools.partial(start_kernel, offsets, per_image, special_count, special_block),
         [
-            bf16(patch_total, width),
             f32(mask_rows, patch_total + heads * special_block),
             bf16(*w_qkv.shape),
         ],
-        (covisible, patch_rows, w_qkv),
-        in_specs=[HBM] * 3,
-        scratch=[pltpu.SMEM(covisible.shape, jnp.int32), pltpu.SemaphoreType.DMA((1 + images + 3,))],
+        (covisible, w_qkv),
+        in_specs=[HBM] * 2,
+        scratch=[pltpu.SMEM(covisible.shape, jnp.int32), pltpu.SemaphoreType.DMA((1 + 3,))],
     )
     if paired:
-        near = [swapped(patches, "blk", 1), crossed(after(patches, everywhere, mask), "blk")]
+        near = [swapped(own, "blk", 1), crossed(after(own, everywhere, mask), "blk")]
     else:
-        near = [shifted(patches, "blk", -offset) for offset in offsets[1:]]
+        near = [shifted(own, "blk", -offset) for offset in offsets[1:]]
     queries, special_queries, *state = call(
         functools.partial(first_kernel, images),
         [bf16(pairs, PAIR, 2 * patch_total), bf16(width, heads * special_block), *state_shape],
-        (mask, own, swapped(patches, "head", 1), *both(specials), weights),
+        (mask, *both(own), *both(specials), weights),
     )
     fixed = (weights, queries, special_queries)
 

time: 42.6 us -> 42.6 us (level)
  no operation moved by 1% of the time
where the time goes in v8:
time: 42.6 us; the launch traced here: 42.4 us
  Pallas kernels  17 us (40%)
  starting transfers between devices  16.4 us (38%)
  waiting for transfers between devices  8.15 us (19%)
  between operations  0.73 us (2%)
    pallas_call x9, Pallas kernels, call(): pl.pallas_call(kernel, out_shape=out_shape, in_specs=in_specs or [VMEM] *...  17 us
    ppermute x12, starting transfers between devices, swapped(): return lax.ppermute(block, axis, [(i ^ bit, i) for i in range(count)])  11.4 us
    ppermute x12, waiting for transfers between devices, swapped(): return lax.ppermute(block, axis, [(i ^ bit, i) for i in range(count)])  8.15 us
    ppermute x1, starting transfers between devices, crossed(): lax.ppermute(block, axis, [(i, (i + (-1 if i % 2 == 0 else 1)) % count) f...  5.05 us
  transfers between devices with their start and end apart: 13, of which 4 were waited for; matrix products, arithmetic and copies ran while one was open for 0% of the time, Pallas kernels for 21%

profile of v8, /device:TPU:0, one launch (start us, length us, event | category | flops | bytes accessed | tf_op | source)
XLA Modules:
  0.0 42.4 jit_solution(5174613026971657942)
XLA Ops:
  0.6 1.1 %shard_map.96 = (bf16[16,512]{1,0:T(8,128)(2,1)S(1)}, bf16[384,512]{1,0:T(8,128)(2,1)S(1)}) custom-call(s32[2]{0:T(128)} %frame_order.1, bf16[5,2,512]{2,1,0:T(2,128)(2,1)} %bitcast.5, bf16[5,1024]{1,0:T(8,128)(2,1)} %role_first.1, bf16[5,1024]{1,0:T(8,128)(2,1)} %role_rest.1, bf16[384,512]{1,0:T(8,128)(2,1)} %bitcast.4), custom_call_target="tpu_custom_call" | custom-call | tf_op jit(solution)/shard_map/pallas_call | solution.py:364
  1.7 3.0 %collective-permute-start = (bf16[16,512]{1,0:T(8,128)(2,1)S(1)}, bf16[16,512]{1,0:T(8,128)(2,1)S(1)}, u32[]{:S(2)}, u32[]{:S(2)}) collective-permute-start(bf16[16,512]{1,0:T(8,128)(2,1)S(1)} %get-tuple-element.27.first.special), channel_id=1, source_target_pairs={{2,0},{0,2},{6,4},{4,6},{10,8},{8,10},{14,12},{12,14},{3,1},{1,3},... | collective-permute-start | bytes 49160 | tf_op jit(solution)/shard_map/ppermute | solution.py:30
  4.7 0.0 collective-permute-start.4
  4.7 0.2 collective-permute-start.3
  4.9 1.6 %collective-permute-done.second = bf16[16,512]{1,0:T(8,128)(2,1)S(1)} collective-permute-done((bf16[16,512]{1,0:T(8,128)(2,1)S(1)}, bf16[16,512]{1,0:T(8,128)(2,1)S(1)}, u32[]{:S(2)}, u32[]{:S(2)}) %collective-permute-start) | collective-permute-done | bytes 16416 | tf_op jit(solution)/shard_map/ppermute | solution.py:30
  6.5 2.1 %collective-permute-start.1 = (bf16[32,512]{1,0:T(8,128)(2,1)S(1)}, bf16[32,512]{1,0:T(8,128)(2,1)S(1)}, u32[]{:S(2)}, u32[]{:S(2)}) collective-permute-start(bf16[32,512]{1,0:T(8,128)(2,1)S(1)} %shard_map.97.first), channel_id=1, source_target_pairs={{4,0},{6,2},{0,4},{2,6},{12,8},{14,10},{8,12},{10,14},{5,1},{7,3},... | collective-permute-start | bytes 98312 | tf_op jit(solution)/shard_map/ppermute | solution.py:30
  8.6 0.0 collective-permute-start.5
  8.6 1.9 %shard_map.95 = (f32[8,512]{1,0:T(8,128)S(1)}, bf16[3,1024,512]{2,1,0:T(8,128)(2,1)S(1)}) custom-call(s32[2,16]{1,0:T(2,128)} %covisible.1, bf16[3,1024,512]{2,1,0:T(8,128)(2,1)} %w_qkv.1), custom_call_target="tpu_custom_call" | custom-call | tf_op jit(solution)/shard_map/pallas_call | solution.py:364
  10.5 0.0 collective-permute-done.1.second
  10.5 5.0 %collective-permute-start.2 = (bf16[384,512]{1,0:T(8,128)(2,1)S(1)}, bf16[384,512]{1,0:T(8,128)(2,1)S(1)}, u32[]{:S(2)}, u32[]{:S(2)}) collective-permute-start(bf16[384,512]{1,0:T(8,128)(2,1)S(1)} %get-tuple-element.28.own), channel_id=1, source_target_pairs={{0,14},{2,4},{4,2},{6,8},{8,6},{10,12},{12,10},{14,0},{1,15},{3,5}... | collective-permute-start | bytes 1179656 | tf_op jit(solution)/shard_map/ppermute | solution.py:35
  15.5 0.0 collective-permute-done.5.other_special
  15.5 0.0 collective-permute-done.4.other
  15.5 3.4 %shard_map.99 = (bf16[4,128,768]{2,1,0:T(8,128)(2,1)S(1)}, bf16[512,128]{1,0:T(8,128)(2,1)S(1)}, f32[8,768]{1,0:T(8,128)S(1)}, f32[8,768]{1,0:T(8,128)S(1)}, f32...) custom-call(f32[8,512]{1,0:T(8,128)S(1)} %get-tuple-element.25.mask, bf16[384,512]{1,0:T(8,128)(2,1)S(1)} %get-tuple-element.28.own, ...), custom_call_target="tpu_custom_call" | custom-call | tf_op jit(solution)/shard_map/pallas_call | solution.py:364
  19.0 3.7 %collective-permute-done.3 = bf16[384,512]{1,0:T(8,128)(2,1)S(1)} collective-permute-done((bf16[384,512]{1,0:T(8,128)(2,1)S(1)}, bf16[384,512]{1,0:T(8,128)(2,1)S(1)}, u32[]{:S(2)}, u32[]{:S(2)}) %collective-permute-start.3) | collective-permute-done | bytes 393248 | tf_op jit(solution)/shard_map/ppermute | solution.py:30
  22.7 0.1 collective-permute-start.7
  22.8 0.5 %collective-permute-start.6 = (bf16[192,512]{1,0:T(8,128)(2,1)S(1)}, bf16[192,512]{1,0:T(8,128)(2,1)S(1)}, u32[]{:S(2)}, u32[]{:S(2)}) collective-permute-start(bf16[192,512]{1,0:T(8,128)(2,1)S(1)} %get-tuple-element.51.refs_0_), channel_id=1, source_target_pairs={{1,0},{0,1},{3,2},{2,3},{5,4},{4,5},{7,6},{6,7},{9,8},{8,9},{11,10... | collective-permute-start | bytes 589832 | tf_op jit(solution)/shard_map/ppermute | solution.py:30
  23.3 4.6 %collective-permute-start.8 = (bf16[64,512]{1,0:T(8,128)(2,1)S(1)}, bf16[64,512]{1,0:T(8,128)(2,1)S(1)}, u32[]{:S(2)}, u32[]{:S(2)}) collective-permute-start(bf16[64,512]{1,0:T(8,128)(2,1)S(1)} %shard_map.98.first), channel_id=1, source_target_pairs={{8,0},{10,2},{12,4},{14,6},{0,8},{2,10},{4,12},{6,14},{9,1},{11,3}... | collective-permute-start | bytes 196616 | tf_op jit(solution)/shard_map/ppermute | solution.py:30
  27.9 0.0 collective-permute-done.7.refs_3_
  27.9 0.0 collective-permute-done.6.refs_2_
  27.9 3.5 %shard_map.100 = (f32[8,768]{1,0:T(8,128)S(1)}, f32[8,768]{1,0:T(8,128)S(1)}, f32[4,64,768]{2,1,0:T(8,128)S(1)}, f32[512,128]{1,0:T(8,128)S(1)}) custom-call(f32[8,512]{1,0:T(8,128)S(1)} %get-tuple-element.25.mask, bf16[192,512]{1,0:T(8,128)(2,1)S(1)} %get-tuple-element.51.refs_0_, bf16[192,512]{1,0:T(8,128)(2,1)S(1)} %get-tuple-element.50.refs_1_, ...), custom_call_target="tpu_custom_call" | custom-call | tf_op jit(solution)/shard_map/pallas_call | solution.py:364
  31.4 0.0 collective-permute-done.2
  31.5 0.1 collective-permute-start.10
  31.5 0.5 %collective-permute-start.9 = (bf16[192,512]{1,0:T(8,128)(2,1)S(1)}, bf16[192,512]{1,0:T(8,128)(2,1)S(1)}, u32[]{:S(2)}, u32[]{:S(2)}) collective-permute-start(bf16[192,512]{1,0:T(8,128)(2,1)S(1)} %get-tuple-element.49.refs_0_), channel_id=1, source_target_pairs={{1,0},{0,1},{3,2},{2,3},{5,4},{4,5},{7,6},{6,7},{9,8},{8,9},{11,10... | collective-permute-start | bytes 589832 | tf_op jit(solution)/shard_map/ppermute | solution.py:30
  32.0 0.0 collective-permute-done.8.second
  32.0 0.1 collective-permute-start.11
  32.2 1.3 %collective-permute-done.11.refs_5_ = bf16[128,512]{1,0:T(8,128)(2,1)S(1)} collective-permute-done((bf16[128,512]{1,0:T(8,128)(2,1)S(1)}, bf16[128,512]{1,0:T(8,128)(2,1)S(1)}, u32[]{:S(2)}, u32[]{:S(2)}) %collective-permute-start.11) | collective-permute-done | bytes 131104 | tf_op jit(solution)/shard_map/ppermute | solution.py:30
  33.5 0.0 collective-permute-done.10.refs_4_
  33.5 0.0 collective-permute-done.9.refs_3_
  33.5 6.3 %shard_map.102 = (f32[400,512]{1,0:T(8,128)S(1)}, bf16[400,512]{1,0:T(8,128)(2,1)S(1)}) custom-call(f32[8,512]{1,0:T(8,128)S(1)} %get-tuple-element.25.mask, bf16[192,512]{1,0:T(8,128)(2,1)S(1)} %get-tuple-element.49.refs_0_, bf16[192,512]{1,0:T(8,128)(2,1)S(1)} %get-tuple-element.48.refs_1_, bf16[128,512]{1,0:T(8,128)(2,1)S(1)} %shard_map.101.refs_2_, ...), custom_call_target="tpu_custom_call" | custom-call | tf_op jit(solution)/shard_map/pallas_call | solution.py:364
  39.7 0.3 collective-permute-start.12
  40.0 1.5 %collective-permute-done.12.received = bf16[400,512]{1,0:T(8,128)(2,1)S(1)} collective-permute-done((bf16[400,512]{1,0:T(8,128)(2,1)S(1)}, bf16[400,512]{1,0:T(8,128)(2,1)S(1)}, u32[]{:S(2)}, u32[]{:S(2)}) %collective-permute-start.12) | collective-permute-done | bytes 409632 | tf_op jit(solution)/shard_map/ppermute | solution.py:30
  41.6 0.8 %shard_map.103 = (bf16[384,512]{1,0:T(8,128)(2,1)}, bf16[5,2,512]{2,1,0:T(2,128)(2,1)}) custom-call(f32[400,512]{1,0:T(8,128)S(1)} %get-tuple-element.44.kept, bf16[400,512]{1,0:T(8,128)(2,1)S(1)} %collective-permute-done.12.received), custom_call_target="tpu_custom_call" | custom-call | tf_op jit(solution)/shard_map/pallas_call | solution.py:364
  (5 shorter events, 0.1 us)
Async XLA Ops:
  1.7 4.7 %collective-permute-start = (bf16[16,512]{1,0:T(8,128)(2,1)S(1)}, bf16[16,512]{1,0:T(8,128)(2,1)S(1)}, u32[]{:S(2)}, u32[]{:S(2)}) collective-permute-start(bf16[16,512]{1,0:T(8,128)(2,1)S(1)} %get-tuple-element.27.first.special), channel_id=1, source_target_pairs={{2,0},{0,2},{6,4},{4,6},{10,8},{8,10},{14,12},{12,14},{3,1},{1,3},... | collective-permute-start | bytes 49160 | tf_op jit(solution)/shard_map/ppermute | solution.py:30
  4.7 10.8 %collective-permute-start.4 = (bf16[384,512]{1,0:T(8,128)(2,1)S(1)}, bf16[384,512]{1,0:T(8,128)(2,1)S(1)}, u32[]{:S(2)}, u32[]{:S(2)}) collective-permute-start(bf16[384,512]{1,0:T(8,128)(2,1)S(1)} %get-tuple-element.28.own), channel_id=1, source_target_pairs={{1,0},{0,1},{3,2},{2,3},{5,4},{4,5},{7,6},{6,7},{9,8},{8,9},{11,10... | collective-permute-start | bytes 1179656 | tf_op jit(solution)/shard_map/ppermute | solution.py:30
  4.7 18.0 %collective-permute-start.3 = (bf16[384,512]{1,0:T(8,128)(2,1)S(1)}, bf16[384,512]{1,0:T(8,128)(2,1)S(1)}, u32[]{:S(2)}, u32[]{:S(2)}) collective-permute-start(bf16[384,512]{1,0:T(8,128)(2,1)S(1)} %get-tuple-element.28.own), channel_id=1, source_target_pairs={{2,0},{0,2},{6,4},{4,6},{10,8},{8,10},{14,12},{12,14},{3,1},{1,3},... | collective-permute-start | bytes 1179656 | tf_op jit(solution)/shard_map/ppermute | solution.py:30
  6.5 4.0 %collective-permute-start.1 = (bf16[32,512]{1,0:T(8,128)(2,1)S(1)}, bf16[32,512]{1,0:T(8,128)(2,1)S(1)}, u32[]{:S(2)}, u32[]{:S(2)}) collective-permute-start(bf16[32,512]{1,0:T(8,128)(2,1)S(1)} %shard_map.97.first), channel_id=1, source_target_pairs={{4,0},{6,2},{0,4},{2,6},{12,8},{14,10},{8,12},{10,14},{5,1},{7,3},... | collective-permute-start | bytes 98312 | tf_op jit(solution)/shard_map/ppermute | solution.py:30
  8.6 7.0 %collective-permute-start.5 = (bf16[16,512]{1,0:T(8,128)(2,1)S(1)}, bf16[16,512]{1,0:T(8,128)(2,1)S(1)}, u32[]{:S(2)}, u32[]{:S(2)}) collective-permute-start(bf16[16,512]{1,0:T(8,128)(2,1)S(1)} %get-tuple-element.27.first.special), channel_id=1, source_target_pairs={{1,0},{0,1},{3,2},{2,3},{5,4},{4,5},{7,6},{6,7},{9,8},{8,9},{11,10... | collective-permute-start | bytes 49160 | tf_op jit(solution)/shard_map/ppermute | solution.py:30
  10.5 20.9 %collective-permute-start.2 = (bf16[384,512]{1,0:T(8,128)(2,1)S(1)}, bf16[384,512]{1,0:T(8,128)(2,1)S(1)}, u32[]{:S(2)}, u32[]{:S(2)}) collective-permute-start(bf16[384,512]{1,0:T(8,128)(2,1)S(1)} %get-tuple-element.28.own), channel_id=1, source_target_pairs={{0,14},{2,4},{4,2},{6,8},{8,6},{10,12},{12,10},{14,0},{1,15},{3,5}... | collective-permute-start | bytes 1179656 | tf_op jit(solution)/shard_map/ppermute | solution.py:35
  22.7 5.2 %collective-permute-start.7 = (bf16[192,512]{1,0:T(8,128)(2,1)S(1)}, bf16[192,512]{1,0:T(8,128)(2,1)S(1)}, u32[]{:S(2)}, u32[]{:S(2)}) collective-permute-start(bf16[192,512]{1,0:T(8,128)(2,1)S(1)} %get-tuple-element.50.refs_1_), channel_id=1, source_target_pairs={{1,0},{0,1},{3,2},{2,3},{5,4},{4,5},{7,6},{6,7},{9,8},{8,9},{11,10... | collective-permute-start | bytes 589832 | tf_op jit(solution)/shard_map/ppermute | solution.py:30
  22.8 5.1 %collective-permute-start.6 = (bf16[192,512]{1,0:T(8,128)(2,1)S(1)}, bf16[192,512]{1,0:T(8,128)(2,1)S(1)}, u32[]{:S(2)}, u32[]{:S(2)}) collective-permute-start(bf16[192,512]{1,0:T(8,128)(2,1)S(1)} %get-tuple-element.51.refs_0_), channel_id=1, source_target_pairs={{1,0},{0,1},{3,2},{2,3},{5,4},{4,5},{7,6},{6,7},{9,8},{8,9},{11,10... | collective-permute-start | bytes 589832 | tf_op jit(solution)/shard_map/ppermute | solution.py:30
  23.3 8.7 %collective-permute-start.8 = (bf16[64,512]{1,0:T(8,128)(2,1)S(1)}, bf16[64,512]{1,0:T(8,128)(2,1)S(1)}, u32[]{:S(2)}, u32[]{:S(2)}) collective-permute-start(bf16[64,512]{1,0:T(8,128)(2,1)S(1)} %shard_map.98.first), channel_id=1, source_target_pairs={{8,0},{10,2},{12,4},{14,6},{0,8},{2,10},{4,12},{6,14},{9,1},{11,3}... | collective-permute-start | bytes 196616 | tf_op jit(solution)/shard_map/ppermute | solution.py:30
  31.5 2.0 %collective-permute-start.10 = (bf16[192,512]{1,0:T(8,128)(2,1)S(1)}, bf16[192,512]{1,0:T(8,128)(2,1)S(1)}, u32[]{:S(2)}, u32[]{:S(2)}) collective-permute-start(bf16[192,512]{1,0:T(8,128)(2,1)S(1)} %get-tuple-element.48.refs_1_), channel_id=1, source_target_pairs={{1,0},{0,1},{3,2},{2,3},{5,4},{4,5},{7,6},{6,7},{9,8},{8,9},{11,10... | collective-permute-start | bytes 589832 | tf_op jit(solution)/shard_map/ppermute | solution.py:30
  31.5 1.9 %collective-permute-start.9 = (bf16[192,512]{1,0:T(8,128)(2,1)S(1)}, bf16[192,512]{1,0:T(8,128)(2,1)S(1)}, u32[]{:S(2)}, u32[]{:S(2)}) collective-permute-start(bf16[192,512]{1,0:T(8,128)(2,1)S(1)} %get-tuple-element.49.refs_0_), channel_id=1, source_target_pairs={{1,0},{0,1},{3,2},{2,3},{5,4},{4,5},{7,6},{6,7},{9,8},{8,9},{11,10... | collective-permute-start | bytes 589832 | tf_op jit(solution)/shard_map/ppermute | solution.py:30
  32.0 1.4 %collective-permute-start.11 = (bf16[128,512]{1,0:T(8,128)(2,1)S(1)}, bf16[128,512]{1,0:T(8,128)(2,1)S(1)}, u32[]{:S(2)}, u32[]{:S(2)}) collective-permute-start(bf16[128,512]{1,0:T(8,128)(2,1)S(1)} %shard_map.101.refs_2_), channel_id=1, source_target_pairs={{1,0},{0,1},{3,2},{2,3},{5,4},{4,5},{7,6},{6,7},{9,8},{8,9},{11,10... | collective-permute-start | bytes 393224 | tf_op jit(solution)/shard_map/ppermute | solution.py:30
  39.7 1.8 %collective-permute-start.12 = (bf16[400,512]{1,0:T(8,128)(2,1)S(1)}, bf16[400,512]{1,0:T(8,128)(2,1)S(1)}, u32[]{:S(2)}, u32[]{:S(2)}) collective-permute-start(bf16[400,512]{1,0:T(8,128)(2,1)S(1)} %get-tuple-element.45), channel_id=1, source_target_pairs={{1,0},{0,1},{3,2},{2,3},{5,4},{4,5},{7,6},{6,7},{9,8},{8,9},{11,10... | collective-permute-start | bytes 1228808 | tf_op jit(solution)/shard_map/ppermute | solution.py:30

commit v9 on v8

--- a/solution.py
+++ b/solution.py
@@ -378,11 +378,9 @@
     out[count:, :] = second[...]
 
 
-def gathered(block, axis, bits, flops=0):
-    for bit in bits:
-        shape = jax.ShapeDtypeStruct((2 * block.shape[0], block.shape[1]), block.dtype)
-        (block,) = call(stack_kernel, [shape], (block, swapped(block, axis, bit)), flops=flops)
-    return block
+def stacked(first, second, flops=0):
+    shape = jax.ShapeDtypeStruct((2 * first.shape[0], first.shape[1]), first.dtype)
+    return call(stack_kernel, [shape], (first, second), flops=flops)[0]
 
 
 def after(array, *others):
@@ -405,7 +403,7 @@
     paired = reach == 1 and owner_count % 2 == 0
 
     if paired:
-        offsets = [0, (1, -1), (-1, 1)]
+        offsets = [0, (-1, 1), (1, -1)]
     else:
         offsets = [0] + [sign * d for d in range(1, reach + 1) for sign in (-1, 1)]
     mask_rows = -(-len(offsets) * images // 8) * 8
@@ -421,7 +419,7 @@
     both = lambda part: (part, swapped(part, "head", 1))
     patches = patch_rows.reshape(patch_total, width)
     turned = jnp.transpose(special_rows, (1, 0, 2))
-    power = owner_count & (owner_count - 1) == 0
+    power = owner_count >= 8 and owner_count & (owner_count - 1) == 0
     specials, own = call(
         rows_kernel,
         [bf16(special_block, width), bf16(patch_total, width)],
@@ -435,8 +433,10 @@
             pltpu.SemaphoreType.DMA((5,)),
         ],
     )
-    bits = [1 << i for i in range(owner_count.bit_length() - 1)] if power else []
-    everywhere = gathered(gathered(specials, "blk", bits[:1], FIRST), "blk", bits[1:2])
+    bits = [1 << i for i in range(1, owner_count.bit_length() - 1)] + [1] if power else []
+    everywhere = specials
+    if power:
+        everywhere = stacked(specials, swapped(specials, "blk", bits[0]), FIRST)
     mask, weights = call(
         functools.partial(start_kernel, offsets, per_image, special_count, special_block),
         [
@@ -448,13 +448,13 @@
         scratch=[pltpu.SMEM(covisible.shape, jnp.int32), pltpu.SemaphoreType.DMA((1 + 3,))],
     )
     if paired:
-        near = [swapped(own, "blk", 1), crossed(after(own, everywhere, mask), "blk")]
+        near = [crossed(own, "blk"), swapped(own, "blk", 1)]
     else:
         near = [shifted(own, "blk", -offset) for offset in offsets[1:]]
     queries, special_queries, *state = call(
         functools.partial(first_kernel, images),
         [bf16(pairs, PAIR, 2 * patch_total), bf16(width, heads * special_block), *state_shape],
-        (mask, *both(own), *both(specials), weights),
+        (after(mask, everywhere), *both(own), *both(specials), weights),
     )
     fixed = (weights, queries, special_queries)
 
@@ -468,17 +468,19 @@
     image_rows = lambda owner: [(per_image, owner * images + b) for b in range(images)]
     for i, part in enumerate(near):
         part = after(part, state[0])
-        if i == 0:
-            if power:
-                everywhere = gathered(after(everywhere, part), "blk", bits[2:])
-            else:
-                everywhere = lax.all_gather(specials, "blk", axis=0, tiled=True)
-        stretches = [[image] for image in image_rows(i + 1)]
         parts = [both(part[b * per_image : (b + 1) * per_image]) for b in range(images)]
-        if i < len(near) - 1:
-            state = later(stretches, parts, state)
-    stretches.append([(everywhere.shape[0], None)])
-    parts.append(both(after(everywhere, state[0])))
+        if i == 0 and power:
+            everywhere = after(everywhere, part)
+            for bit in bits[1:-2]:
+                everywhere = stacked(everywhere, swapped(everywhere, "blk", bit))
+            arrived = swapped(everywhere, "blk", bits[-2])
+        state = later([[image] for image in image_rows(i + 1)], parts, state)
+        if i == 0 and power:
+            everywhere = stacked(after(everywhere, state[0]), arrived)
+            everywhere = stacked(everywhere, swapped(everywhere, "blk", bits[-1]))
+    if not power:
+        everywhere = lax.all_gather(specials, "blk", axis=0, tiled=True)
+    stretches, parts = [[(everywhere.shape[0], None)]], [both(everywhere)]
     kept, sent = call(
         functools.partial(last_kernel, stretches, real_rows),
         [f32(rows, width), bf16(rows, width)],

time: 42.6 us -> 42.1 us (0.988)
  starting transfers between devices: 16.4 us -> 9.45 us
  waiting for transfers between devices: 8.15 us -> 13.5 us
  Pallas kernels: 17 us -> 18.1 us
    ppermute x12, starting transfers between devices: 11.4 us -> 6.05 us  [swapped(): return lax.ppermute(block, axis, [(i ^ bit, i) for i in range(count)])]
    ppermute x1, waiting for transfers between devices: 0.01 us -> 4.27 us  [crossed(): lax.ppermute(block, axis, [(i, (i + (-1 if i % 2 == 0 else 1)) % count) f...]
    ppermute x1, starting transfers between devices: 5.05 us -> 3.4 us  [crossed(): lax.ppermute(block, axis, [(i, (i + (-1 if i % 2 == 0 else 1)) % count) f...]
    ppermute x12, waiting for transfers between devices: 8.15 us -> 9.24 us  [swapped(): return lax.ppermute(block, axis, [(i ^ bit, i) for i in range(count)])]
    pallas_call x9 -> x10, Pallas kernels: 17 us -> 18.1 us  [call(): pl.pallas_call(kernel, out_shape=out_shape, in_specs=in_specs or [VMEM] *...]
  transfers between devices with their start and end apart: 13 -> 13, of which waited for: 4 -> 6; matrix products, arithmetic and copies ran while one was open for 0% -> 0% of each run, Pallas kernels for 21% -> 30%
where the time goes in v9:
time: 42.1 us; the launch traced here: 41.8 us
  Pallas kernels  18.1 us (43%)
  waiting for transfers between devices  13.5 us (32%)
  starting transfers between devices  9.45 us (22%)
  between operations  0.77 us (2%)
    pallas_call x10, Pallas kernels, call(): pl.pallas_call(kernel, out_shape=out_shape, in_specs=in_specs or [VMEM] *...  18.1 us
    ppermute x12, waiting for transfers between devices, swapped(): return lax.ppermute(block, axis, [(i ^ bit, i) for i in range(count)])  9.24 us
    ppermute x12, starting transfers between devices, swapped(): return lax.ppermute(block, axis, [(i ^ bit, i) for i in range(count)])  6.05 us
    ppermute x1, waiting for transfers between devices, crossed(): lax.ppermute(block, axis, [(i, (i + (-1 if i % 2 == 0 else 1)) % count) f...  4.27 us
    ppermute x1, starting transfers between devices, crossed(): lax.ppermute(block, axis, [(i, (i + (-1 if i % 2 == 0 else 1)) % count) f...  3.4 us
  transfers between devices with their start and end apart: 13, of which 6 were waited for; matrix products, arithmetic and copies ran while one was open for 0% of the time, Pallas kernels for 30%

profile of v9, /device:TPU:0, one launch (start us, length us, event | category | flops | bytes accessed | tf_op | source)
XLA Modules:
  0.0 41.8 jit_solution(5785351596651595867)
XLA Ops:
  0.6 1.1 %shard_map.96 = (bf16[16,512]{1,0:T(8,128)(2,1)S(1)}, bf16[384,512]{1,0:T(8,128)(2,1)S(1)}) custom-call(s32[2]{0:T(128)} %frame_order.1, bf16[5,2,512]{2,1,0:T(2,128)(2,1)} %bitcast.5, bf16[5,1024]{1,0:T(8,128)(2,1)} %role_first.1, bf16[5,1024]{1,0:T(8,128)(2,1)} %role_rest.1, bf16[384,512]{1,0:T(8,128)(2,1)} %bitcast.4), custom_call_target="tpu_custom_call" | custom-call | tf_op jit(solution)/shard_map/pallas_call | solution.py:364
  1.7 3.1 %collective-permute-start = (bf16[16,512]{1,0:T(8,128)(2,1)S(1)}, bf16[16,512]{1,0:T(8,128)(2,1)S(1)}, u32[]{:S(2)}, u32[]{:S(2)}) collective-permute-start(bf16[16,512]{1,0:T(8,128)(2,1)S(1)} %get-tuple-element.30.first.special), channel_id=1, source_target_pairs={{4,0},{6,2},{0,4},{2,6},{12,8},{14,10},{8,12},{10,14},{5,1},{7,3},... | collective-permute-start | bytes 49160 | tf_op jit(solution)/shard_map/ppermute | solution.py:30
  4.8 3.4 %collective-permute-start.1 = (bf16[384,512]{1,0:T(8,128)(2,1)S(1)}, bf16[384,512]{1,0:T(8,128)(2,1)S(1)}, u32[]{:S(2)}, u32[]{:S(2)}) collective-permute-start(bf16[384,512]{1,0:T(8,128)(2,1)S(1)} %get-tuple-element.31.own), channel_id=1, source_target_pairs={{0,14},{2,4},{4,2},{6,8},{8,6},{10,12},{12,10},{14,0},{1,15},{3,5}... | collective-permute-start | bytes 1179656 | tf_op jit(solution)/shard_map/ppermute | solution.py:35
  8.2 0.0 collective-permute-start.2
  8.2 0.5 %collective-permute-start.3 = (bf16[16,512]{1,0:T(8,128)(2,1)S(1)}, bf16[16,512]{1,0:T(8,128)(2,1)S(1)}, u32[]{:S(2)}, u32[]{:S(2)}) collective-permute-start(bf16[16,512]{1,0:T(8,128)(2,1)S(1)} %get-tuple-element.30.first.special), channel_id=1, source_target_pairs={{1,0},{0,1},{3,2},{2,3},{5,4},{4,5},{7,6},{6,7},{9,8},{8,9},{11,10... | collective-permute-start | bytes 49160 | tf_op jit(solution)/shard_map/ppermute | solution.py:30
  8.7 0.0 collective-permute-start.9
  8.7 1.9 %shard_map.95 = (f32[8,512]{1,0:T(8,128)S(1)}, bf16[3,1024,512]{2,1,0:T(8,128)(2,1)S(1)}) custom-call(s32[2,16]{1,0:T(2,128)} %covisible.1, bf16[3,1024,512]{2,1,0:T(8,128)(2,1)} %w_qkv.1), custom_call_target="tpu_custom_call" | custom-call | tf_op jit(solution)/shard_map/pallas_call | solution.py:364
  10.6 0.0 collective-permute-done.second
  10.7 0.0 collective-permute-done.3.other_special
  10.7 0.0 collective-permute-done.2.other
  10.7 3.4 %shard_map.98 = (bf16[4,128,768]{2,1,0:T(8,128)(2,1)S(1)}, bf16[512,128]{1,0:T(8,128)(2,1)S(1)}, f32[8,768]{1,0:T(8,128)S(1)}, f32[8,768]{1,0:T(8,128)S(1)}, f32...) custom-call(f32[8,512]{1,0:T(8,128)S(1)} %get-tuple-element.32.mask, bf16[384,512]{1,0:T(8,128)(2,1)S(1)} %get-tuple-element.31.own, ...), custom_call_target="tpu_custom_call" | custom-call | tf_op jit(solution)/shard_map/pallas_call | solution.py:364
  14.1 4.3 %collective-permute-done.1 = bf16[384,512]{1,0:T(8,128)(2,1)S(1)} collective-permute-done((bf16[384,512]{1,0:T(8,128)(2,1)S(1)}, bf16[384,512]{1,0:T(8,128)(2,1)S(1)}, u32[]{:S(2)}, u32[]{:S(2)}) %collective-permute-start.1) | collective-permute-done | bytes 393248 | tf_op jit(solution)/shard_map/ppermute | solution.py:35
  18.4 0.1 collective-permute-start.4
  18.5 0.5 %collective-permute-start.5 = (bf16[192,512]{1,0:T(8,128)(2,1)S(1)}, bf16[192,512]{1,0:T(8,128)(2,1)S(1)}, u32[]{:S(2)}, u32[]{:S(2)}) collective-permute-start(bf16[192,512]{1,0:T(8,128)(2,1)S(1)} %get-tuple-element.58.refs_1_), channel_id=1, source_target_pairs={{1,0},{0,1},{3,2},{2,3},{5,4},{4,5},{7,6},{6,7},{9,8},{8,9},{11,10... | collective-permute-start | bytes 589832 | tf_op jit(solution)/shard_map/ppermute | solution.py:30
  19.0 0.6 %collective-permute-start.6 = (bf16[32,512]{1,0:T(8,128)(2,1)S(1)}, bf16[32,512]{1,0:T(8,128)(2,1)S(1)}, u32[]{:S(2)}, u32[]{:S(2)}) collective-permute-start(bf16[32,512]{1,0:T(8,128)(2,1)S(1)} %shard_map.97.first), channel_id=1, source_target_pairs={{8,0},{10,2},{12,4},{14,6},{0,8},{2,10},{4,12},{6,14},{9,1},{11,3}... | collective-permute-start | bytes 98312 | tf_op jit(solution)/shard_map/ppermute | solution.py:30
  19.6 0.3 collective-permute-done.4.refs_2_
  19.9 0.3 collective-permute-done.5.refs_3_
  20.2 3.5 %shard_map.99 = (f32[8,768]{1,0:T(8,128)S(1)}, f32[8,768]{1,0:T(8,128)S(1)}, f32[4,64,768]{2,1,0:T(8,128)S(1)}, f32[512,128]{1,0:T(8,128)S(1)}) custom-call(f32[8,512]{1,0:T(8,128)S(1)} %get-tuple-element.32.mask, bf16[192,512]{1,0:T(8,128)(2,1)S(1)} %get-tuple-element.59.refs_0_, bf16[192,512]{1,0:T(8,128)(2,1)S(1)} %get-tuple-element.58.refs_1_, ...), custom_call_target="tpu_custom_call" | custom-call | tf_op jit(solution)/shard_map/pallas_call | solution.py:364
  23.7 3.0 %collective-permute-done.9 = bf16[384,512]{1,0:T(8,128)(2,1)S(1)} collective-permute-done((bf16[384,512]{1,0:T(8,128)(2,1)S(1)}, bf16[384,512]{1,0:T(8,128)(2,1)S(1)}, u32[]{:S(2)}, u32[]{:S(2)}) %collective-permute-start.9) | collective-permute-done | bytes 393248 | tf_op jit(solution)/shard_map/ppermute | solution.py:30
  26.7 0.1 collective-permute-start.10
  26.8 0.5 %collective-permute-start.11 = (bf16[192,512]{1,0:T(8,128)(2,1)S(1)}, bf16[192,512]{1,0:T(8,128)(2,1)S(1)}, u32[]{:S(2)}, u32[]{:S(2)}) collective-permute-start(bf16[192,512]{1,0:T(8,128)(2,1)S(1)} %get-tuple-element.56.refs_1_), channel_id=1, source_target_pairs={{1,0},{0,1},{3,2},{2,3},{5,4},{4,5},{7,6},{6,7},{9,8},{8,9},{11,10... | collective-permute-start | bytes 589832 | tf_op jit(solution)/shard_map/ppermute | solution.py:30
  27.3 0.0 collective-permute-done.6.second
  27.3 0.1 collective-permute-start.7
  27.4 4.3 %collective-permute-done.7.second = bf16[64,512]{1,0:T(8,128)(2,1)S(1)} collective-permute-done((bf16[64,512]{1,0:T(8,128)(2,1)S(1)}, bf16[64,512]{1,0:T(8,128)(2,1)S(1)}, u32[]{:S(2)}, u32[]{:S(2)}) %collective-permute-start.7) | collective-permute-done | bytes 65568 | tf_op jit(solution)/shard_map/ppermute | solution.py:30
  31.7 0.1 collective-permute-start.8
  31.7 0.0 collective-permute-done.10.refs_2_
  31.8 3.5 %shard_map.102 = (f32[8,768]{1,0:T(8,128)S(1)}, f32[8,768]{1,0:T(8,128)S(1)}, f32[4,64,768]{2,1,0:T(8,128)S(1)}, f32[512,128]{1,0:T(8,128)S(1)}) custom-call(f32[8,512]{1,0:T(8,128)S(1)} %get-tuple-element.32.mask, bf16[192,512]{1,0:T(8,128)(2,1)S(1)} %get-tuple-element.57.refs_0_, bf16[192,512]{1,0:T(8,128)(2,1)S(1)} %get-tuple-element.56.refs_1_, ...), custom_call_target="tpu_custom_call" | custom-call | tf_op jit(solution)/shard_map/pallas_call | solution.py:364
  35.3 0.0 collective-permute-done.8.refs_1_
  35.3 3.8 %shard_map.103 = (f32[400,512]{1,0:T(8,128)S(1)}, bf16[400,512]{1,0:T(8,128)(2,1)S(1)}) custom-call(f32[8,512]{1,0:T(8,128)S(1)} %get-tuple-element.32.mask, bf16[128,512]{1,0:T(8,128)(2,1)S(1)} %shard_map.101.refs_0_, bf16[128,512]{1,0:T(8,128)(2,1)S(1)} %collective-permute-done.8.refs_1_, ...), custom_call_target="tpu_custom_call" | custom-call | tf_op jit(solution)/shard_map/pallas_call | solution.py:364
  39.1 0.6 %collective-permute-start.12 = (bf16[400,512]{1,0:T(8,128)(2,1)S(1)}, bf16[400,512]{1,0:T(8,128)(2,1)S(1)}, u32[]{:S(2)}, u32[]{:S(2)}) collective-permute-start(bf16[400,512]{1,0:T(8,128)(2,1)S(1)} %get-tuple-element.53), channel_id=1, source_target_pairs={{1,0},{0,1},{3,2},{2,3},{5,4},{4,5},{7,6},{6,7},{9,8},{8,9},{11,10... | collective-permute-start | bytes 1228808 | tf_op jit(solution)/shard_map/ppermute | solution.py:30
  39.7 1.4 %collective-permute-done.12.received = bf16[400,512]{1,0:T(8,128)(2,1)S(1)} collective-permute-done((bf16[400,512]{1,0:T(8,128)(2,1)S(1)}, bf16[400,512]{1,0:T(8,128)(2,1)S(1)}, u32[]{:S(2)}, u32[]{:S(2)}) %collective-permute-start.12) | collective-permute-done | bytes 409632 | tf_op jit(solution)/shard_map/ppermute | solution.py:30
  41.0 0.8 %shard_map.104 = (bf16[384,512]{1,0:T(8,128)(2,1)}, bf16[5,2,512]{2,1,0:T(2,128)(2,1)}) custom-call(f32[400,512]{1,0:T(8,128)S(1)} %get-tuple-element.52.kept, bf16[400,512]{1,0:T(8,128)(2,1)S(1)} %collective-permute-done.12.received), custom_call_target="tpu_custom_call" | custom-call | tf_op jit(solution)/shard_map/pallas_call | solution.py:364
  (6 shorter events, 0.1 us)
Async XLA Ops:
  1.7 8.9 %collective-permute-start = (bf16[16,512]{1,0:T(8,128)(2,1)S(1)}, bf16[16,512]{1,0:T(8,128)(2,1)S(1)}, u32[]{:S(2)}, u32[]{:S(2)}) collective-permute-start(bf16[16,512]{1,0:T(8,128)(2,1)S(1)} %get-tuple-element.30.first.special), channel_id=1, source_target_pairs={{4,0},{6,2},{0,4},{2,6},{12,8},{14,10},{8,12},{10,14},{5,1},{7,3},... | collective-permute-start | bytes 49160 | tf_op jit(solution)/shard_map/ppermute | solution.py:30
  4.8 13.6 %collective-permute-start.1 = (bf16[384,512]{1,0:T(8,128)(2,1)S(1)}, bf16[384,512]{1,0:T(8,128)(2,1)S(1)}, u32[]{:S(2)}, u32[]{:S(2)}) collective-permute-start(bf16[384,512]{1,0:T(8,128)(2,1)S(1)} %get-tuple-element.31.own), channel_id=1, source_target_pairs={{0,14},{2,4},{4,2},{6,8},{8,6},{10,12},{12,10},{14,0},{1,15},{3,5}... | collective-permute-start | bytes 1179656 | tf_op jit(solution)/shard_map/ppermute | solution.py:35
  8.2 2.4 %collective-permute-start.2 = (bf16[384,512]{1,0:T(8,128)(2,1)S(1)}, bf16[384,512]{1,0:T(8,128)(2,1)S(1)}, u32[]{:S(2)}, u32[]{:S(2)}) collective-permute-start(bf16[384,512]{1,0:T(8,128)(2,1)S(1)} %get-tuple-element.31.own), channel_id=1, source_target_pairs={{1,0},{0,1},{3,2},{2,3},{5,4},{4,5},{7,6},{6,7},{9,8},{8,9},{11,10... | collective-permute-start | bytes 1179656 | tf_op jit(solution)/shard_map/ppermute | solution.py:30
  8.2 2.4 %collective-permute-start.3 = (bf16[16,512]{1,0:T(8,128)(2,1)S(1)}, bf16[16,512]{1,0:T(8,128)(2,1)S(1)}, u32[]{:S(2)}, u32[]{:S(2)}) collective-permute-start(bf16[16,512]{1,0:T(8,128)(2,1)S(1)} %get-tuple-element.30.first.special), channel_id=1, source_target_pairs={{1,0},{0,1},{3,2},{2,3},{5,4},{4,5},{7,6},{6,7},{9,8},{8,9},{11,10... | collective-permute-start | bytes 49160 | tf_op jit(solution)/shard_map/ppermute | solution.py:30
  8.7 18.0 %collective-permute-start.9 = (bf16[384,512]{1,0:T(8,128)(2,1)S(1)}, bf16[384,512]{1,0:T(8,128)(2,1)S(1)}, u32[]{:S(2)}, u32[]{:S(2)}) collective-permute-start(bf16[384,512]{1,0:T(8,128)(2,1)S(1)} %get-tuple-element.31.own), channel_id=1, source_target_pairs={{2,0},{0,2},{6,4},{4,6},{10,8},{8,10},{14,12},{12,14},{3,1},{1,3},... | collective-permute-start | bytes 1179656 | tf_op jit(solution)/shard_map/ppermute | solution.py:30
  18.4 1.5 %collective-permute-start.4 = (bf16[192,512]{1,0:T(8,128)(2,1)S(1)}, bf16[192,512]{1,0:T(8,128)(2,1)S(1)}, u32[]{:S(2)}, u32[]{:S(2)}) collective-permute-start(bf16[192,512]{1,0:T(8,128)(2,1)S(1)} %get-tuple-element.59.refs_0_), channel_id=1, source_target_pairs={{1,0},{0,1},{3,2},{2,3},{5,4},{4,5},{7,6},{6,7},{9,8},{8,9},{11,10... | collective-permute-start | bytes 589832 | tf_op jit(solution)/shard_map/ppermute | solution.py:30
  18.5 1.7 %collective-permute-start.5 = (bf16[192,512]{1,0:T(8,128)(2,1)S(1)}, bf16[192,512]{1,0:T(8,128)(2,1)S(1)}, u32[]{:S(2)}, u32[]{:S(2)}) collective-permute-start(bf16[192,512]{1,0:T(8,128)(2,1)S(1)} %get-tuple-element.58.refs_1_), channel_id=1, source_target_pairs={{1,0},{0,1},{3,2},{2,3},{5,4},{4,5},{7,6},{6,7},{9,8},{8,9},{11,10... | collective-permute-start | bytes 589832 | tf_op jit(solution)/shard_map/ppermute | solution.py:30
  19.0 8.3 %collective-permute-start.6 = (bf16[32,512]{1,0:T(8,128)(2,1)S(1)}, bf16[32,512]{1,0:T(8,128)(2,1)S(1)}, u32[]{:S(2)}, u32[]{:S(2)}) collective-permute-start(bf16[32,512]{1,0:T(8,128)(2,1)S(1)} %shard_map.97.first), channel_id=1, source_target_pairs={{8,0},{10,2},{12,4},{14,6},{0,8},{2,10},{4,12},{6,14},{9,1},{11,3}... | collective-permute-start | bytes 98312 | tf_op jit(solution)/shard_map/ppermute | solution.py:30
  26.7 5.0 %collective-permute-start.10 = (bf16[192,512]{1,0:T(8,128)(2,1)S(1)}, bf16[192,512]{1,0:T(8,128)(2,1)S(1)}, u32[]{:S(2)}, u32[]{:S(2)}) collective-permute-start(bf16[192,512]{1,0:T(8,128)(2,1)S(1)} %get-tuple-element.57.refs_0_), channel_id=1, source_target_pairs={{1,0},{0,1},{3,2},{2,3},{5,4},{4,5},{7,6},{6,7},{9,8},{8,9},{11,10... | collective-permute-start | bytes 589832 | tf_op jit(solution)/shard_map/ppermute | solution.py:30
  26.8 4.9 %collective-permute-start.11 = (bf16[192,512]{1,0:T(8,128)(2,1)S(1)}, bf16[192,512]{1,0:T(8,128)(2,1)S(1)}, u32[]{:S(2)}, u32[]{:S(2)}) collective-permute-start(bf16[192,512]{1,0:T(8,128)(2,1)S(1)} %get-tuple-element.56.refs_1_), channel_id=1, source_target_pairs={{1,0},{0,1},{3,2},{2,3},{5,4},{4,5},{7,6},{6,7},{9,8},{8,9},{11,10... | collective-permute-start | bytes 589832 | tf_op jit(solution)/shard_map/ppermute | solution.py:30
  27.3 4.3 %collective-permute-start.7 = (bf16[64,512]{1,0:T(8,128)(2,1)S(1)}, bf16[64,512]{1,0:T(8,128)(2,1)S(1)}, u32[]{:S(2)}, u32[]{:S(2)}) collective-permute-start(bf16[64,512]{1,0:T(8,128)(2,1)S(1)} %shard_map.100.first), channel_id=1, source_target_pairs={{2,0},{0,2},{6,4},{4,6},{10,8},{8,10},{14,12},{12,14},{3,1},{1,3},... | collective-permute-start | bytes 196616 | tf_op jit(solution)/shard_map/ppermute | solution.py:30
  31.7 3.6 %collective-permute-start.8 = (bf16[128,512]{1,0:T(8,128)(2,1)S(1)}, bf16[128,512]{1,0:T(8,128)(2,1)S(1)}, u32[]{:S(2)}, u32[]{:S(2)}) collective-permute-start(bf16[128,512]{1,0:T(8,128)(2,1)S(1)} %shard_map.101.refs_0_), channel_id=1, source_target_pairs={{1,0},{0,1},{3,2},{2,3},{5,4},{4,5},{7,6},{6,7},{9,8},{8,9},{11,10... | collective-permute-start | bytes 393224 | tf_op jit(solution)/shard_map/ppermute | solution.py:30
  39.1 1.9 %collective-permute-start.12 = (bf16[400,512]{1,0:T(8,128)(2,1)S(1)}, bf16[400,512]{1,0:T(8,128)(2,1)S(1)}, u32[]{:S(2)}, u32[]{:S(2)}) collective-permute-start(bf16[400,512]{1,0:T(8,128)(2,1)S(1)} %get-tuple-element.53), channel_id=1, source_target_pairs={{1,0},{0,1},{3,2},{2,3},{5,4},{4,5},{7,6},{6,7},{9,8},{8,9},{11,10... | collective-permute-start | bytes 1228808 | tf_op jit(solution)/shard_map/ppermute | solution.py:30

commit v10 on v9

--- a/solution.py
+++ b/solution.py
@@ -448,13 +448,13 @@
         scratch=[pltpu.SMEM(covisible.shape, jnp.int32), pltpu.SemaphoreType.DMA((1 + 3,))],
     )
     if paired:
-        near = [crossed(own, "blk"), swapped(own, "blk", 1)]
+        near = [crossed(patches, "blk"), swapped(patches, "blk", 1)]
     else:
-        near = [shifted(own, "blk", -offset) for offset in offsets[1:]]
+        near = [shifted(patches, "blk", -offset) for offset in offsets[1:]]
     queries, special_queries, *state = call(
         functools.partial(first_kernel, images),
         [bf16(pairs, PAIR, 2 * patch_total), bf16(width, heads * special_block), *state_shape],
-        (after(mask, everywhere), *both(own), *both(specials), weights),
+        (mask, own, swapped(patches, "head", 1), *both(specials), weights),
     )
     fixed = (weights, queries, special_queries)
 
@@ -477,7 +477,7 @@
         state = later([[image] for image in image_rows(i + 1)], parts, state)
         if i == 0 and power:
             everywhere = stacked(after(everywhere, state[0]), arrived)
-            everywhere = stacked(everywhere, swapped(everywhere, "blk", bits[-1]))
+            everywhere = stacked(everywhere, swapped(everywhere, "blk", bits[-1]), FIRST)
     if not power:
         everywhere = lax.all_gather(specials, "blk", axis=0, tiled=True)
     stretches, parts = [[(everywhere.shape[0], None)]], [both(everywhere)]

time: 42.1 us -> 37.4 us (0.89)
  waiting for transfers between devices: 13.5 us -> 8.54 us
    ppermute x12, waiting for transfers between devices: 9.24 us -> 5.18 us  [swapped(): return lax.ppermute(block, axis, [(i ^ bit, i) for i in range(count)])]
    ppermute x1, starting transfers between devices: 3.4 us -> 5.6 us  [crossed(): lax.ppermute(block, axis, [(i, (i + (-1 if i % 2 == 0 else 1)) % count) f...]
    ppermute x12, starting transfers between devices: 6.05 us -> 3.97 us  [swapped(): return lax.ppermute(block, axis, [(i ^ bit, i) for i in range(count)])]
    ppermute x1, waiting for transfers between devices: 4.27 us -> 3.36 us  [crossed(): lax.ppermute(block, axis, [(i, (i + (-1 if i % 2 == 0 else 1)) % count) f...]
  transfers between devices with their start and end apart: 13 -> 13, of which waited for: 6 -> 8; matrix products, arithmetic and copies ran while one was open for 0% -> 0% of each run, Pallas kernels for 30% -> 36%
where the time goes in v10:
time: 37.4 us; the launch traced here: 37 us
  Pallas kernels  18.1 us (48%)
  starting transfers between devices  9.57 us (26%)
  waiting for transfers between devices  8.54 us (23%)
  between operations  0.73 us (2%)
    pallas_call x10, Pallas kernels, call(): pl.pallas_call(kernel, out_shape=out_shape, in_specs=in_specs or [VMEM] *...  18.1 us
    ppermute x1, starting transfers between devices, crossed(): lax.ppermute(block, axis, [(i, (i + (-1 if i % 2 == 0 else 1)) % count) f...  5.6 us
    ppermute x12, waiting for transfers between devices, swapped(): return lax.ppermute(block, axis, [(i ^ bit, i) for i in range(count)])  5.18 us
    ppermute x12, starting transfers between devices, swapped(): return lax.ppermute(block, axis, [(i ^ bit, i) for i in range(count)])  3.97 us
    ppermute x1, waiting for transfers between devices, crossed(): lax.ppermute(block, axis, [(i, (i + (-1 if i % 2 == 0 else 1)) % count) f...  3.36 us
  transfers between devices with their start and end apart: 13, of which 8 were waited for; matrix products, arithmetic and copies ran while one was open for 0% of the time, Pallas kernels for 36%

profile of v10, /device:TPU:0, one launch (start us, length us, event | category | flops | bytes accessed | tf_op | source)
XLA Modules:
  0.0 37.0 jit_solution(4015605179852601661)
XLA Ops:
  0.6 0.5 %collective-permute-start.2 = (bf16[384,512]{1,0:T(8,128)(2,1)}, bf16[384,512]{1,0:T(8,128)(2,1)S(1)}, u32[]{:S(2)}, u32[]{:S(2)}) collective-permute-start(bf16[384,512]{1,0:T(8,128)(2,1)} %bitcast.4), channel_id=1, source_target_pairs={{1,0},{0,1},{3,2},{2,3},{5,4},{4,5},{7,6},{6,7},{9,8},{8,9},{11,10... | collective-permute-start | bytes 1179656 | tf_op jit(solution)/shard_map/ppermute | solution.py:30
  1.1 5.6 %collective-permute-start.1 = (bf16[384,512]{1,0:T(8,128)(2,1)}, bf16[384,512]{1,0:T(8,128)(2,1)S(1)}, u32[]{:S(2)}, u32[]{:S(2)}) collective-permute-start(bf16[384,512]{1,0:T(8,128)(2,1)} %bitcast.5), channel_id=1, source_target_pairs={{0,14},{2,4},{4,2},{6,8},{8,6},{10,12},{12,10},{14,0},{1,15},{3,5}... | collective-permute-start | bytes 1179656 | tf_op jit(solution)/shard_map/ppermute | solution.py:35
  6.8 1.1 %shard_map.96 = (bf16[16,512]{1,0:T(8,128)(2,1)S(1)}, bf16[384,512]{1,0:T(8,128)(2,1)S(1)}) custom-call(s32[2]{0:T(128)} %frame_order.1, bf16[5,2,512]{2,1,0:T(2,128)(2,1)} %bitcast.8, bf16[5,1024]{1,0:T(8,128)(2,1)} %role_first.1, bf16[5,1024]{1,0:T(8,128)(2,1)} %role_rest.1, bf16[384,512]{1,0:T(8,128)(2,1)} %bitcast.6), custom_call_target="tpu_custom_call" | custom-call | tf_op jit(solution)/shard_map/pallas_call | solution.py:364
  7.9 0.2 collective-permute-start.3
  8.1 0.0 collective-permute-start
  8.1 0.1 collective-permute-start.9
  8.2 1.9 %shard_map.95 = (f32[8,512]{1,0:T(8,128)S(1)}, bf16[3,1024,512]{2,1,0:T(8,128)(2,1)S(1)}) custom-call(s32[2,16]{1,0:T(2,128)} %covisible.1, bf16[3,1024,512]{2,1,0:T(8,128)(2,1)} %w_qkv.1), custom_call_target="tpu_custom_call" | custom-call | tf_op jit(solution)/shard_map/pallas_call | solution.py:364
  10.1 0.0 collective-permute-done.3.other_special
  10.1 0.0 collective-permute-done.2.other
  10.1 3.4 %shard_map.98 = (bf16[4,128,768]{2,1,0:T(8,128)(2,1)S(1)}, bf16[512,128]{1,0:T(8,128)(2,1)S(1)}, f32[8,768]{1,0:T(8,128)S(1)}, f32[8,768]{1,0:T(8,128)S(1)}, f32...) custom-call(f32[8,512]{1,0:T(8,128)S(1)} %get-tuple-element.28.mask, bf16[384,512]{1,0:T(8,128)(2,1)S(1)} %get-tuple-element.30.own, ...), custom_call_target="tpu_custom_call" | custom-call | tf_op jit(solution)/shard_map/pallas_call | solution.py:364
  13.5 3.4 %collective-permute-done.1 = bf16[384,512]{1,0:T(8,128)(2,1)S(1)} collective-permute-done((bf16[384,512]{1,0:T(8,128)(2,1)}, bf16[384,512]{1,0:T(8,128)(2,1)S(1)}, u32[]{:S(2)}, u32[]{:S(2)}) %collective-permute-start.1) | collective-permute-done | bytes 393248 | tf_op jit(solution)/shard_map/ppermute | solution.py:35
  16.9 0.1 collective-permute-start.4
  17.0 0.5 %collective-permute-start.5 = (bf16[192,512]{1,0:T(8,128)(2,1)S(1)}, bf16[192,512]{1,0:T(8,128)(2,1)S(1)}, u32[]{:S(2)}, u32[]{:S(2)}) collective-permute-start(bf16[192,512]{1,0:T(8,128)(2,1)S(1)} %get-tuple-element.56.refs_1_), channel_id=1, source_target_pairs={{1,0},{0,1},{3,2},{2,3},{5,4},{4,5},{7,6},{6,7},{9,8},{8,9},{11,10... | collective-permute-start | bytes 589832 | tf_op jit(solution)/shard_map/ppermute | solution.py:30
  17.5 0.0 collective-permute-done.second
  17.5 0.6 %collective-permute-start.6 = (bf16[32,512]{1,0:T(8,128)(2,1)S(1)}, bf16[32,512]{1,0:T(8,128)(2,1)S(1)}, u32[]{:S(2)}, u32[]{:S(2)}) collective-permute-start(bf16[32,512]{1,0:T(8,128)(2,1)S(1)} %shard_map.97.first), channel_id=1, source_target_pairs={{8,0},{10,2},{12,4},{14,6},{0,8},{2,10},{4,12},{6,14},{9,1},{11,3}... | collective-permute-start | bytes 98312 | tf_op jit(solution)/shard_map/ppermute | solution.py:30
  18.1 0.3 collective-permute-done.4.refs_2_
  18.4 0.3 collective-permute-done.5.refs_3_
  18.7 3.5 %shard_map.99 = (f32[8,768]{1,0:T(8,128)S(1)}, f32[8,768]{1,0:T(8,128)S(1)}, f32[4,64,768]{2,1,0:T(8,128)S(1)}, f32[512,128]{1,0:T(8,128)S(1)}) custom-call(f32[8,512]{1,0:T(8,128)S(1)} %get-tuple-element.28.mask, bf16[192,512]{1,0:T(8,128)(2,1)S(1)} %get-tuple-element.57.refs_0_, bf16[192,512]{1,0:T(8,128)(2,1)S(1)} %get-tuple-element.56.refs_1_, ...), custom_call_target="tpu_custom_call" | custom-call | tf_op jit(solution)/shard_map/pallas_call | solution.py:364
  22.2 0.1 collective-permute-done.6.second
  22.3 1.0 %collective-permute-start.7 = (bf16[64,512]{1,0:T(8,128)(2,1)S(1)}, bf16[64,512]{1,0:T(8,128)(2,1)S(1)}, u32[]{:S(2)}, u32[]{:S(2)}) collective-permute-start(bf16[64,512]{1,0:T(8,128)(2,1)S(1)} %shard_map.100.first), channel_id=1, source_target_pairs={{2,0},{0,2},{6,4},{4,6},{10,8},{8,10},{14,12},{12,14},{3,1},{1,3},... | collective-permute-start | bytes 196616 | tf_op jit(solution)/shard_map/ppermute | solution.py:30
  23.3 1.8 %collective-permute-done.9 = bf16[384,512]{1,0:T(8,128)(2,1)S(1)} collective-permute-done((bf16[384,512]{1,0:T(8,128)(2,1)}, bf16[384,512]{1,0:T(8,128)(2,1)S(1)}, u32[]{:S(2)}, u32[]{:S(2)}) %collective-permute-start.9) | collective-permute-done | bytes 393248 | tf_op jit(solution)/shard_map/ppermute | solution.py:30
  25.2 0.1 collective-permute-start.10
  25.3 0.5 %collective-permute-start.11 = (bf16[192,512]{1,0:T(8,128)(2,1)S(1)}, bf16[192,512]{1,0:T(8,128)(2,1)S(1)}, u32[]{:S(2)}, u32[]{:S(2)}) collective-permute-start(bf16[192,512]{1,0:T(8,128)(2,1)S(1)} %get-tuple-element.54.refs_1_), channel_id=1, source_target_pairs={{1,0},{0,1},{3,2},{2,3},{5,4},{4,5},{7,6},{6,7},{9,8},{8,9},{11,10... | collective-permute-start | bytes 589832 | tf_op jit(solution)/shard_map/ppermute | solution.py:30
  25.8 0.8 %collective-permute-done.7.second = bf16[64,512]{1,0:T(8,128)(2,1)S(1)} collective-permute-done((bf16[64,512]{1,0:T(8,128)(2,1)S(1)}, bf16[64,512]{1,0:T(8,128)(2,1)S(1)}, u32[]{:S(2)}, u32[]{:S(2)}) %collective-permute-start.7) | collective-permute-done | bytes 65568 | tf_op jit(solution)/shard_map/ppermute | solution.py:30
  26.6 0.1 collective-permute-start.8
  26.7 0.0 collective-permute-done.10.refs_2_
  26.7 0.3 collective-permute-done.11.refs_3_
  27.0 3.5 %shard_map.102 = (f32[8,768]{1,0:T(8,128)S(1)}, f32[8,768]{1,0:T(8,128)S(1)}, f32[4,64,768]{2,1,0:T(8,128)S(1)}, f32[512,128]{1,0:T(8,128)S(1)}) custom-call(f32[8,512]{1,0:T(8,128)S(1)} %get-tuple-element.28.mask, bf16[192,512]{1,0:T(8,128)(2,1)S(1)} %get-tuple-element.55.refs_0_, bf16[192,512]{1,0:T(8,128)(2,1)S(1)} %get-tuple-element.54.refs_1_, ...), custom_call_target="tpu_custom_call" | custom-call | tf_op jit(solution)/shard_map/pallas_call | solution.py:364
  30.5 3.8 %shard_map.103 = (f32[400,512]{1,0:T(8,128)S(1)}, bf16[400,512]{1,0:T(8,128)(2,1)S(1)}) custom-call(f32[8,512]{1,0:T(8,128)S(1)} %get-tuple-element.28.mask, bf16[128,512]{1,0:T(8,128)(2,1)S(1)} %shard_map.101.refs_0_, bf16[128,512]{1,0:T(8,128)(2,1)S(1)} %collective-permute-done.8.refs_1_, ...), custom_call_target="tpu_custom_call" | custom-call | tf_op jit(solution)/shard_map/pallas_call | solution.py:364
  34.4 0.3 collective-permute-start.12
  34.7 1.5 %collective-permute-done.12.received = bf16[400,512]{1,0:T(8,128)(2,1)S(1)} collective-permute-done((bf16[400,512]{1,0:T(8,128)(2,1)S(1)}, bf16[400,512]{1,0:T(8,128)(2,1)S(1)}, u32[]{:S(2)}, u32[]{:S(2)}) %collective-permute-start.12) | collective-permute-done | bytes 409632 | tf_op jit(solution)/shard_map/ppermute | solution.py:30
  36.2 0.8 %shard_map.104 = (bf16[384,512]{1,0:T(8,128)(2,1)}, bf16[5,2,512]{2,1,0:T(2,128)(2,1)}) custom-call(f32[400,512]{1,0:T(8,128)S(1)} %get-tuple-element.50.kept, bf16[400,512]{1,0:T(8,128)(2,1)S(1)} %collective-permute-done.12.received), custom_call_target="tpu_custom_call" | custom-call | tf_op jit(solution)/shard_map/pallas_call | solution.py:364
  (6 shorter events, 0.1 us)
Async XLA Ops:
  0.6 9.5 %collective-permute-start.2 = (bf16[384,512]{1,0:T(8,128)(2,1)}, bf16[384,512]{1,0:T(8,128)(2,1)S(1)}, u32[]{:S(2)}, u32[]{:S(2)}) collective-permute-start(bf16[384,512]{1,0:T(8,128)(2,1)} %bitcast.4), channel_id=1, source_target_pairs={{1,0},{0,1},{3,2},{2,3},{5,4},{4,5},{7,6},{6,7},{9,8},{8,9},{11,10... | collective-permute-start | bytes 1179656 | tf_op jit(solution)/shard_map/ppermute | solution.py:30
  1.1 15.7 %collective-permute-start.1 = (bf16[384,512]{1,0:T(8,128)(2,1)}, bf16[384,512]{1,0:T(8,128)(2,1)S(1)}, u32[]{:S(2)}, u32[]{:S(2)}) collective-permute-start(bf16[384,512]{1,0:T(8,128)(2,1)} %bitcast.5), channel_id=1, source_target_pairs={{0,14},{2,4},{4,2},{6,8},{8,6},{10,12},{12,10},{14,0},{1,15},{3,5}... | collective-permute-start | bytes 1179656 | tf_op jit(solution)/shard_map/ppermute | solution.py:35
  7.9 2.2 %collective-permute-start.3 = (bf16[16,512]{1,0:T(8,128)(2,1)S(1)}, bf16[16,512]{1,0:T(8,128)(2,1)S(1)}, u32[]{:S(2)}, u32[]{:S(2)}) collective-permute-start(bf16[16,512]{1,0:T(8,128)(2,1)S(1)} %get-tuple-element.29.first.special), channel_id=1, source_target_pairs={{1,0},{0,1},{3,2},{2,3},{5,4},{4,5},{7,6},{6,7},{9,8},{8,9},{11,10... | collective-permute-start | bytes 49160 | tf_op jit(solution)/shard_map/ppermute | solution.py:30
  8.1 9.4 %collective-permute-start = (bf16[16,512]{1,0:T(8,128)(2,1)S(1)}, bf16[16,512]{1,0:T(8,128)(2,1)S(1)}, u32[]{:S(2)}, u32[]{:S(2)}) collective-permute-start(bf16[16,512]{1,0:T(8,128)(2,1)S(1)} %get-tuple-element.29.first.special), channel_id=1, source_target_pairs={{4,0},{6,2},{0,4},{2,6},{12,8},{14,10},{8,12},{10,14},{5,1},{7,3},... | collective-permute-start | bytes 49160 | tf_op jit(solution)/shard_map/ppermute | solution.py:30
  8.1 17.1 %collective-permute-start.9 = (bf16[384,512]{1,0:T(8,128)(2,1)}, bf16[384,512]{1,0:T(8,128)(2,1)S(1)}, u32[]{:S(2)}, u32[]{:S(2)}) collective-permute-start(bf16[384,512]{1,0:T(8,128)(2,1)} %bitcast.7), channel_id=1, source_target_pairs={{2,0},{0,2},{6,4},{4,6},{10,8},{8,10},{14,12},{12,14},{3,1},{1,3},... | collective-permute-start | bytes 1179656 | tf_op jit(solution)/shard_map/ppermute | solution.py:30
  16.9 1.5 %collective-permute-start.4 = (bf16[192,512]{1,0:T(8,128)(2,1)S(1)}, bf16[192,512]{1,0:T(8,128)(2,1)S(1)}, u32[]{:S(2)}, u32[]{:S(2)}) collective-permute-start(bf16[192,512]{1,0:T(8,128)(2,1)S(1)} %get-tuple-element.57.refs_0_), channel_id=1, source_target_pairs={{1,0},{0,1},{3,2},{2,3},{5,4},{4,5},{7,6},{6,7},{9,8},{8,9},{11,10... | collective-permute-start | bytes 589832 | tf_op jit(solution)/shard_map/ppermute | solution.py:30
  17.0 1.7 %collective-permute-start.5 = (bf16[192,512]{1,0:T(8,128)(2,1)S(1)}, bf16[192,512]{1,0:T(8,128)(2,1)S(1)}, u32[]{:S(2)}, u32[]{:S(2)}) collective-permute-start(bf16[192,512]{1,0:T(8,128)(2,1)S(1)} %get-tuple-element.56.refs_1_), channel_id=1, source_target_pairs={{1,0},{0,1},{3,2},{2,3},{5,4},{4,5},{7,6},{6,7},{9,8},{8,9},{11,10... | collective-permute-start | bytes 589832 | tf_op jit(solution)/shard_map/ppermute | solution.py:30
  17.5 4.8 %collective-permute-start.6 = (bf16[32,512]{1,0:T(8,128)(2,1)S(1)}, bf16[32,512]{1,0:T(8,128)(2,1)S(1)}, u32[]{:S(2)}, u32[]{:S(2)}) collective-permute-start(bf16[32,512]{1,0:T(8,128)(2,1)S(1)} %shard_map.97.first), channel_id=1, source_target_pairs={{8,0},{10,2},{12,4},{14,6},{0,8},{2,10},{4,12},{6,14},{9,1},{11,3}... | collective-permute-start | bytes 98312 | tf_op jit(solution)/shard_map/ppermute | solution.py:30
  22.3 4.3 %collective-permute-start.7 = (bf16[64,512]{1,0:T(8,128)(2,1)S(1)}, bf16[64,512]{1,0:T(8,128)(2,1)S(1)}, u32[]{:S(2)}, u32[]{:S(2)}) collective-permute-start(bf16[64,512]{1,0:T(8,128)(2,1)S(1)} %shard_map.100.first), channel_id=1, source_target_pairs={{2,0},{0,2},{6,4},{4,6},{10,8},{8,10},{14,12},{12,14},{3,1},{1,3},... | collective-permute-start | bytes 196616 | tf_op jit(solution)/shard_map/ppermute | solution.py:30
  25.2 1.5 %collective-permute-start.10 = (bf16[192,512]{1,0:T(8,128)(2,1)S(1)}, bf16[192,512]{1,0:T(8,128)(2,1)S(1)}, u32[]{:S(2)}, u32[]{:S(2)}) collective-permute-start(bf16[192,512]{1,0:T(8,128)(2,1)S(1)} %get-tuple-element.55.refs_0_), channel_id=1, source_target_pairs={{1,0},{0,1},{3,2},{2,3},{5,4},{4,5},{7,6},{6,7},{9,8},{8,9},{11,10... | collective-permute-start | bytes 589832 | tf_op jit(solution)/shard_map/ppermute | solution.py:30
  25.3 1.7 %collective-permute-start.11 = (bf16[192,512]{1,0:T(8,128)(2,1)S(1)}, bf16[192,512]{1,0:T(8,128)(2,1)S(1)}, u32[]{:S(2)}, u32[]{:S(2)}) collective-permute-start(bf16[192,512]{1,0:T(8,128)(2,1)S(1)} %get-tuple-element.54.refs_1_), channel_id=1, source_target_pairs={{1,0},{0,1},{3,2},{2,3},{5,4},{4,5},{7,6},{6,7},{9,8},{8,9},{11,10... | collective-permute-start | bytes 589832 | tf_op jit(solution)/shard_map/ppermute | solution.py:30
  26.6 3.9 %collective-permute-start.8 = (bf16[128,512]{1,0:T(8,128)(2,1)S(1)}, bf16[128,512]{1,0:T(8,128)(2,1)S(1)}, u32[]{:S(2)}, u32[]{:S(2)}) collective-permute-start(bf16[128,512]{1,0:T(8,128)(2,1)S(1)} %shard_map.101.refs_0_), channel_id=1, source_target_pairs={{1,0},{0,1},{3,2},{2,3},{5,4},{4,5},{7,6},{6,7},{9,8},{8,9},{11,10... | collective-permute-start | bytes 393224 | tf_op jit(solution)/shard_map/ppermute | solution.py:30
  34.4 1.8 %collective-permute-start.12 = (bf16[400,512]{1,0:T(8,128)(2,1)S(1)}, bf16[400,512]{1,0:T(8,128)(2,1)S(1)}, u32[]{:S(2)}, u32[]{:S(2)}) collective-permute-start(bf16[400,512]{1,0:T(8,128)(2,1)S(1)} %get-tuple-element.51), channel_id=1, source_target_pairs={{1,0},{0,1},{3,2},{2,3},{5,4},{4,5},{7,6},{6,7},{9,8},{8,9},{11,10... | collective-permute-start | bytes 1228808 | tf_op jit(solution)/shard_map/ppermute | solution.py:30

commit v11 on v10

--- a/solution.py
+++ b/solution.py
@@ -13,6 +13,7 @@
 TILE_ROWS = 16
 LOG2_E = 1.4426950408889634
 FIRST = 20_000_000_000
+LAST = FIRST
 VMEM_BYTES = 32 * 1024 * 1024
 SMEM = pl.BlockSpec(memory_space=pltpu.SMEM)
 VMEM = pl.BlockSpec(memory_space=pltpu.VMEM)
@@ -56,17 +57,20 @@
 
 def rows_kernel(
     frame_order, specials, role_first, role_rest, patches,
-    special_out, patches_out, order, here, first_rows, rest_rows, copied,
+    special_out, patches_out, early_out, late_out, order, here, first_rows, rest_rows, copied,
 ):
+    cut = early_out.shape[0]
     special_count, images, width = specials.shape
     moves = [(specials, here), (role_first, first_rows), (role_rest, rest_rows), (frame_order, order)]
+    moves.append((patches.at[pl.ds(0, cut)], early_out))
     moves.append((patches, patches_out))
+    moves.append((patches.at[pl.ds(cut, late_out.shape[0])], late_out))
     copies = [
         pltpu.make_async_copy(source, target, copied.at[i]) for i, (source, target) in enumerate(moves)
     ]
     for copy in copies:
         copy.start()
-    for copy in copies[:-1]:
+    for copy in copies[:4]:
         copy.wait()
     mine, _ = halves(width)
     first = first_rows[:, mine].astype(jnp.float32)
@@ -76,7 +80,8 @@
     ]
     summed.append(jnp.zeros((special_out.shape[0] - images * special_count, width), jnp.float32))
     special_out[...] = jnp.concatenate(summed, axis=0).astype(jnp.bfloat16)
-    copies[-1].wait()
+    for copy in copies[4:]:
+        copy.wait()
 
 
 def start_kernel(
@@ -180,21 +185,20 @@
     scores = prepared(order[0])
     for step, pair in enumerate(order):
         if pair < pairs:
-            left = [
-                values_of(pair // 2)[first : first + HEAD_DIM]
-                for first in ((pair % 2) * PAIR, (pair % 2) * PAIR + HEAD_DIM)
-            ]
+            left = values_of(pair // 2)[(pair % 2) * PAIR : (pair % 2 + 1) * PAIR]
         else:
-            left = [jnp.concatenate([values_of(quad) for quad in range(quads)], axis=0)]
+            left = jnp.concatenate([values_of(quad) for quad in range(quads)], axis=0)
         following = prepared(order[step + 1]) if step < pairs else None
         largest, factor, weights = attend(
             scores, both if pair < pairs else only, state and state.largest(pair)
         )
-        width = scores.shape[1] // len(left)
-        for sub, part in enumerate(left):
+        added = product(jnp.concatenate([left, ones], axis=0), weights)
+        height, subs = (HEAD_DIM, 2) if pair < pairs else (left.shape[0], 1)
+        width = scores.shape[1] // subs
+        for sub in range(subs):
             lanes = slice(sub * width, (sub + 1) * width)
-            added = product(jnp.concatenate([part, ones], axis=0), weights[:, lanes])
-            total, weight = added[: part.shape[0]], added[part.shape[0] : part.shape[0] + 1]
+            total = added[sub * height : (sub + 1) * height, lanes]
+            weight = added[left.shape[0] : left.shape[0] + 1, lanes]
             if state is not None:
                 total = total + state.total(pair, sub) * factor[:, lanes]
                 weight = weight + state.weight(pair, sub) * factor[:, lanes]
@@ -235,12 +239,12 @@
 
 
 def first_kernel(
-    images, mask, own, other, special, other_special, weights, queries_out, special_out, *state_out
+    images, mask, own, other, special, weights, queries_out, special_out, *state_out
 ):
     patch_total = own.shape[0]
     columns = projector(
-        jnp.concatenate([own[...], special[...]], axis=0),
-        jnp.concatenate([other[...], other_special[...]], axis=0),
+        jnp.concatenate([own[...], special[0]], axis=0),
+        jnp.concatenate([other[...], special[1]], axis=0),
         weights,
     )
     pairs = queries_out.shape[0]
@@ -287,8 +291,9 @@
 
 def joined(stretches, mask, refs):
     count = len(stretches)
-    own = jnp.concatenate([ref[...] for ref in refs[:count]], axis=0)
-    other = jnp.concatenate([ref[...] for ref in refs[count : 2 * count]], axis=0)
+    flat = lambda ref, i: ref[i] if len(ref.shape) == 3 else ref[...]
+    own = jnp.concatenate([flat(ref, 0) for ref in refs[:count]], axis=0)
+    other = jnp.concatenate([flat(ref, 1) for ref in refs[count : 2 * count]], axis=0)
     masks = [
         (rows, None if i is None else mask[i : i + 1, :]) for part in stretches for rows, i in part
     ]
@@ -372,14 +377,19 @@
     )(*operands)
 
 
+def pair_kernel(first, second, out):
+    out[0] = first[...]
+    out[1] = second[...]
+
+
 def stack_kernel(first, second, out):
-    count = first.shape[0]
-    out[:count, :] = first[...]
-    out[count:, :] = second[...]
+    count = first.shape[1]
+    out[:, :count, :] = first[...]
+    out[:, count:, :] = second[...]
 
 
 def stacked(first, second, flops=0):
-    shape = jax.ShapeDtypeStruct((2 * first.shape[0], first.shape[1]), first.dtype)
+    shape = jax.ShapeDtypeStruct((2, 2 * first.shape[1], first.shape[2]), first.dtype)
     return call(stack_kernel, [shape], (first, second), flops=flops)[0]
 
 
@@ -398,6 +408,7 @@
     reach = max(1, owner_count // 64)
     patch_total = images * per_image
     rows = patch_total + special_block
+    cut = per_image * max(1, images // 2)
     heads = width // HEAD_DIM
     pairs = heads // 2
     paired = reach == 1 and owner_count % 2 == 0
@@ -420,9 +431,14 @@
     patches = patch_rows.reshape(patch_total, width)
     turned = jnp.transpose(special_rows, (1, 0, 2))
     power = owner_count >= 8 and owner_count & (owner_count - 1) == 0
-    specials, own = call(
+    specials, own, *pieces = call(
         rows_kernel,
-        [bf16(special_block, width), bf16(patch_total, width)],
+        [
+            bf16(special_block, width),
+            bf16(patch_total, width),
+            bf16(cut, width),
+            bf16(patch_total - cut, width),
+        ],
         (frame_order, turned, role_first, role_rest, patches),
         in_specs=[HBM] * 5,
         scratch=[
@@ -430,12 +446,13 @@
             pltpu.VMEM(turned.shape, jnp.bfloat16),
             pltpu.VMEM(role_first.shape, jnp.bfloat16),
             pltpu.VMEM(role_rest.shape, jnp.bfloat16),
-            pltpu.SemaphoreType.DMA((5,)),
+            pltpu.SemaphoreType.DMA((7,)),
         ],
     )
     bits = [1 << i for i in range(1, owner_count.bit_length() - 1)] + [1] if power else []
+    (specials,) = call(pair_kernel, [bf16(2, special_block, width)], both(specials))
     everywhere = specials
-    if power:
+    if paired and power:
         everywhere = stacked(specials, swapped(specials, "blk", bits[0]), FIRST)
     mask, weights = call(
         functools.partial(start_kernel, offsets, per_image, special_count, special_block),
@@ -447,14 +464,10 @@
         in_specs=[HBM] * 2,
         scratch=[pltpu.SMEM(covisible.shape, jnp.int32), pltpu.SemaphoreType.DMA((1 + 3,))],
     )
-    if paired:
-        near = [crossed(patches, "blk"), swapped(patches, "blk", 1)]
-    else:
-        near = [shifted(patches, "blk", -offset) for offset in offsets[1:]]
     queries, special_queries, *state = call(
         functools.partial(first_kernel, images),
         [bf16(pairs, PAIR, 2 * patch_total), bf16(width, heads * special_block), *state_shape],
-        (mask, own, swapped(patches, "head", 1), *both(specials), weights),
+        (mask, own, swapped(patches, "head", 1), specials, weights),
     )
     fixed = (weights, queries, special_queries)
 
@@ -466,21 +479,40 @@
         )
 
     image_rows = lambda owner: [(per_image, owner * images + b) for b in range(images)]
-    for i, part in enumerate(near):
-        part = after(part, state[0])
-        parts = [both(part[b * per_image : (b + 1) * per_image]) for b in range(images)]
-        if i == 0 and power:
-            everywhere = after(everywhere, part)
+    def halved(part, gate):
+        part = after(part, gate)
+        starts = range(0, part.shape[0], per_image)
+        return [both(part[start : start + per_image]) for start in starts]
+
+    stretches = lambda owner, first, last: [[image] for image in image_rows(owner)[first:last]]
+    if paired:
+        far = after(crossed(patches, "blk"), state[0])
+        near = [swapped(pieces[0], "blk", 1), swapped(after(pieces[1], far), "blk", 1)]
+        if power:
+            everywhere = after(everywhere, far)
             for bit in bits[1:-2]:
                 everywhere = stacked(everywhere, swapped(everywhere, "blk", bit))
             arrived = swapped(everywhere, "blk", bits[-2])
-        state = later([[image] for image in image_rows(i + 1)], parts, state)
-        if i == 0 and power:
-            everywhere = stacked(after(everywhere, state[0]), arrived)
-            everywhere = stacked(everywhere, swapped(everywhere, "blk", bits[-1]), FIRST)
-    if not power:
-        everywhere = lax.all_gather(specials, "blk", axis=0, tiled=True)
-    stretches, parts = [[(everywhere.shape[0], None)]], [both(everywhere)]
+        state = later(stretches(1, 0, images), halved(far, state[0]), state)
+        if power:
+            everywhere = stacked(after(everywhere, state[0]), arrived, FIRST)
+            arrived = swapped(everywhere, "blk", bits[-1])
+        near = [halved(part, state[0]) for part in near]
+        count = len(near[0])
+        state = later(stretches(2, 0, count), near[0], state)
+        if power:
+            everywhere = stacked(after(everywhere, state[0]), arrived, LAST)
+        last_stretches, parts = stretches(2, count, images), near[1]
+    else:
+        for i, offset in enumerate(offsets[1:]):
+            parts = halved(shifted(patches, "blk", -offset), state[0])
+            last_stretches = stretches(i + 1, 0, images)
+            if i < len(offsets) - 2:
+                state = later(last_stretches, parts, state)
+    if not (paired and power):
+        everywhere = lax.all_gather(specials, "blk", axis=1, tiled=True)
+    stretches = last_stretches + [[(everywhere.shape[1], None)]]
+    parts = parts + [(everywhere, everywhere)]
     kept, sent = call(
         functools.partial(last_kernel, stretches, real_rows),
         [f32(rows, width), bf16(rows, width)],

time: 37.4 us -> 37.9 us (1.013)
  the two profiles are of different devices: /device:TPU:0 before, /device:TPU:9 now
where the time goes in v11:
time: 37.9 us; the launch traced here: 37.7 us
  Pallas kernels  17.7 us (47%)
  starting transfers between devices  14.3 us (38%)
  waiting for transfers between devices  4.93 us (13%)
  between operations  0.75 us (2%)
    pallas_call x11, Pallas kernels, call(): pl.pallas_call(kernel, out_shape=out_shape, in_specs=in_specs or [VMEM] *...  17.7 us
    ppermute x12, starting transfers between devices, swapped(): return lax.ppermute(block, axis, [(i ^ bit, i) for i in range(count)])  13.2 us
    ppermute x12, waiting for transfers between devices, swapped(): return lax.ppermute(block, axis, [(i ^ bit, i) for i in range(count)])  4.6 us
    ppermute x1, starting transfers between devices, crossed(): lax.ppermute(block, axis, [(i, (i + (-1 if i % 2 == 0 else 1)) % count) f...  1.11 us
  transfers between devices with their start and end apart: 13, of which 4 were waited for; matrix products, arithmetic and copies ran while one was open for 0% of the time, Pallas kernels for 32%

profile of v11, /device:TPU:9, one launch (start us, length us, event | category | flops | bytes accessed | tf_op | source)
XLA Modules:
  0.0 37.7 jit_solution(14302485521066900995)
XLA Ops:
  0.6 0.7 %collective-permute-start.1 = (bf16[384,512]{1,0:T(8,128)(2,1)}, bf16[384,512]{1,0:T(8,128)(2,1)S(1)}, u32[]{:S(2)}, u32[]{:S(2)}) collective-permute-start(bf16[384,512]{1,0:T(8,128)(2,1)} %bitcast.4), channel_id=1, source_target_pairs={{1,0},{0,1},{3,2},{2,3},{5,4},{4,5},{7,6},{6,7},{9,8},{8,9},{11,10... | collective-permute-start | bytes 1179656 | tf_op jit(solution)/shard_map/ppermute | solution.py:31
  1.4 1.1 %collective-permute-start = (bf16[384,512]{1,0:T(8,128)(2,1)}, bf16[384,512]{1,0:T(8,128)(2,1)S(1)}, u32[]{:S(2)}, u32[]{:S(2)}) collective-permute-start(bf16[384,512]{1,0:T(8,128)(2,1)} %bitcast.5), channel_id=1, source_target_pairs={{0,14},{2,4},{4,2},{6,8},{8,6},{10,12},{12,10},{14,0},{1,15},{3,5}... | collective-permute-start | bytes 1179656 | tf_op jit(solution)/shard_map/ppermute | solution.py:36
  2.5 1.2 %shard_map.96 = (bf16[16,512]{1,0:T(8,128)(2,1)S(1)}, bf16[384,512]{1,0:T(8,128)(2,1)S(1)}, bf16[192,512]{1,0:T(8,128)(2,1)S(1)}, bf16[192,512]{1,0:T(8,128)(2,1)S(1)}) custom-call(s32[2]{0:T(128)} %frame_order.1, bf16[5,2,512]{2,1,0:T(2,128)(2,1)} %bitcast.7, bf16[5,1024]{1,0:T(8,128)(2,1)} %role_first.1, bf16[5,1024]{1,0:T(8,128)(2,1)} %role_rest.1, ...), custom_call_target="tpu_custom_call" | custom-call | tf_op jit(solution)/shard_map/pallas_call | solution.py:369
  3.7 0.4 %collective-permute-start.2 = (bf16[16,512]{1,0:T(8,128)(2,1)S(1)}, bf16[16,512]{1,0:T(8,128)(2,1)S(1)}, u32[]{:S(2)}, u32[]{:S(2)}) collective-permute-start(bf16[16,512]{1,0:T(8,128)(2,1)S(1)} %get-tuple-element.37.first), channel_id=1, source_target_pairs={{1,0},{0,1},{3,2},{2,3},{5,4},{4,5},{7,6},{6,7},{9,8},{8,9},{11,10... | collective-permute-start | bytes 49160 | tf_op jit(solution)/shard_map/ppermute | solution.py:31
  4.2 1.4 %collective-permute-start.8 = (bf16[192,512]{1,0:T(8,128)(2,1)S(1)}, bf16[192,512]{1,0:T(8,128)(2,1)S(1)}, u32[]{:S(2)}, u32[]{:S(2)}) collective-permute-start(bf16[192,512]{1,0:T(8,128)(2,1)S(1)} %get-tuple-element.52), channel_id=1, source_target_pairs={{2,0},{0,2},{6,4},{4,6},{10,8},{8,10},{14,12},{12,14},{3,1},{1,3},... | collective-permute-start | bytes 589832 | tf_op jit(solution)/shard_map/ppermute | solution.py:31
  5.5 1.9 %shard_map.95 = (f32[8,512]{1,0:T(8,128)S(1)}, bf16[3,1024,512]{2,1,0:T(8,128)(2,1)S(1)}) custom-call(s32[2,16]{1,0:T(2,128)} %covisible.1, bf16[3,1024,512]{2,1,0:T(8,128)(2,1)} %w_qkv.1), custom_call_target="tpu_custom_call" | custom-call | tf_op jit(solution)/shard_map/pallas_call | solution.py:369
  7.4 0.0 collective-permute-done.2.second
  7.5 2.0 %collective-permute-start.6 = (bf16[2,16,512]{2,1,0:T(8,128)(2,1)S(1)}, bf16[2,16,512]{2,1,0:T(8,128)(2,1)S(1)}, u32[]{:S(2)}, u32[]{:S(2)}) collective-permute-start(bf16[2,16,512]{2,1,0:T(8,128)(2,1)S(1)} %shard_map.97.special.first), channel_id=1, source_target_pairs={{4,0},{6,2},{0,4},{2,6},{12,8},{14,10},{8,12},{10,14},{5,1},{7,3},... | collective-permute-start | bytes 98312 | tf_op jit(solution)/shard_map/ppermute | solution.py:31
  9.5 0.0 collective-permute-done.1.other
  9.5 3.4 %shard_map.98 = (bf16[4,128,768]{2,1,0:T(8,128)(2,1)S(1)}, bf16[512,128]{1,0:T(8,128)(2,1)S(1)}, f32[8,768]{1,0:T(8,128)S(1)}, f32[8,768]{1,0:T(8,128)S(1)}, f32...) custom-call(f32[8,512]{1,0:T(8,128)S(1)} %get-tuple-element.34.mask, bf16[384,512]{1,0:T(8,128)(2,1)S(1)} %get-tuple-element.36.own, ...), custom_call_target="tpu_custom_call" | custom-call | tf_op jit(solution)/shard_map/pallas_call | solution.py:369
  12.9 0.3 collective-permute-done
  13.2 1.3 %collective-permute-start.5 = (bf16[192,512]{1,0:T(8,128)(2,1)S(1)}, bf16[192,512]{1,0:T(8,128)(2,1)S(1)}, u32[]{:S(2)}, u32[]{:S(2)}) collective-permute-start(bf16[192,512]{1,0:T(8,128)(2,1)S(1)} %get-tuple-element.66.refs_1_), channel_id=1, source_target_pairs={{1,0},{0,1},{3,2},{2,3},{5,4},{4,5},{7,6},{6,7},{9,8},{8,9},{11,10... | collective-permute-start | bytes 589832 | tf_op jit(solution)/shard_map/ppermute | solution.py:31
  14.5 0.1 collective-permute-start.4
  14.6 1.4 %collective-permute-done.6.second = bf16[2,16,512]{2,1,0:T(8,128)(2,1)S(1)} collective-permute-done((bf16[2,16,512]{2,1,0:T(8,128)(2,1)S(1)}, bf16[2,16,512]{2,1,0:T(8,128)(2,1)S(1)}, u32[]{:S(2)}, u32[]{:S(2)}) %collective-permute-start.6) | collective-permute-done | bytes 32800 | tf_op jit(solution)/shard_map/ppermute | solution.py:31
  16.0 2.5 %collective-permute-start.7 = (bf16[2,32,512]{2,1,0:T(8,128)(2,1)S(1)}, bf16[2,32,512]{2,1,0:T(8,128)(2,1)S(1)}, u32[]{:S(2)}, u32[]{:S(2)}) collective-permute-start(bf16[2,32,512]{2,1,0:T(8,128)(2,1)S(1)} %shard_map.100.first), channel_id=1, source_target_pairs={{8,0},{10,2},{12,4},{14,6},{0,8},{2,10},{4,12},{6,14},{9,1},{11,3}... | collective-permute-start | bytes 196616 | tf_op jit(solution)/shard_map/ppermute | solution.py:31
  18.4 1.6 %collective-permute-start.3 = (bf16[192,512]{1,0:T(8,128)(2,1)S(1)}, bf16[192,512]{1,0:T(8,128)(2,1)S(1)}, u32[]{:S(2)}, u32[]{:S(2)}) collective-permute-start(bf16[192,512]{1,0:T(8,128)(2,1)S(1)} %get-tuple-element.41), channel_id=1, source_target_pairs={{2,0},{0,2},{6,4},{4,6},{10,8},{8,10},{14,12},{12,14},{3,1},{1,3},... | collective-permute-start | bytes 589832 | tf_op jit(solution)/shard_map/ppermute | solution.py:31
  20.0 0.0 collective-permute-done.5.refs_3_
  20.0 3.4 %shard_map.99 = (f32[8,768]{1,0:T(8,128)S(1)}, f32[8,768]{1,0:T(8,128)S(1)}, f32[4,64,768]{2,1,0:T(8,128)S(1)}, f32[512,128]{1,0:T(8,128)S(1)}) custom-call(f32[8,512]{1,0:T(8,128)S(1)} %get-tuple-element.34.mask, bf16[192,512]{1,0:T(8,128)(2,1)S(1)} %get-tuple-element.67.refs_0_, bf16[192,512]{1,0:T(8,128)(2,1)S(1)} %get-tuple-element.66.refs_1_, ...), custom_call_target="tpu_custom_call" | custom-call | tf_op jit(solution)/shard_map/pallas_call | solution.py:369
  23.4 0.0 collective-permute-done.8.refs_0_
  23.4 1.1 %collective-permute-start.9 = (bf16[192,512]{1,0:T(8,128)(2,1)S(1)}, bf16[192,512]{1,0:T(8,128)(2,1)S(1)}, u32[]{:S(2)}, u32[]{:S(2)}) collective-permute-start(bf16[192,512]{1,0:T(8,128)(2,1)S(1)} %collective-permute-done.8.refs_0_), channel_id=1, source_target_pairs={{1,0},{0,1},{3,2},{2,3},{5,4},{4,5},{7,6},{6,7},{9,8},{8,9},{11,10... | collective-permute-start | bytes 589832 | tf_op jit(solution)/shard_map/ppermute | solution.py:31
  24.5 0.0 collective-permute-done.7.second
  24.5 0.1 collective-permute-start.10
  24.6 0.0 collective-permute-done.3.refs_0_
  24.6 1.2 %collective-permute-start.11 = (bf16[192,512]{1,0:T(8,128)(2,1)S(1)}, bf16[192,512]{1,0:T(8,128)(2,1)S(1)}, u32[]{:S(2)}, u32[]{:S(2)}) collective-permute-start(bf16[192,512]{1,0:T(8,128)(2,1)S(1)} %collective-permute-done.3.refs_0_), channel_id=1, source_target_pairs={{1,0},{0,1},{3,2},{2,3},{5,4},{4,5},{7,6},{6,7},{9,8},{8,9},{11,10... | collective-permute-start | bytes 589832 | tf_op jit(solution)/shard_map/ppermute | solution.py:31
  25.8 0.0 collective-permute-done.9.refs_1_
  25.9 2.0 %shard_map.102 = (f32[8,768]{1,0:T(8,128)S(1)}, f32[8,768]{1,0:T(8,128)S(1)}, f32[4,64,768]{2,1,0:T(8,128)S(1)}, f32[512,128]{1,0:T(8,128)S(1)}) custom-call(f32[8,512]{1,0:T(8,128)S(1)} %get-tuple-element.34.mask, bf16[192,512]{1,0:T(8,128)(2,1)S(1)} %collective-permute-done.8.refs_0_, bf16[192,512]{1,0:T(8,128)(2,1)S(1)} %collective-permute-done.9.refs_1_, ...), custom_call_target="tpu_custom_call" | custom-call | tf_op jit(solution)/shard_map/pallas_call | solution.py:369
  27.8 1.8 %collective-permute-done.10.second = bf16[2,64,512]{2,1,0:T(8,128)(2,1)S(1)} collective-permute-done((bf16[2,64,512]{2,1,0:T(8,128)(2,1)S(1)}, bf16[2,64,512]{2,1,0:T(8,128)(2,1)S(1)}, u32[]{:S(2)}, u32[]{:S(2)}) %collective-permute-start.10) | collective-permute-done | bytes 131104 | tf_op jit(solution)/shard_map/ppermute | solution.py:31
  29.7 0.0 collective-permute-done.11.refs_2_
  29.7 4.9 %shard_map.104 = (f32[400,512]{1,0:T(8,128)S(1)}, bf16[400,512]{1,0:T(8,128)(2,1)S(1)}) custom-call(f32[8,512]{1,0:T(8,128)S(1)} %get-tuple-element.34.mask, bf16[192,512]{1,0:T(8,128)(2,1)S(1)} %collective-permute-done.3.refs_0_, bf16[2,128,512]{2,1,0:T(8,128)(2,1)S(1)} %shard_map.103.refs_1_.refs_3_, bf16[192,512]{1,0:T(8,128)(2,1)S(1)} %collective-permute-done.11.refs_2_, ...), custom_call_target="tpu_custom_call" | custom-call | tf_op jit(solution)/shard_map/pallas_call | solution.py:369
  34.6 0.9 %collective-permute-start.12 = (bf16[400,512]{1,0:T(8,128)(2,1)S(1)}, bf16[400,512]{1,0:T(8,128)(2,1)S(1)}, u32[]{:S(2)}, u32[]{:S(2)}) collective-permute-start(bf16[400,512]{1,0:T(8,128)(2,1)S(1)} %get-tuple-element.63), channel_id=1, source_target_pairs={{1,0},{0,1},{3,2},{2,3},{5,4},{4,5},{7,6},{6,7},{9,8},{8,9},{11,10... | collective-permute-start | bytes 1228808 | tf_op jit(solution)/shard_map/ppermute | solution.py:31
  35.5 1.4 %collective-permute-done.12.received = bf16[400,512]{1,0:T(8,128)(2,1)S(1)} collective-permute-done((bf16[400,512]{1,0:T(8,128)(2,1)S(1)}, bf16[400,512]{1,0:T(8,128)(2,1)S(1)}, u32[]{:S(2)}, u32[]{:S(2)}) %collective-permute-start.12) | collective-permute-done | bytes 409632 | tf_op jit(solution)/shard_map/ppermute | solution.py:31
  36.8 0.8 %shard_map.105 = (bf16[384,512]{1,0:T(8,128)(2,1)}, bf16[5,2,512]{2,1,0:T(2,128)(2,1)}) custom-call(f32[400,512]{1,0:T(8,128)S(1)} %get-tuple-element.62.kept, bf16[400,512]{1,0:T(8,128)(2,1)S(1)} %collective-permute-done.12.received), custom_call_target="tpu_custom_call" | custom-call | tf_op jit(solution)/shard_map/pallas_call | solution.py:369
  (6 shorter events, 0.1 us)
Async XLA Ops:
  0.6 8.8 %collective-permute-start.1 = (bf16[384,512]{1,0:T(8,128)(2,1)}, bf16[384,512]{1,0:T(8,128)(2,1)S(1)}, u32[]{:S(2)}, u32[]{:S(2)}) collective-permute-start(bf16[384,512]{1,0:T(8,128)(2,1)} %bitcast.4), channel_id=1, source_target_pairs={{1,0},{0,1},{3,2},{2,3},{5,4},{4,5},{7,6},{6,7},{9,8},{8,9},{11,10... | collective-permute-start | bytes 1179656 | tf_op jit(solution)/shard_map/ppermute | solution.py:31
  1.4 11.8 %collective-permute-start = (bf16[384,512]{1,0:T(8,128)(2,1)}, bf16[384,512]{1,0:T(8,128)(2,1)S(1)}, u32[]{:S(2)}, u32[]{:S(2)}) collective-permute-start(bf16[384,512]{1,0:T(8,128)(2,1)} %bitcast.5), channel_id=1, source_target_pairs={{0,14},{2,4},{4,2},{6,8},{8,6},{10,12},{12,10},{14,0},{1,15},{3,5}... | collective-permute-start | bytes 1179656 | tf_op jit(solution)/shard_map/ppermute | solution.py:36
  3.7 3.7 %collective-permute-start.2 = (bf16[16,512]{1,0:T(8,128)(2,1)S(1)}, bf16[16,512]{1,0:T(8,128)(2,1)S(1)}, u32[]{:S(2)}, u32[]{:S(2)}) collective-permute-start(bf16[16,512]{1,0:T(8,128)(2,1)S(1)} %get-tuple-element.37.first), channel_id=1, source_target_pairs={{1,0},{0,1},{3,2},{2,3},{5,4},{4,5},{7,6},{6,7},{9,8},{8,9},{11,10... | collective-permute-start | bytes 49160 | tf_op jit(solution)/shard_map/ppermute | solution.py:31
  4.2 19.3 %collective-permute-start.8 = (bf16[192,512]{1,0:T(8,128)(2,1)S(1)}, bf16[192,512]{1,0:T(8,128)(2,1)S(1)}, u32[]{:S(2)}, u32[]{:S(2)}) collective-permute-start(bf16[192,512]{1,0:T(8,128)(2,1)S(1)} %get-tuple-element.52), channel_id=1, source_target_pairs={{2,0},{0,2},{6,4},{4,6},{10,8},{8,10},{14,12},{12,14},{3,1},{1,3},... | collective-permute-start | bytes 589832 | tf_op jit(solution)/shard_map/ppermute | solution.py:31
  7.5 8.5 %collective-permute-start.6 = (bf16[2,16,512]{2,1,0:T(8,128)(2,1)S(1)}, bf16[2,16,512]{2,1,0:T(8,128)(2,1)S(1)}, u32[]{:S(2)}, u32[]{:S(2)}) collective-permute-start(bf16[2,16,512]{2,1,0:T(8,128)(2,1)S(1)} %shard_map.97.special.first), channel_id=1, source_target_pairs={{4,0},{6,2},{0,4},{2,6},{12,8},{14,10},{8,12},{10,14},{5,1},{7,3},... | collective-permute-start | bytes 98312 | tf_op jit(solution)/shard_map/ppermute | solution.py:31
  13.2 6.7 %collective-permute-start.5 = (bf16[192,512]{1,0:T(8,128)(2,1)S(1)}, bf16[192,512]{1,0:T(8,128)(2,1)S(1)}, u32[]{:S(2)}, u32[]{:S(2)}) collective-permute-start(bf16[192,512]{1,0:T(8,128)(2,1)S(1)} %get-tuple-element.66.refs_1_), channel_id=1, source_target_pairs={{1,0},{0,1},{3,2},{2,3},{5,4},{4,5},{7,6},{6,7},{9,8},{8,9},{11,10... | collective-permute-start | bytes 589832 | tf_op jit(solution)/shard_map/ppermute | solution.py:31
  14.5 5.5 %collective-permute-start.4 = (bf16[192,512]{1,0:T(8,128)(2,1)S(1)}, bf16[192,512]{1,0:T(8,128)(2,1)S(1)}, u32[]{:S(2)}, u32[]{:S(2)}) collective-permute-start(bf16[192,512]{1,0:T(8,128)(2,1)S(1)} %get-tuple-element.67.refs_0_), channel_id=1, source_target_pairs={{1,0},{0,1},{3,2},{2,3},{5,4},{4,5},{7,6},{6,7},{9,8},{8,9},{11,10... | collective-permute-start | bytes 589832 | tf_op jit(solution)/shard_map/ppermute | solution.py:31
  16.0 8.5 %collective-permute-start.7 = (bf16[2,32,512]{2,1,0:T(8,128)(2,1)S(1)}, bf16[2,32,512]{2,1,0:T(8,128)(2,1)S(1)}, u32[]{:S(2)}, u32[]{:S(2)}) collective-permute-start(bf16[2,32,512]{2,1,0:T(8,128)(2,1)S(1)} %shard_map.100.first), channel_id=1, source_target_pairs={{8,0},{10,2},{12,4},{14,6},{0,8},{2,10},{4,12},{6,14},{9,1},{11,3}... | collective-permute-start | bytes 196616 | tf_op jit(solution)/shard_map/ppermute | solution.py:31
  18.4 6.2 %collective-permute-start.3 = (bf16[192,512]{1,0:T(8,128)(2,1)S(1)}, bf16[192,512]{1,0:T(8,128)(2,1)S(1)}, u32[]{:S(2)}, u32[]{:S(2)}) collective-permute-start(bf16[192,512]{1,0:T(8,128)(2,1)S(1)} %get-tuple-element.41), channel_id=1, source_target_pairs={{2,0},{0,2},{6,4},{4,6},{10,8},{8,10},{14,12},{12,14},{3,1},{1,3},... | collective-permute-start | bytes 589832 | tf_op jit(solution)/shard_map/ppermute | solution.py:31
  23.4 2.4 %collective-permute-start.9 = (bf16[192,512]{1,0:T(8,128)(2,1)S(1)}, bf16[192,512]{1,0:T(8,128)(2,1)S(1)}, u32[]{:S(2)}, u32[]{:S(2)}) collective-permute-start(bf16[192,512]{1,0:T(8,128)(2,1)S(1)} %collective-permute-done.8.refs_0_), channel_id=1, source_target_pairs={{1,0},{0,1},{3,2},{2,3},{5,4},{4,5},{7,6},{6,7},{9,8},{8,9},{11,10... | collective-permute-start | bytes 589832 | tf_op jit(solution)/shard_map/ppermute | solution.py:31
  24.5 5.2 %collective-permute-start.10 = (bf16[2,64,512]{2,1,0:T(8,128)(2,1)S(1)}, bf16[2,64,512]{2,1,0:T(8,128)(2,1)S(1)}, u32[]{:S(2)}, u32[]{:S(2)}) collective-permute-start(bf16[2,64,512]{2,1,0:T(8,128)(2,1)S(1)} %shard_map.101.first), channel_id=1, source_target_pairs={{2,0},{0,2},{6,4},{4,6},{10,8},{8,10},{14,12},{12,14},{3,1},{1,3},... | collective-permute-start | bytes 393224 | tf_op jit(solution)/shard_map/ppermute | solution.py:31
  24.6 5.1 %collective-permute-start.11 = (bf16[192,512]{1,0:T(8,128)(2,1)S(1)}, bf16[192,512]{1,0:T(8,128)(2,1)S(1)}, u32[]{:S(2)}, u32[]{:S(2)}) collective-permute-start(bf16[192,512]{1,0:T(8,128)(2,1)S(1)} %collective-permute-done.3.refs_0_), channel_id=1, source_target_pairs={{1,0},{0,1},{3,2},{2,3},{5,4},{4,5},{7,6},{6,7},{9,8},{8,9},{11,10... | collective-permute-start | bytes 589832 | tf_op jit(solution)/shard_map/ppermute | solution.py:31
  34.6 2.2 %collective-permute-start.12 = (bf16[400,512]{1,0:T(8,128)(2,1)S(1)}, bf16[400,512]{1,0:T(8,128)(2,1)S(1)}, u32[]{:S(2)}, u32[]{:S(2)}) collective-permute-start(bf16[400,512]{1,0:T(8,128)(2,1)S(1)} %get-tuple-element.63), channel_id=1, source_target_pairs={{1,0},{0,1},{3,2},{2,3},{5,4},{4,5},{7,6},{6,7},{9,8},{8,9},{11,10... | collective-permute-start | bytes 1228808 | tf_op jit(solution)/shard_map/ppermute | solution.py:31

commit v12 on v11

--- a/solution.py
+++ b/solution.py
@@ -13,7 +13,6 @@
 TILE_ROWS = 16
 LOG2_E = 1.4426950408889634
 FIRST = 20_000_000_000
-LAST = FIRST
 VMEM_BYTES = 32 * 1024 * 1024
 SMEM = pl.BlockSpec(memory_space=pltpu.SMEM)
 VMEM = pl.BlockSpec(memory_space=pltpu.VMEM)
@@ -57,14 +56,11 @@
 
 def rows_kernel(
     frame_order, specials, role_first, role_rest, patches,
-    special_out, patches_out, early_out, late_out, order, here, first_rows, rest_rows, copied,
+    special_out, patches_out, order, here, first_rows, rest_rows, copied,
 ):
-    cut = early_out.shape[0]
     special_count, images, width = specials.shape
     moves = [(specials, here), (role_first, first_rows), (role_rest, rest_rows), (frame_order, order)]
-    moves.append((patches.at[pl.ds(0, cut)], early_out))
     moves.append((patches, patches_out))
-    moves.append((patches.at[pl.ds(cut, late_out.shape[0])], late_out))
     copies = [
         pltpu.make_async_copy(source, target, copied.at[i]) for i, (source, target) in enumerate(moves)
     ]
@@ -90,7 +86,10 @@
     images = covisible.shape[0]
     patch_total = images * per_image
     moves = [(covisible, seen)]
-    moves += [(w_qkv.at[i], weights_out.at[i]) for i in range(3)]
+    depth = w_qkv.shape[1] // 2
+    for i in range(3):
+        for j, rows in enumerate(halves(depth)):
+            moves.append((w_qkv.at[i, rows], weights_out.at[i, pl.ds(j * depth, depth)]))
     copies = [
         pltpu.make_async_copy(source, target, copied.at[i]) for i, (source, target) in enumerate(moves)
     ]
@@ -114,11 +113,10 @@
 
 
 def projector(own, other, weights):
-    mine, theirs = halves(own.shape[1])
+    rows = jnp.concatenate([own, other], axis=1)
 
     def columns(which, quad):
-        lanes = slice(quad * QUAD, (quad + 1) * QUAD)
-        return product(own, weights[which, mine, lanes]) + product(other, weights[which, theirs, lanes])
+        return product(rows, weights[which, :, quad * QUAD : (quad + 1) * QUAD])
 
     return columns
 
@@ -151,7 +149,7 @@
 
     def values_of(quad):
         if quad not in values:
-            values[quad] = jnp.transpose(columns(2, quad)).astype(jnp.bfloat16)
+            values[quad] = jnp.transpose(columns(2, quad).astype(jnp.bfloat16))
         return values[quad]
 
     def prepared(pair):
@@ -258,7 +256,7 @@
         if quad not in made:
             queries = columns(0, quad) * (HEAD_DIM ** (-0.5) * LOG2_E)
             made[quad] = queries[patch_total:]
-            turned = jnp.transpose(queries[:patch_total]).astype(jnp.bfloat16)
+            turned = jnp.transpose(queries[:patch_total].astype(jnp.bfloat16))
             for i in range(2):
                 first = i * PAIR
                 upper = jnp.concatenate([turned[first : first + HEAD_DIM], zero], axis=1)
@@ -276,7 +274,7 @@
         block = jnp.concatenate([block] * (2 * pairs), axis=0)
         row = lax.broadcasted_iota(jnp.int32, block.shape, 0) // count
         lane = lax.broadcasted_iota(jnp.int32, block.shape, 1) // HEAD_DIM
-        block = jnp.transpose(jnp.where(row == lane, block, 0.0)).astype(jnp.bfloat16)
+        block = jnp.transpose(jnp.where(row == lane, block, 0.0).astype(jnp.bfloat16))
         special_out[...] = block
         return block
 
@@ -339,7 +337,7 @@
             continue
         columns.append(share)
         if pair % 2 == 1 and sub == 1:
-            quad = jnp.transpose(jnp.concatenate(columns, axis=0)).astype(jnp.bfloat16)
+            quad = jnp.transpose(jnp.concatenate(columns, axis=0).astype(jnp.bfloat16))
             features = slice((pair // 2) * QUAD, (pair // 2 + 1) * QUAD)
             added = [product(quad, w_here[features, side]) for side in sides]
             out = added if out is None else [before + more for before, more in zip(out, added)]
@@ -408,7 +406,6 @@
     reach = max(1, owner_count // 64)
     patch_total = images * per_image
     rows = patch_total + special_block
-    cut = per_image * max(1, images // 2)
     heads = width // HEAD_DIM
     pairs = heads // 2
     paired = reach == 1 and owner_count % 2 == 0
@@ -431,13 +428,11 @@
     patches = patch_rows.reshape(patch_total, width)
     turned = jnp.transpose(special_rows, (1, 0, 2))
     power = owner_count >= 8 and owner_count & (owner_count - 1) == 0
-    specials, own, *pieces = call(
+    specials, own = call(
         rows_kernel,
         [
             bf16(special_block, width),
             bf16(patch_total, width),
-            bf16(cut, width),
-            bf16(patch_total - cut, width),
         ],
         (frame_order, turned, role_first, role_rest, patches),
         in_specs=[HBM] * 5,
@@ -446,7 +441,7 @@
             pltpu.VMEM(turned.shape, jnp.bfloat16),
             pltpu.VMEM(role_first.shape, jnp.bfloat16),
             pltpu.VMEM(role_rest.shape, jnp.bfloat16),
-            pltpu.SemaphoreType.DMA((7,)),
+            pltpu.SemaphoreType.DMA((5,)),
         ],
     )
     bits = [1 << i for i in range(1, owner_count.bit_length() - 1)] + [1] if power else []
@@ -462,7 +457,7 @@
         ],
         (covisible, w_qkv),
         in_specs=[HBM] * 2,
-        scratch=[pltpu.SMEM(covisible.shape, jnp.int32), pltpu.SemaphoreType.DMA((1 + 3,))],
+        scratch=[pltpu.SMEM(covisible.shape, jnp.int32), pltpu.SemaphoreType.DMA((1 + 6,))],
     )
     queries, special_queries, *state = call(
         functools.partial(first_kernel, images),
@@ -484,35 +479,28 @@
         starts = range(0, part.shape[0], per_image)
         return [both(part[start : start + per_image]) for start in starts]
 
-    stretches = lambda owner, first, last: [[image] for image in image_rows(owner)[first:last]]
+    stretches = lambda owner: [[image] for image in image_rows(owner)]
     if paired:
         far = after(crossed(patches, "blk"), state[0])
-        near = [swapped(pieces[0], "blk", 1), swapped(after(pieces[1], far), "blk", 1)]
+        near = swapped(patches, "blk", 1)
         if power:
             everywhere = after(everywhere, far)
             for bit in bits[1:-2]:
                 everywhere = stacked(everywhere, swapped(everywhere, "blk", bit))
             arrived = swapped(everywhere, "blk", bits[-2])
-        state = later(stretches(1, 0, images), halved(far, state[0]), state)
+        state = later(stretches(1), halved(far, state[0]), state)
         if power:
             everywhere = stacked(after(everywhere, state[0]), arrived, FIRST)
             arrived = swapped(everywhere, "blk", bits[-1])
-        near = [halved(part, state[0]) for part in near]
-        count = len(near[0])
-        state = later(stretches(2, 0, count), near[0], state)
+        state = later(stretches(2), halved(near, state[0]), state)
         if power:
-            everywhere = stacked(after(everywhere, state[0]), arrived, LAST)
-        last_stretches, parts = stretches(2, count, images), near[1]
+            everywhere = stacked(after(everywhere, state[0]), arrived)
     else:
         for i, offset in enumerate(offsets[1:]):
-            parts = halved(shifted(patches, "blk", -offset), state[0])
-            last_stretches = stretches(i + 1, 0, images)
-            if i < len(offsets) - 2:
-                state = later(last_stretches, parts, state)
+            state = later(stretches(i + 1), halved(shifted(patches, "blk", -offset), state[0]), state)
     if not (paired and power):
         everywhere = lax.all_gather(specials, "blk", axis=1, tiled=True)
-    stretches = last_stretches + [[(everywhere.shape[1], None)]]
-    parts = parts + [(everywhere, everywhere)]
+    stretches, parts = [[(everywhere.shape[1], None)]], [(everywhere, everywhere)]
     kept, sent = call(
         functools.partial(last_kernel, stretches, real_rows),
         [f32(rows, width), bf16(rows, width)],

time: 37.9 us -> 37.6 us (level)
  the two profiles are of different devices: /device:TPU:9 before, /device:TPU:0 now
where the time goes in v12:
time: 37.6 us; the launch traced here: 37.3 us
  Pallas kernels  17.5 us (47%)
  waiting for transfers between devices  9.76 us (26%)
  starting transfers between devices  9.33 us (25%)
  between operations  0.74 us (2%)
    pallas_call x11, Pallas kernels, call(): pl.pallas_call(kernel, out_shape=out_shape, in_specs=in_specs or [VMEM] *...  17.5 us
    ppermute x11, waiting for transfers between devices, swapped(): return lax.ppermute(block, axis, [(i ^ bit, i) for i in range(count)])  6.38 us
    ppermute x1, starting transfers between devices, crossed(): lax.ppermute(block, axis, [(i, (i + (-1 if i % 2 == 0 else 1)) % count) f...  5.6 us
    ppermute x11, starting transfers between devices, swapped(): return lax.ppermute(block, axis, [(i ^ bit, i) for i in range(count)])  3.72 us
    ppermute x1, waiting for transfers between devices, crossed(): lax.ppermute(block, axis, [(i, (i + (-1 if i % 2 == 0 else 1)) % count) f...  3.39 us
  transfers between devices with their start and end apart: 12, of which 6 were waited for; matrix products, arithmetic and copies ran while one was open for 0% of the time, Pallas kernels for 35%

profile of v12, /device:TPU:0, one launch (start us, length us, event | category | flops | bytes accessed | tf_op | source)
XLA Modules:
  0.0 37.3 jit_solution(4463002807317338679)
XLA Ops:
  0.6 0.5 %collective-permute-start.3 = (bf16[384,512]{1,0:T(8,128)(2,1)}, bf16[384,512]{1,0:T(8,128)(2,1)S(1)}, u32[]{:S(2)}, u32[]{:S(2)}) collective-permute-start(bf16[384,512]{1,0:T(8,128)(2,1)} %bitcast.4), channel_id=1, source_target_pairs={{1,0},{0,1},{3,2},{2,3},{5,4},{4,5},{7,6},{6,7},{9,8},{8,9},{11,10... | collective-permute-start | bytes 1179656 | tf_op jit(solution)/shard_map/ppermute | solution.py:30
  1.1 5.6 %collective-permute-start.2 = (bf16[384,512]{1,0:T(8,128)(2,1)}, bf16[384,512]{1,0:T(8,128)(2,1)S(1)}, u32[]{:S(2)}, u32[]{:S(2)}) collective-permute-start(bf16[384,512]{1,0:T(8,128)(2,1)} %bitcast.5), channel_id=1, source_target_pairs={{0,14},{2,4},{4,2},{6,8},{8,6},{10,12},{12,10},{14,0},{1,15},{3,5}... | collective-permute-start | bytes 1179656 | tf_op jit(solution)/shard_map/ppermute | solution.py:35
  6.8 1.1 %shard_map.96 = (bf16[16,512]{1,0:T(8,128)(2,1)S(1)}, bf16[384,512]{1,0:T(8,128)(2,1)S(1)}) custom-call(s32[2]{0:T(128)} %frame_order.1, bf16[5,2,512]{2,1,0:T(2,128)(2,1)} %bitcast.8, bf16[5,1024]{1,0:T(8,128)(2,1)} %role_first.1, bf16[5,1024]{1,0:T(8,128)(2,1)} %role_rest.1, bf16[384,512]{1,0:T(8,128)(2,1)} %bitcast.6), custom_call_target="tpu_custom_call" | custom-call | tf_op jit(solution)/shard_map/pallas_call | solution.py:367
  7.9 0.2 collective-permute-start
  8.1 0.0 collective-permute-start.7
  8.1 1.9 %shard_map.95 = (f32[8,512]{1,0:T(8,128)S(1)}, bf16[3,1024,512]{2,1,0:T(8,128)(2,1)S(1)}) custom-call(s32[2,16]{1,0:T(2,128)} %covisible.1, bf16[3,1024,512]{2,1,0:T(8,128)(2,1)} %w_qkv.1), custom_call_target="tpu_custom_call" | custom-call | tf_op jit(solution)/shard_map/pallas_call | solution.py:367
  10.0 0.0 collective-permute-done.second
  10.0 0.1 collective-permute-start.1
  10.2 0.0 collective-permute-done.3.other
  10.2 3.4 %shard_map.99 = (bf16[4,128,768]{2,1,0:T(8,128)(2,1)S(1)}, bf16[512,128]{1,0:T(8,128)(2,1)S(1)}, f32[8,768]{1,0:T(8,128)S(1)}, f32[8,768]{1,0:T(8,128)S(1)}, f32...) custom-call(f32[8,512]{1,0:T(8,128)S(1)} %get-tuple-element.30.mask, bf16[384,512]{1,0:T(8,128)(2,1)S(1)} %get-tuple-element.32.own, ...), custom_call_target="tpu_custom_call" | custom-call | tf_op jit(solution)/shard_map/pallas_call | solution.py:367
  13.6 3.4 %collective-permute-done.2 = bf16[384,512]{1,0:T(8,128)(2,1)S(1)} collective-permute-done((bf16[384,512]{1,0:T(8,128)(2,1)}, bf16[384,512]{1,0:T(8,128)(2,1)S(1)}, u32[]{:S(2)}, u32[]{:S(2)}) %collective-permute-start.2) | collective-permute-done | bytes 393248 | tf_op jit(solution)/shard_map/ppermute | solution.py:35
  17.0 0.1 collective-permute-start.4
  17.0 0.5 %collective-permute-start.5 = (bf16[192,512]{1,0:T(8,128)(2,1)S(1)}, bf16[192,512]{1,0:T(8,128)(2,1)S(1)}, u32[]{:S(2)}, u32[]{:S(2)}) collective-permute-start(bf16[192,512]{1,0:T(8,128)(2,1)S(1)} %get-tuple-element.60.refs_1_), channel_id=1, source_target_pairs={{1,0},{0,1},{3,2},{2,3},{5,4},{4,5},{7,6},{6,7},{9,8},{8,9},{11,10... | collective-permute-start | bytes 589832 | tf_op jit(solution)/shard_map/ppermute | solution.py:30
  17.5 0.0 collective-permute-done.1.second
  17.6 1.5 %collective-permute-start.6 = (bf16[2,32,512]{2,1,0:T(8,128)(2,1)S(1)}, bf16[2,32,512]{2,1,0:T(8,128)(2,1)S(1)}, u32[]{:S(2)}, u32[]{:S(2)}) collective-permute-start(bf16[2,32,512]{2,1,0:T(8,128)(2,1)S(1)} %shard_map.98.first), channel_id=1, source_target_pairs={{8,0},{10,2},{12,4},{14,6},{0,8},{2,10},{4,12},{6,14},{9,1},{11,3}... | collective-permute-start | bytes 196616 | tf_op jit(solution)/shard_map/ppermute | solution.py:30
  19.1 0.0 collective-permute-done.4.refs_2_
  19.1 0.0 collective-permute-done.5.refs_3_
  19.1 3.4 %shard_map.100 = (f32[8,768]{1,0:T(8,128)S(1)}, f32[8,768]{1,0:T(8,128)S(1)}, f32[4,64,768]{2,1,0:T(8,128)S(1)}, f32[512,128]{1,0:T(8,128)S(1)}) custom-call(f32[8,512]{1,0:T(8,128)S(1)} %get-tuple-element.30.mask, bf16[192,512]{1,0:T(8,128)(2,1)S(1)} %get-tuple-element.61.refs_0_, bf16[192,512]{1,0:T(8,128)(2,1)S(1)} %get-tuple-element.60.refs_1_, ...), custom_call_target="tpu_custom_call" | custom-call | tf_op jit(solution)/shard_map/pallas_call | solution.py:367
  22.5 2.6 %collective-permute-done.7 = bf16[384,512]{1,0:T(8,128)(2,1)S(1)} collective-permute-done((bf16[384,512]{1,0:T(8,128)(2,1)}, bf16[384,512]{1,0:T(8,128)(2,1)S(1)}, u32[]{:S(2)}, u32[]{:S(2)}) %collective-permute-start.7) | collective-permute-done | bytes 393248 | tf_op jit(solution)/shard_map/ppermute | solution.py:30
  25.1 0.1 collective-permute-start.8
  25.2 0.5 %collective-permute-start.9 = (bf16[192,512]{1,0:T(8,128)(2,1)S(1)}, bf16[192,512]{1,0:T(8,128)(2,1)S(1)}, u32[]{:S(2)}, u32[]{:S(2)}) collective-permute-start(bf16[192,512]{1,0:T(8,128)(2,1)S(1)} %get-tuple-element.58.refs_1_), channel_id=1, source_target_pairs={{1,0},{0,1},{3,2},{2,3},{5,4},{4,5},{7,6},{6,7},{9,8},{8,9},{11,10... | collective-permute-start | bytes 589832 | tf_op jit(solution)/shard_map/ppermute | solution.py:30
  25.7 0.0 collective-permute-done.6.second
  25.7 0.1 collective-permute-start.10
  25.8 0.8 %collective-permute-done.8.refs_2_ = bf16[192,512]{1,0:T(8,128)(2,1)S(1)} collective-permute-done((bf16[192,512]{1,0:T(8,128)(2,1)S(1)}, bf16[192,512]{1,0:T(8,128)(2,1)S(1)}, u32[]{:S(2)}, u32[]{:S(2)}) %collective-permute-start.8) | collective-permute-done | bytes 196640 | tf_op jit(solution)/shard_map/ppermute | solution.py:30
  26.6 0.3 collective-permute-done.9.refs_3_
  26.9 3.4 %shard_map.102 = (f32[8,768]{1,0:T(8,128)S(1)}, f32[8,768]{1,0:T(8,128)S(1)}, f32[4,64,768]{2,1,0:T(8,128)S(1)}, f32[512,128]{1,0:T(8,128)S(1)}) custom-call(f32[8,512]{1,0:T(8,128)S(1)} %get-tuple-element.30.mask, bf16[192,512]{1,0:T(8,128)(2,1)S(1)} %get-tuple-element.59.refs_0_, bf16[192,512]{1,0:T(8,128)(2,1)S(1)} %get-tuple-element.58.refs_1_, ...), custom_call_target="tpu_custom_call" | custom-call | tf_op jit(solution)/shard_map/pallas_call | solution.py:367
  30.3 0.9 %collective-permute-done.10.second = bf16[2,64,512]{2,1,0:T(8,128)(2,1)S(1)} collective-permute-done((bf16[2,64,512]{2,1,0:T(8,128)(2,1)S(1)}, bf16[2,64,512]{2,1,0:T(8,128)(2,1)S(1)}, u32[]{:S(2)}, u32[]{:S(2)}) %collective-permute-start.10) | collective-permute-done | bytes 131104 | tf_op jit(solution)/shard_map/ppermute | solution.py:30
  31.3 3.4 %shard_map.104 = (f32[400,512]{1,0:T(8,128)S(1)}, bf16[400,512]{1,0:T(8,128)(2,1)S(1)}) custom-call(f32[8,512]{1,0:T(8,128)S(1)} %get-tuple-element.30.mask, bf16[2,128,512]{2,1,0:T(8,128)(2,1)S(1)} %shard_map.103.refs_0_.refs_1_, bf16[2,128,512]{2,1,0:T(8,128)(2,1)S(1)} %shard_map.103.refs_0_.refs_1_, ...), custom_call_target="tpu_custom_call" | custom-call | tf_op jit(solution)/shard_map/pallas_call | solution.py:367
  34.7 0.1 collective-permute-start.11
  34.8 1.7 %collective-permute-done.11.received = bf16[400,512]{1,0:T(8,128)(2,1)S(1)} collective-permute-done((bf16[400,512]{1,0:T(8,128)(2,1)S(1)}, bf16[400,512]{1,0:T(8,128)(2,1)S(1)}, u32[]{:S(2)}, u32[]{:S(2)}) %collective-permute-start.11) | collective-permute-done | bytes 409632 | tf_op jit(solution)/shard_map/ppermute | solution.py:30
  36.5 0.8 %shard_map.105 = (bf16[384,512]{1,0:T(8,128)(2,1)}, bf16[5,2,512]{2,1,0:T(2,128)(2,1)}) custom-call(f32[400,512]{1,0:T(8,128)S(1)} %get-tuple-element.54.kept, bf16[400,512]{1,0:T(8,128)(2,1)S(1)} %collective-permute-done.11.received), custom_call_target="tpu_custom_call" | custom-call | tf_op jit(solution)/shard_map/pallas_call | solution.py:367
  (6 shorter events, 0.1 us)
Async XLA Ops:
  0.6 9.6 %collective-permute-start.3 = (bf16[384,512]{1,0:T(8,128)(2,1)}, bf16[384,512]{1,0:T(8,128)(2,1)S(1)}, u32[]{:S(2)}, u32[]{:S(2)}) collective-permute-start(bf16[384,512]{1,0:T(8,128)(2,1)} %bitcast.4), channel_id=1, source_target_pairs={{1,0},{0,1},{3,2},{2,3},{5,4},{4,5},{7,6},{6,7},{9,8},{8,9},{11,10... | collective-permute-start | bytes 1179656 | tf_op jit(solution)/shard_map/ppermute | solution.py:30
  1.1 15.8 %collective-permute-start.2 = (bf16[384,512]{1,0:T(8,128)(2,1)}, bf16[384,512]{1,0:T(8,128)(2,1)S(1)}, u32[]{:S(2)}, u32[]{:S(2)}) collective-permute-start(bf16[384,512]{1,0:T(8,128)(2,1)} %bitcast.5), channel_id=1, source_target_pairs={{0,14},{2,4},{4,2},{6,8},{8,6},{10,12},{12,10},{14,0},{1,15},{3,5}... | collective-permute-start | bytes 1179656 | tf_op jit(solution)/shard_map/ppermute | solution.py:35
  7.9 2.1 %collective-permute-start = (bf16[16,512]{1,0:T(8,128)(2,1)S(1)}, bf16[16,512]{1,0:T(8,128)(2,1)S(1)}, u32[]{:S(2)}, u32[]{:S(2)}) collective-permute-start(bf16[16,512]{1,0:T(8,128)(2,1)S(1)} %get-tuple-element.31.first), channel_id=1, source_target_pairs={{1,0},{0,1},{3,2},{2,3},{5,4},{4,5},{7,6},{6,7},{9,8},{8,9},{11,10... | collective-permute-start | bytes 49160 | tf_op jit(solution)/shard_map/ppermute | solution.py:30
  8.1 17.0 %collective-permute-start.7 = (bf16[384,512]{1,0:T(8,128)(2,1)}, bf16[384,512]{1,0:T(8,128)(2,1)S(1)}, u32[]{:S(2)}, u32[]{:S(2)}) collective-permute-start(bf16[384,512]{1,0:T(8,128)(2,1)} %bitcast.7), channel_id=1, source_target_pairs={{2,0},{0,2},{6,4},{4,6},{10,8},{8,10},{14,12},{12,14},{3,1},{1,3},... | collective-permute-start | bytes 1179656 | tf_op jit(solution)/shard_map/ppermute | solution.py:30
  10.0 7.5 %collective-permute-start.1 = (bf16[2,16,512]{2,1,0:T(8,128)(2,1)S(1)}, bf16[2,16,512]{2,1,0:T(8,128)(2,1)S(1)}, u32[]{:S(2)}, u32[]{:S(2)}) collective-permute-start(bf16[2,16,512]{2,1,0:T(8,128)(2,1)S(1)} %shard_map.97.first.special), channel_id=1, source_target_pairs={{4,0},{6,2},{0,4},{2,6},{12,8},{14,10},{8,12},{10,14},{5,1},{7,3},... | collective-permute-start | bytes 98312 | tf_op jit(solution)/shard_map/ppermute | solution.py:30
  17.0 2.1 %collective-permute-start.4 = (bf16[192,512]{1,0:T(8,128)(2,1)S(1)}, bf16[192,512]{1,0:T(8,128)(2,1)S(1)}, u32[]{:S(2)}, u32[]{:S(2)}) collective-permute-start(bf16[192,512]{1,0:T(8,128)(2,1)S(1)} %get-tuple-element.61.refs_0_), channel_id=1, source_target_pairs={{1,0},{0,1},{3,2},{2,3},{5,4},{4,5},{7,6},{6,7},{9,8},{8,9},{11,10... | collective-permute-start | bytes 589832 | tf_op jit(solution)/shard_map/ppermute | solution.py:30
  17.0 2.1 %collective-permute-start.5 = (bf16[192,512]{1,0:T(8,128)(2,1)S(1)}, bf16[192,512]{1,0:T(8,128)(2,1)S(1)}, u32[]{:S(2)}, u32[]{:S(2)}) collective-permute-start(bf16[192,512]{1,0:T(8,128)(2,1)S(1)} %get-tuple-element.60.refs_1_), channel_id=1, source_target_pairs={{1,0},{0,1},{3,2},{2,3},{5,4},{4,5},{7,6},{6,7},{9,8},{8,9},{11,10... | collective-permute-start | bytes 589832 | tf_op jit(solution)/shard_map/ppermute | solution.py:30
  17.6 8.1 %collective-permute-start.6 = (bf16[2,32,512]{2,1,0:T(8,128)(2,1)S(1)}, bf16[2,32,512]{2,1,0:T(8,128)(2,1)S(1)}, u32[]{:S(2)}, u32[]{:S(2)}) collective-permute-start(bf16[2,32,512]{2,1,0:T(8,128)(2,1)S(1)} %shard_map.98.first), channel_id=1, source_target_pairs={{8,0},{10,2},{12,4},{14,6},{0,8},{2,10},{4,12},{6,14},{9,1},{11,3}... | collective-permute-start | bytes 196616 | tf_op jit(solution)/shard_map/ppermute | solution.py:30
  25.1 1.5 %collective-permute-start.8 = (bf16[192,512]{1,0:T(8,128)(2,1)S(1)}, bf16[192,512]{1,0:T(8,128)(2,1)S(1)}, u32[]{:S(2)}, u32[]{:S(2)}) collective-permute-start(bf16[192,512]{1,0:T(8,128)(2,1)S(1)} %get-tuple-element.59.refs_0_), channel_id=1, source_target_pairs={{1,0},{0,1},{3,2},{2,3},{5,4},{4,5},{7,6},{6,7},{9,8},{8,9},{11,10... | collective-permute-start | bytes 589832 | tf_op jit(solution)/shard_map/ppermute | solution.py:30
  25.2 1.7 %collective-permute-start.9 = (bf16[192,512]{1,0:T(8,128)(2,1)S(1)}, bf16[192,512]{1,0:T(8,128)(2,1)S(1)}, u32[]{:S(2)}, u32[]{:S(2)}) collective-permute-start(bf16[192,512]{1,0:T(8,128)(2,1)S(1)} %get-tuple-element.58.refs_1_), channel_id=1, source_target_pairs={{1,0},{0,1},{3,2},{2,3},{5,4},{4,5},{7,6},{6,7},{9,8},{8,9},{11,10... | collective-permute-start | bytes 589832 | tf_op jit(solution)/shard_map/ppermute | solution.py:30
  25.7 5.5 %collective-permute-start.10 = (bf16[2,64,512]{2,1,0:T(8,128)(2,1)S(1)}, bf16[2,64,512]{2,1,0:T(8,128)(2,1)S(1)}, u32[]{:S(2)}, u32[]{:S(2)}) collective-permute-start(bf16[2,64,512]{2,1,0:T(8,128)(2,1)S(1)} %shard_map.101.first), channel_id=1, source_target_pairs={{2,0},{0,2},{6,4},{4,6},{10,8},{8,10},{14,12},{12,14},{3,1},{1,3},... | collective-permute-start | bytes 393224 | tf_op jit(solution)/shard_map/ppermute | solution.py:30
  34.7 1.8 %collective-permute-start.11 = (bf16[400,512]{1,0:T(8,128)(2,1)S(1)}, bf16[400,512]{1,0:T(8,128)(2,1)S(1)}, u32[]{:S(2)}, u32[]{:S(2)}) collective-permute-start(bf16[400,512]{1,0:T(8,128)(2,1)S(1)} %get-tuple-element.55), channel_id=1, source_target_pairs={{1,0},{0,1},{3,2},{2,3},{5,4},{4,5},{7,6},{6,7},{9,8},{8,9},{11,10... | collective-permute-start | bytes 1228808 | tf_op jit(solution)/shard_map/ppermute | solution.py:30

commit v13 on v12

--- a/solution.py
+++ b/solution.py
@@ -56,11 +56,14 @@
 
 def rows_kernel(
     frame_order, specials, role_first, role_rest, patches,
-    special_out, patches_out, order, here, first_rows, rest_rows, copied,
+    special_out, patches_out, early_out, late_out, order, here, first_rows, rest_rows, copied,
 ):
+    cut = early_out.shape[0]
     special_count, images, width = specials.shape
     moves = [(specials, here), (role_first, first_rows), (role_rest, rest_rows), (frame_order, order)]
+    moves.append((patches.at[pl.ds(0, cut)], early_out))
     moves.append((patches, patches_out))
+    moves.append((patches.at[pl.ds(cut, late_out.shape[0])], late_out))
     copies = [
         pltpu.make_async_copy(source, target, copied.at[i]) for i, (source, target) in enumerate(moves)
     ]
@@ -237,12 +240,12 @@
 
 
 def first_kernel(
-    images, mask, own, other, special, weights, queries_out, special_out, *state_out
+    images, special_block, mask, own, other, special, weights, queries_out, special_out, *state_out
 ):
     patch_total = own.shape[0]
     columns = projector(
-        jnp.concatenate([own[...], special[0]], axis=0),
-        jnp.concatenate([other[...], special[1]], axis=0),
+        jnp.concatenate([own[...], special[0, :special_block, :]], axis=0),
+        jnp.concatenate([other[...], special[1, :special_block, :]], axis=0),
         weights,
     )
     pairs = queries_out.shape[0]
@@ -381,13 +384,13 @@
 
 
 def stack_kernel(first, second, out):
-    count = first.shape[1]
-    out[:, :count, :] = first[...]
-    out[:, count:, :] = second[...]
+    count = first.shape[-2]
+    out[..., :count, :] = first[...]
+    out[..., count:, :] = second[...]
 
 
 def stacked(first, second, flops=0):
-    shape = jax.ShapeDtypeStruct((2, 2 * first.shape[1], first.shape[2]), first.dtype)
+    shape = jax.ShapeDtypeStruct((*first.shape[:-2], 2 * first.shape[-2], first.shape[-1]), first.dtype)
     return call(stack_kernel, [shape], (first, second), flops=flops)[0]
 
 
@@ -406,6 +409,7 @@
     reach = max(1, owner_count // 64)
     patch_total = images * per_image
     rows = patch_total + special_block
+    cut = per_image * max(1, images // 2)
     heads = width // HEAD_DIM
     pairs = heads // 2
     paired = reach == 1 and owner_count % 2 == 0
@@ -428,11 +432,13 @@
     patches = patch_rows.reshape(patch_total, width)
     turned = jnp.transpose(special_rows, (1, 0, 2))
     power = owner_count >= 8 and owner_count & (owner_count - 1) == 0
-    specials, own = call(
+    specials, own, early, late = call(
         rows_kernel,
         [
             bf16(special_block, width),
             bf16(patch_total, width),
+            bf16(cut, width),
+            bf16(patch_total - cut, width),
         ],
         (frame_order, turned, role_first, role_rest, patches),
         in_specs=[HBM] * 5,
@@ -441,14 +447,14 @@
             pltpu.VMEM(turned.shape, jnp.bfloat16),
             pltpu.VMEM(role_first.shape, jnp.bfloat16),
             pltpu.VMEM(role_rest.shape, jnp.bfloat16),
-            pltpu.SemaphoreType.DMA((5,)),
+            pltpu.SemaphoreType.DMA((7,)),
         ],
     )
-    bits = [1 << i for i in range(1, owner_count.bit_length() - 1)] + [1] if power else []
-    (specials,) = call(pair_kernel, [bf16(2, special_block, width)], both(specials))
     everywhere = specials
     if paired and power:
-        everywhere = stacked(specials, swapped(specials, "blk", bits[0]), FIRST)
+        everywhere = stacked(specials, swapped(specials, "blk", 2), FIRST)
+    (everywhere,) = call(pair_kernel, [bf16(2, *everywhere.shape)], both(everywhere))
+    specials = everywhere
     mask, weights = call(
         functools.partial(start_kernel, offsets, per_image, special_count, special_block),
         [
@@ -460,7 +466,7 @@
         scratch=[pltpu.SMEM(covisible.shape, jnp.int32), pltpu.SemaphoreType.DMA((1 + 6,))],
     )
     queries, special_queries, *state = call(
-        functools.partial(first_kernel, images),
+        functools.partial(first_kernel, images, special_block),
         [bf16(pairs, PAIR, 2 * patch_total), bf16(width, heads * special_block), *state_shape],
         (mask, own, swapped(patches, "head", 1), specials, weights),
     )
@@ -474,33 +480,41 @@
         )
 
     image_rows = lambda owner: [(per_image, owner * images + b) for b in range(images)]
-    def halved(part, gate):
+    def halved(part, gate, step=per_image):
         part = after(part, gate)
-        starts = range(0, part.shape[0], per_image)
-        return [both(part[start : start + per_image]) for start in starts]
+        return [both(part[start : start + step]) for start in range(0, part.shape[0], step)]
 
     stretches = lambda owner: [[image] for image in image_rows(owner)]
     if paired:
-        far = after(crossed(patches, "blk"), state[0])
-        near = swapped(patches, "blk", 1)
         if power:
-            everywhere = after(everywhere, far)
-            for bit in bits[1:-2]:
-                everywhere = stacked(everywhere, swapped(everywhere, "blk", bit))
-            arrived = swapped(everywhere, "blk", bits[-2])
-        state = later(stretches(1), halved(far, state[0]), state)
+            bit = 4
+            while bit < owner_count:
+                everywhere = stacked(everywhere, swapped(everywhere, "blk", bit), FIRST)
+                bit *= 2
+        far = halved(crossed(patches, "blk"), state[0])
+        early = swapped(early, "blk", 1)
+        late = swapped(after(late,mask), "blk", 1)
+        count = early.shape[0] // per_image
+        state[0] = after(state[0], everywhere)
+        state = later(stretches(1), far, state)
+        if power:
+            everywhere = after(everywhere, state[0])
+            arrived = swapped(everywhere, "blk", 1)
+        step = per_image // 2
+        stretches_early = [[(step, image)] for (_, image), in stretches(2)[:count] for _ in range(2)]
+        state = later(stretches_early, halved(early, state[0], step), state)
         if power:
             everywhere = stacked(after(everywhere, state[0]), arrived, FIRST)
-            arrived = swapped(everywhere, "blk", bits[-1])
-        state = later(stretches(2), halved(near, state[0]), state)
-        if power:
-            everywhere = stacked(after(everywhere, state[0]), arrived)
+        stretches, parts = stretches(2)[count:], halved(late, state[0])
     else:
         for i, offset in enumerate(offsets[1:]):
-            state = later(stretches(i + 1), halved(shifted(patches, "blk", -offset), state[0]), state)
+            parts = halved(shifted(patches, "blk", -offset), state[0])
+            if i < len(offsets) - 2:
+                state = later(stretches(i + 1), parts, state)
+        stretches = stretches(len(offsets) - 1)
     if not (paired and power):
         everywhere = lax.all_gather(specials, "blk", axis=1, tiled=True)
-    stretches, parts = [[(everywhere.shape[1], None)]], [(everywhere, everywhere)]
+    stretches, parts = stretches + [[(everywhere.shape[1], None)]], parts + [(everywhere, everywhere)]
     kept, sent = call(
         functools.partial(last_kernel, stretches, real_rows),
         [f32(rows, width), bf16(rows, width)],

time: 37.6 us -> 38.9 us (1.035)
  starting transfers between devices: 9.33 us -> 13.2 us
  waiting for transfers between devices: 9.76 us -> 7.32 us
    ppermute x11 -> x13, starting transfers between devices: 3.72 us -> 9.76 us  [swapped(): return lax.ppermute(block, axis, [(i ^ bit, i) for i in range(count)])]
    ppermute x1, starting transfers between devices: 5.6 us -> 3.4 us  [crossed(): lax.ppermute(block, axis, [(i, (i + (-1 if i % 2 == 0 else 1)) % count) f...]
    ppermute x11 -> x13, waiting for transfers between devices: 6.38 us -> 4.6 us  [swapped(): return lax.ppermute(block, axis, [(i ^ bit, i) for i in range(count)])]
    ppermute x1, waiting for transfers between devices: 3.39 us -> 2.72 us  [crossed(): lax.ppermute(block, axis, [(i, (i + (-1 if i % 2 == 0 else 1)) % count) f...]
  transfers between devices with their start and end apart: 12 -> 14, of which waited for: 6 -> 8; matrix products, arithmetic and copies ran while one was open for 0% -> 0% of each run, Pallas kernels for 35% -> 28%
where the time goes in v13:
time: 38.9 us; the launch traced here: 38.7 us
  Pallas kernels  17.5 us (45%)
  starting transfers between devices  13.2 us (34%)
  waiting for transfers between devices  7.32 us (19%)
  between operations  0.74 us (2%)
    pallas_call x11, Pallas kernels, call(): pl.pallas_call(kernel, out_shape=out_shape, in_specs=in_specs or [VMEM] *...  17.5 us
    ppermute x13, starting transfers between devices, swapped(): return lax.ppermute(block, axis, [(i ^ bit, i) for i in range(count)])  9.76 us
    ppermute x13, waiting for transfers between devices, swapped(): return lax.ppermute(block, axis, [(i ^ bit, i) for i in range(count)])  4.6 us
    ppermute x1, starting transfers between devices, crossed(): lax.ppermute(block, axis, [(i, (i + (-1 if i % 2 == 0 else 1)) % count) f...  3.4 us
    ppermute x1, waiting for transfers between devices, crossed(): lax.ppermute(block, axis, [(i, (i + (-1 if i % 2 == 0 else 1)) % count) f...  2.72 us
  transfers between devices with their start and end apart: 14, of which 8 were waited for; matrix products, arithmetic and copies ran while one was open for 0% of the time, Pallas kernels for 28%

profile of v13, /device:TPU:0, one launch (start us, length us, event | category | flops | bytes accessed | tf_op | source)
XLA Modules:
  0.0 38.7 jit_solution(6246904921451301352)
XLA Ops:
  0.6 1.3 %shard_map.96 = (bf16[16,512]{1,0:T(8,128)(2,1)S(1)}, bf16[384,512]{1,0:T(8,128)(2,1)S(1)}, bf16[192,512]{1,0:T(8,128)(2,1)S(1)}, bf16[192,512]{1,0:T(8,128)(2,1)S(1)}) custom-call(s32[2]{0:T(128)} %frame_order.1, bf16[5,2,512]{2,1,0:T(2,128)(2,1)} %bitcast.7, bf16[5,1024]{1,0:T(8,128)(2,1)} %role_first.1, bf16[5,1024]{1,0:T(8,128)(2,1)} %role_rest.1, ...), custom_call_target="tpu_custom_call" | custom-call | tf_op jit(solution)/shard_map/pallas_call | solution.py:370
  1.9 3.1 %collective-permute-start.4 = (bf16[16,512]{1,0:T(8,128)(2,1)S(1)}, bf16[16,512]{1,0:T(8,128)(2,1)S(1)}, u32[]{:S(2)}, u32[]{:S(2)}) collective-permute-start(bf16[16,512]{1,0:T(8,128)(2,1)S(1)} %get-tuple-element.38.first), channel_id=1, source_target_pairs={{4,0},{6,2},{0,4},{2,6},{12,8},{14,10},{8,12},{10,14},{5,1},{7,3},... | collective-permute-start | bytes 49160 | tf_op jit(solution)/shard_map/ppermute | solution.py:30
  5.0 3.4 %collective-permute-start.2 = (bf16[384,512]{1,0:T(8,128)(2,1)}, bf16[384,512]{1,0:T(8,128)(2,1)S(1)}, u32[]{:S(2)}, u32[]{:S(2)}) collective-permute-start(bf16[384,512]{1,0:T(8,128)(2,1)} %bitcast.6), channel_id=1, source_target_pairs={{0,14},{2,4},{4,2},{6,8},{8,6},{10,12},{12,10},{14,0},{1,15},{3,5}... | collective-permute-start | bytes 1179656 | tf_op jit(solution)/shard_map/ppermute | solution.py:35
  8.4 0.0 collective-permute-done.4.second
  8.4 0.2 collective-permute-start.5
  8.6 0.0 collective-permute-start.1
  8.6 1.9 %shard_map.95 = (f32[8,512]{1,0:T(8,128)S(1)}, bf16[3,1024,512]{2,1,0:T(8,128)(2,1)S(1)}) custom-call(s32[2,16]{1,0:T(2,128)} %covisible.1, bf16[3,1024,512]{2,1,0:T(8,128)(2,1)} %w_qkv.1), custom_call_target="tpu_custom_call" | custom-call | tf_op jit(solution)/shard_map/pallas_call | solution.py:370
  10.5 2.1 %collective-permute-start = (bf16[192,512]{1,0:T(8,128)(2,1)S(1)}, bf16[192,512]{1,0:T(8,128)(2,1)S(1)}, u32[]{:S(2)}, u32[]{:S(2)}) collective-permute-start(bf16[192,512]{1,0:T(8,128)(2,1)S(1)} %get-tuple-element.35), channel_id=1, source_target_pairs={{2,0},{0,2},{6,4},{4,6},{10,8},{8,10},{14,12},{12,14},{3,1},{1,3},... | collective-permute-start | bytes 589832 | tf_op jit(solution)/shard_map/ppermute | solution.py:30
  12.6 1.2 %collective-permute-start.8 = (bf16[2,32,512]{2,1,0:T(8,128)(2,1)S(1)}, bf16[2,32,512]{2,1,0:T(8,128)(2,1)S(1)}, u32[]{:S(2)}, u32[]{:S(2)}) collective-permute-start(bf16[2,32,512]{2,1,0:T(8,128)(2,1)S(1)} %shard_map.98.special.first), channel_id=1, source_target_pairs={{8,0},{10,2},{12,4},{14,6},{0,8},{2,10},{4,12},{6,14},{9,1},{11,3}... | collective-permute-start | bytes 196616 | tf_op jit(solution)/shard_map/ppermute | solution.py:30
  13.8 3.4 %shard_map.99 = (bf16[4,128,768]{2,1,0:T(8,128)(2,1)S(1)}, bf16[512,128]{1,0:T(8,128)(2,1)S(1)}, f32[8,768]{1,0:T(8,128)S(1)}, f32[8,768]{1,0:T(8,128)S(1)}, f32...) custom-call(f32[8,512]{1,0:T(8,128)S(1)} %get-tuple-element.33.mask, bf16[384,512]{1,0:T(8,128)(2,1)S(1)} %get-tuple-element.37.own, ...), custom_call_target="tpu_custom_call" | custom-call | tf_op jit(solution)/shard_map/pallas_call | solution.py:370
  17.2 2.7 %collective-permute-done.2 = bf16[384,512]{1,0:T(8,128)(2,1)S(1)} collective-permute-done((bf16[384,512]{1,0:T(8,128)(2,1)}, bf16[384,512]{1,0:T(8,128)(2,1)S(1)}, u32[]{:S(2)}, u32[]{:S(2)}) %collective-permute-start.2) | collective-permute-done | bytes 393248 | tf_op jit(solution)/shard_map/ppermute | solution.py:35
  19.9 0.1 collective-permute-start.7
  20.0 0.5 %collective-permute-start.6 = (bf16[192,512]{1,0:T(8,128)(2,1)S(1)}, bf16[192,512]{1,0:T(8,128)(2,1)S(1)}, u32[]{:S(2)}, u32[]{:S(2)}) collective-permute-start(bf16[192,512]{1,0:T(8,128)(2,1)S(1)} %get-tuple-element.65.refs_0_), channel_id=1, source_target_pairs={{1,0},{0,1},{3,2},{2,3},{5,4},{4,5},{7,6},{6,7},{9,8},{8,9},{11,10... | collective-permute-start | bytes 589832 | tf_op jit(solution)/shard_map/ppermute | solution.py:30
  20.5 0.0 collective-permute-done.8.second
  20.5 0.9 %collective-permute-done.7.refs_3_ = bf16[192,512]{1,0:T(8,128)(2,1)S(1)} collective-permute-done((bf16[192,512]{1,0:T(8,128)(2,1)S(1)}, bf16[192,512]{1,0:T(8,128)(2,1)S(1)}, u32[]{:S(2)}, u32[]{:S(2)}) %collective-permute-start.7) | collective-permute-done | bytes 196640 | tf_op jit(solution)/shard_map/ppermute | solution.py:30
  21.4 0.3 collective-permute-done.6.refs_2_
  21.7 3.4 %shard_map.101 = (f32[8,768]{1,0:T(8,128)S(1)}, f32[8,768]{1,0:T(8,128)S(1)}, f32[4,64,768]{2,1,0:T(8,128)S(1)}, f32[512,128]{1,0:T(8,128)S(1)}) custom-call(f32[8,512]{1,0:T(8,128)S(1)} %get-tuple-element.33.mask, bf16[192,512]{1,0:T(8,128)(2,1)S(1)} %get-tuple-element.65.refs_0_, bf16[192,512]{1,0:T(8,128)(2,1)S(1)} %get-tuple-element.64.refs_1_, ...), custom_call_target="tpu_custom_call" | custom-call | tf_op jit(solution)/shard_map/pallas_call | solution.py:370
  25.1 0.0 collective-permute-done.1
  25.1 1.2 %collective-permute-start.11 = (bf16[2,64,512]{2,1,0:T(8,128)(2,1)S(1)}, bf16[2,64,512]{2,1,0:T(8,128)(2,1)S(1)}, u32[]{:S(2)}, u32[]{:S(2)}) collective-permute-start(bf16[2,64,512]{2,1,0:T(8,128)(2,1)S(1)} %shard_map.100.first), channel_id=1, source_target_pairs={{2,0},{0,2},{6,4},{4,6},{10,8},{8,10},{14,12},{12,14},{3,1},{1,3},... | collective-permute-start | bytes 393224 | tf_op jit(solution)/shard_map/ppermute | solution.py:30
  26.3 0.1 collective-permute-start.10
  26.4 0.5 %collective-permute-start.9 = (bf16[96,512]{1,0:T(8,128)(2,1)S(1)}, bf16[96,512]{1,0:T(8,128)(2,1)S(1)}, u32[]{:S(2)}, u32[]{:S(2)}) collective-permute-start(bf16[96,512]{1,0:T(8,128)(2,1)S(1)} %get-tuple-element.67.refs_0_), channel_id=1, source_target_pairs={{1,0},{0,1},{3,2},{2,3},{5,4},{4,5},{7,6},{6,7},{9,8},{8,9},{11,10... | collective-permute-start | bytes 294920 | tf_op jit(solution)/shard_map/ppermute | solution.py:30
  26.9 0.8 %collective-permute-done.10.refs_3_ = bf16[96,512]{1,0:T(8,128)(2,1)S(1)} collective-permute-done((bf16[96,512]{1,0:T(8,128)(2,1)S(1)}, bf16[96,512]{1,0:T(8,128)(2,1)S(1)}, u32[]{:S(2)}, u32[]{:S(2)}) %collective-permute-start.10) | collective-permute-done | bytes 98336 | tf_op jit(solution)/shard_map/ppermute | solution.py:30
  27.7 0.2 collective-permute-done.9.refs_2_
  27.9 2.0 %shard_map.102 = (f32[8,768]{1,0:T(8,128)S(1)}, f32[8,768]{1,0:T(8,128)S(1)}, f32[4,64,768]{2,1,0:T(8,128)S(1)}, f32[512,128]{1,0:T(8,128)S(1)}) custom-call(f32[8,512]{1,0:T(8,128)S(1)} %get-tuple-element.33.mask, bf16[96,512]{1,0:T(8,128)(2,1)S(1)} %get-tuple-element.67.refs_0_, bf16[96,512]{1,0:T(8,128)(2,1)S(1)} %get-tuple-element.66.refs_1_, ...), custom_call_target="tpu_custom_call" | custom-call | tf_op jit(solution)/shard_map/pallas_call | solution.py:370
  29.8 0.0 collective-permute-done.refs_0_
  29.8 0.4 %collective-permute-start.12 = (bf16[192,512]{1,0:T(8,128)(2,1)S(1)}, bf16[192,512]{1,0:T(8,128)(2,1)S(1)}, u32[]{:S(2)}, u32[]{:S(2)}) collective-permute-start(bf16[192,512]{1,0:T(8,128)(2,1)S(1)} %collective-permute-done.refs_0_), channel_id=1, source_target_pairs={{1,0},{0,1},{3,2},{2,3},{5,4},{4,5},{7,6},{6,7},{9,8},{8,9},{11,10... | collective-permute-start | bytes 589832 | tf_op jit(solution)/shard_map/ppermute | solution.py:30
  30.3 0.6 %collective-permute-done.11.second = bf16[2,64,512]{2,1,0:T(8,128)(2,1)S(1)} collective-permute-done((bf16[2,64,512]{2,1,0:T(8,128)(2,1)S(1)}, bf16[2,64,512]{2,1,0:T(8,128)(2,1)S(1)}, u32[]{:S(2)}, u32[]{:S(2)}) %collective-permute-start.11) | collective-permute-done | bytes 131104 | tf_op jit(solution)/shard_map/ppermute | solution.py:30
  30.9 0.5 %collective-permute-done.12.refs_2_ = bf16[192,512]{1,0:T(8,128)(2,1)S(1)} collective-permute-done((bf16[192,512]{1,0:T(8,128)(2,1)S(1)}, bf16[192,512]{1,0:T(8,128)(2,1)S(1)}, u32[]{:S(2)}, u32[]{:S(2)}) %collective-permute-start.12) | collective-permute-done | bytes 196640 | tf_op jit(solution)/shard_map/ppermute | solution.py:30
  31.4 4.7 %shard_map.104 = (f32[400,512]{1,0:T(8,128)S(1)}, bf16[400,512]{1,0:T(8,128)(2,1)S(1)}) custom-call(f32[8,512]{1,0:T(8,128)S(1)} %get-tuple-element.33.mask, bf16[192,512]{1,0:T(8,128)(2,1)S(1)} %collective-permute-done.refs_0_, bf16[2,128,512]{2,1,0:T(8,128)(2,1)S(1)} %shard_map.103.refs_1_.refs_3_, bf16[192,512]{1,0:T(8,128)(2,1)S(1)} %collective-permute-done.12.refs_2_, ...), custom_call_target="tpu_custom_call" | custom-call | tf_op jit(solution)/shard_map/pallas_call | solution.py:370
  36.1 0.4 %collective-permute-start.13 = (bf16[400,512]{1,0:T(8,128)(2,1)S(1)}, bf16[400,512]{1,0:T(8,128)(2,1)S(1)}, u32[]{:S(2)}, u32[]{:S(2)}) collective-permute-start(bf16[400,512]{1,0:T(8,128)(2,1)S(1)} %get-tuple-element.61), channel_id=1, source_target_pairs={{1,0},{0,1},{3,2},{2,3},{5,4},{4,5},{7,6},{6,7},{9,8},{8,9},{11,10... | collective-permute-start | bytes 1228808 | tf_op jit(solution)/shard_map/ppermute | solution.py:30
  36.5 1.4 %collective-permute-done.13.received = bf16[400,512]{1,0:T(8,128)(2,1)S(1)} collective-permute-done((bf16[400,512]{1,0:T(8,128)(2,1)S(1)}, bf16[400,512]{1,0:T(8,128)(2,1)S(1)}, u32[]{:S(2)}, u32[]{:S(2)}) %collective-permute-start.13) | collective-permute-done | bytes 409632 | tf_op jit(solution)/shard_map/ppermute | solution.py:30
  37.9 0.8 %shard_map.105 = (bf16[384,512]{1,0:T(8,128)(2,1)}, bf16[5,2,512]{2,1,0:T(2,128)(2,1)}) custom-call(f32[400,512]{1,0:T(8,128)S(1)} %get-tuple-element.60.kept, bf16[400,512]{1,0:T(8,128)(2,1)S(1)} %collective-permute-done.13.received), custom_call_target="tpu_custom_call" | custom-call | tf_op jit(solution)/shard_map/pallas_call | solution.py:370
  (9 shorter events, 0.1 us)
Async XLA Ops:
  1.9 6.5 %collective-permute-start.4 = (bf16[16,512]{1,0:T(8,128)(2,1)S(1)}, bf16[16,512]{1,0:T(8,128)(2,1)S(1)}, u32[]{:S(2)}, u32[]{:S(2)}) collective-permute-start(bf16[16,512]{1,0:T(8,128)(2,1)S(1)} %get-tuple-element.38.first), channel_id=1, source_target_pairs={{4,0},{6,2},{0,4},{2,6},{12,8},{14,10},{8,12},{10,14},{5,1},{7,3},... | collective-permute-start | bytes 49160 | tf_op jit(solution)/shard_map/ppermute | solution.py:30
  5.0 8.8 %collective-permute-start.3 = (bf16[384,512]{1,0:T(8,128)(2,1)}, bf16[384,512]{1,0:T(8,128)(2,1)S(1)}, u32[]{:S(2)}, u32[]{:S(2)}) collective-permute-start(bf16[384,512]{1,0:T(8,128)(2,1)} %bitcast.5), channel_id=1, source_target_pairs={{1,0},{0,1},{3,2},{2,3},{5,4},{4,5},{7,6},{6,7},{9,8},{8,9},{11,10... | collective-permute-start | bytes 1179656 | tf_op jit(solution)/shard_map/ppermute | solution.py:30
  5.0 14.9 %collective-permute-start.2 = (bf16[384,512]{1,0:T(8,128)(2,1)}, bf16[384,512]{1,0:T(8,128)(2,1)S(1)}, u32[]{:S(2)}, u32[]{:S(2)}) collective-permute-start(bf16[384,512]{1,0:T(8,128)(2,1)} %bitcast.6), channel_id=1, source_target_pairs={{0,14},{2,4},{4,2},{6,8},{8,6},{10,12},{12,10},{14,0},{1,15},{3,5}... | collective-permute-start | bytes 1179656 | tf_op jit(solution)/shard_map/ppermute | solution.py:35
  8.4 4.2 %collective-permute-start.5 = (bf16[32,512]{1,0:T(8,128)(2,1)S(1)}, bf16[32,512]{1,0:T(8,128)(2,1)S(1)}, u32[]{:S(2)}, u32[]{:S(2)}) collective-permute-start(bf16[32,512]{1,0:T(8,128)(2,1)S(1)} %shard_map.97.first), channel_id=1, source_target_pairs={{1,0},{0,1},{3,2},{2,3},{5,4},{4,5},{7,6},{6,7},{9,8},{8,9},{11,10... | collective-permute-start | bytes 98312 | tf_op jit(solution)/shard_map/ppermute | solution.py:30
  8.6 16.5 %collective-permute-start.1 = (bf16[192,512]{1,0:T(8,128)(2,1)S(1)}, bf16[192,512]{1,0:T(8,128)(2,1)S(1)}, u32[]{:S(2)}, u32[]{:S(2)}) collective-permute-start(bf16[192,512]{1,0:T(8,128)(2,1)S(1)} %get-tuple-element.36), channel_id=1, source_target_pairs={{2,0},{0,2},{6,4},{4,6},{10,8},{8,10},{14,12},{12,14},{3,1},{1,3},... | collective-permute-start | bytes 589832 | tf_op jit(solution)/shard_map/ppermute | solution.py:30
  10.5 19.3 %collective-permute-start = (bf16[192,512]{1,0:T(8,128)(2,1)S(1)}, bf16[192,512]{1,0:T(8,128)(2,1)S(1)}, u32[]{:S(2)}, u32[]{:S(2)}) collective-permute-start(bf16[192,512]{1,0:T(8,128)(2,1)S(1)} %get-tuple-element.35), channel_id=1, source_target_pairs={{2,0},{0,2},{6,4},{4,6},{10,8},{8,10},{14,12},{12,14},{3,1},{1,3},... | collective-permute-start | bytes 589832 | tf_op jit(solution)/shard_map/ppermute | solution.py:30
  12.6 7.9 %collective-permute-start.8 = (bf16[2,32,512]{2,1,0:T(8,128)(2,1)S(1)}, bf16[2,32,512]{2,1,0:T(8,128)(2,1)S(1)}, u32[]{:S(2)}, u32[]{:S(2)}) collective-permute-start(bf16[2,32,512]{2,1,0:T(8,128)(2,1)S(1)} %shard_map.98.special.first), channel_id=1, source_target_pairs={{8,0},{10,2},{12,4},{14,6},{0,8},{2,10},{4,12},{6,14},{9,1},{11,3}... | collective-permute-start | bytes 196616 | tf_op jit(solution)/shard_map/ppermute | solution.py:30
  19.9 1.5 %collective-permute-start.7 = (bf16[192,512]{1,0:T(8,128)(2,1)S(1)}, bf16[192,512]{1,0:T(8,128)(2,1)S(1)}, u32[]{:S(2)}, u32[]{:S(2)}) collective-permute-start(bf16[192,512]{1,0:T(8,128)(2,1)S(1)} %get-tuple-element.64.refs_1_), channel_id=1, source_target_pairs={{1,0},{0,1},{3,2},{2,3},{5,4},{4,5},{7,6},{6,7},{9,8},{8,9},{11,10... | collective-permute-start | bytes 589832 | tf_op jit(solution)/shard_map/ppermute | solution.py:30
  20.0 1.7 %collective-permute-start.6 = (bf16[192,512]{1,0:T(8,128)(2,1)S(1)}, bf16[192,512]{1,0:T(8,128)(2,1)S(1)}, u32[]{:S(2)}, u32[]{:S(2)}) collective-permute-start(bf16[192,512]{1,0:T(8,128)(2,1)S(1)} %get-tuple-element.65.refs_0_), channel_id=1, source_target_pairs={{1,0},{0,1},{3,2},{2,3},{5,4},{4,5},{7,6},{6,7},{9,8},{8,9},{11,10... | collective-permute-start | bytes 589832 | tf_op jit(solution)/shard_map/ppermute | solution.py:30
  25.1 5.7 %collective-permute-start.11 = (bf16[2,64,512]{2,1,0:T(8,128)(2,1)S(1)}, bf16[2,64,512]{2,1,0:T(8,128)(2,1)S(1)}, u32[]{:S(2)}, u32[]{:S(2)}) collective-permute-start(bf16[2,64,512]{2,1,0:T(8,128)(2,1)S(1)} %shard_map.100.first), channel_id=1, source_target_pairs={{2,0},{0,2},{6,4},{4,6},{10,8},{8,10},{14,12},{12,14},{3,1},{1,3},... | collective-permute-start | bytes 393224 | tf_op jit(solution)/shard_map/ppermute | solution.py:30
  26.3 1.4 %collective-permute-start.10 = (bf16[96,512]{1,0:T(8,128)(2,1)S(1)}, bf16[96,512]{1,0:T(8,128)(2,1)S(1)}, u32[]{:S(2)}, u32[]{:S(2)}) collective-permute-start(bf16[96,512]{1,0:T(8,128)(2,1)S(1)} %get-tuple-element.66.refs_1_), channel_id=1, source_target_pairs={{1,0},{0,1},{3,2},{2,3},{5,4},{4,5},{7,6},{6,7},{9,8},{8,9},{11,10... | collective-permute-start | bytes 294920 | tf_op jit(solution)/shard_map/ppermute | solution.py:30
  26.4 1.4 %collective-permute-start.9 = (bf16[96,512]{1,0:T(8,128)(2,1)S(1)}, bf16[96,512]{1,0:T(8,128)(2,1)S(1)}, u32[]{:S(2)}, u32[]{:S(2)}) collective-permute-start(bf16[96,512]{1,0:T(8,128)(2,1)S(1)} %get-tuple-element.67.refs_0_), channel_id=1, source_target_pairs={{1,0},{0,1},{3,2},{2,3},{5,4},{4,5},{7,6},{6,7},{9,8},{8,9},{11,10... | collective-permute-start | bytes 294920 | tf_op jit(solution)/shard_map/ppermute | solution.py:30
  29.8 1.5 %collective-permute-start.12 = (bf16[192,512]{1,0:T(8,128)(2,1)S(1)}, bf16[192,512]{1,0:T(8,128)(2,1)S(1)}, u32[]{:S(2)}, u32[]{:S(2)}) collective-permute-start(bf16[192,512]{1,0:T(8,128)(2,1)S(1)} %collective-permute-done.refs_0_), channel_id=1, source_target_pairs={{1,0},{0,1},{3,2},{2,3},{5,4},{4,5},{7,6},{6,7},{9,8},{8,9},{11,10... | collective-permute-start | bytes 589832 | tf_op jit(solution)/shard_map/ppermute | solution.py:30
  36.1 1.8 %collective-permute-start.13 = (bf16[400,512]{1,0:T(8,128)(2,1)S(1)}, bf16[400,512]{1,0:T(8,128)(2,1)S(1)}, u32[]{:S(2)}, u32[]{:S(2)}) collective-permute-start(bf16[400,512]{1,0:T(8,128)(2,1)S(1)} %get-tuple-element.61), channel_id=1, source_target_pairs={{1,0},{0,1},{3,2},{2,3},{5,4},{4,5},{7,6},{6,7},{9,8},{8,9},{11,10... | collective-permute-start | bytes 1228808 | tf_op jit(solution)/shard_map/ppermute | solution.py:30

commit v14 on v12

--- a/solution.py
+++ b/solution.py
@@ -474,12 +474,14 @@
         )
 
     image_rows = lambda owner: [(per_image, owner * images + b) for b in range(images)]
-    def halved(part, gate):
+    def halved(part, gate, step):
         part = after(part, gate)
-        starts = range(0, part.shape[0], per_image)
-        return [both(part[start : start + per_image]) for start in starts]
-
-    stretches = lambda owner: [[image] for image in image_rows(owner)]
+        return [both(part[start : start + step]) for start in range(0, part.shape[0], step)]
+
+    def stretches(owner, step):
+        count = per_image // step
+        return [[(step, image)] for _, image in image_rows(owner) for _ in range(count)]
+
     if paired:
         far = after(crossed(patches, "blk"), state[0])
         near = swapped(patches, "blk", 1)
@@ -488,19 +490,25 @@
             for bit in bits[1:-2]:
                 everywhere = stacked(everywhere, swapped(everywhere, "blk", bit))
             arrived = swapped(everywhere, "blk", bits[-2])
-        state = later(stretches(1), halved(far, state[0]), state)
-        if power:
-            everywhere = stacked(after(everywhere, state[0]), arrived, FIRST)
-            arrived = swapped(everywhere, "blk", bits[-1])
-        state = later(stretches(2), halved(near, state[0]), state)
+        far = halved(far, state[0], per_image)
+        state = later(stretches(1, per_image)[:1], far[:1], state)
         if power:
             everywhere = stacked(after(everywhere, state[0]), arrived)
+            arrived = swapped(everywhere, "blk", bits[-1])
+        state = later(stretches(1, per_image)[1:], far[1:], state)
+        step = per_image // 2
+        stretches, parts = stretches(2, step), halved(near, state[0], step)
+        if power:
+            everywhere = stacked(everywhere, arrived)
     else:
         for i, offset in enumerate(offsets[1:]):
-            state = later(stretches(i + 1), halved(shifted(patches, "blk", -offset), state[0]), state)
+            parts = halved(shifted(patches, "blk", -offset), state[0], per_image)
+            if i < len(offsets) - 2:
+                state = later(stretches(i + 1, per_image), parts, state)
+        stretches = stretches(len(offsets) - 1, per_image)
     if not (paired and power):
         everywhere = lax.all_gather(specials, "blk", axis=1, tiled=True)
-    stretches, parts = [[(everywhere.shape[1], None)]], [(everywhere, everywhere)]
+    stretches, parts = stretches + [[(everywhere.shape[1], None)]], parts + [(everywhere, everywhere)]
     kept, sent = call(
         functools.partial(last_kernel, stretches, real_rows),
         [f32(rows, width), bf16(rows, width)],

time: 37.6 us -> 37.9 us (level)
  starting transfers between devices: 9.33 us -> 9.83 us
  Pallas kernels: 17.5 us -> 17.1 us
    ppermute x11 -> x13, starting transfers between devices: 3.72 us -> 4.23 us  [swapped(): return lax.ppermute(block, axis, [(i ^ bit, i) for i in range(count)])]
    pallas_call x11, Pallas kernels: 17.5 us -> 17.1 us  [call(): pl.pallas_call(kernel, out_shape=out_shape, in_specs=in_specs or [VMEM] *...]
    ppermute x11 -> x13, waiting for transfers between devices: 6.38 us -> 6.51 us  [swapped(): return lax.ppermute(block, axis, [(i ^ bit, i) for i in range(count)])]
  transfers between devices with their start and end apart: 12 -> 14, of which waited for: 6 -> 4; matrix products, arithmetic and copies ran while one was open for 0% -> 0% of each run, Pallas kernels for 35% -> 28%
where the time goes in v14:
time: 37.9 us; the launch traced here: 37.6 us
  Pallas kernels  17.1 us (45%)
  waiting for transfers between devices  9.89 us (26%)
  starting transfers between devices  9.83 us (26%)
  between operations  0.8 us (2%)
    pallas_call x11, Pallas kernels, call(): pl.pallas_call(kernel, out_shape=out_shape, in_specs=in_specs or [VMEM] *...  17.1 us
    ppermute x13, waiting for transfers between devices, swapped(): return lax.ppermute(block, axis, [(i ^ bit, i) for i in range(count)])  6.51 us
    ppermute x1, starting transfers between devices, crossed(): lax.ppermute(block, axis, [(i, (i + (-1 if i % 2 == 0 else 1)) % count) f...  5.6 us
    ppermute x13, starting transfers between devices, swapped(): return lax.ppermute(block, axis, [(i ^ bit, i) for i in range(count)])  4.23 us
    ppermute x1, waiting for transfers between devices, crossed(): lax.ppermute(block, axis, [(i, (i + (-1 if i % 2 == 0 else 1)) % count) f...  3.39 us
  transfers between devices with their start and end apart: 14, of which 4 were waited for; matrix products, arithmetic and copies ran while one was open for 0% of the time, Pallas kernels for 28%

profile of v14, /device:TPU:0, one launch (start us, length us, event | category | flops | bytes accessed | tf_op | source)
XLA Modules:
  0.0 37.6 jit_solution(10149016513537663059)
XLA Ops:
  0.6 0.5 %collective-permute-start.2 = (bf16[384,512]{1,0:T(8,128)(2,1)}, bf16[384,512]{1,0:T(8,128)(2,1)S(1)}, u32[]{:S(2)}, u32[]{:S(2)}) collective-permute-start(bf16[384,512]{1,0:T(8,128)(2,1)} %bitcast.4), channel_id=1, source_target_pairs={{1,0},{0,1},{3,2},{2,3},{5,4},{4,5},{7,6},{6,7},{9,8},{8,9},{11,10... | collective-permute-start | bytes 1179656 | tf_op jit(solution)/shard_map/ppermute | solution.py:30
  1.1 5.6 %collective-permute-start.1 = (bf16[384,512]{1,0:T(8,128)(2,1)}, bf16[384,512]{1,0:T(8,128)(2,1)S(1)}, u32[]{:S(2)}, u32[]{:S(2)}) collective-permute-start(bf16[384,512]{1,0:T(8,128)(2,1)} %bitcast.5), channel_id=1, source_target_pairs={{0,14},{2,4},{4,2},{6,8},{8,6},{10,12},{12,10},{14,0},{1,15},{3,5}... | collective-permute-start | bytes 1179656 | tf_op jit(solution)/shard_map/ppermute | solution.py:35
  6.8 1.1 %shard_map.96 = (bf16[16,512]{1,0:T(8,128)(2,1)S(1)}, bf16[384,512]{1,0:T(8,128)(2,1)S(1)}) custom-call(s32[2]{0:T(128)} %frame_order.1, bf16[5,2,512]{2,1,0:T(2,128)(2,1)} %bitcast.8, bf16[5,1024]{1,0:T(8,128)(2,1)} %role_first.1, bf16[5,1024]{1,0:T(8,128)(2,1)} %role_rest.1, bf16[384,512]{1,0:T(8,128)(2,1)} %bitcast.6), custom_call_target="tpu_custom_call" | custom-call | tf_op jit(solution)/shard_map/pallas_call | solution.py:367
  7.9 0.2 collective-permute-start.3
  8.1 0.0 collective-permute-start
  8.1 1.9 %shard_map.95 = (f32[8,512]{1,0:T(8,128)S(1)}, bf16[3,1024,512]{2,1,0:T(8,128)(2,1)S(1)}) custom-call(s32[2,16]{1,0:T(2,128)} %covisible.1, bf16[3,1024,512]{2,1,0:T(8,128)(2,1)} %w_qkv.1), custom_call_target="tpu_custom_call" | custom-call | tf_op jit(solution)/shard_map/pallas_call | solution.py:367
  10.0 0.1 collective-permute-start.6
  10.2 0.0 collective-permute-done.2.other
  10.2 3.4 %shard_map.98 = (bf16[4,128,768]{2,1,0:T(8,128)(2,1)S(1)}, bf16[512,128]{1,0:T(8,128)(2,1)S(1)}, f32[8,768]{1,0:T(8,128)S(1)}, f32[8,768]{1,0:T(8,128)S(1)}, f32...) custom-call(f32[8,512]{1,0:T(8,128)S(1)} %get-tuple-element.29.mask, bf16[384,512]{1,0:T(8,128)(2,1)S(1)} %get-tuple-element.30.own, ...), custom_call_target="tpu_custom_call" | custom-call | tf_op jit(solution)/shard_map/pallas_call | solution.py:367
  13.6 3.4 %collective-permute-done.1 = bf16[384,512]{1,0:T(8,128)(2,1)S(1)} collective-permute-done((bf16[384,512]{1,0:T(8,128)(2,1)}, bf16[384,512]{1,0:T(8,128)(2,1)S(1)}, u32[]{:S(2)}, u32[]{:S(2)}) %collective-permute-start.1) | collective-permute-done | bytes 393248 | tf_op jit(solution)/shard_map/ppermute | solution.py:35
  17.0 0.1 collective-permute-start.5
  17.0 0.5 %collective-permute-start.4 = (bf16[192,512]{1,0:T(8,128)(2,1)S(1)}, bf16[192,512]{1,0:T(8,128)(2,1)S(1)}, u32[]{:S(2)}, u32[]{:S(2)}) collective-permute-start(bf16[192,512]{1,0:T(8,128)(2,1)S(1)} %get-tuple-element.61.refs_0_), channel_id=1, source_target_pairs={{1,0},{0,1},{3,2},{2,3},{5,4},{4,5},{7,6},{6,7},{9,8},{8,9},{11,10... | collective-permute-start | bytes 589832 | tf_op jit(solution)/shard_map/ppermute | solution.py:30
  17.5 0.0 collective-permute-done.6.second
  17.6 1.5 %collective-permute-start.7 = (bf16[2,32,512]{2,1,0:T(8,128)(2,1)S(1)}, bf16[2,32,512]{2,1,0:T(8,128)(2,1)S(1)}, u32[]{:S(2)}, u32[]{:S(2)}) collective-permute-start(bf16[2,32,512]{2,1,0:T(8,128)(2,1)S(1)} %shard_map.101.first), channel_id=1, source_target_pairs={{8,0},{10,2},{12,4},{14,6},{0,8},{2,10},{4,12},{6,14},{9,1},{11,3}... | collective-permute-start | bytes 196616 | tf_op jit(solution)/shard_map/ppermute | solution.py:30
  19.1 2.0 %shard_map.99 = (f32[8,768]{1,0:T(8,128)S(1)}, f32[8,768]{1,0:T(8,128)S(1)}, f32[4,64,768]{2,1,0:T(8,128)S(1)}, f32[512,128]{1,0:T(8,128)S(1)}) custom-call(f32[8,512]{1,0:T(8,128)S(1)} %get-tuple-element.29.mask, bf16[192,512]{1,0:T(8,128)(2,1)S(1)} %get-tuple-element.60.refs_0_, bf16[192,512]{1,0:T(8,128)(2,1)S(1)} %collective-permute-done.5.refs_1_, ...), custom_call_target="tpu_custom_call" | custom-call | tf_op jit(solution)/shard_map/pallas_call | solution.py:367
  21.1 2.9 %collective-permute-done.7.second = bf16[2,32,512]{2,1,0:T(8,128)(2,1)S(1)} collective-permute-done((bf16[2,32,512]{2,1,0:T(8,128)(2,1)S(1)}, bf16[2,32,512]{2,1,0:T(8,128)(2,1)S(1)}, u32[]{:S(2)}, u32[]{:S(2)}) %collective-permute-start.7) | collective-permute-done | bytes 65568 | tf_op jit(solution)/shard_map/ppermute | solution.py:30
  24.0 0.1 collective-permute-start.8
  24.1 0.0 collective-permute-done.4.refs_1_
  24.1 2.0 %shard_map.100 = (f32[8,768]{1,0:T(8,128)S(1)}, f32[8,768]{1,0:T(8,128)S(1)}, f32[4,64,768]{2,1,0:T(8,128)S(1)}, f32[512,128]{1,0:T(8,128)S(1)}) custom-call(f32[8,512]{1,0:T(8,128)S(1)} %get-tuple-element.29.mask, bf16[192,512]{1,0:T(8,128)(2,1)S(1)} %get-tuple-element.61.refs_0_, bf16[192,512]{1,0:T(8,128)(2,1)S(1)} %collective-permute-done.4.refs_1_, ...), custom_call_target="tpu_custom_call" | custom-call | tf_op jit(solution)/shard_map/pallas_call | solution.py:367
  26.1 0.0 collective-permute-done
  26.1 0.1 collective-permute-start.12
  26.2 0.5 %collective-permute-start.11 = (bf16[96,512]{1,0:T(8,128)(2,1)S(1)}, bf16[96,512]{1,0:T(8,128)(2,1)S(1)}, u32[]{:S(2)}, u32[]{:S(2)}) collective-permute-start(bf16[96,512]{1,0:T(8,128)(2,1)S(1)} %get-tuple-element.57.refs_2_), channel_id=1, source_target_pairs={{1,0},{0,1},{3,2},{2,3},{5,4},{4,5},{7,6},{6,7},{9,8},{8,9},{11,10... | collective-permute-start | bytes 294920 | tf_op jit(solution)/shard_map/ppermute | solution.py:30
  26.7 0.1 collective-permute-start.10
  26.8 0.4 %collective-permute-start.9 = (bf16[96,512]{1,0:T(8,128)(2,1)S(1)}, bf16[96,512]{1,0:T(8,128)(2,1)S(1)}, u32[]{:S(2)}, u32[]{:S(2)}) collective-permute-start(bf16[96,512]{1,0:T(8,128)(2,1)S(1)} %get-tuple-element.59.refs_0_), channel_id=1, source_target_pairs={{1,0},{0,1},{3,2},{2,3},{5,4},{4,5},{7,6},{6,7},{9,8},{8,9},{11,10... | collective-permute-start | bytes 294920 | tf_op jit(solution)/shard_map/ppermute | solution.py:30
  27.2 1.8 %collective-permute-done.8.second = bf16[2,64,512]{2,1,0:T(8,128)(2,1)S(1)} collective-permute-done((bf16[2,64,512]{2,1,0:T(8,128)(2,1)S(1)}, bf16[2,64,512]{2,1,0:T(8,128)(2,1)S(1)}, u32[]{:S(2)}, u32[]{:S(2)}) %collective-permute-start.8) | collective-permute-done | bytes 131104 | tf_op jit(solution)/shard_map/ppermute | solution.py:30
  29.1 0.0 collective-permute-done.12.refs_8_
  29.1 0.0 collective-permute-done.11.refs_7_
  29.1 0.0 collective-permute-done.9.refs_5_
  29.1 5.9 %shard_map.104 = (f32[400,512]{1,0:T(8,128)S(1)}, bf16[400,512]{1,0:T(8,128)(2,1)S(1)}) custom-call(f32[8,512]{1,0:T(8,128)S(1)} %get-tuple-element.29.mask, bf16[96,512]{1,0:T(8,128)(2,1)S(1)} %get-tuple-element.59.refs_0_, bf16[96,512]{1,0:T(8,128)(2,1)S(1)} %get-tuple-element.58.refs_1_, bf16[96,512]{1,0:T(8,128)(2,1)S(1)} %get-tuple-element.57.refs_2_, ...), custom_call_target="tpu_custom_call" | custom-call | tf_op jit(solution)/shard_map/pallas_call | solution.py:367
  35.0 0.1 collective-permute-start.13
  35.1 1.7 %collective-permute-done.13.received = bf16[400,512]{1,0:T(8,128)(2,1)S(1)} collective-permute-done((bf16[400,512]{1,0:T(8,128)(2,1)S(1)}, bf16[400,512]{1,0:T(8,128)(2,1)S(1)}, u32[]{:S(2)}, u32[]{:S(2)}) %collective-permute-start.13) | collective-permute-done | bytes 409632 | tf_op jit(solution)/shard_map/ppermute | solution.py:30
  36.8 0.8 %shard_map.105 = (bf16[384,512]{1,0:T(8,128)(2,1)}, bf16[5,2,512]{2,1,0:T(2,128)(2,1)}) custom-call(f32[400,512]{1,0:T(8,128)S(1)} %get-tuple-element.52.kept, bf16[400,512]{1,0:T(8,128)(2,1)S(1)} %collective-permute-done.13.received), custom_call_target="tpu_custom_call" | custom-call | tf_op jit(solution)/shard_map/pallas_call | solution.py:367
  (9 shorter events, 0.1 us)
Async XLA Ops:
  0.6 9.6 %collective-permute-start.2 = (bf16[384,512]{1,0:T(8,128)(2,1)}, bf16[384,512]{1,0:T(8,128)(2,1)S(1)}, u32[]{:S(2)}, u32[]{:S(2)}) collective-permute-start(bf16[384,512]{1,0:T(8,128)(2,1)} %bitcast.4), channel_id=1, source_target_pairs={{1,0},{0,1},{3,2},{2,3},{5,4},{4,5},{7,6},{6,7},{9,8},{8,9},{11,10... | collective-permute-start | bytes 1179656 | tf_op jit(solution)/shard_map/ppermute | solution.py:30
  1.1 15.8 %collective-permute-start.1 = (bf16[384,512]{1,0:T(8,128)(2,1)}, bf16[384,512]{1,0:T(8,128)(2,1)S(1)}, u32[]{:S(2)}, u32[]{:S(2)}) collective-permute-start(bf16[384,512]{1,0:T(8,128)(2,1)} %bitcast.5), channel_id=1, source_target_pairs={{0,14},{2,4},{4,2},{6,8},{8,6},{10,12},{12,10},{14,0},{1,15},{3,5}... | collective-permute-start | bytes 1179656 | tf_op jit(solution)/shard_map/ppermute | solution.py:35
  7.9 2.1 %collective-permute-start.3 = (bf16[16,512]{1,0:T(8,128)(2,1)S(1)}, bf16[16,512]{1,0:T(8,128)(2,1)S(1)}, u32[]{:S(2)}, u32[]{:S(2)}) collective-permute-start(bf16[16,512]{1,0:T(8,128)(2,1)S(1)} %get-tuple-element.31.first), channel_id=1, source_target_pairs={{1,0},{0,1},{3,2},{2,3},{5,4},{4,5},{7,6},{6,7},{9,8},{8,9},{11,10... | collective-permute-start | bytes 49160 | tf_op jit(solution)/shard_map/ppermute | solution.py:30
  8.1 18.0 %collective-permute-start = (bf16[384,512]{1,0:T(8,128)(2,1)}, bf16[384,512]{1,0:T(8,128)(2,1)S(1)}, u32[]{:S(2)}, u32[]{:S(2)}) collective-permute-start(bf16[384,512]{1,0:T(8,128)(2,1)} %bitcast.7), channel_id=1, source_target_pairs={{2,0},{0,2},{6,4},{4,6},{10,8},{8,10},{14,12},{12,14},{3,1},{1,3},... | collective-permute-start | bytes 1179656 | tf_op jit(solution)/shard_map/ppermute | solution.py:30
  10.0 7.5 %collective-permute-start.6 = (bf16[2,16,512]{2,1,0:T(8,128)(2,1)S(1)}, bf16[2,16,512]{2,1,0:T(8,128)(2,1)S(1)}, u32[]{:S(2)}, u32[]{:S(2)}) collective-permute-start(bf16[2,16,512]{2,1,0:T(8,128)(2,1)S(1)} %shard_map.97.special.first), channel_id=1, source_target_pairs={{4,0},{6,2},{0,4},{2,6},{12,8},{14,10},{8,12},{10,14},{5,1},{7,3},... | collective-permute-start | bytes 98312 | tf_op jit(solution)/shard_map/ppermute | solution.py:30
  17.0 2.1 %collective-permute-start.5 = (bf16[192,512]{1,0:T(8,128)(2,1)S(1)}, bf16[192,512]{1,0:T(8,128)(2,1)S(1)}, u32[]{:S(2)}, u32[]{:S(2)}) collective-permute-start(bf16[192,512]{1,0:T(8,128)(2,1)S(1)} %get-tuple-element.60.refs_0_), channel_id=1, source_target_pairs={{1,0},{0,1},{3,2},{2,3},{5,4},{4,5},{7,6},{6,7},{9,8},{8,9},{11,10... | collective-permute-start | bytes 589832 | tf_op jit(solution)/shard_map/ppermute | solution.py:30
  17.0 7.0 %collective-permute-start.4 = (bf16[192,512]{1,0:T(8,128)(2,1)S(1)}, bf16[192,512]{1,0:T(8,128)(2,1)S(1)}, u32[]{:S(2)}, u32[]{:S(2)}) collective-permute-start(bf16[192,512]{1,0:T(8,128)(2,1)S(1)} %get-tuple-element.61.refs_0_), channel_id=1, source_target_pairs={{1,0},{0,1},{3,2},{2,3},{5,4},{4,5},{7,6},{6,7},{9,8},{8,9},{11,10... | collective-permute-start | bytes 589832 | tf_op jit(solution)/shard_map/ppermute | solution.py:30
  17.6 6.4 %collective-permute-start.7 = (bf16[2,32,512]{2,1,0:T(8,128)(2,1)S(1)}, bf16[2,32,512]{2,1,0:T(8,128)(2,1)S(1)}, u32[]{:S(2)}, u32[]{:S(2)}) collective-permute-start(bf16[2,32,512]{2,1,0:T(8,128)(2,1)S(1)} %shard_map.101.first), channel_id=1, source_target_pairs={{8,0},{10,2},{12,4},{14,6},{0,8},{2,10},{4,12},{6,14},{9,1},{11,3}... | collective-permute-start | bytes 196616 | tf_op jit(solution)/shard_map/ppermute | solution.py:30
  24.0 5.0 %collective-permute-start.8 = (bf16[2,64,512]{2,1,0:T(8,128)(2,1)S(1)}, bf16[2,64,512]{2,1,0:T(8,128)(2,1)S(1)}, u32[]{:S(2)}, u32[]{:S(2)}) collective-permute-start(bf16[2,64,512]{2,1,0:T(8,128)(2,1)S(1)} %shard_map.102.first), channel_id=1, source_target_pairs={{2,0},{0,2},{6,4},{4,6},{10,8},{8,10},{14,12},{12,14},{3,1},{1,3},... | collective-permute-start | bytes 393224 | tf_op jit(solution)/shard_map/ppermute | solution.py:30
  26.1 2.9 %collective-permute-start.12 = (bf16[96,512]{1,0:T(8,128)(2,1)S(1)}, bf16[96,512]{1,0:T(8,128)(2,1)S(1)}, u32[]{:S(2)}, u32[]{:S(2)}) collective-permute-start(bf16[96,512]{1,0:T(8,128)(2,1)S(1)} %get-tuple-element.56.refs_3_), channel_id=1, source_target_pairs={{1,0},{0,1},{3,2},{2,3},{5,4},{4,5},{7,6},{6,7},{9,8},{8,9},{11,10... | collective-permute-start | bytes 294920 | tf_op jit(solution)/shard_map/ppermute | solution.py:30
  26.2 2.9 %collective-permute-start.11 = (bf16[96,512]{1,0:T(8,128)(2,1)S(1)}, bf16[96,512]{1,0:T(8,128)(2,1)S(1)}, u32[]{:S(2)}, u32[]{:S(2)}) collective-permute-start(bf16[96,512]{1,0:T(8,128)(2,1)S(1)} %get-tuple-element.57.refs_2_), channel_id=1, source_target_pairs={{1,0},{0,1},{3,2},{2,3},{5,4},{4,5},{7,6},{6,7},{9,8},{8,9},{11,10... | collective-permute-start | bytes 294920 | tf_op jit(solution)/shard_map/ppermute | solution.py:30
  26.7 2.4 %collective-permute-start.10 = (bf16[96,512]{1,0:T(8,128)(2,1)S(1)}, bf16[96,512]{1,0:T(8,128)(2,1)S(1)}, u32[]{:S(2)}, u32[]{:S(2)}) collective-permute-start(bf16[96,512]{1,0:T(8,128)(2,1)S(1)} %get-tuple-element.58.refs_1_), channel_id=1, source_target_pairs={{1,0},{0,1},{3,2},{2,3},{5,4},{4,5},{7,6},{6,7},{9,8},{8,9},{11,10... | collective-permute-start | bytes 294920 | tf_op jit(solution)/shard_map/ppermute | solution.py:30
  26.8 2.3 %collective-permute-start.9 = (bf16[96,512]{1,0:T(8,128)(2,1)S(1)}, bf16[96,512]{1,0:T(8,128)(2,1)S(1)}, u32[]{:S(2)}, u32[]{:S(2)}) collective-permute-start(bf16[96,512]{1,0:T(8,128)(2,1)S(1)} %get-tuple-element.59.refs_0_), channel_id=1, source_target_pairs={{1,0},{0,1},{3,2},{2,3},{5,4},{4,5},{7,6},{6,7},{9,8},{8,9},{11,10... | collective-permute-start | bytes 294920 | tf_op jit(solution)/shard_map/ppermute | solution.py:30
  35.0 1.8 %collective-permute-start.13 = (bf16[400,512]{1,0:T(8,128)(2,1)S(1)}, bf16[400,512]{1,0:T(8,128)(2,1)S(1)}, u32[]{:S(2)}, u32[]{:S(2)}) collective-permute-start(bf16[400,512]{1,0:T(8,128)(2,1)S(1)} %get-tuple-element.53), channel_id=1, source_target_pairs={{1,0},{0,1},{3,2},{2,3},{5,4},{4,5},{7,6},{6,7},{9,8},{8,9},{11,10... | collective-permute-start | bytes 1228808 | tf_op jit(solution)/shard_map/ppermute | solution.py:30

commit v15 on v14

--- a/solution.py
+++ b/solution.py
@@ -381,13 +381,13 @@
 
 
 def stack_kernel(first, second, out):
-    count = first.shape[1]
-    out[:, :count, :] = first[...]
-    out[:, count:, :] = second[...]
+    count = first.shape[0]
+    out[:count, :] = first[...]
+    out[count:, :] = second[...]
 
 
 def stacked(first, second, flops=0):
-    shape = jax.ShapeDtypeStruct((2, 2 * first.shape[1], first.shape[2]), first.dtype)
+    shape = jax.ShapeDtypeStruct((2 * first.shape[0], first.shape[1]), first.dtype)
     return call(stack_kernel, [shape], (first, second), flops=flops)[0]
 
 
@@ -444,11 +444,10 @@
             pltpu.SemaphoreType.DMA((5,)),
         ],
     )
-    bits = [1 << i for i in range(1, owner_count.bit_length() - 1)] + [1] if power else []
+    everywhere = specials
     (specials,) = call(pair_kernel, [bf16(2, special_block, width)], both(specials))
-    everywhere = specials
     if paired and power:
-        everywhere = stacked(specials, swapped(specials, "blk", bits[0]), FIRST)
+        everywhere = stacked(everywhere, swapped(everywhere, "blk", 1), FIRST)
     mask, weights = call(
         functools.partial(start_kernel, offsets, per_image, special_count, special_block),
         [
@@ -484,22 +483,24 @@
 
     if paired:
         far = after(crossed(patches, "blk"), state[0])
-        near = swapped(patches, "blk", 1)
+        near = swapped(after(own, mask), "blk", 1)
         if power:
             everywhere = after(everywhere, far)
-            for bit in bits[1:-2]:
+            bit = owner_count // 2
+            while bit > 4:
                 everywhere = stacked(everywhere, swapped(everywhere, "blk", bit))
-            arrived = swapped(everywhere, "blk", bits[-2])
+                bit //= 2
+            arrived = swapped(everywhere, "blk", bit)
         far = halved(far, state[0], per_image)
         state = later(stretches(1, per_image)[:1], far[:1], state)
         if power:
             everywhere = stacked(after(everywhere, state[0]), arrived)
-            arrived = swapped(everywhere, "blk", bits[-1])
+            arrived = swapped(everywhere, "blk", 2)
         state = later(stretches(1, per_image)[1:], far[1:], state)
         step = per_image // 2
         stretches, parts = stretches(2, step), halved(near, state[0], step)
         if power:
-            everywhere = stacked(everywhere, arrived)
+            everywhere = stacked(after(everywhere, state[0]), arrived)
     else:
         for i, offset in enumerate(offsets[1:]):
             parts = halved(shifted(patches, "blk", -offset), state[0], per_image)
@@ -507,8 +508,8 @@
                 state = later(stretches(i + 1, per_image), parts, state)
         stretches = stretches(len(offsets) - 1, per_image)
     if not (paired and power):
-        everywhere = lax.all_gather(specials, "blk", axis=1, tiled=True)
-    stretches, parts = stretches + [[(everywhere.shape[1], None)]], parts + [(everywhere, everywhere)]
+        everywhere = lax.all_gather(everywhere, "blk", axis=0, tiled=True)
+    stretches, parts = stretches + [[(everywhere.shape[0], None)]], parts + [both(everywhere)]
     kept, sent = call(
         functools.partial(last_kernel, stretches, real_rows),
         [f32(rows, width), bf16(rows, width)],

time: 37.9 us -> 37.7 us (level)
  waiting for transfers between devices: 9.89 us -> 8.49 us
  starting transfers between devices: 9.83 us -> 11.2 us
    ppermute x1, waiting for transfers between devices: 3.39 us -> 1.29 us  [crossed(): lax.ppermute(block, axis, [(i, (i + (-1 if i % 2 == 0 else 1)) % count) f...]
    ppermute x13 -> x14, starting transfers between devices: 4.23 us -> 5.58 us  [swapped(): return lax.ppermute(block, axis, [(i ^ bit, i) for i in range(count)])]
    ppermute x13 -> x14, waiting for transfers between devices: 6.51 us -> 7.2 us  [swapped(): return lax.ppermute(block, axis, [(i ^ bit, i) for i in range(count)])]
  transfers between devices with their start and end apart: 14 -> 15, of which waited for: 4 -> 10; matrix products, arithmetic and copies ran while one was open for 0% -> 0% of each run, Pallas kernels for 28% -> 28%
where the time goes in v15:
time: 37.7 us; the launch traced here: 37.5 us
  Pallas kernels  17 us (45%)
  starting transfers between devices  11.2 us (30%)
  waiting for transfers between devices  8.49 us (23%)
  between operations  0.74 us (2%)
    pallas_call x11, Pallas kernels, call(): pl.pallas_call(kernel, out_shape=out_shape, in_specs=in_specs or [VMEM] *...  17 us
    ppermute x14, waiting for transfers between devices, swapped(): return lax.ppermute(block, axis, [(i ^ bit, i) for i in range(count)])  7.2 us
    ppermute x1, starting transfers between devices, crossed(): lax.ppermute(block, axis, [(i, (i + (-1 if i % 2 == 0 else 1)) % count) f...  5.6 us
    ppermute x14, starting transfers between devices, swapped(): return lax.ppermute(block, axis, [(i ^ bit, i) for i in range(count)])  5.58 us
    ppermute x1, waiting for transfers between devices, crossed(): lax.ppermute(block, axis, [(i, (i + (-1 if i % 2 == 0 else 1)) % count) f...  1.29 us
  transfers between devices with their start and end apart: 15, of which 10 were waited for; matrix products, arithmetic and copies ran while one was open for 0% of the time, Pallas kernels for 28%

profile of v15, /device:TPU:0, one launch (start us, length us, event | category | flops | bytes accessed | tf_op | source)
XLA Modules:
  0.0 37.5 jit_solution(14770196460515448434)
XLA Ops:
  0.6 0.5 %collective-permute-start.2 = (bf16[384,512]{1,0:T(8,128)(2,1)}, bf16[384,512]{1,0:T(8,128)(2,1)S(1)}, u32[]{:S(2)}, u32[]{:S(2)}) collective-permute-start(bf16[384,512]{1,0:T(8,128)(2,1)} %bitcast.4), channel_id=1, source_target_pairs={{1,0},{0,1},{3,2},{2,3},{5,4},{4,5},{7,6},{6,7},{9,8},{8,9},{11,10... | collective-permute-start | bytes 1179656 | tf_op jit(solution)/shard_map/ppermute | solution.py:30
  1.1 5.6 %collective-permute-start.1 = (bf16[384,512]{1,0:T(8,128)(2,1)}, bf16[384,512]{1,0:T(8,128)(2,1)S(1)}, u32[]{:S(2)}, u32[]{:S(2)}) collective-permute-start(bf16[384,512]{1,0:T(8,128)(2,1)} %bitcast.5), channel_id=1, source_target_pairs={{0,14},{2,4},{4,2},{6,8},{8,6},{10,12},{12,10},{14,0},{1,15},{3,5}... | collective-permute-start | bytes 1179656 | tf_op jit(solution)/shard_map/ppermute | solution.py:35
  6.8 1.1 %shard_map.96 = (bf16[16,512]{1,0:T(8,128)(2,1)S(1)}, bf16[384,512]{1,0:T(8,128)(2,1)S(1)}) custom-call(s32[2]{0:T(128)} %frame_order.1, bf16[5,2,512]{2,1,0:T(2,128)(2,1)} %bitcast.7, bf16[5,1024]{1,0:T(8,128)(2,1)} %role_first.1, bf16[5,1024]{1,0:T(8,128)(2,1)} %role_rest.1, bf16[384,512]{1,0:T(8,128)(2,1)} %bitcast.6), custom_call_target="tpu_custom_call" | custom-call | tf_op jit(solution)/shard_map/pallas_call | solution.py:367
  7.9 0.2 collective-permute-start.3
  8.1 1.9 %shard_map.95 = (f32[8,512]{1,0:T(8,128)S(1)}, bf16[3,1024,512]{2,1,0:T(8,128)(2,1)S(1)}) custom-call(s32[2,16]{1,0:T(2,128)} %covisible.1, bf16[3,1024,512]{2,1,0:T(8,128)(2,1)} %w_qkv.1), custom_call_target="tpu_custom_call" | custom-call | tf_op jit(solution)/shard_map/pallas_call | solution.py:367
  10.0 2.1 %collective-permute-start = (bf16[384,512]{1,0:T(8,128)(2,1)S(1)}, bf16[384,512]{1,0:T(8,128)(2,1)S(1)}, u32[]{:S(2)}, u32[]{:S(2)}) collective-permute-start(bf16[384,512]{1,0:T(8,128)(2,1)S(1)} %get-tuple-element.33.own), channel_id=1, source_target_pairs={{2,0},{0,2},{6,4},{4,6},{10,8},{8,10},{14,12},{12,14},{3,1},{1,3},... | collective-permute-start | bytes 1179656 | tf_op jit(solution)/shard_map/ppermute | solution.py:30
  12.1 0.0 collective-permute-done.3.second
  12.1 0.0 collective-permute-done.2.other
  12.1 3.4 %shard_map.98 = (bf16[4,128,768]{2,1,0:T(8,128)(2,1)S(1)}, bf16[512,128]{1,0:T(8,128)(2,1)S(1)}, f32[8,768]{1,0:T(8,128)S(1)}, f32[8,768]{1,0:T(8,128)S(1)}, f32...) custom-call(f32[8,512]{1,0:T(8,128)S(1)} %get-tuple-element.31.mask, bf16[384,512]{1,0:T(8,128)(2,1)S(1)} %get-tuple-element.33.own, ...), custom_call_target="tpu_custom_call" | custom-call | tf_op jit(solution)/shard_map/pallas_call | solution.py:367
  15.5 1.3 %collective-permute-done.1 = bf16[384,512]{1,0:T(8,128)(2,1)S(1)} collective-permute-done((bf16[384,512]{1,0:T(8,128)(2,1)}, bf16[384,512]{1,0:T(8,128)(2,1)S(1)}, u32[]{:S(2)}, u32[]{:S(2)}) %collective-permute-start.1) | collective-permute-done | bytes 393248 | tf_op jit(solution)/shard_map/ppermute | solution.py:35
  16.8 0.1 collective-permute-start.5
  16.9 0.5 %collective-permute-start.4 = (bf16[192,512]{1,0:T(8,128)(2,1)S(1)}, bf16[192,512]{1,0:T(8,128)(2,1)S(1)}, u32[]{:S(2)}, u32[]{:S(2)}) collective-permute-start(bf16[192,512]{1,0:T(8,128)(2,1)S(1)} %get-tuple-element.65.refs_0_), channel_id=1, source_target_pairs={{1,0},{0,1},{3,2},{2,3},{5,4},{4,5},{7,6},{6,7},{9,8},{8,9},{11,10... | collective-permute-start | bytes 589832 | tf_op jit(solution)/shard_map/ppermute | solution.py:30
  17.4 0.7 %collective-permute-start.7 = (bf16[32,512]{1,0:T(8,128)(2,1)S(1)}, bf16[32,512]{1,0:T(8,128)(2,1)S(1)}, u32[]{:S(2)}, u32[]{:S(2)}) collective-permute-start(bf16[32,512]{1,0:T(8,128)(2,1)S(1)} %shard_map.101.first), channel_id=1, source_target_pairs={{8,0},{10,2},{12,4},{14,6},{0,8},{2,10},{4,12},{6,14},{9,1},{11,3}... | collective-permute-start | bytes 98312 | tf_op jit(solution)/shard_map/ppermute | solution.py:30
  18.1 0.2 collective-permute-done.5.refs_1_
  18.3 2.0 %shard_map.99 = (f32[8,768]{1,0:T(8,128)S(1)}, f32[8,768]{1,0:T(8,128)S(1)}, f32[4,64,768]{2,1,0:T(8,128)S(1)}, f32[512,128]{1,0:T(8,128)S(1)}) custom-call(f32[8,512]{1,0:T(8,128)S(1)} %get-tuple-element.31.mask, bf16[192,512]{1,0:T(8,128)(2,1)S(1)} %get-tuple-element.64.refs_0_, bf16[192,512]{1,0:T(8,128)(2,1)S(1)} %collective-permute-done.5.refs_1_, ...), custom_call_target="tpu_custom_call" | custom-call | tf_op jit(solution)/shard_map/pallas_call | solution.py:367
  20.3 1.9 %collective-permute-done.7.second = bf16[32,512]{1,0:T(8,128)(2,1)S(1)} collective-permute-done((bf16[32,512]{1,0:T(8,128)(2,1)S(1)}, bf16[32,512]{1,0:T(8,128)(2,1)S(1)}, u32[]{:S(2)}, u32[]{:S(2)}) %collective-permute-start.7) | collective-permute-done | bytes 32800 | tf_op jit(solution)/shard_map/ppermute | solution.py:30
  22.2 2.0 %shard_map.100 = (f32[8,768]{1,0:T(8,128)S(1)}, f32[8,768]{1,0:T(8,128)S(1)}, f32[4,64,768]{2,1,0:T(8,128)S(1)}, f32[512,128]{1,0:T(8,128)S(1)}) custom-call(f32[8,512]{1,0:T(8,128)S(1)} %get-tuple-element.31.mask, bf16[192,512]{1,0:T(8,128)(2,1)S(1)} %get-tuple-element.65.refs_0_, bf16[192,512]{1,0:T(8,128)(2,1)S(1)} %collective-permute-done.4.refs_1_, ...), custom_call_target="tpu_custom_call" | custom-call | tf_op jit(solution)/shard_map/pallas_call | solution.py:367
  24.2 1.2 %collective-permute-done = bf16[384,512]{1,0:T(8,128)(2,1)S(1)} collective-permute-done((bf16[384,512]{1,0:T(8,128)(2,1)S(1)}, bf16[384,512]{1,0:T(8,128)(2,1)S(1)}, u32[]{:S(2)}, u32[]{:S(2)}) %collective-permute-start) | collective-permute-done | bytes 393248 | tf_op jit(solution)/shard_map/ppermute | solution.py:30
  25.4 1.0 %collective-permute-done.8.second = bf16[64,512]{1,0:T(8,128)(2,1)S(1)} collective-permute-done((bf16[64,512]{1,0:T(8,128)(2,1)S(1)}, bf16[64,512]{1,0:T(8,128)(2,1)S(1)}, u32[]{:S(2)}, u32[]{:S(2)}) %collective-permute-start.8) | collective-permute-done | bytes 65568 | tf_op jit(solution)/shard_map/ppermute | solution.py:30
  26.5 0.1 collective-permute-start.13
  26.6 0.6 %collective-permute-start.12 = (bf16[96,512]{1,0:T(8,128)(2,1)S(1)}, bf16[96,512]{1,0:T(8,128)(2,1)S(1)}, u32[]{:S(2)}, u32[]{:S(2)}) collective-permute-start(bf16[96,512]{1,0:T(8,128)(2,1)S(1)} %get-tuple-element.60.refs_3_), channel_id=1, source_target_pairs={{1,0},{0,1},{3,2},{2,3},{5,4},{4,5},{7,6},{6,7},{9,8},{8,9},{11,10... | collective-permute-start | bytes 294920 | tf_op jit(solution)/shard_map/ppermute | solution.py:30
  27.2 0.1 collective-permute-start.11
  27.2 0.4 %collective-permute-start.10 = (bf16[96,512]{1,0:T(8,128)(2,1)S(1)}, bf16[96,512]{1,0:T(8,128)(2,1)S(1)}, u32[]{:S(2)}, u32[]{:S(2)}) collective-permute-start(bf16[96,512]{1,0:T(8,128)(2,1)S(1)} %get-tuple-element.62.refs_1_), channel_id=1, source_target_pairs={{1,0},{0,1},{3,2},{2,3},{5,4},{4,5},{7,6},{6,7},{9,8},{8,9},{11,10... | collective-permute-start | bytes 294920 | tf_op jit(solution)/shard_map/ppermute | solution.py:30
  27.7 0.1 collective-permute-start.9
  27.8 0.4 collective-permute-done.12.refs_8_
  28.1 0.4 collective-permute-done.11.refs_7_
  28.5 0.2 collective-permute-done.10.refs_6_
  28.6 0.4 collective-permute-done.9.refs_5_
  29.0 5.9 %shard_map.104 = (f32[400,512]{1,0:T(8,128)S(1)}, bf16[400,512]{1,0:T(8,128)(2,1)S(1)}) custom-call(f32[8,512]{1,0:T(8,128)S(1)} %get-tuple-element.31.mask, bf16[96,512]{1,0:T(8,128)(2,1)S(1)} %get-tuple-element.63.refs_0_, bf16[96,512]{1,0:T(8,128)(2,1)S(1)} %get-tuple-element.62.refs_1_, bf16[96,512]{1,0:T(8,128)(2,1)S(1)} %get-tuple-element.61.refs_2_, ...), custom_call_target="tpu_custom_call" | custom-call | tf_op jit(solution)/shard_map/pallas_call | solution.py:367
  34.9 0.2 collective-permute-start.14
  35.1 1.6 %collective-permute-done.14.received = bf16[400,512]{1,0:T(8,128)(2,1)S(1)} collective-permute-done((bf16[400,512]{1,0:T(8,128)(2,1)S(1)}, bf16[400,512]{1,0:T(8,128)(2,1)S(1)}, u32[]{:S(2)}, u32[]{:S(2)}) %collective-permute-start.14) | collective-permute-done | bytes 409632 | tf_op jit(solution)/shard_map/ppermute | solution.py:30
  36.7 0.8 %shard_map.105 = (bf16[384,512]{1,0:T(8,128)(2,1)}, bf16[5,2,512]{2,1,0:T(2,128)(2,1)}) custom-call(f32[400,512]{1,0:T(8,128)S(1)} %get-tuple-element.56.kept, bf16[400,512]{1,0:T(8,128)(2,1)S(1)} %collective-permute-done.14.received), custom_call_target="tpu_custom_call" | custom-call | tf_op jit(solution)/shard_map/pallas_call | solution.py:367
  (11 shorter events, 0.1 us)
Async XLA Ops:
  0.6 11.5 %collective-permute-start.2 = (bf16[384,512]{1,0:T(8,128)(2,1)}, bf16[384,512]{1,0:T(8,128)(2,1)S(1)}, u32[]{:S(2)}, u32[]{:S(2)}) collective-permute-start(bf16[384,512]{1,0:T(8,128)(2,1)} %bitcast.4), channel_id=1, source_target_pairs={{1,0},{0,1},{3,2},{2,3},{5,4},{4,5},{7,6},{6,7},{9,8},{8,9},{11,10... | collective-permute-start | bytes 1179656 | tf_op jit(solution)/shard_map/ppermute | solution.py:30
  1.1 15.6 %collective-permute-start.1 = (bf16[384,512]{1,0:T(8,128)(2,1)}, bf16[384,512]{1,0:T(8,128)(2,1)S(1)}, u32[]{:S(2)}, u32[]{:S(2)}) collective-permute-start(bf16[384,512]{1,0:T(8,128)(2,1)} %bitcast.5), channel_id=1, source_target_pairs={{0,14},{2,4},{4,2},{6,8},{8,6},{10,12},{12,10},{14,0},{1,15},{3,5}... | collective-permute-start | bytes 1179656 | tf_op jit(solution)/shard_map/ppermute | solution.py:35
  7.9 4.2 %collective-permute-start.3 = (bf16[16,512]{1,0:T(8,128)(2,1)S(1)}, bf16[16,512]{1,0:T(8,128)(2,1)S(1)}, u32[]{:S(2)}, u32[]{:S(2)}) collective-permute-start(bf16[16,512]{1,0:T(8,128)(2,1)S(1)} %get-tuple-element.34.first), channel_id=1, source_target_pairs={{1,0},{0,1},{3,2},{2,3},{5,4},{4,5},{7,6},{6,7},{9,8},{8,9},{11,10... | collective-permute-start | bytes 49160 | tf_op jit(solution)/shard_map/ppermute | solution.py:30
  8.1 9.3 %collective-permute-start.6 = (bf16[16,512]{1,0:T(8,128)(2,1)S(1)}, bf16[16,512]{1,0:T(8,128)(2,1)S(1)}, u32[]{:S(2)}, u32[]{:S(2)}) collective-permute-start(bf16[16,512]{1,0:T(8,128)(2,1)S(1)} %get-tuple-element.34.first), channel_id=1, source_target_pairs={{2,0},{0,2},{6,4},{4,6},{10,8},{8,10},{14,12},{12,14},{3,1},{1,3},... | collective-permute-start | bytes 49160 | tf_op jit(solution)/shard_map/ppermute | solution.py:30
  10.0 15.4 %collective-permute-start = (bf16[384,512]{1,0:T(8,128)(2,1)S(1)}, bf16[384,512]{1,0:T(8,128)(2,1)S(1)}, u32[]{:S(2)}, u32[]{:S(2)}) collective-permute-start(bf16[384,512]{1,0:T(8,128)(2,1)S(1)} %get-tuple-element.33.own), channel_id=1, source_target_pairs={{2,0},{0,2},{6,4},{4,6},{10,8},{8,10},{14,12},{12,14},{3,1},{1,3},... | collective-permute-start | bytes 1179656 | tf_op jit(solution)/shard_map/ppermute | solution.py:30
  16.8 1.5 %collective-permute-start.5 = (bf16[192,512]{1,0:T(8,128)(2,1)S(1)}, bf16[192,512]{1,0:T(8,128)(2,1)S(1)}, u32[]{:S(2)}, u32[]{:S(2)}) collective-permute-start(bf16[192,512]{1,0:T(8,128)(2,1)S(1)} %get-tuple-element.64.refs_0_), channel_id=1, source_target_pairs={{1,0},{0,1},{3,2},{2,3},{5,4},{4,5},{7,6},{6,7},{9,8},{8,9},{11,10... | collective-permute-start | bytes 589832 | tf_op jit(solution)/shard_map/ppermute | solution.py:30
  16.9 5.3 %collective-permute-start.4 = (bf16[192,512]{1,0:T(8,128)(2,1)S(1)}, bf16[192,512]{1,0:T(8,128)(2,1)S(1)}, u32[]{:S(2)}, u32[]{:S(2)}) collective-permute-start(bf16[192,512]{1,0:T(8,128)(2,1)S(1)} %get-tuple-element.65.refs_0_), channel_id=1, source_target_pairs={{1,0},{0,1},{3,2},{2,3},{5,4},{4,5},{7,6},{6,7},{9,8},{8,9},{11,10... | collective-permute-start | bytes 589832 | tf_op jit(solution)/shard_map/ppermute | solution.py:30
  17.4 4.8 %collective-permute-start.7 = (bf16[32,512]{1,0:T(8,128)(2,1)S(1)}, bf16[32,512]{1,0:T(8,128)(2,1)S(1)}, u32[]{:S(2)}, u32[]{:S(2)}) collective-permute-start(bf16[32,512]{1,0:T(8,128)(2,1)S(1)} %shard_map.101.first), channel_id=1, source_target_pairs={{8,0},{10,2},{12,4},{14,6},{0,8},{2,10},{4,12},{6,14},{9,1},{11,3}... | collective-permute-start | bytes 98312 | tf_op jit(solution)/shard_map/ppermute | solution.py:30
  22.2 4.3 %collective-permute-start.8 = (bf16[64,512]{1,0:T(8,128)(2,1)S(1)}, bf16[64,512]{1,0:T(8,128)(2,1)S(1)}, u32[]{:S(2)}, u32[]{:S(2)}) collective-permute-start(bf16[64,512]{1,0:T(8,128)(2,1)S(1)} %shard_map.102.first), channel_id=1, source_target_pairs={{4,0},{6,2},{0,4},{2,6},{12,8},{14,10},{8,12},{10,14},{5,1},{7,3},... | collective-permute-start | bytes 196616 | tf_op jit(solution)/shard_map/ppermute | solution.py:30
  26.5 2.5 %collective-permute-start.13 = (bf16[128,512]{1,0:T(8,128)(2,1)S(1)}, bf16[128,512]{1,0:T(8,128)(2,1)S(1)}, u32[]{:S(2)}, u32[]{:S(2)}) collective-permute-start(bf16[128,512]{1,0:T(8,128)(2,1)S(1)} %shard_map.103.refs_4_), channel_id=1, source_target_pairs={{1,0},{0,1},{3,2},{2,3},{5,4},{4,5},{7,6},{6,7},{9,8},{8,9},{11,10... | collective-permute-start | bytes 393224 | tf_op jit(solution)/shard_map/ppermute | solution.py:30
  26.6 1.5 %collective-permute-start.12 = (bf16[96,512]{1,0:T(8,128)(2,1)S(1)}, bf16[96,512]{1,0:T(8,128)(2,1)S(1)}, u32[]{:S(2)}, u32[]{:S(2)}) collective-permute-start(bf16[96,512]{1,0:T(8,128)(2,1)S(1)} %get-tuple-element.60.refs_3_), channel_id=1, source_target_pairs={{1,0},{0,1},{3,2},{2,3},{5,4},{4,5},{7,6},{6,7},{9,8},{8,9},{11,10... | collective-permute-start | bytes 294920 | tf_op jit(solution)/shard_map/ppermute | solution.py:30
  27.2 1.3 %collective-permute-start.11 = (bf16[96,512]{1,0:T(8,128)(2,1)S(1)}, bf16[96,512]{1,0:T(8,128)(2,1)S(1)}, u32[]{:S(2)}, u32[]{:S(2)}) collective-permute-start(bf16[96,512]{1,0:T(8,128)(2,1)S(1)} %get-tuple-element.61.refs_2_), channel_id=1, source_target_pairs={{1,0},{0,1},{3,2},{2,3},{5,4},{4,5},{7,6},{6,7},{9,8},{8,9},{11,10... | collective-permute-start | bytes 294920 | tf_op jit(solution)/shard_map/ppermute | solution.py:30
  27.2 1.4 %collective-permute-start.10 = (bf16[96,512]{1,0:T(8,128)(2,1)S(1)}, bf16[96,512]{1,0:T(8,128)(2,1)S(1)}, u32[]{:S(2)}, u32[]{:S(2)}) collective-permute-start(bf16[96,512]{1,0:T(8,128)(2,1)S(1)} %get-tuple-element.62.refs_1_), channel_id=1, source_target_pairs={{1,0},{0,1},{3,2},{2,3},{5,4},{4,5},{7,6},{6,7},{9,8},{8,9},{11,10... | collective-permute-start | bytes 294920 | tf_op jit(solution)/shard_map/ppermute | solution.py:30
  27.7 1.3 %collective-permute-start.9 = (bf16[96,512]{1,0:T(8,128)(2,1)S(1)}, bf16[96,512]{1,0:T(8,128)(2,1)S(1)}, u32[]{:S(2)}, u32[]{:S(2)}) collective-permute-start(bf16[96,512]{1,0:T(8,128)(2,1)S(1)} %get-tuple-element.63.refs_0_), channel_id=1, source_target_pairs={{1,0},{0,1},{3,2},{2,3},{5,4},{4,5},{7,6},{6,7},{9,8},{8,9},{11,10... | collective-permute-start | bytes 294920 | tf_op jit(solution)/shard_map/ppermute | solution.py:30
  34.9 1.8 %collective-permute-start.14 = (bf16[400,512]{1,0:T(8,128)(2,1)S(1)}, bf16[400,512]{1,0:T(8,128)(2,1)S(1)}, u32[]{:S(2)}, u32[]{:S(2)}) collective-permute-start(bf16[400,512]{1,0:T(8,128)(2,1)S(1)} %get-tuple-element.57), channel_id=1, source_target_pairs={{1,0},{0,1},{3,2},{2,3},{5,4},{4,5},{7,6},{6,7},{9,8},{8,9},{11,10... | collective-permute-start | bytes 1228808 | tf_op jit(solution)/shard_map/ppermute | solution.py:30

commit v16 on v12

--- a/solution.py
+++ b/solution.py
@@ -81,7 +81,8 @@
 
 
 def start_kernel(
-    offsets, per_image, special_count, special_total, covisible, w_qkv, mask_out, weights_out, seen, copied
+    offsets, per_image, special_count, special_total, covisible, special, other_special, w_qkv,
+    mask_out, weights_out, pairs_out, seen, copied,
 ):
     images = covisible.shape[0]
     patch_total = images * per_image
@@ -108,8 +109,12 @@
                 hidden = seen[a, owner_at(offset) * images + b] <= 0
                 row = jnp.where((image == a) & hidden, -jnp.inf, row)
             mask_out[i * images + b : i * images + b + 1, :] = row
+    rows = jnp.concatenate([special[...], other_special[...]], axis=1)
+    width = weights_out.shape[2]
     for copy in copies[1:]:
         copy.wait()
+    for i in range(2):
+        pairs_out[:, i * width : (i + 1) * width] = product(rows, weights_out[i + 1]).astype(jnp.bfloat16)
 
 
 def projector(own, other, weights):
@@ -237,12 +242,12 @@
 
 
 def first_kernel(
-    images, mask, own, other, special, weights, queries_out, special_out, *state_out
+    images, mask, own, other, special, other_special, weights, queries_out, special_out, *state_out
 ):
     patch_total = own.shape[0]
     columns = projector(
-        jnp.concatenate([own[...], special[0]], axis=0),
-        jnp.concatenate([other[...], special[1]], axis=0),
+        jnp.concatenate([own[...], special[...]], axis=0),
+        jnp.concatenate([other[...], other_special[...]], axis=0),
         weights,
     )
     pairs = queries_out.shape[0]
@@ -289,13 +294,20 @@
 
 def joined(stretches, mask, refs):
     count = len(stretches)
-    flat = lambda ref, i: ref[i] if len(ref.shape) == 3 else ref[...]
-    own = jnp.concatenate([flat(ref, 0) for ref in refs[:count]], axis=0)
-    other = jnp.concatenate([flat(ref, 1) for ref in refs[count : 2 * count]], axis=0)
-    masks = [
-        (rows, None if i is None else mask[i : i + 1, :]) for part in stretches for rows, i in part
-    ]
+    own = jnp.concatenate([ref[...] for ref in refs[:count]], axis=0)
+    other = jnp.concatenate([ref[...] for ref in refs[count : 2 * count]], axis=0)
+    masks = [(rows, mask[i : i + 1, :]) for part in stretches for rows, i in part]
     return own, other, masks, refs[2 * count :]
+
+
+def given(pairs):
+    width = pairs.shape[1] // 2
+
+    def columns(which, quad):
+        first = (which - 1) * width + quad * QUAD
+        return pairs[:, first : first + QUAD]
+
+    return columns
 
 
 def later_kernel(stretches, special_real, mask, *refs):
@@ -311,18 +323,19 @@
         state.put(*result)
 
 
-def last_kernel(stretches, special_real, mask, *refs):
-    own, other, masks, refs = joined(stretches, mask, refs)
-    weights, queries, special_queries = refs[:3]
-    state_in = refs[3:7]
-    w_out, kept_out, sent_out, w_here, copied = refs[7:]
+def last_kernel(
+    special_real, mask, special_pairs, queries, special_queries, *refs
+):
+    state_in = refs[:4]
+    w_out, kept_out, sent_out, w_here, copied = refs[4:]
+    masks = [(special_pairs.shape[0], None)]
     copy = pltpu.make_async_copy(w_out, w_here, copied)
     copy.start()
     pairs, rows = queries.shape[0], queries.shape[2] // 2
     columns, out, special = [], None, None
     sides = halves(kept_out.shape[1])
     for pair, sub, _, total, weight in attend_all(
-        projector(own, other, weights), masks, lambda pair: queries[pair], lambda: special_queries[...],
+        given(special_pairs), masks, lambda pair: queries[pair], lambda: special_queries[...],
         State(rows, state_in), pairs, rows, special_real,
     ):
         if pair == 0 and sub == 0:
@@ -375,19 +388,14 @@
     )(*operands)
 
 
-def pair_kernel(first, second, out):
-    out[0] = first[...]
-    out[1] = second[...]
-
-
 def stack_kernel(first, second, out):
-    count = first.shape[1]
-    out[:, :count, :] = first[...]
-    out[:, count:, :] = second[...]
+    count = first.shape[0]
+    out[:count, :] = first[...]
+    out[count:, :] = second[...]
 
 
 def stacked(first, second, flops=0):
-    shape = jax.ShapeDtypeStruct((2, 2 * first.shape[1], first.shape[2]), first.dtype)
+    shape = jax.ShapeDtypeStruct((2 * first.shape[0], first.shape[1]), first.dtype)
     return call(stack_kernel, [shape], (first, second), flops=flops)[0]
 
 
@@ -444,25 +452,24 @@
             pltpu.SemaphoreType.DMA((5,)),
         ],
     )
-    bits = [1 << i for i in range(1, owner_count.bit_length() - 1)] + [1] if power else []
-    (specials,) = call(pair_kernel, [bf16(2, special_block, width)], both(specials))
-    everywhere = specials
-    if paired and power:
-        everywhere = stacked(specials, swapped(specials, "blk", bits[0]), FIRST)
-    mask, weights = call(
+    specials = both(specials)
+    mask, weights, everywhere = call(
         functools.partial(start_kernel, offsets, per_image, special_count, special_block),
         [
             f32(mask_rows, patch_total + heads * special_block),
             bf16(*w_qkv.shape),
+            bf16(special_block, 2 * width),
         ],
-        (covisible, w_qkv),
-        in_specs=[HBM] * 2,
+        (covisible, *specials, w_qkv),
+        in_specs=[HBM, VMEM, VMEM, HBM],
         scratch=[pltpu.SMEM(covisible.shape, jnp.int32), pltpu.SemaphoreType.DMA((1 + 6,))],
     )
+    if paired and power:
+        everywhere = stacked(everywhere, swapped(everywhere, "blk", 1), FIRST)
     queries, special_queries, *state = call(
         functools.partial(first_kernel, images),
         [bf16(pairs, PAIR, 2 * patch_total), bf16(width, heads * special_block), *state_shape],
-        (mask, own, swapped(patches, "head", 1), specials, weights),
+        (mask, own, swapped(patches, "head", 1), *specials, weights),
     )
     fixed = (weights, queries, special_queries)
 
@@ -482,16 +489,18 @@
     stretches = lambda owner: [[image] for image in image_rows(owner)]
     if paired:
         far = after(crossed(patches, "blk"), state[0])
-        near = swapped(patches, "blk", 1)
+        near = swapped(after(own, mask), "blk", 1)
         if power:
             everywhere = after(everywhere, far)
-            for bit in bits[1:-2]:
+            bit = owner_count // 2
+            while bit > 4:
                 everywhere = stacked(everywhere, swapped(everywhere, "blk", bit))
-            arrived = swapped(everywhere, "blk", bits[-2])
+                bit //= 2
+            arrived = swapped(everywhere, "blk", bit)
         state = later(stretches(1), halved(far, state[0]), state)
         if power:
             everywhere = stacked(after(everywhere, state[0]), arrived, FIRST)
-            arrived = swapped(everywhere, "blk", bits[-1])
+            arrived = swapped(everywhere, "blk", 2)
         state = later(stretches(2), halved(near, state[0]), state)
         if power:
             everywhere = stacked(after(everywhere, state[0]), arrived)
@@ -499,15 +508,12 @@
         for i, offset in enumerate(offsets[1:]):
             state = later(stretches(i + 1), halved(shifted(patches, "blk", -offset), state[0]), state)
     if not (paired and power):
-        everywhere = lax.all_gather(specials, "blk", axis=1, tiled=True)
-    stretches, parts = [[(everywhere.shape[1], None)]], [(everywhere, everywhere)]
+        everywhere = lax.all_gather(everywhere, "blk", axis=0, tiled=True)
     kept, sent = call(
-        functools.partial(last_kernel, stretches, real_rows),
+        functools.partial(last_kernel, real_rows),
         [f32(rows, width), bf16(rows, width)],
-        (
-            mask, *[part[0] for part in parts], *[part[1] for part in parts], *fixed, *state, w_out,
-        ),
-        in_specs=[VMEM] * (1 + 2 * len(parts) + len(fixed) + len(state)) + [HBM],
+        (mask, everywhere, queries, special_queries, *state, w_out),
+        in_specs=[VMEM] * (4 + len(state)) + [HBM],
         scratch=[pltpu.VMEM(w_out.shape, jnp.bfloat16), pltpu.SemaphoreType.DMA],
     )
     received = swapped(sent, "head", 1)

time: 37.6 us -> 37.9 us (level)
  starting transfers between devices: 9.33 us -> 10.4 us
  waiting for transfers between devices: 9.76 us -> 9.01 us
    ppermute x1, waiting for transfers between devices: 3.39 us -> 0.01 us  [crossed(): lax.ppermute(block, axis, [(i, (i + (-1 if i % 2 == 0 else 1)) % count) f...]
    ppermute x11, waiting for transfers between devices: 6.38 us -> 9.01 us  [swapped(): return lax.ppermute(block, axis, [(i ^ bit, i) for i in range(count)])]
    ppermute x11, starting transfers between devices: 3.72 us -> 4.8 us  [swapped(): return lax.ppermute(block, axis, [(i ^ bit, i) for i in range(count)])]
    pallas_call x11 -> x10, Pallas kernels: 17.5 us -> 17.5 us  [call(): pl.pallas_call(kernel, out_shape=out_shape, in_specs=in_specs or [VMEM] *...]
  transfers between devices with their start and end apart: 12 -> 12, of which waited for: 6 -> 8; matrix products, arithmetic and copies ran while one was open for 0% -> 0% of each run, Pallas kernels for 35% -> 36%
where the time goes in v16:
time: 37.9 us; the launch traced here: 37.7 us
  Pallas kernels  17.5 us (46%)
  starting transfers between devices  10.4 us (27%)
  waiting for transfers between devices  9.01 us (24%)
  between operations  0.75 us (2%)
    pallas_call x10, Pallas kernels, call(): pl.pallas_call(kernel, out_shape=out_shape, in_specs=in_specs or [VMEM] *...  17.5 us
    ppermute x11, waiting for transfers between devices, swapped(): return lax.ppermute(block, axis, [(i ^ bit, i) for i in range(count)])  9.01 us
    ppermute x1, starting transfers between devices, crossed(): lax.ppermute(block, axis, [(i, (i + (-1 if i % 2 == 0 else 1)) % count) f...  5.6 us
    ppermute x11, starting transfers between devices, swapped(): return lax.ppermute(block, axis, [(i ^ bit, i) for i in range(count)])  4.8 us
  transfers between devices with their start and end apart: 12, of which 8 were waited for; matrix products, arithmetic and copies ran while one was open for 0% of the time, Pallas kernels for 36%

profile of v16, /device:TPU:0, one launch (start us, length us, event | category | flops | bytes accessed | tf_op | source)
XLA Modules:
  0.0 37.7 jit_solution(6710800188076496062)
XLA Ops:
  0.6 0.5 %collective-permute-start.3 = (bf16[384,512]{1,0:T(8,128)(2,1)}, bf16[384,512]{1,0:T(8,128)(2,1)S(1)}, u32[]{:S(2)}, u32[]{:S(2)}) collective-permute-start(bf16[384,512]{1,0:T(8,128)(2,1)} %bitcast.4), channel_id=1, source_target_pairs={{1,0},{0,1},{3,2},{2,3},{5,4},{4,5},{7,6},{6,7},{9,8},{8,9},{11,10... | collective-permute-start | bytes 1179656 | tf_op jit(solution)/shard_map/ppermute | solution.py:30
  1.1 5.6 %collective-permute-start.2 = (bf16[384,512]{1,0:T(8,128)(2,1)}, bf16[384,512]{1,0:T(8,128)(2,1)S(1)}, u32[]{:S(2)}, u32[]{:S(2)}) collective-permute-start(bf16[384,512]{1,0:T(8,128)(2,1)} %bitcast.5), channel_id=1, source_target_pairs={{0,14},{2,4},{4,2},{6,8},{8,6},{10,12},{12,10},{14,0},{1,15},{3,5}... | collective-permute-start | bytes 1179656 | tf_op jit(solution)/shard_map/ppermute | solution.py:35
  6.8 1.1 %shard_map.95 = (bf16[16,512]{1,0:T(8,128)(2,1)S(1)}, bf16[384,512]{1,0:T(8,128)(2,1)S(1)}) custom-call(s32[2]{0:T(128)} %frame_order.1, bf16[5,2,512]{2,1,0:T(2,128)(2,1)} %bitcast.7, bf16[5,1024]{1,0:T(8,128)(2,1)} %role_first.1, bf16[5,1024]{1,0:T(8,128)(2,1)} %role_rest.1, bf16[384,512]{1,0:T(8,128)(2,1)} %bitcast.6), custom_call_target="tpu_custom_call" | custom-call | tf_op jit(solution)/shard_map/pallas_call | solution.py:380
  7.9 0.2 collective-permute-start
  8.1 1.0 %collective-permute-done.other_special = bf16[16,512]{1,0:T(8,128)(2,1)S(1)} collective-permute-done((bf16[16,512]{1,0:T(8,128)(2,1)S(1)}, bf16[16,512]{1,0:T(8,128)(2,1)S(1)}, u32[]{:S(2)}, u32[]{:S(2)}) %collective-permute-start) | collective-permute-done | bytes 16416 | tf_op jit(solution)/shard_map/ppermute | solution.py:30
  9.1 2.3 %shard_map.96 = (f32[8,512]{1,0:T(8,128)S(1)}, bf16[3,1024,512]{2,1,0:T(8,128)(2,1)S(1)}, bf16[16,1024]{1,0:T(8,128)(2,1)S(1)}) custom-call(s32[2,16]{1,0:T(2,128)} %covisible.1, bf16[16,512]{1,0:T(8,128)(2,1)S(1)} %get-tuple-element.32.special, bf16[16,512]{1,0:T(8,128)(2,1)S(1)} %collective-permute-done.other_special, bf16[3,1024,512]{2,1,0:T(8,128)(2,1)} %w_qkv.1), custom_call_target="tpu_custom_call" | custom-call | tf_op jit(solution)/shard_map/pallas_call | solution.py:380
  11.4 0.1 collective-permute-start.1
  11.5 2.0 %collective-permute-start.7 = (bf16[384,512]{1,0:T(8,128)(2,1)S(1)}, bf16[384,512]{1,0:T(8,128)(2,1)S(1)}, u32[]{:S(2)}, u32[]{:S(2)}) collective-permute-start(bf16[384,512]{1,0:T(8,128)(2,1)S(1)} %get-tuple-element.48.own), channel_id=1, source_target_pairs={{2,0},{0,2},{6,4},{4,6},{10,8},{8,10},{14,12},{12,14},{3,1},{1,3},... | collective-permute-start | bytes 1179656 | tf_op jit(solution)/shard_map/ppermute | solution.py:30
  13.5 0.0 collective-permute-done.3.other
  13.5 3.4 %shard_map.98 = (bf16[4,128,768]{2,1,0:T(8,128)(2,1)S(1)}, bf16[512,128]{1,0:T(8,128)(2,1)S(1)}, f32[8,768]{1,0:T(8,128)S(1)}, f32[8,768]{1,0:T(8,128)S(1)}, f32...) custom-call(f32[8,512]{1,0:T(8,128)S(1)} %get-tuple-element.33.mask, bf16[384,512]{1,0:T(8,128)(2,1)S(1)} %get-tuple-element.48.own, ...), custom_call_target="tpu_custom_call" | custom-call | tf_op jit(solution)/shard_map/pallas_call | solution.py:380
  16.9 0.0 collective-permute-done.2
  16.9 0.1 collective-permute-start.4
  17.0 0.5 %collective-permute-start.5 = (bf16[192,512]{1,0:T(8,128)(2,1)S(1)}, bf16[192,512]{1,0:T(8,128)(2,1)S(1)}, u32[]{:S(2)}, u32[]{:S(2)}) collective-permute-start(bf16[192,512]{1,0:T(8,128)(2,1)S(1)} %get-tuple-element.64.refs_1_), channel_id=1, source_target_pairs={{1,0},{0,1},{3,2},{2,3},{5,4},{4,5},{7,6},{6,7},{9,8},{8,9},{11,10... | collective-permute-start | bytes 589832 | tf_op jit(solution)/shard_map/ppermute | solution.py:30
  17.5 0.0 collective-permute-done.1.second
  17.5 0.7 %collective-permute-start.6 = (bf16[32,1024]{1,0:T(8,128)(2,1)S(1)}, bf16[32,1024]{1,0:T(8,128)(2,1)S(1)}, u32[]{:S(2)}, u32[]{:S(2)}) collective-permute-start(bf16[32,1024]{1,0:T(8,128)(2,1)S(1)} %shard_map.97.first), channel_id=1, source_target_pairs={{8,0},{10,2},{12,4},{14,6},{0,8},{2,10},{4,12},{6,14},{9,1},{11,3}... | collective-permute-start | bytes 196616 | tf_op jit(solution)/shard_map/ppermute | solution.py:30
  18.2 0.2 collective-permute-done.4.refs_2_
  18.4 0.3 collective-permute-done.5.refs_3_
  18.7 3.4 %shard_map.99 = (f32[8,768]{1,0:T(8,128)S(1)}, f32[8,768]{1,0:T(8,128)S(1)}, f32[4,64,768]{2,1,0:T(8,128)S(1)}, f32[512,128]{1,0:T(8,128)S(1)}) custom-call(f32[8,512]{1,0:T(8,128)S(1)} %get-tuple-element.33.mask, bf16[192,512]{1,0:T(8,128)(2,1)S(1)} %get-tuple-element.65.refs_0_, bf16[192,512]{1,0:T(8,128)(2,1)S(1)} %get-tuple-element.64.refs_1_, ...), custom_call_target="tpu_custom_call" | custom-call | tf_op jit(solution)/shard_map/pallas_call | solution.py:380
  22.1 3.7 %collective-permute-done.7 = bf16[384,512]{1,0:T(8,128)(2,1)S(1)} collective-permute-done((bf16[384,512]{1,0:T(8,128)(2,1)S(1)}, bf16[384,512]{1,0:T(8,128)(2,1)S(1)}, u32[]{:S(2)}, u32[]{:S(2)}) %collective-permute-start.7) | collective-permute-done | bytes 393248 | tf_op jit(solution)/shard_map/ppermute | solution.py:30
  25.8 0.1 collective-permute-start.8
  25.9 0.5 %collective-permute-start.9 = (bf16[192,512]{1,0:T(8,128)(2,1)S(1)}, bf16[192,512]{1,0:T(8,128)(2,1)S(1)}, u32[]{:S(2)}, u32[]{:S(2)}) collective-permute-start(bf16[192,512]{1,0:T(8,128)(2,1)S(1)} %get-tuple-element.62.refs_1_), channel_id=1, source_target_pairs={{1,0},{0,1},{3,2},{2,3},{5,4},{4,5},{7,6},{6,7},{9,8},{8,9},{11,10... | collective-permute-start | bytes 589832 | tf_op jit(solution)/shard_map/ppermute | solution.py:30
  26.4 0.0 collective-permute-done.6.second
  26.4 0.1 collective-permute-start.10
  26.5 0.8 %collective-permute-done.8.refs_2_ = bf16[192,512]{1,0:T(8,128)(2,1)S(1)} collective-permute-done((bf16[192,512]{1,0:T(8,128)(2,1)S(1)}, bf16[192,512]{1,0:T(8,128)(2,1)S(1)}, u32[]{:S(2)}, u32[]{:S(2)}) %collective-permute-start.8) | collective-permute-done | bytes 196640 | tf_op jit(solution)/shard_map/ppermute | solution.py:30
  27.3 0.3 collective-permute-done.9.refs_3_
  27.6 3.4 %shard_map.101 = (f32[8,768]{1,0:T(8,128)S(1)}, f32[8,768]{1,0:T(8,128)S(1)}, f32[4,64,768]{2,1,0:T(8,128)S(1)}, f32[512,128]{1,0:T(8,128)S(1)}) custom-call(f32[8,512]{1,0:T(8,128)S(1)} %get-tuple-element.33.mask, bf16[192,512]{1,0:T(8,128)(2,1)S(1)} %get-tuple-element.63.refs_0_, bf16[192,512]{1,0:T(8,128)(2,1)S(1)} %get-tuple-element.62.refs_1_, ...), custom_call_target="tpu_custom_call" | custom-call | tf_op jit(solution)/shard_map/pallas_call | solution.py:380
  31.0 0.9 %collective-permute-done.10.second = bf16[64,1024]{1,0:T(8,128)(2,1)S(1)} collective-permute-done((bf16[64,1024]{1,0:T(8,128)(2,1)S(1)}, bf16[64,1024]{1,0:T(8,128)(2,1)S(1)}, u32[]{:S(2)}, u32[]{:S(2)}) %collective-permute-start.10) | collective-permute-done | bytes 131104 | tf_op jit(solution)/shard_map/ppermute | solution.py:30
  32.0 3.0 %shard_map.103 = (f32[400,512]{1,0:T(8,128)S(1)}, bf16[400,512]{1,0:T(8,128)(2,1)S(1)}) custom-call(f32[8,512]{1,0:T(8,128)S(1)} %get-tuple-element.33.mask, bf16[128,1024]{1,0:T(8,128)(2,1)S(1)} %shard_map.102.special_pairs, bf16[4,128,768]{2,1,0:T(8,128)(2,1)S(1)} %get-tuple-element.41.refs_5_.queries, ...), custom_call_target="tpu_custom_call" | custom-call | tf_op jit(solution)/shard_map/pallas_call | solution.py:380
  35.0 0.1 collective-permute-start.11
  35.1 1.7 %collective-permute-done.11.received = bf16[400,512]{1,0:T(8,128)(2,1)S(1)} collective-permute-done((bf16[400,512]{1,0:T(8,128)(2,1)S(1)}, bf16[400,512]{1,0:T(8,128)(2,1)S(1)}, u32[]{:S(2)}, u32[]{:S(2)}) %collective-permute-start.11) | collective-permute-done | bytes 409632 | tf_op jit(solution)/shard_map/ppermute | solution.py:30
  36.9 0.8 %shard_map.104 = (bf16[384,512]{1,0:T(8,128)(2,1)}, bf16[5,2,512]{2,1,0:T(2,128)(2,1)}) custom-call(f32[400,512]{1,0:T(8,128)S(1)} %get-tuple-element.58.kept, bf16[400,512]{1,0:T(8,128)(2,1)S(1)} %collective-permute-done.11.received), custom_call_target="tpu_custom_call" | custom-call | tf_op jit(solution)/shard_map/pallas_call | solution.py:380
  (5 shorter events, 0.1 us)
Async XLA Ops:
  0.6 12.9 %collective-permute-start.3 = (bf16[384,512]{1,0:T(8,128)(2,1)}, bf16[384,512]{1,0:T(8,128)(2,1)S(1)}, u32[]{:S(2)}, u32[]{:S(2)}) collective-permute-start(bf16[384,512]{1,0:T(8,128)(2,1)} %bitcast.4), channel_id=1, source_target_pairs={{1,0},{0,1},{3,2},{2,3},{5,4},{4,5},{7,6},{6,7},{9,8},{8,9},{11,10... | collective-permute-start | bytes 1179656 | tf_op jit(solution)/shard_map/ppermute | solution.py:30
  1.1 15.7 %collective-permute-start.2 = (bf16[384,512]{1,0:T(8,128)(2,1)}, bf16[384,512]{1,0:T(8,128)(2,1)S(1)}, u32[]{:S(2)}, u32[]{:S(2)}) collective-permute-start(bf16[384,512]{1,0:T(8,128)(2,1)} %bitcast.5), channel_id=1, source_target_pairs={{0,14},{2,4},{4,2},{6,8},{8,6},{10,12},{12,10},{14,0},{1,15},{3,5}... | collective-permute-start | bytes 1179656 | tf_op jit(solution)/shard_map/ppermute | solution.py:35
  7.9 1.2 %collective-permute-start = (bf16[16,512]{1,0:T(8,128)(2,1)S(1)}, bf16[16,512]{1,0:T(8,128)(2,1)S(1)}, u32[]{:S(2)}, u32[]{:S(2)}) collective-permute-start(bf16[16,512]{1,0:T(8,128)(2,1)S(1)} %get-tuple-element.32.special), channel_id=1, source_target_pairs={{1,0},{0,1},{3,2},{2,3},{5,4},{4,5},{7,6},{6,7},{9,8},{8,9},{11,10... | collective-permute-start | bytes 49160 | tf_op jit(solution)/shard_map/ppermute | solution.py:30
  11.4 6.1 %collective-permute-start.1 = (bf16[16,1024]{1,0:T(8,128)(2,1)S(1)}, bf16[16,1024]{1,0:T(8,128)(2,1)S(1)}, u32[]{:S(2)}, u32[]{:S(2)}) collective-permute-start(bf16[16,1024]{1,0:T(8,128)(2,1)S(1)} %get-tuple-element.34.first), channel_id=1, source_target_pairs={{2,0},{0,2},{6,4},{4,6},{10,8},{8,10},{14,12},{12,14},{3,1},{1,3},... | collective-permute-start | bytes 98312 | tf_op jit(solution)/shard_map/ppermute | solution.py:30
  11.5 14.3 %collective-permute-start.7 = (bf16[384,512]{1,0:T(8,128)(2,1)S(1)}, bf16[384,512]{1,0:T(8,128)(2,1)S(1)}, u32[]{:S(2)}, u32[]{:S(2)}) collective-permute-start(bf16[384,512]{1,0:T(8,128)(2,1)S(1)} %get-tuple-element.48.own), channel_id=1, source_target_pairs={{2,0},{0,2},{6,4},{4,6},{10,8},{8,10},{14,12},{12,14},{3,1},{1,3},... | collective-permute-start | bytes 1179656 | tf_op jit(solution)/shard_map/ppermute | solution.py:30
  16.9 1.5 %collective-permute-start.4 = (bf16[192,512]{1,0:T(8,128)(2,1)S(1)}, bf16[192,512]{1,0:T(8,128)(2,1)S(1)}, u32[]{:S(2)}, u32[]{:S(2)}) collective-permute-start(bf16[192,512]{1,0:T(8,128)(2,1)S(1)} %get-tuple-element.65.refs_0_), channel_id=1, source_target_pairs={{1,0},{0,1},{3,2},{2,3},{5,4},{4,5},{7,6},{6,7},{9,8},{8,9},{11,10... | collective-permute-start | bytes 589832 | tf_op jit(solution)/shard_map/ppermute | solution.py:30
  17.0 1.7 %collective-permute-start.5 = (bf16[192,512]{1,0:T(8,128)(2,1)S(1)}, bf16[192,512]{1,0:T(8,128)(2,1)S(1)}, u32[]{:S(2)}, u32[]{:S(2)}) collective-permute-start(bf16[192,512]{1,0:T(8,128)(2,1)S(1)} %get-tuple-element.64.refs_1_), channel_id=1, source_target_pairs={{1,0},{0,1},{3,2},{2,3},{5,4},{4,5},{7,6},{6,7},{9,8},{8,9},{11,10... | collective-permute-start | bytes 589832 | tf_op jit(solution)/shard_map/ppermute | solution.py:30
  17.5 8.9 %collective-permute-start.6 = (bf16[32,1024]{1,0:T(8,128)(2,1)S(1)}, bf16[32,1024]{1,0:T(8,128)(2,1)S(1)}, u32[]{:S(2)}, u32[]{:S(2)}) collective-permute-start(bf16[32,1024]{1,0:T(8,128)(2,1)S(1)} %shard_map.97.first), channel_id=1, source_target_pairs={{8,0},{10,2},{12,4},{14,6},{0,8},{2,10},{4,12},{6,14},{9,1},{11,3}... | collective-permute-start | bytes 196616 | tf_op jit(solution)/shard_map/ppermute | solution.py:30
  25.8 1.5 %collective-permute-start.8 = (bf16[192,512]{1,0:T(8,128)(2,1)S(1)}, bf16[192,512]{1,0:T(8,128)(2,1)S(1)}, u32[]{:S(2)}, u32[]{:S(2)}) collective-permute-start(bf16[192,512]{1,0:T(8,128)(2,1)S(1)} %get-tuple-element.63.refs_0_), channel_id=1, source_target_pairs={{1,0},{0,1},{3,2},{2,3},{5,4},{4,5},{7,6},{6,7},{9,8},{8,9},{11,10... | collective-permute-start | bytes 589832 | tf_op jit(solution)/shard_map/ppermute | solution.py:30
  25.9 1.7 %collective-permute-start.9 = (bf16[192,512]{1,0:T(8,128)(2,1)S(1)}, bf16[192,512]{1,0:T(8,128)(2,1)S(1)}, u32[]{:S(2)}, u32[]{:S(2)}) collective-permute-start(bf16[192,512]{1,0:T(8,128)(2,1)S(1)} %get-tuple-element.62.refs_1_), channel_id=1, source_target_pairs={{1,0},{0,1},{3,2},{2,3},{5,4},{4,5},{7,6},{6,7},{9,8},{8,9},{11,10... | collective-permute-start | bytes 589832 | tf_op jit(solution)/shard_map/ppermute | solution.py:30
  26.4 5.5 %collective-permute-start.10 = (bf16[64,1024]{1,0:T(8,128)(2,1)S(1)}, bf16[64,1024]{1,0:T(8,128)(2,1)S(1)}, u32[]{:S(2)}, u32[]{:S(2)}) collective-permute-start(bf16[64,1024]{1,0:T(8,128)(2,1)S(1)} %shard_map.100.first), channel_id=1, source_target_pairs={{4,0},{6,2},{0,4},{2,6},{12,8},{14,10},{8,12},{10,14},{5,1},{7,3},... | collective-permute-start | bytes 393224 | tf_op jit(solution)/shard_map/ppermute | solution.py:30
  35.0 1.8 %collective-permute-start.11 = (bf16[400,512]{1,0:T(8,128)(2,1)S(1)}, bf16[400,512]{1,0:T(8,128)(2,1)S(1)}, u32[]{:S(2)}, u32[]{:S(2)}) collective-permute-start(bf16[400,512]{1,0:T(8,128)(2,1)S(1)} %get-tuple-element.59), channel_id=1, source_target_pairs={{1,0},{0,1},{3,2},{2,3},{5,4},{4,5},{7,6},{6,7},{9,8},{8,9},{11,10... | collective-permute-start | bytes 1228808 | tf_op jit(solution)/shard_map/ppermute | solution.py:30

commit v17 on v16

--- a/solution.py
+++ b/solution.py
@@ -81,8 +81,8 @@
 
 
 def start_kernel(
-    offsets, per_image, special_count, special_total, covisible, special, other_special, w_qkv,
-    mask_out, weights_out, pairs_out, seen, copied,
+    offsets, per_image, special_count, special_total, covisible, special, other_special, w_qkv, w_out,
+    mask_out, weights_out, pairs_out, w_out_here, seen, copied,
 ):
     images = covisible.shape[0]
     patch_total = images * per_image
@@ -91,6 +91,7 @@
     for i in range(3):
         for j, rows in enumerate(halves(depth)):
             moves.append((w_qkv.at[i, rows], weights_out.at[i, pl.ds(j * depth, depth)]))
+    moves.append((w_out, w_out_here))
     copies = [
         pltpu.make_async_copy(source, target, copied.at[i]) for i, (source, target) in enumerate(moves)
     ]
@@ -111,10 +112,11 @@
             mask_out[i * images + b : i * images + b + 1, :] = row
     rows = jnp.concatenate([special[...], other_special[...]], axis=1)
     width = weights_out.shape[2]
-    for copy in copies[1:]:
+    for copy in copies[1:-1]:
         copy.wait()
     for i in range(2):
         pairs_out[:, i * width : (i + 1) * width] = product(rows, weights_out[i + 1]).astype(jnp.bfloat16)
+    copies[-1].wait()
 
 
 def projector(own, other, weights):
@@ -327,10 +329,8 @@
     special_real, mask, special_pairs, queries, special_queries, *refs
 ):
     state_in = refs[:4]
-    w_out, kept_out, sent_out, w_here, copied = refs[4:]
+    w_here, kept_out, sent_out = refs[4:]
     masks = [(special_pairs.shape[0], None)]
-    copy = pltpu.make_async_copy(w_out, w_here, copied)
-    copy.start()
     pairs, rows = queries.shape[0], queries.shape[2] // 2
     columns, out, special = [], None, None
     sides = halves(kept_out.shape[1])
@@ -338,8 +338,6 @@
         given(special_pairs), masks, lambda pair: queries[pair], lambda: special_queries[...],
         State(rows, state_in), pairs, rows, special_real,
     ):
-        if pair == 0 and sub == 0:
-            copy.wait()
         share = total * (1.0 / weight)
         if pair == pairs:
             row = lax.broadcasted_iota(jnp.int32, share.shape, 0) // HEAD_DIM
@@ -453,19 +451,20 @@
         ],
     )
     specials = both(specials)
-    mask, weights, everywhere = call(
+    mask, weights, everywhere, w_here = call(
         functools.partial(start_kernel, offsets, per_image, special_count, special_block),
         [
             f32(mask_rows, patch_total + heads * special_block),
             bf16(*w_qkv.shape),
             bf16(special_block, 2 * width),
+            bf16(*w_out.shape),
         ],
-        (covisible, *specials, w_qkv),
-        in_specs=[HBM, VMEM, VMEM, HBM],
-        scratch=[pltpu.SMEM(covisible.shape, jnp.int32), pltpu.SemaphoreType.DMA((1 + 6,))],
+        (covisible, *specials, w_qkv, w_out),
+        in_specs=[HBM, VMEM, VMEM, HBM, HBM],
+        scratch=[pltpu.SMEM(covisible.shape, jnp.int32), pltpu.SemaphoreType.DMA((1 + 7,))],
     )
     if paired and power:
-        everywhere = stacked(everywhere, swapped(everywhere, "blk", 1), FIRST)
+        everywhere = stacked(everywhere, swapped(everywhere, "blk", 2), FIRST)
     queries, special_queries, *state = call(
         functools.partial(first_kernel, images),
         [bf16(pairs, PAIR, 2 * patch_total), bf16(width, heads * special_block), *state_shape],
@@ -489,18 +488,18 @@
     stretches = lambda owner: [[image] for image in image_rows(owner)]
     if paired:
         far = after(crossed(patches, "blk"), state[0])
-        near = swapped(after(own, mask), "blk", 1)
+        near = swapped(patches, "blk", 1)
         if power:
             everywhere = after(everywhere, far)
-            bit = owner_count // 2
-            while bit > 4:
+            bit = 4
+            while 2 * bit < owner_count:
                 everywhere = stacked(everywhere, swapped(everywhere, "blk", bit))
-                bit //= 2
+                bit *= 2
             arrived = swapped(everywhere, "blk", bit)
         state = later(stretches(1), halved(far, state[0]), state)
         if power:
             everywhere = stacked(after(everywhere, state[0]), arrived, FIRST)
-            arrived = swapped(everywhere, "blk", 2)
+            arrived = swapped(everywhere, "blk", 1)
         state = later(stretches(2), halved(near, state[0]), state)
         if power:
             everywhere = stacked(after(everywhere, state[0]), arrived)
@@ -512,9 +511,7 @@
     kept, sent = call(
         functools.partial(last_kernel, real_rows),
         [f32(rows, width), bf16(rows, width)],
-        (mask, everywhere, queries, special_queries, *state, w_out),
-        in_specs=[VMEM] * (4 + len(state)) + [HBM],
-        scratch=[pltpu.VMEM(w_out.shape, jnp.bfloat16), pltpu.SemaphoreType.DMA],
+        (mask, everywhere, queries, special_queries, *state, w_here),
     )
     received = swapped(sent, "head", 1)
     patch_out, special_out = call(

time: 37.9 us -> 36.3 us (0.958)
  starting transfers between devices: 10.4 us -> 9.25 us
  Pallas kernels: 17.5 us -> 16.5 us
  waiting for transfers between devices: 9.01 us -> 9.44 us
    ppermute x1, waiting for transfers between devices: 0.01 us -> 2.05 us  [crossed(): lax.ppermute(block, axis, [(i, (i + (-1 if i % 2 == 0 else 1)) % count) f...]
    ppermute x11, waiting for transfers between devices: 9.01 us -> 7.39 us  [swapped(): return lax.ppermute(block, axis, [(i ^ bit, i) for i in range(count)])]
    ppermute x11, starting transfers between devices: 4.8 us -> 3.65 us  [swapped(): return lax.ppermute(block, axis, [(i ^ bit, i) for i in range(count)])]
    pallas_call x10, Pallas kernels: 17.5 us -> 16.5 us  [call(): pl.pallas_call(kernel, out_shape=out_shape, in_specs=in_specs or [VMEM] *...]
  transfers between devices with their start and end apart: 12 -> 12, of which waited for: 8 -> 7; matrix products, arithmetic and copies ran while one was open for 0% -> 0% of each run, Pallas kernels for 36% -> 38%
where the time goes in v17:
time: 36.3 us; the launch traced here: 36 us
  Pallas kernels  16.5 us (45%)
  waiting for transfers between devices  9.44 us (26%)
  starting transfers between devices  9.25 us (25%)
  between operations  0.74 us (2%)
    pallas_call x10, Pallas kernels, call(): pl.pallas_call(kernel, out_shape=out_shape, in_specs=in_specs or [VMEM] *...  16.5 us
    ppermute x11, waiting for transfers between devices, swapped(): return lax.ppermute(block, axis, [(i ^ bit, i) for i in range(count)])  7.39 us
    ppermute x1, starting transfers between devices, crossed(): lax.ppermute(block, axis, [(i, (i + (-1 if i % 2 == 0 else 1)) % count) f...  5.6 us
    ppermute x11, starting transfers between devices, swapped(): return lax.ppermute(block, axis, [(i ^ bit, i) for i in range(count)])  3.65 us
    ppermute x1, waiting for transfers between devices, crossed(): lax.ppermute(block, axis, [(i, (i + (-1 if i % 2 == 0 else 1)) % count) f...  2.05 us
  transfers between devices with their start and end apart: 12, of which 7 were waited for; matrix products, arithmetic and copies ran while one was open for 0% of the time, Pallas kernels for 38%

profile of v17, /device:TPU:0, one launch (start us, length us, event | category | flops | bytes accessed | tf_op | source)
XLA Modules:
  0.0 36.0 jit_solution(5123699974862870850)
XLA Ops:
  0.6 0.5 %collective-permute-start.3 = (bf16[384,512]{1,0:T(8,128)(2,1)}, bf16[384,512]{1,0:T(8,128)(2,1)S(1)}, u32[]{:S(2)}, u32[]{:S(2)}) collective-permute-start(bf16[384,512]{1,0:T(8,128)(2,1)} %bitcast.4), channel_id=1, source_target_pairs={{1,0},{0,1},{3,2},{2,3},{5,4},{4,5},{7,6},{6,7},{9,8},{8,9},{11,10... | collective-permute-start | bytes 1179656 | tf_op jit(solution)/shard_map/ppermute | solution.py:30
  1.1 5.6 %collective-permute-start.2 = (bf16[384,512]{1,0:T(8,128)(2,1)}, bf16[384,512]{1,0:T(8,128)(2,1)S(1)}, u32[]{:S(2)}, u32[]{:S(2)}) collective-permute-start(bf16[384,512]{1,0:T(8,128)(2,1)} %bitcast.5), channel_id=1, source_target_pairs={{0,14},{2,4},{4,2},{6,8},{8,6},{10,12},{12,10},{14,0},{1,15},{3,5}... | collective-permute-start | bytes 1179656 | tf_op jit(solution)/shard_map/ppermute | solution.py:35
  6.8 1.1 %shard_map.95 = (bf16[16,512]{1,0:T(8,128)(2,1)S(1)}, bf16[384,512]{1,0:T(8,128)(2,1)S(1)}) custom-call(s32[2]{0:T(128)} %frame_order.1, bf16[5,2,512]{2,1,0:T(2,128)(2,1)} %bitcast.8, bf16[5,1024]{1,0:T(8,128)(2,1)} %role_first.1, bf16[5,1024]{1,0:T(8,128)(2,1)} %role_rest.1, bf16[384,512]{1,0:T(8,128)(2,1)} %bitcast.6), custom_call_target="tpu_custom_call" | custom-call | tf_op jit(solution)/shard_map/pallas_call | solution.py:378
  7.9 0.2 collective-permute-start
  8.1 0.0 collective-permute-start.7
  8.1 1.0 %collective-permute-done.other_special = bf16[16,512]{1,0:T(8,128)(2,1)S(1)} collective-permute-done((bf16[16,512]{1,0:T(8,128)(2,1)S(1)}, bf16[16,512]{1,0:T(8,128)(2,1)S(1)}, u32[]{:S(2)}, u32[]{:S(2)}) %collective-permute-start) | collective-permute-done | bytes 16416 | tf_op jit(solution)/shard_map/ppermute | solution.py:30
  9.1 2.3 %shard_map.96 = (f32[8,512]{1,0:T(8,128)S(1)}, bf16[3,1024,512]{2,1,0:T(8,128)(2,1)S(1)}, bf16[16,1024]{1,0:T(8,128)(2,1)S(1)}, bf16[512,1024]{1,0:T(8,128)(2,1)S(1)}) custom-call(s32[2,16]{1,0:T(2,128)} %covisible.1, bf16[16,512]{1,0:T(8,128)(2,1)S(1)} %get-tuple-element.32.special, bf16[16,512]{1,0:T(8,128)(2,1)S(1)} %collective-permute-done.other_special, ...), custom_call_target="tpu_custom_call" | custom-call | tf_op jit(solution)/shard_map/pallas_call | solution.py:378
  11.4 0.1 collective-permute-start.1
  11.5 0.0 collective-permute-done.3.other
  11.5 3.4 %shard_map.98 = (bf16[4,128,768]{2,1,0:T(8,128)(2,1)S(1)}, bf16[512,128]{1,0:T(8,128)(2,1)S(1)}, f32[8,768]{1,0:T(8,128)S(1)}, f32[8,768]{1,0:T(8,128)S(1)}, f32...) custom-call(f32[8,512]{1,0:T(8,128)S(1)} %get-tuple-element.33.mask, bf16[384,512]{1,0:T(8,128)(2,1)S(1)} %get-tuple-element.35.own, ...), custom_call_target="tpu_custom_call" | custom-call | tf_op jit(solution)/shard_map/pallas_call | solution.py:378
  14.9 2.1 %collective-permute-done.2 = bf16[384,512]{1,0:T(8,128)(2,1)S(1)} collective-permute-done((bf16[384,512]{1,0:T(8,128)(2,1)}, bf16[384,512]{1,0:T(8,128)(2,1)S(1)}, u32[]{:S(2)}, u32[]{:S(2)}) %collective-permute-start.2) | collective-permute-done | bytes 393248 | tf_op jit(solution)/shard_map/ppermute | solution.py:35
  17.0 0.1 collective-permute-start.4
  17.0 0.5 %collective-permute-start.5 = (bf16[192,512]{1,0:T(8,128)(2,1)S(1)}, bf16[192,512]{1,0:T(8,128)(2,1)S(1)}, u32[]{:S(2)}, u32[]{:S(2)}) collective-permute-start(bf16[192,512]{1,0:T(8,128)(2,1)S(1)} %get-tuple-element.64.refs_1_), channel_id=1, source_target_pairs={{1,0},{0,1},{3,2},{2,3},{5,4},{4,5},{7,6},{6,7},{9,8},{8,9},{11,10... | collective-permute-start | bytes 589832 | tf_op jit(solution)/shard_map/ppermute | solution.py:30
  17.5 0.0 collective-permute-done.1.second
  17.6 1.5 %collective-permute-start.6 = (bf16[32,1024]{1,0:T(8,128)(2,1)S(1)}, bf16[32,1024]{1,0:T(8,128)(2,1)S(1)}, u32[]{:S(2)}, u32[]{:S(2)}) collective-permute-start(bf16[32,1024]{1,0:T(8,128)(2,1)S(1)} %shard_map.97.first), channel_id=1, source_target_pairs={{8,0},{10,2},{12,4},{14,6},{0,8},{2,10},{4,12},{6,14},{9,1},{11,3}... | collective-permute-start | bytes 196616 | tf_op jit(solution)/shard_map/ppermute | solution.py:30
  19.1 0.0 collective-permute-done.4.refs_2_
  19.1 0.0 collective-permute-done.5.refs_3_
  19.1 3.4 %shard_map.99 = (f32[8,768]{1,0:T(8,128)S(1)}, f32[8,768]{1,0:T(8,128)S(1)}, f32[4,64,768]{2,1,0:T(8,128)S(1)}, f32[512,128]{1,0:T(8,128)S(1)}) custom-call(f32[8,512]{1,0:T(8,128)S(1)} %get-tuple-element.33.mask, bf16[192,512]{1,0:T(8,128)(2,1)S(1)} %get-tuple-element.65.refs_0_, bf16[192,512]{1,0:T(8,128)(2,1)S(1)} %get-tuple-element.64.refs_1_, ...), custom_call_target="tpu_custom_call" | custom-call | tf_op jit(solution)/shard_map/pallas_call | solution.py:378
  22.5 2.6 %collective-permute-done.7 = bf16[384,512]{1,0:T(8,128)(2,1)S(1)} collective-permute-done((bf16[384,512]{1,0:T(8,128)(2,1)}, bf16[384,512]{1,0:T(8,128)(2,1)S(1)}, u32[]{:S(2)}, u32[]{:S(2)}) %collective-permute-start.7) | collective-permute-done | bytes 393248 | tf_op jit(solution)/shard_map/ppermute | solution.py:30
  25.1 0.1 collective-permute-start.8
  25.2 0.5 %collective-permute-start.9 = (bf16[192,512]{1,0:T(8,128)(2,1)S(1)}, bf16[192,512]{1,0:T(8,128)(2,1)S(1)}, u32[]{:S(2)}, u32[]{:S(2)}) collective-permute-start(bf16[192,512]{1,0:T(8,128)(2,1)S(1)} %get-tuple-element.62.refs_1_), channel_id=1, source_target_pairs={{1,0},{0,1},{3,2},{2,3},{5,4},{4,5},{7,6},{6,7},{9,8},{8,9},{11,10... | collective-permute-start | bytes 589832 | tf_op jit(solution)/shard_map/ppermute | solution.py:30
  25.7 0.0 collective-permute-done.6.second
  25.7 0.1 collective-permute-start.10
  25.8 0.8 %collective-permute-done.8.refs_2_ = bf16[192,512]{1,0:T(8,128)(2,1)S(1)} collective-permute-done((bf16[192,512]{1,0:T(8,128)(2,1)S(1)}, bf16[192,512]{1,0:T(8,128)(2,1)S(1)}, u32[]{:S(2)}, u32[]{:S(2)}) %collective-permute-start.8) | collective-permute-done | bytes 196640 | tf_op jit(solution)/shard_map/ppermute | solution.py:30
  26.6 0.3 collective-permute-done.9.refs_3_
  26.9 3.4 %shard_map.101 = (f32[8,768]{1,0:T(8,128)S(1)}, f32[8,768]{1,0:T(8,128)S(1)}, f32[4,64,768]{2,1,0:T(8,128)S(1)}, f32[512,128]{1,0:T(8,128)S(1)}) custom-call(f32[8,512]{1,0:T(8,128)S(1)} %get-tuple-element.33.mask, bf16[192,512]{1,0:T(8,128)(2,1)S(1)} %get-tuple-element.63.refs_0_, bf16[192,512]{1,0:T(8,128)(2,1)S(1)} %get-tuple-element.62.refs_1_, ...), custom_call_target="tpu_custom_call" | custom-call | tf_op jit(solution)/shard_map/pallas_call | solution.py:378
  30.3 0.9 %collective-permute-done.10.second = bf16[64,1024]{1,0:T(8,128)(2,1)S(1)} collective-permute-done((bf16[64,1024]{1,0:T(8,128)(2,1)S(1)}, bf16[64,1024]{1,0:T(8,128)(2,1)S(1)}, u32[]{:S(2)}, u32[]{:S(2)}) %collective-permute-start.10) | collective-permute-done | bytes 131104 | tf_op jit(solution)/shard_map/ppermute | solution.py:30
  31.3 2.1 %shard_map.103 = (f32[400,512]{1,0:T(8,128)S(1)}, bf16[400,512]{1,0:T(8,128)(2,1)S(1)}) custom-call(f32[8,512]{1,0:T(8,128)S(1)} %get-tuple-element.33.mask, bf16[128,1024]{1,0:T(8,128)(2,1)S(1)} %shard_map.102.special_pairs, bf16[4,128,768]{2,1,0:T(8,128)(2,1)S(1)} %get-tuple-element.41.refs_5_.queries, ...), custom_call_target="tpu_custom_call" | custom-call | tf_op jit(solution)/shard_map/pallas_call | solution.py:378
  33.4 0.1 collective-permute-start.11
  33.5 1.7 %collective-permute-done.11.received = bf16[400,512]{1,0:T(8,128)(2,1)S(1)} collective-permute-done((bf16[400,512]{1,0:T(8,128)(2,1)S(1)}, bf16[400,512]{1,0:T(8,128)(2,1)S(1)}, u32[]{:S(2)}, u32[]{:S(2)}) %collective-permute-start.11) | collective-permute-done | bytes 409632 | tf_op jit(solution)/shard_map/ppermute | solution.py:30
  35.2 0.8 %shard_map.104 = (bf16[384,512]{1,0:T(8,128)(2,1)}, bf16[5,2,512]{2,1,0:T(2,128)(2,1)}) custom-call(f32[400,512]{1,0:T(8,128)S(1)} %get-tuple-element.58.kept, bf16[400,512]{1,0:T(8,128)(2,1)S(1)} %collective-permute-done.11.received), custom_call_target="tpu_custom_call" | custom-call | tf_op jit(solution)/shard_map/pallas_call | solution.py:378
  (5 shorter events, 0.1 us)
Async XLA Ops:
  0.6 10.9 %collective-permute-start.3 = (bf16[384,512]{1,0:T(8,128)(2,1)}, bf16[384,512]{1,0:T(8,128)(2,1)S(1)}, u32[]{:S(2)}, u32[]{:S(2)}) collective-permute-start(bf16[384,512]{1,0:T(8,128)(2,1)} %bitcast.4), channel_id=1, source_target_pairs={{1,0},{0,1},{3,2},{2,3},{5,4},{4,5},{7,6},{6,7},{9,8},{8,9},{11,10... | collective-permute-start | bytes 1179656 | tf_op jit(solution)/shard_map/ppermute | solution.py:30
  1.1 15.8 %collective-permute-start.2 = (bf16[384,512]{1,0:T(8,128)(2,1)}, bf16[384,512]{1,0:T(8,128)(2,1)S(1)}, u32[]{:S(2)}, u32[]{:S(2)}) collective-permute-start(bf16[384,512]{1,0:T(8,128)(2,1)} %bitcast.5), channel_id=1, source_target_pairs={{0,14},{2,4},{4,2},{6,8},{8,6},{10,12},{12,10},{14,0},{1,15},{3,5}... | collective-permute-start | bytes 1179656 | tf_op jit(solution)/shard_map/ppermute | solution.py:35
  7.9 1.2 %collective-permute-start = (bf16[16,512]{1,0:T(8,128)(2,1)S(1)}, bf16[16,512]{1,0:T(8,128)(2,1)S(1)}, u32[]{:S(2)}, u32[]{:S(2)}) collective-permute-start(bf16[16,512]{1,0:T(8,128)(2,1)S(1)} %get-tuple-element.32.special), channel_id=1, source_target_pairs={{1,0},{0,1},{3,2},{2,3},{5,4},{4,5},{7,6},{6,7},{9,8},{8,9},{11,10... | collective-permute-start | bytes 49160 | tf_op jit(solution)/shard_map/ppermute | solution.py:30
  8.1 17.0 %collective-permute-start.7 = (bf16[384,512]{1,0:T(8,128)(2,1)}, bf16[384,512]{1,0:T(8,128)(2,1)S(1)}, u32[]{:S(2)}, u32[]{:S(2)}) collective-permute-start(bf16[384,512]{1,0:T(8,128)(2,1)} %bitcast.7), channel_id=1, source_target_pairs={{2,0},{0,2},{6,4},{4,6},{10,8},{8,10},{14,12},{12,14},{3,1},{1,3},... | collective-permute-start | bytes 1179656 | tf_op jit(solution)/shard_map/ppermute | solution.py:30
  11.4 6.1 %collective-permute-start.1 = (bf16[16,1024]{1,0:T(8,128)(2,1)S(1)}, bf16[16,1024]{1,0:T(8,128)(2,1)S(1)}, u32[]{:S(2)}, u32[]{:S(2)}) collective-permute-start(bf16[16,1024]{1,0:T(8,128)(2,1)S(1)} %get-tuple-element.34.first), channel_id=1, source_target_pairs={{4,0},{6,2},{0,4},{2,6},{12,8},{14,10},{8,12},{10,14},{5,1},{7,3},... | collective-permute-start | bytes 98312 | tf_op jit(solution)/shard_map/ppermute | solution.py:30
  17.0 2.1 %collective-permute-start.4 = (bf16[192,512]{1,0:T(8,128)(2,1)S(1)}, bf16[192,512]{1,0:T(8,128)(2,1)S(1)}, u32[]{:S(2)}, u32[]{:S(2)}) collective-permute-start(bf16[192,512]{1,0:T(8,128)(2,1)S(1)} %get-tuple-element.65.refs_0_), channel_id=1, source_target_pairs={{1,0},{0,1},{3,2},{2,3},{5,4},{4,5},{7,6},{6,7},{9,8},{8,9},{11,10... | collective-permute-start | bytes 589832 | tf_op jit(solution)/shard_map/ppermute | solution.py:30
  17.0 2.1 %collective-permute-start.5 = (bf16[192,512]{1,0:T(8,128)(2,1)S(1)}, bf16[192,512]{1,0:T(8,128)(2,1)S(1)}, u32[]{:S(2)}, u32[]{:S(2)}) collective-permute-start(bf16[192,512]{1,0:T(8,128)(2,1)S(1)} %get-tuple-element.64.refs_1_), channel_id=1, source_target_pairs={{1,0},{0,1},{3,2},{2,3},{5,4},{4,5},{7,6},{6,7},{9,8},{8,9},{11,10... | collective-permute-start | bytes 589832 | tf_op jit(solution)/shard_map/ppermute | solution.py:30
  17.6 8.1 %collective-permute-start.6 = (bf16[32,1024]{1,0:T(8,128)(2,1)S(1)}, bf16[32,1024]{1,0:T(8,128)(2,1)S(1)}, u32[]{:S(2)}, u32[]{:S(2)}) collective-permute-start(bf16[32,1024]{1,0:T(8,128)(2,1)S(1)} %shard_map.97.first), channel_id=1, source_target_pairs={{8,0},{10,2},{12,4},{14,6},{0,8},{2,10},{4,12},{6,14},{9,1},{11,3}... | collective-permute-start | bytes 196616 | tf_op jit(solution)/shard_map/ppermute | solution.py:30
  25.1 1.5 %collective-permute-start.8 = (bf16[192,512]{1,0:T(8,128)(2,1)S(1)}, bf16[192,512]{1,0:T(8,128)(2,1)S(1)}, u32[]{:S(2)}, u32[]{:S(2)}) collective-permute-start(bf16[192,512]{1,0:T(8,128)(2,1)S(1)} %get-tuple-element.63.refs_0_), channel_id=1, source_target_pairs={{1,0},{0,1},{3,2},{2,3},{5,4},{4,5},{7,6},{6,7},{9,8},{8,9},{11,10... | collective-permute-start | bytes 589832 | tf_op jit(solution)/shard_map/ppermute | solution.py:30
  25.2 1.7 %collective-permute-start.9 = (bf16[192,512]{1,0:T(8,128)(2,1)S(1)}, bf16[192,512]{1,0:T(8,128)(2,1)S(1)}, u32[]{:S(2)}, u32[]{:S(2)}) collective-permute-start(bf16[192,512]{1,0:T(8,128)(2,1)S(1)} %get-tuple-element.62.refs_1_), channel_id=1, source_target_pairs={{1,0},{0,1},{3,2},{2,3},{5,4},{4,5},{7,6},{6,7},{9,8},{8,9},{11,10... | collective-permute-start | bytes 589832 | tf_op jit(solution)/shard_map/ppermute | solution.py:30
  25.7 5.5 %collective-permute-start.10 = (bf16[64,1024]{1,0:T(8,128)(2,1)S(1)}, bf16[64,1024]{1,0:T(8,128)(2,1)S(1)}, u32[]{:S(2)}, u32[]{:S(2)}) collective-permute-start(bf16[64,1024]{1,0:T(8,128)(2,1)S(1)} %shard_map.100.first), channel_id=1, source_target_pairs={{2,0},{0,2},{6,4},{4,6},{10,8},{8,10},{14,12},{12,14},{3,1},{1,3},... | collective-permute-start | bytes 393224 | tf_op jit(solution)/shard_map/ppermute | solution.py:30
  33.4 1.8 %collective-permute-start.11 = (bf16[400,512]{1,0:T(8,128)(2,1)S(1)}, bf16[400,512]{1,0:T(8,128)(2,1)S(1)}, u32[]{:S(2)}, u32[]{:S(2)}) collective-permute-start(bf16[400,512]{1,0:T(8,128)(2,1)S(1)} %get-tuple-element.59), channel_id=1, source_target_pairs={{1,0},{0,1},{3,2},{2,3},{5,4},{4,5},{7,6},{6,7},{9,8},{8,9},{11,10... | collective-permute-start | bytes 1228808 | tf_op jit(solution)/shard_map/ppermute | solution.py:30

commit v18 on v17

--- a/solution.py
+++ b/solution.py
@@ -174,7 +174,7 @@
             part = scores[start : start + count]
             if mask is None:
                 key_row = lax.broadcasted_iota(jnp.int32, (count, 1), 0)
-                part = jnp.where(lax.rem(key_row, TILE_ROWS) < special_real, part, -jnp.inf)
+                part = jnp.where(lax.rem(key_row, special_real[0]) < special_real[1], part, -jnp.inf)
             parts.append(part)
             start += count
         return jnp.concatenate(parts, axis=0)
@@ -312,7 +312,7 @@
     return columns
 
 
-def later_kernel(stretches, special_real, mask, *refs):
+def later_kernel(stretches, mask, *refs):
     own, other, masks, refs = joined(stretches, mask, refs)
     weights, queries, special_queries = refs[:3]
     state_in, state_out = refs[3:7], refs[7:]
@@ -320,7 +320,39 @@
     state = State(rows, state_out)
     for result in attend_all(
         projector(own, other, weights), masks, lambda pair: queries[pair], lambda: special_queries[...],
-        State(rows, state_in), pairs, rows, special_real,
+        State(rows, state_in), pairs, rows, None,
+    ):
+        state.put(*result)
+
+
+def half_kernel(count, *refs):
+    weights, sums_out = refs[count:]
+    rows = jnp.concatenate([ref[...] for ref in refs[:count]], axis=0)
+    for i in range(2):
+        sums_out[i] = product(rows, weights[i + 1, : rows.shape[1], :])
+
+
+def begun(sums, other, weights):
+    depth = other.shape[1]
+
+    def columns(which, quad):
+        lanes = slice(quad * QUAD, (quad + 1) * QUAD)
+        return sums[which - 1, :, lanes] + product(other, weights[which, depth:, lanes])
+
+    return columns
+
+
+def begun_kernel(stretches, mask, sums, *refs):
+    count = len(stretches)
+    other = jnp.concatenate([ref[...] for ref in refs[:count]], axis=0)
+    masks = [(rows, mask[i : i + 1, :]) for part in stretches for rows, i in part]
+    weights, queries, special_queries = refs[count : count + 3]
+    state_in, state_out = refs[count + 3 : count + 7], refs[count + 7 :]
+    pairs, rows = queries.shape[0], queries.shape[2] // 2
+    state = State(rows, state_out)
+    for result in attend_all(
+        begun(sums, other, weights), masks, lambda pair: queries[pair], lambda: special_queries[...],
+        State(rows, state_in), pairs, rows, None,
     ):
         state.put(*result)
 
@@ -392,6 +424,18 @@
     out[count:, :] = second[...]
 
 
+def compact_kernel(block, real, first, second, out):
+    rows = [
+        part[start : start + real, :].astype(jnp.float32)
+        for part in (first, second)
+        for start in range(0, part.shape[0], block)
+    ]
+    padding = out.shape[0] - sum(part.shape[0] for part in rows)
+    if padding:
+        rows.append(jnp.zeros((padding, out.shape[1]), jnp.float32))
+    out[...] = jnp.concatenate(rows, axis=0).astype(jnp.bfloat16)
+
+
 def stacked(first, second, flops=0):
     shape = jax.ShapeDtypeStruct((2 * first.shape[0], first.shape[1]), first.dtype)
     return call(stack_kernel, [shape], (first, second), flops=flops)[0]
@@ -474,7 +518,7 @@
 
     def later(stretches, parts, state):
         return call(
-            functools.partial(later_kernel, stretches, real_rows),
+            functools.partial(later_kernel, stretches),
             state_shape,
             (mask, *[part[0] for part in parts], *[part[1] for part in parts], *fixed, *state),
         )
@@ -498,18 +542,37 @@
             arrived = swapped(everywhere, "blk", bit)
         state = later(stretches(1), halved(far, state[0]), state)
         if power:
-            everywhere = stacked(after(everywhere, state[0]), arrived, FIRST)
+            real = real_rows * owner_count // 2
+            blocks = (real + -real % TILE_ROWS, real)
+            (everywhere,) = call(
+                functools.partial(compact_kernel, special_block, real_rows),
+                [bf16(blocks[0], 2 * width)],
+                (after(everywhere, state[0]), arrived),
+                flops=FIRST,
+            )
             arrived = swapped(everywhere, "blk", 1)
-        state = later(stretches(2), halved(near, state[0]), state)
+        parts = halved(near, state[0])
+        (sums,) = call(
+            functools.partial(half_kernel, len(parts)),
+            [f32(2, patch_total, width)],
+            (*[part[0] for part in parts], weights),
+            flops=0,
+        )
+        state = call(
+            functools.partial(begun_kernel, stretches(2)),
+            state_shape,
+            (mask, sums, *[part[1] for part in parts], *fixed, *state),
+        )
         if power:
             everywhere = stacked(after(everywhere, state[0]), arrived)
     else:
         for i, offset in enumerate(offsets[1:]):
             state = later(stretches(i + 1), halved(shifted(patches, "blk", -offset), state[0]), state)
     if not (paired and power):
+        blocks = (special_block, real_rows)
         everywhere = lax.all_gather(everywhere, "blk", axis=0, tiled=True)
     kept, sent = call(
-        functools.partial(last_kernel, real_rows),
+        functools.partial(last_kernel, blocks),
         [f32(rows, width), bf16(rows, width)],
         (mask, everywhere, queries, special_queries, *state, w_here),
     )

time: 36.3 us -> 35.5 us (0.978)
  Pallas kernels: 16.5 us -> 16.1 us
    pallas_call x10 -> x11, Pallas kernels: 16.5 us -> 16.1 us  [call(): pl.pallas_call(kernel, out_shape=out_shape, in_specs=in_specs or [VMEM] *...]
  transfers between devices with their start and end apart: 12 -> 12, of which waited for: 7 -> 7; matrix products, arithmetic and copies ran while one was open for 0% -> 0% of each run, Pallas kernels for 38% -> 37%
where the time goes in v18:
time: 35.5 us; the launch traced here: 35.3 us
  Pallas kernels  16.1 us (45%)
  starting transfers between devices  9.25 us (26%)
  waiting for transfers between devices  9.19 us (26%)
  between operations  0.75 us (2%)
    pallas_call x11, Pallas kernels, call(): pl.pallas_call(kernel, out_shape=out_shape, in_specs=in_specs or [VMEM] *...  16.1 us
    ppermute x11, waiting for transfers between devices, swapped(): return lax.ppermute(block, axis, [(i ^ bit, i) for i in range(count)])  7.14 us
    ppermute x1, starting transfers between devices, crossed(): lax.ppermute(block, axis, [(i, (i + (-1 if i % 2 == 0 else 1)) % count) f...  5.6 us
    ppermute x11, starting transfers between devices, swapped(): return lax.ppermute(block, axis, [(i ^ bit, i) for i in range(count)])  3.65 us
    ppermute x1, waiting for transfers between devices, crossed(): lax.ppermute(block, axis, [(i, (i + (-1 if i % 2 == 0 else 1)) % count) f...  2.05 us
  transfers between devices with their start and end apart: 12, of which 7 were waited for; matrix products, arithmetic and copies ran while one was open for 0% of the time, Pallas kernels for 37%

profile of v18, /device:TPU:0, one launch (start us, length us, event | category | flops | bytes accessed | tf_op | source)
XLA Modules:
  0.0 35.3 jit_solution(14390554638607706979)
XLA Ops:
  0.6 0.5 %collective-permute-start.3 = (bf16[384,512]{1,0:T(8,128)(2,1)}, bf16[384,512]{1,0:T(8,128)(2,1)S(1)}, u32[]{:S(2)}, u32[]{:S(2)}) collective-permute-start(bf16[384,512]{1,0:T(8,128)(2,1)} %bitcast.4), channel_id=1, source_target_pairs={{1,0},{0,1},{3,2},{2,3},{5,4},{4,5},{7,6},{6,7},{9,8},{8,9},{11,10... | collective-permute-start | bytes 1179656 | tf_op jit(solution)/shard_map/ppermute | solution.py:30
  1.1 5.6 %collective-permute-start.2 = (bf16[384,512]{1,0:T(8,128)(2,1)}, bf16[384,512]{1,0:T(8,128)(2,1)S(1)}, u32[]{:S(2)}, u32[]{:S(2)}) collective-permute-start(bf16[384,512]{1,0:T(8,128)(2,1)} %bitcast.5), channel_id=1, source_target_pairs={{0,14},{2,4},{4,2},{6,8},{8,6},{10,12},{12,10},{14,0},{1,15},{3,5}... | collective-permute-start | bytes 1179656 | tf_op jit(solution)/shard_map/ppermute | solution.py:35
  6.8 1.1 %shard_map.95 = (bf16[16,512]{1,0:T(8,128)(2,1)S(1)}, bf16[384,512]{1,0:T(8,128)(2,1)S(1)}) custom-call(s32[2]{0:T(128)} %frame_order.1, bf16[5,2,512]{2,1,0:T(2,128)(2,1)} %bitcast.8, bf16[5,1024]{1,0:T(8,128)(2,1)} %role_first.1, bf16[5,1024]{1,0:T(8,128)(2,1)} %role_rest.1, bf16[384,512]{1,0:T(8,128)(2,1)} %bitcast.6), custom_call_target="tpu_custom_call" | custom-call | tf_op jit(solution)/shard_map/pallas_call | solution.py:410
  7.9 0.2 collective-permute-start
  8.1 0.0 collective-permute-start.7
  8.1 1.0 %collective-permute-done.other_special = bf16[16,512]{1,0:T(8,128)(2,1)S(1)} collective-permute-done((bf16[16,512]{1,0:T(8,128)(2,1)S(1)}, bf16[16,512]{1,0:T(8,128)(2,1)S(1)}, u32[]{:S(2)}, u32[]{:S(2)}) %collective-permute-start) | collective-permute-done | bytes 16416 | tf_op jit(solution)/shard_map/ppermute | solution.py:30
  9.1 2.3 %shard_map.96 = (f32[8,512]{1,0:T(8,128)S(1)}, bf16[3,1024,512]{2,1,0:T(8,128)(2,1)S(1)}, bf16[16,1024]{1,0:T(8,128)(2,1)S(1)}, bf16[512,1024]{1,0:T(8,128)(2,1)S(1)}) custom-call(s32[2,16]{1,0:T(2,128)} %covisible.1, bf16[16,512]{1,0:T(8,128)(2,1)S(1)} %get-tuple-element.32.special, bf16[16,512]{1,0:T(8,128)(2,1)S(1)} %collective-permute-done.other_special, ...), custom_call_target="tpu_custom_call" | custom-call | tf_op jit(solution)/shard_map/pallas_call | solution.py:410
  11.4 0.1 collective-permute-start.1
  11.5 0.0 collective-permute-done.3.other
  11.5 3.4 %shard_map.98 = (bf16[4,128,768]{2,1,0:T(8,128)(2,1)S(1)}, bf16[512,128]{1,0:T(8,128)(2,1)S(1)}, f32[8,768]{1,0:T(8,128)S(1)}, f32[8,768]{1,0:T(8,128)S(1)}, f32...) custom-call(f32[8,512]{1,0:T(8,128)S(1)} %get-tuple-element.33.mask, bf16[384,512]{1,0:T(8,128)(2,1)S(1)} %get-tuple-element.35.own, ...), custom_call_target="tpu_custom_call" | custom-call | tf_op jit(solution)/shard_map/pallas_call | solution.py:410
  14.9 2.1 %collective-permute-done.2 = bf16[384,512]{1,0:T(8,128)(2,1)S(1)} collective-permute-done((bf16[384,512]{1,0:T(8,128)(2,1)}, bf16[384,512]{1,0:T(8,128)(2,1)S(1)}, u32[]{:S(2)}, u32[]{:S(2)}) %collective-permute-start.2) | collective-permute-done | bytes 393248 | tf_op jit(solution)/shard_map/ppermute | solution.py:35
  17.0 0.1 collective-permute-start.4
  17.0 0.5 %collective-permute-start.5 = (bf16[192,512]{1,0:T(8,128)(2,1)S(1)}, bf16[192,512]{1,0:T(8,128)(2,1)S(1)}, u32[]{:S(2)}, u32[]{:S(2)}) collective-permute-start(bf16[192,512]{1,0:T(8,128)(2,1)S(1)} %get-tuple-element.64.refs_1_), channel_id=1, source_target_pairs={{1,0},{0,1},{3,2},{2,3},{5,4},{4,5},{7,6},{6,7},{9,8},{8,9},{11,10... | collective-permute-start | bytes 589832 | tf_op jit(solution)/shard_map/ppermute | solution.py:30
  17.5 0.0 collective-permute-done.1.second
  17.6 1.5 %collective-permute-start.6 = (bf16[32,1024]{1,0:T(8,128)(2,1)S(1)}, bf16[32,1024]{1,0:T(8,128)(2,1)S(1)}, u32[]{:S(2)}, u32[]{:S(2)}) collective-permute-start(bf16[32,1024]{1,0:T(8,128)(2,1)S(1)} %shard_map.97.first), channel_id=1, source_target_pairs={{8,0},{10,2},{12,4},{14,6},{0,8},{2,10},{4,12},{6,14},{9,1},{11,3}... | collective-permute-start | bytes 196616 | tf_op jit(solution)/shard_map/ppermute | solution.py:30
  19.1 0.0 collective-permute-done.4.refs_2_
  19.1 0.0 collective-permute-done.5.refs_3_
  19.1 3.4 %shard_map.99 = (f32[8,768]{1,0:T(8,128)S(1)}, f32[8,768]{1,0:T(8,128)S(1)}, f32[4,64,768]{2,1,0:T(8,128)S(1)}, f32[512,128]{1,0:T(8,128)S(1)}) custom-call(f32[8,512]{1,0:T(8,128)S(1)} %get-tuple-element.33.mask, bf16[192,512]{1,0:T(8,128)(2,1)S(1)} %get-tuple-element.65.refs_0_, bf16[192,512]{1,0:T(8,128)(2,1)S(1)} %get-tuple-element.64.refs_1_, ...), custom_call_target="tpu_custom_call" | custom-call | tf_op jit(solution)/shard_map/pallas_call | solution.py:410
  22.5 2.6 %collective-permute-done.7 = bf16[384,512]{1,0:T(8,128)(2,1)S(1)} collective-permute-done((bf16[384,512]{1,0:T(8,128)(2,1)}, bf16[384,512]{1,0:T(8,128)(2,1)S(1)}, u32[]{:S(2)}, u32[]{:S(2)}) %collective-permute-start.7) | collective-permute-done | bytes 393248 | tf_op jit(solution)/shard_map/ppermute | solution.py:30
  25.1 0.1 collective-permute-start.8
  25.2 0.5 %collective-permute-start.9 = (bf16[192,512]{1,0:T(8,128)(2,1)S(1)}, bf16[192,512]{1,0:T(8,128)(2,1)S(1)}, u32[]{:S(2)}, u32[]{:S(2)}) collective-permute-start(bf16[192,512]{1,0:T(8,128)(2,1)S(1)} %get-tuple-element.62.refs_1_), channel_id=1, source_target_pairs={{1,0},{0,1},{3,2},{2,3},{5,4},{4,5},{7,6},{6,7},{9,8},{8,9},{11,10... | collective-permute-start | bytes 589832 | tf_op jit(solution)/shard_map/ppermute | solution.py:30
  25.7 0.0 collective-permute-done.6.second
  25.7 0.1 collective-permute-start.10
  25.8 0.6 %shard_map.101.sums = f32[2,384,512]{2,1,0:T(8,128)S(1)} custom-call(bf16[192,512]{1,0:T(8,128)(2,1)S(1)} %get-tuple-element.63.refs_0_, bf16[192,512]{1,0:T(8,128)(2,1)S(1)} %get-tuple-element.62.refs_1_, bf16[3,1024,512]{2,1,0:T(8,128)(2,1)S(1)} %get-tuple-element.36.weights.refs_4_.refs_2_), custom_call_target="tpu_custom_call" | custom-call | tf_op jit(solution)/shard_map/pallas_call | solution.py:410
  26.4 0.2 collective-permute-done.8.refs_0_
  26.6 0.3 collective-permute-done.9.refs_1_
  26.9 2.4 %shard_map.102 = (f32[8,768]{1,0:T(8,128)S(1)}, f32[8,768]{1,0:T(8,128)S(1)}, f32[4,64,768]{2,1,0:T(8,128)S(1)}, f32[512,128]{1,0:T(8,128)S(1)}) custom-call(f32[8,512]{1,0:T(8,128)S(1)} %get-tuple-element.33.mask, f32[2,384,512]{2,1,0:T(8,128)S(1)} %shard_map.101.sums, bf16[192,512]{1,0:T(8,128)(2,1)S(1)} %collective-permute-done.8.refs_0_, ...), custom_call_target="tpu_custom_call" | custom-call | tf_op jit(solution)/shard_map/pallas_call | solution.py:410
  29.3 1.3 %collective-permute-done.10.second = bf16[48,1024]{1,0:T(8,128)(2,1)S(1)} collective-permute-done((bf16[48,1024]{1,0:T(8,128)(2,1)S(1)}, bf16[48,1024]{1,0:T(8,128)(2,1)S(1)}, u32[]{:S(2)}, u32[]{:S(2)}) %collective-permute-start.10) | collective-permute-done | bytes 98336 | tf_op jit(solution)/shard_map/ppermute | solution.py:30
  30.6 2.1 %shard_map.104 = (f32[400,512]{1,0:T(8,128)S(1)}, bf16[400,512]{1,0:T(8,128)(2,1)S(1)}) custom-call(f32[8,512]{1,0:T(8,128)S(1)} %get-tuple-element.33.mask, bf16[96,1024]{1,0:T(8,128)(2,1)S(1)} %shard_map.103.special_pairs, bf16[4,128,768]{2,1,0:T(8,128)(2,1)S(1)} %get-tuple-element.41.refs_5_.refs_3_.queries, ...), custom_call_target="tpu_custom_call" | custom-call | tf_op jit(solution)/shard_map/pallas_call | solution.py:410
  32.7 0.1 collective-permute-start.11
  32.7 1.7 %collective-permute-done.11.received = bf16[400,512]{1,0:T(8,128)(2,1)S(1)} collective-permute-done((bf16[400,512]{1,0:T(8,128)(2,1)S(1)}, bf16[400,512]{1,0:T(8,128)(2,1)S(1)}, u32[]{:S(2)}, u32[]{:S(2)}) %collective-permute-start.11) | collective-permute-done | bytes 409632 | tf_op jit(solution)/shard_map/ppermute | solution.py:30
  34.5 0.8 %shard_map.105 = (bf16[384,512]{1,0:T(8,128)(2,1)}, bf16[5,2,512]{2,1,0:T(2,128)(2,1)}) custom-call(f32[400,512]{1,0:T(8,128)S(1)} %get-tuple-element.58.kept, bf16[400,512]{1,0:T(8,128)(2,1)S(1)} %collective-permute-done.11.received), custom_call_target="tpu_custom_call" | custom-call | tf_op jit(solution)/shard_map/pallas_call | solution.py:410
  (5 shorter events, 0.1 us)
Async XLA Ops:
  0.6 10.9 %collective-permute-start.3 = (bf16[384,512]{1,0:T(8,128)(2,1)}, bf16[384,512]{1,0:T(8,128)(2,1)S(1)}, u32[]{:S(2)}, u32[]{:S(2)}) collective-permute-start(bf16[384,512]{1,0:T(8,128)(2,1)} %bitcast.4), channel_id=1, source_target_pairs={{1,0},{0,1},{3,2},{2,3},{5,4},{4,5},{7,6},{6,7},{9,8},{8,9},{11,10... | collective-permute-start | bytes 1179656 | tf_op jit(solution)/shard_map/ppermute | solution.py:30
  1.1 15.8 %collective-permute-start.2 = (bf16[384,512]{1,0:T(8,128)(2,1)}, bf16[384,512]{1,0:T(8,128)(2,1)S(1)}, u32[]{:S(2)}, u32[]{:S(2)}) collective-permute-start(bf16[384,512]{1,0:T(8,128)(2,1)} %bitcast.5), channel_id=1, source_target_pairs={{0,14},{2,4},{4,2},{6,8},{8,6},{10,12},{12,10},{14,0},{1,15},{3,5}... | collective-permute-start | bytes 1179656 | tf_op jit(solution)/shard_map/ppermute | solution.py:35
  7.9 1.2 %collective-permute-start = (bf16[16,512]{1,0:T(8,128)(2,1)S(1)}, bf16[16,512]{1,0:T(8,128)(2,1)S(1)}, u32[]{:S(2)}, u32[]{:S(2)}) collective-permute-start(bf16[16,512]{1,0:T(8,128)(2,1)S(1)} %get-tuple-element.32.special), channel_id=1, source_target_pairs={{1,0},{0,1},{3,2},{2,3},{5,4},{4,5},{7,6},{6,7},{9,8},{8,9},{11,10... | collective-permute-start | bytes 49160 | tf_op jit(solution)/shard_map/ppermute | solution.py:30
  8.1 17.0 %collective-permute-start.7 = (bf16[384,512]{1,0:T(8,128)(2,1)}, bf16[384,512]{1,0:T(8,128)(2,1)S(1)}, u32[]{:S(2)}, u32[]{:S(2)}) collective-permute-start(bf16[384,512]{1,0:T(8,128)(2,1)} %bitcast.7), channel_id=1, source_target_pairs={{2,0},{0,2},{6,4},{4,6},{10,8},{8,10},{14,12},{12,14},{3,1},{1,3},... | collective-permute-start | bytes 1179656 | tf_op jit(solution)/shard_map/ppermute | solution.py:30
  11.4 6.1 %collective-permute-start.1 = (bf16[16,1024]{1,0:T(8,128)(2,1)S(1)}, bf16[16,1024]{1,0:T(8,128)(2,1)S(1)}, u32[]{:S(2)}, u32[]{:S(2)}) collective-permute-start(bf16[16,1024]{1,0:T(8,128)(2,1)S(1)} %get-tuple-element.34.first), channel_id=1, source_target_pairs={{4,0},{6,2},{0,4},{2,6},{12,8},{14,10},{8,12},{10,14},{5,1},{7,3},... | collective-permute-start | bytes 98312 | tf_op jit(solution)/shard_map/ppermute | solution.py:30
  17.0 2.1 %collective-permute-start.4 = (bf16[192,512]{1,0:T(8,128)(2,1)S(1)}, bf16[192,512]{1,0:T(8,128)(2,1)S(1)}, u32[]{:S(2)}, u32[]{:S(2)}) collective-permute-start(bf16[192,512]{1,0:T(8,128)(2,1)S(1)} %get-tuple-element.65.refs_0_), channel_id=1, source_target_pairs={{1,0},{0,1},{3,2},{2,3},{5,4},{4,5},{7,6},{6,7},{9,8},{8,9},{11,10... | collective-permute-start | bytes 589832 | tf_op jit(solution)/shard_map/ppermute | solution.py:30
  17.0 2.1 %collective-permute-start.5 = (bf16[192,512]{1,0:T(8,128)(2,1)S(1)}, bf16[192,512]{1,0:T(8,128)(2,1)S(1)}, u32[]{:S(2)}, u32[]{:S(2)}) collective-permute-start(bf16[192,512]{1,0:T(8,128)(2,1)S(1)} %get-tuple-element.64.refs_1_), channel_id=1, source_target_pairs={{1,0},{0,1},{3,2},{2,3},{5,4},{4,5},{7,6},{6,7},{9,8},{8,9},{11,10... | collective-permute-start | bytes 589832 | tf_op jit(solution)/shard_map/ppermute | solution.py:30
  17.6 8.1 %collective-permute-start.6 = (bf16[32,1024]{1,0:T(8,128)(2,1)S(1)}, bf16[32,1024]{1,0:T(8,128)(2,1)S(1)}, u32[]{:S(2)}, u32[]{:S(2)}) collective-permute-start(bf16[32,1024]{1,0:T(8,128)(2,1)S(1)} %shard_map.97.first), channel_id=1, source_target_pairs={{8,0},{10,2},{12,4},{14,6},{0,8},{2,10},{4,12},{6,14},{9,1},{11,3}... | collective-permute-start | bytes 196616 | tf_op jit(solution)/shard_map/ppermute | solution.py:30
  25.1 1.5 %collective-permute-start.8 = (bf16[192,512]{1,0:T(8,128)(2,1)S(1)}, bf16[192,512]{1,0:T(8,128)(2,1)S(1)}, u32[]{:S(2)}, u32[]{:S(2)}) collective-permute-start(bf16[192,512]{1,0:T(8,128)(2,1)S(1)} %get-tuple-element.63.refs_0_), channel_id=1, source_target_pairs={{1,0},{0,1},{3,2},{2,3},{5,4},{4,5},{7,6},{6,7},{9,8},{8,9},{11,10... | collective-permute-start | bytes 589832 | tf_op jit(solution)/shard_map/ppermute | solution.py:30
  25.2 1.7 %collective-permute-start.9 = (bf16[192,512]{1,0:T(8,128)(2,1)S(1)}, bf16[192,512]{1,0:T(8,128)(2,1)S(1)}, u32[]{:S(2)}, u32[]{:S(2)}) collective-permute-start(bf16[192,512]{1,0:T(8,128)(2,1)S(1)} %get-tuple-element.62.refs_1_), channel_id=1, source_target_pairs={{1,0},{0,1},{3,2},{2,3},{5,4},{4,5},{7,6},{6,7},{9,8},{8,9},{11,10... | collective-permute-start | bytes 589832 | tf_op jit(solution)/shard_map/ppermute | solution.py:30
  25.7 4.8 %collective-permute-start.10 = (bf16[48,1024]{1,0:T(8,128)(2,1)S(1)}, bf16[48,1024]{1,0:T(8,128)(2,1)S(1)}, u32[]{:S(2)}, u32[]{:S(2)}) collective-permute-start(bf16[48,1024]{1,0:T(8,128)(2,1)S(1)} %shard_map.100.first), channel_id=1, source_target_pairs={{2,0},{0,2},{6,4},{4,6},{10,8},{8,10},{14,12},{12,14},{3,1},{1,3},... | collective-permute-start | bytes 294920 | tf_op jit(solution)/shard_map/ppermute | solution.py:30
  32.7 1.8 %collective-permute-start.11 = (bf16[400,512]{1,0:T(8,128)(2,1)S(1)}, bf16[400,512]{1,0:T(8,128)(2,1)S(1)}, u32[]{:S(2)}, u32[]{:S(2)}) collective-permute-start(bf16[400,512]{1,0:T(8,128)(2,1)S(1)} %get-tuple-element.59), channel_id=1, source_target_pairs={{1,0},{0,1},{3,2},{2,3},{5,4},{4,5},{7,6},{6,7},{9,8},{8,9},{11,10... | collective-permute-start | bytes 1228808 | tf_op jit(solution)/shard_map/ppermute | solution.py:30

commit v19 on v18

--- a/solution.py
+++ b/solution.py
@@ -332,26 +332,22 @@
         sums_out[i] = product(rows, weights[i + 1, : rows.shape[1], :])
 
 
-def begun(sums, other, weights):
-    depth = other.shape[1]
-
-    def columns(which, quad):
-        lanes = slice(quad * QUAD, (quad + 1) * QUAD)
-        return sums[which - 1, :, lanes] + product(other, weights[which, depth:, lanes])
-
-    return columns
-
-
-def begun_kernel(stretches, mask, sums, *refs):
-    count = len(stretches)
-    other = jnp.concatenate([ref[...] for ref in refs[:count]], axis=0)
+def finish_kernel(count, sums, *refs):
+    weights, pairs_out = refs[count:]
+    rows = jnp.concatenate([ref[...] for ref in refs[:count]], axis=0)
+    depth, width = rows.shape[1], weights.shape[2]
+    for i in range(2):
+        total = sums[i] + product(rows, weights[i + 1, depth:, :])
+        pairs_out[:, i * width : (i + 1) * width] = total.astype(jnp.bfloat16)
+
+
+def given_kernel(stretches, mask, key_pairs, queries, special_queries, *refs):
     masks = [(rows, mask[i : i + 1, :]) for part in stretches for rows, i in part]
-    weights, queries, special_queries = refs[count : count + 3]
-    state_in, state_out = refs[count + 3 : count + 7], refs[count + 7 :]
+    state_in, state_out = refs[:4], refs[4:]
     pairs, rows = queries.shape[0], queries.shape[2] // 2
     state = State(rows, state_out)
     for result in attend_all(
-        begun(sums, other, weights), masks, lambda pair: queries[pair], lambda: special_queries[...],
+        given(key_pairs), masks, lambda pair: queries[pair], lambda: special_queries[...],
         State(rows, state_in), pairs, rows, None,
     ):
         state.put(*result)
@@ -524,6 +520,23 @@
         )
 
     image_rows = lambda owner: [(per_image, owner * images + b) for b in range(images)]
+    def prepared(owner, parts, state):
+        (sums,) = call(
+            functools.partial(half_kernel, len(parts)),
+            [f32(2, patch_total, width)],
+            (*[part[0] for part in parts], weights),
+        )
+        (key_pairs,) = call(
+            functools.partial(finish_kernel, len(parts)),
+            [bf16(patch_total, 2 * width)],
+            (sums, *[part[1] for part in parts], weights),
+        )
+        return call(
+            functools.partial(given_kernel, stretches(owner)),
+            state_shape,
+            (mask, key_pairs, queries, special_queries, *state),
+        )
+
     def halved(part, gate):
         part = after(part, gate)
         starts = range(0, part.shape[0], per_image)
@@ -540,7 +553,7 @@
                 everywhere = stacked(everywhere, swapped(everywhere, "blk", bit))
                 bit *= 2
             arrived = swapped(everywhere, "blk", bit)
-        state = later(stretches(1), halved(far, state[0]), state)
+        state = prepared(1, halved(far, state[0]), state)
         if power:
             real = real_rows * owner_count // 2
             blocks = (real + -real % TILE_ROWS, real)
@@ -551,18 +564,7 @@
                 flops=FIRST,
             )
             arrived = swapped(everywhere, "blk", 1)
-        parts = halved(near, state[0])
-        (sums,) = call(
-            functools.partial(half_kernel, len(parts)),
-            [f32(2, patch_total, width)],
-            (*[part[0] for part in parts], weights),
-            flops=0,
-        )
-        state = call(
-            functools.partial(begun_kernel, stretches(2)),
-            state_shape,
-            (mask, sums, *[part[1] for part in parts], *fixed, *state),
-        )
+        state = prepared(2, halved(near, state[0]), state)
         if power:
             everywhere = stacked(after(everywhere, state[0]), arrived)
     else:

time: 35.5 us -> 35.5 us (level)
  Pallas kernels: 16.1 us -> 15.6 us
  waiting for transfers between devices: 9.19 us -> 9.55 us
    pallas_call x11 -> x14, Pallas kernels: 16.1 us -> 15.6 us  [call(): pl.pallas_call(kernel, out_shape=out_shape, in_specs=in_specs or [VMEM] *...]
    ppermute x11, waiting for transfers between devices: 7.14 us -> 7.5 us  [swapped(): return lax.ppermute(block, axis, [(i ^ bit, i) for i in range(count)])]
  transfers between devices with their start and end apart: 12 -> 12, of which waited for: 7 -> 7; matrix products, arithmetic and copies ran while one was open for 0% -> 0% of each run, Pallas kernels for 37% -> 36%
where the time goes in v19:
time: 35.5 us; the launch traced here: 35.3 us
  Pallas kernels  15.6 us (44%)
  waiting for transfers between devices  9.55 us (27%)
  starting transfers between devices  9.31 us (26%)
  between operations  0.78 us (2%)
    pallas_call x14, Pallas kernels, call(): pl.pallas_call(kernel, out_shape=out_shape, in_specs=in_specs or [VMEM] *...  15.6 us
    ppermute x11, waiting for transfers between devices, swapped(): return lax.ppermute(block, axis, [(i ^ bit, i) for i in range(count)])  7.5 us
    ppermute x1, starting transfers between devices, crossed(): lax.ppermute(block, axis, [(i, (i + (-1 if i % 2 == 0 else 1)) % count) f...  5.6 us
    ppermute x11, starting transfers between devices, swapped(): return lax.ppermute(block, axis, [(i ^ bit, i) for i in range(count)])  3.71 us
    ppermute x1, waiting for transfers between devices, crossed(): lax.ppermute(block, axis, [(i, (i + (-1 if i % 2 == 0 else 1)) % count) f...  2.05 us
  transfers between devices with their start and end apart: 12, of which 7 were waited for; matrix products, arithmetic and copies ran while one was open for 0% of the time, Pallas kernels for 36%

profile of v19, /device:TPU:0, one launch (start us, length us, event | category | flops | bytes accessed | tf_op | source)
XLA Modules:
  0.0 35.3 jit_solution(5992105116664452384)
XLA Ops:
  0.6 0.5 %collective-permute-start.3 = (bf16[384,512]{1,0:T(8,128)(2,1)}, bf16[384,512]{1,0:T(8,128)(2,1)S(1)}, u32[]{:S(2)}, u32[]{:S(2)}) collective-permute-start(bf16[384,512]{1,0:T(8,128)(2,1)} %bitcast.4), channel_id=1, source_target_pairs={{1,0},{0,1},{3,2},{2,3},{5,4},{4,5},{7,6},{6,7},{9,8},{8,9},{11,10... | collective-permute-start | bytes 1179656 | tf_op jit(solution)/shard_map/ppermute | solution.py:30
  1.1 5.6 %collective-permute-start.2 = (bf16[384,512]{1,0:T(8,128)(2,1)}, bf16[384,512]{1,0:T(8,128)(2,1)S(1)}, u32[]{:S(2)}, u32[]{:S(2)}) collective-permute-start(bf16[384,512]{1,0:T(8,128)(2,1)} %bitcast.5), channel_id=1, source_target_pairs={{0,14},{2,4},{4,2},{6,8},{8,6},{10,12},{12,10},{14,0},{1,15},{3,5}... | collective-permute-start | bytes 1179656 | tf_op jit(solution)/shard_map/ppermute | solution.py:35
  6.8 1.1 %shard_map.95 = (bf16[16,512]{1,0:T(8,128)(2,1)S(1)}, bf16[384,512]{1,0:T(8,128)(2,1)S(1)}) custom-call(s32[2]{0:T(128)} %frame_order.1, bf16[5,2,512]{2,1,0:T(2,128)(2,1)} %bitcast.8, bf16[5,1024]{1,0:T(8,128)(2,1)} %role_first.1, bf16[5,1024]{1,0:T(8,128)(2,1)} %role_rest.1, bf16[384,512]{1,0:T(8,128)(2,1)} %bitcast.6), custom_call_target="tpu_custom_call" | custom-call | tf_op jit(solution)/shard_map/pallas_call | solution.py:406
  7.9 0.2 collective-permute-start
  8.1 0.0 collective-permute-start.7
  8.1 1.0 %collective-permute-done.other_special = bf16[16,512]{1,0:T(8,128)(2,1)S(1)} collective-permute-done((bf16[16,512]{1,0:T(8,128)(2,1)S(1)}, bf16[16,512]{1,0:T(8,128)(2,1)S(1)}, u32[]{:S(2)}, u32[]{:S(2)}) %collective-permute-start) | collective-permute-done | bytes 16416 | tf_op jit(solution)/shard_map/ppermute | solution.py:30
  9.1 2.3 %shard_map.96 = (f32[8,512]{1,0:T(8,128)S(1)}, bf16[3,1024,512]{2,1,0:T(8,128)(2,1)S(1)}, bf16[16,1024]{1,0:T(8,128)(2,1)S(1)}, bf16[512,1024]{1,0:T(8,128)(2,1)S(1)}) custom-call(s32[2,16]{1,0:T(2,128)} %covisible.1, bf16[16,512]{1,0:T(8,128)(2,1)S(1)} %get-tuple-element.32.special, bf16[16,512]{1,0:T(8,128)(2,1)S(1)} %collective-permute-done.other_special, ...), custom_call_target="tpu_custom_call" | custom-call | tf_op jit(solution)/shard_map/pallas_call | solution.py:406
  11.4 0.1 collective-permute-start.1
  11.5 3.4 %shard_map.98 = (bf16[4,128,768]{2,1,0:T(8,128)(2,1)S(1)}, bf16[512,128]{1,0:T(8,128)(2,1)S(1)}, f32[8,768]{1,0:T(8,128)S(1)}, f32[8,768]{1,0:T(8,128)S(1)}, f32...) custom-call(f32[8,512]{1,0:T(8,128)S(1)} %get-tuple-element.33.mask, bf16[384,512]{1,0:T(8,128)(2,1)S(1)} %get-tuple-element.35.own, ...), custom_call_target="tpu_custom_call" | custom-call | tf_op jit(solution)/shard_map/pallas_call | solution.py:406
  14.9 2.1 %collective-permute-done.2 = bf16[384,512]{1,0:T(8,128)(2,1)S(1)} collective-permute-done((bf16[384,512]{1,0:T(8,128)(2,1)}, bf16[384,512]{1,0:T(8,128)(2,1)S(1)}, u32[]{:S(2)}, u32[]{:S(2)}) %collective-permute-start.2) | collective-permute-done | bytes 393248 | tf_op jit(solution)/shard_map/ppermute | solution.py:35
  17.0 0.1 collective-permute-start.4
  17.0 0.5 %collective-permute-start.5 = (bf16[192,512]{1,0:T(8,128)(2,1)S(1)}, bf16[192,512]{1,0:T(8,128)(2,1)S(1)}, u32[]{:S(2)}, u32[]{:S(2)}) collective-permute-start(bf16[192,512]{1,0:T(8,128)(2,1)S(1)} %get-tuple-element.64.refs_1_), channel_id=1, source_target_pairs={{1,0},{0,1},{3,2},{2,3},{5,4},{4,5},{7,6},{6,7},{9,8},{8,9},{11,10... | collective-permute-start | bytes 589832 | tf_op jit(solution)/shard_map/ppermute | solution.py:30
  17.5 0.0 collective-permute-done.1.second
  17.6 0.6 %shard_map.99.sums = f32[2,384,512]{2,1,0:T(8,128)S(1)} custom-call(bf16[192,512]{1,0:T(8,128)(2,1)S(1)} %get-tuple-element.65.refs_0_, bf16[192,512]{1,0:T(8,128)(2,1)S(1)} %get-tuple-element.64.refs_1_, bf16[3,1024,512]{2,1,0:T(8,128)(2,1)S(1)} %get-tuple-element.36.weights.refs_2_), custom_call_target="tpu_custom_call" | custom-call | tf_op jit(solution)/shard_map/pallas_call | solution.py:406
  18.1 1.6 %collective-permute-start.6 = (bf16[32,1024]{1,0:T(8,128)(2,1)S(1)}, bf16[32,1024]{1,0:T(8,128)(2,1)S(1)}, u32[]{:S(2)}, u32[]{:S(2)}) collective-permute-start(bf16[32,1024]{1,0:T(8,128)(2,1)S(1)} %shard_map.97.first), channel_id=1, source_target_pairs={{8,0},{10,2},{12,4},{14,6},{0,8},{2,10},{4,12},{6,14},{9,1},{11,3}... | collective-permute-start | bytes 196616 | tf_op jit(solution)/shard_map/ppermute | solution.py:30
  19.7 0.0 collective-permute-done.5.refs_1_
  19.7 0.6 %shard_map.100.key_pairs = bf16[384,1024]{1,0:T(8,128)(2,1)S(1)} custom-call(f32[2,384,512]{2,1,0:T(8,128)S(1)} %shard_map.99.sums, bf16[192,512]{1,0:T(8,128)(2,1)S(1)} %collective-permute-done.4.refs_0_, bf16[192,512]{1,0:T(8,128)(2,1)S(1)} %collective-permute-done.5.refs_1_, bf16[3,1024,512]{2,1,0:T(8,128)(2,1)S(1)} %get-tuple-element.36.weights.refs_2_), custom_call_target="tpu_custom_call" | custom-call | tf_op jit(solution)/shard_map/pallas_call | solution.py:406
  20.3 1.8 %shard_map.101 = (f32[8,768]{1,0:T(8,128)S(1)}, f32[8,768]{1,0:T(8,128)S(1)}, f32[4,64,768]{2,1,0:T(8,128)S(1)}, f32[512,128]{1,0:T(8,128)S(1)}) custom-call(f32[8,512]{1,0:T(8,128)S(1)} %get-tuple-element.33.mask, bf16[384,1024]{1,0:T(8,128)(2,1)S(1)} %shard_map.100.key_pairs, bf16[4,128,768]{2,1,0:T(8,128)(2,1)S(1)} %get-tuple-element.41.queries, ...), custom_call_target="tpu_custom_call" | custom-call | tf_op jit(solution)/shard_map/pallas_call | solution.py:406
  22.1 2.9 %collective-permute-done.7 = bf16[384,512]{1,0:T(8,128)(2,1)S(1)} collective-permute-done((bf16[384,512]{1,0:T(8,128)(2,1)}, bf16[384,512]{1,0:T(8,128)(2,1)S(1)}, u32[]{:S(2)}, u32[]{:S(2)}) %collective-permute-start.7) | collective-permute-done | bytes 393248 | tf_op jit(solution)/shard_map/ppermute | solution.py:30
  25.1 0.1 collective-permute-start.8
  25.2 0.5 %collective-permute-start.9 = (bf16[192,512]{1,0:T(8,128)(2,1)S(1)}, bf16[192,512]{1,0:T(8,128)(2,1)S(1)}, u32[]{:S(2)}, u32[]{:S(2)}) collective-permute-start(bf16[192,512]{1,0:T(8,128)(2,1)S(1)} %get-tuple-element.62.refs_1_), channel_id=1, source_target_pairs={{1,0},{0,1},{3,2},{2,3},{5,4},{4,5},{7,6},{6,7},{9,8},{8,9},{11,10... | collective-permute-start | bytes 589832 | tf_op jit(solution)/shard_map/ppermute | solution.py:30
  25.7 0.1 collective-permute-start.10
  25.8 0.6 %shard_map.103.sums = f32[2,384,512]{2,1,0:T(8,128)S(1)} custom-call(bf16[192,512]{1,0:T(8,128)(2,1)S(1)} %get-tuple-element.63.refs_0_, bf16[192,512]{1,0:T(8,128)(2,1)S(1)} %get-tuple-element.62.refs_1_, bf16[3,1024,512]{2,1,0:T(8,128)(2,1)S(1)} %get-tuple-element.36.weights.refs_2_), custom_call_target="tpu_custom_call" | custom-call | tf_op jit(solution)/shard_map/pallas_call | solution.py:406
  26.4 0.2 collective-permute-done.8.refs_0_
  26.6 0.3 collective-permute-done.9.refs_1_
  26.9 0.6 %shard_map.104.key_pairs = bf16[384,1024]{1,0:T(8,128)(2,1)S(1)} custom-call(f32[2,384,512]{2,1,0:T(8,128)S(1)} %shard_map.103.sums, bf16[192,512]{1,0:T(8,128)(2,1)S(1)} %collective-permute-done.8.refs_0_, bf16[192,512]{1,0:T(8,128)(2,1)S(1)} %collective-permute-done.9.refs_1_, bf16[3,1024,512]{2,1,0:T(8,128)(2,1)S(1)} %get-tuple-element.36.weights.refs_2_), custom_call_target="tpu_custom_call" | custom-call | tf_op jit(solution)/shard_map/pallas_call | solution.py:406
  27.5 1.8 %shard_map.105 = (f32[8,768]{1,0:T(8,128)S(1)}, f32[8,768]{1,0:T(8,128)S(1)}, f32[4,64,768]{2,1,0:T(8,128)S(1)}, f32[512,128]{1,0:T(8,128)S(1)}) custom-call(f32[8,512]{1,0:T(8,128)S(1)} %get-tuple-element.33.mask, bf16[384,1024]{1,0:T(8,128)(2,1)S(1)} %shard_map.104.key_pairs, bf16[4,128,768]{2,1,0:T(8,128)(2,1)S(1)} %get-tuple-element.41.queries, ...), custom_call_target="tpu_custom_call" | custom-call | tf_op jit(solution)/shard_map/pallas_call | solution.py:406
  29.3 1.3 %collective-permute-done.10.second = bf16[48,1024]{1,0:T(8,128)(2,1)S(1)} collective-permute-done((bf16[48,1024]{1,0:T(8,128)(2,1)S(1)}, bf16[48,1024]{1,0:T(8,128)(2,1)S(1)}, u32[]{:S(2)}, u32[]{:S(2)}) %collective-permute-start.10) | collective-permute-done | bytes 98336 | tf_op jit(solution)/shard_map/ppermute | solution.py:30
  30.6 2.1 %shard_map.107 = (f32[400,512]{1,0:T(8,128)S(1)}, bf16[400,512]{1,0:T(8,128)(2,1)S(1)}) custom-call(f32[8,512]{1,0:T(8,128)S(1)} %get-tuple-element.33.mask, bf16[96,1024]{1,0:T(8,128)(2,1)S(1)} %shard_map.106.special_pairs, bf16[4,128,768]{2,1,0:T(8,128)(2,1)S(1)} %get-tuple-element.41.queries, bf16[512,128]{1,0:T(8,128)(2,1)S(1)} %get-tuple-element.42.special_queries, ...), custom_call_target="tpu_custom_call" | custom-call | tf_op jit(solution)/shard_map/pallas_call | solution.py:406
  32.7 0.1 collective-permute-start.11
  32.7 1.7 %collective-permute-done.11.received = bf16[400,512]{1,0:T(8,128)(2,1)S(1)} collective-permute-done((bf16[400,512]{1,0:T(8,128)(2,1)S(1)}, bf16[400,512]{1,0:T(8,128)(2,1)S(1)}, u32[]{:S(2)}, u32[]{:S(2)}) %collective-permute-start.11) | collective-permute-done | bytes 409632 | tf_op jit(solution)/shard_map/ppermute | solution.py:30
  34.5 0.8 %shard_map.108 = (bf16[384,512]{1,0:T(8,128)(2,1)}, bf16[5,2,512]{2,1,0:T(2,128)(2,1)}) custom-call(f32[400,512]{1,0:T(8,128)S(1)} %get-tuple-element.58.kept, bf16[400,512]{1,0:T(8,128)(2,1)S(1)} %collective-permute-done.11.received), custom_call_target="tpu_custom_call" | custom-call | tf_op jit(solution)/shard_map/pallas_call | solution.py:406
  (8 shorter events, 0.1 us)
Async XLA Ops:
  0.6 10.9 %collective-permute-start.3 = (bf16[384,512]{1,0:T(8,128)(2,1)}, bf16[384,512]{1,0:T(8,128)(2,1)S(1)}, u32[]{:S(2)}, u32[]{:S(2)}) collective-permute-start(bf16[384,512]{1,0:T(8,128)(2,1)} %bitcast.4), channel_id=1, source_target_pairs={{1,0},{0,1},{3,2},{2,3},{5,4},{4,5},{7,6},{6,7},{9,8},{8,9},{11,10... | collective-permute-start | bytes 1179656 | tf_op jit(solution)/shard_map/ppermute | solution.py:30
  1.1 15.8 %collective-permute-start.2 = (bf16[384,512]{1,0:T(8,128)(2,1)}, bf16[384,512]{1,0:T(8,128)(2,1)S(1)}, u32[]{:S(2)}, u32[]{:S(2)}) collective-permute-start(bf16[384,512]{1,0:T(8,128)(2,1)} %bitcast.5), channel_id=1, source_target_pairs={{0,14},{2,4},{4,2},{6,8},{8,6},{10,12},{12,10},{14,0},{1,15},{3,5}... | collective-permute-start | bytes 1179656 | tf_op jit(solution)/shard_map/ppermute | solution.py:35
  7.9 1.2 %collective-permute-start = (bf16[16,512]{1,0:T(8,128)(2,1)S(1)}, bf16[16,512]{1,0:T(8,128)(2,1)S(1)}, u32[]{:S(2)}, u32[]{:S(2)}) collective-permute-start(bf16[16,512]{1,0:T(8,128)(2,1)S(1)} %get-tuple-element.32.special), channel_id=1, source_target_pairs={{1,0},{0,1},{3,2},{2,3},{5,4},{4,5},{7,6},{6,7},{9,8},{8,9},{11,10... | collective-permute-start | bytes 49160 | tf_op jit(solution)/shard_map/ppermute | solution.py:30
  8.1 17.0 %collective-permute-start.7 = (bf16[384,512]{1,0:T(8,128)(2,1)}, bf16[384,512]{1,0:T(8,128)(2,1)S(1)}, u32[]{:S(2)}, u32[]{:S(2)}) collective-permute-start(bf16[384,512]{1,0:T(8,128)(2,1)} %bitcast.7), channel_id=1, source_target_pairs={{2,0},{0,2},{6,4},{4,6},{10,8},{8,10},{14,12},{12,14},{3,1},{1,3},... | collective-permute-start | bytes 1179656 | tf_op jit(solution)/shard_map/ppermute | solution.py:30
  11.4 6.1 %collective-permute-start.1 = (bf16[16,1024]{1,0:T(8,128)(2,1)S(1)}, bf16[16,1024]{1,0:T(8,128)(2,1)S(1)}, u32[]{:S(2)}, u32[]{:S(2)}) collective-permute-start(bf16[16,1024]{1,0:T(8,128)(2,1)S(1)} %get-tuple-element.34.first), channel_id=1, source_target_pairs={{4,0},{6,2},{0,4},{2,6},{12,8},{14,10},{8,12},{10,14},{5,1},{7,3},... | collective-permute-start | bytes 98312 | tf_op jit(solution)/shard_map/ppermute | solution.py:30
  17.0 2.8 %collective-permute-start.4 = (bf16[192,512]{1,0:T(8,128)(2,1)S(1)}, bf16[192,512]{1,0:T(8,128)(2,1)S(1)}, u32[]{:S(2)}, u32[]{:S(2)}) collective-permute-start(bf16[192,512]{1,0:T(8,128)(2,1)S(1)} %get-tuple-element.65.refs_0_), channel_id=1, source_target_pairs={{1,0},{0,1},{3,2},{2,3},{5,4},{4,5},{7,6},{6,7},{9,8},{8,9},{11,10... | collective-permute-start | bytes 589832 | tf_op jit(solution)/shard_map/ppermute | solution.py:30
  17.0 2.7 %collective-permute-start.5 = (bf16[192,512]{1,0:T(8,128)(2,1)S(1)}, bf16[192,512]{1,0:T(8,128)(2,1)S(1)}, u32[]{:S(2)}, u32[]{:S(2)}) collective-permute-start(bf16[192,512]{1,0:T(8,128)(2,1)S(1)} %get-tuple-element.64.refs_1_), channel_id=1, source_target_pairs={{1,0},{0,1},{3,2},{2,3},{5,4},{4,5},{7,6},{6,7},{9,8},{8,9},{11,10... | collective-permute-start | bytes 589832 | tf_op jit(solution)/shard_map/ppermute | solution.py:30
  18.1 7.6 %collective-permute-start.6 = (bf16[32,1024]{1,0:T(8,128)(2,1)S(1)}, bf16[32,1024]{1,0:T(8,128)(2,1)S(1)}, u32[]{:S(2)}, u32[]{:S(2)}) collective-permute-start(bf16[32,1024]{1,0:T(8,128)(2,1)S(1)} %shard_map.97.first), channel_id=1, source_target_pairs={{8,0},{10,2},{12,4},{14,6},{0,8},{2,10},{4,12},{6,14},{9,1},{11,3}... | collective-permute-start | bytes 196616 | tf_op jit(solution)/shard_map/ppermute | solution.py:30
  25.1 1.5 %collective-permute-start.8 = (bf16[192,512]{1,0:T(8,128)(2,1)S(1)}, bf16[192,512]{1,0:T(8,128)(2,1)S(1)}, u32[]{:S(2)}, u32[]{:S(2)}) collective-permute-start(bf16[192,512]{1,0:T(8,128)(2,1)S(1)} %get-tuple-element.63.refs_0_), channel_id=1, source_target_pairs={{1,0},{0,1},{3,2},{2,3},{5,4},{4,5},{7,6},{6,7},{9,8},{8,9},{11,10... | collective-permute-start | bytes 589832 | tf_op jit(solution)/shard_map/ppermute | solution.py:30
  25.2 1.7 %collective-permute-start.9 = (bf16[192,512]{1,0:T(8,128)(2,1)S(1)}, bf16[192,512]{1,0:T(8,128)(2,1)S(1)}, u32[]{:S(2)}, u32[]{:S(2)}) collective-permute-start(bf16[192,512]{1,0:T(8,128)(2,1)S(1)} %get-tuple-element.62.refs_1_), channel_id=1, source_target_pairs={{1,0},{0,1},{3,2},{2,3},{5,4},{4,5},{7,6},{6,7},{9,8},{8,9},{11,10... | collective-permute-start | bytes 589832 | tf_op jit(solution)/shard_map/ppermute | solution.py:30
  25.7 4.8 %collective-permute-start.10 = (bf16[48,1024]{1,0:T(8,128)(2,1)S(1)}, bf16[48,1024]{1,0:T(8,128)(2,1)S(1)}, u32[]{:S(2)}, u32[]{:S(2)}) collective-permute-start(bf16[48,1024]{1,0:T(8,128)(2,1)S(1)} %shard_map.102.first), channel_id=1, source_target_pairs={{2,0},{0,2},{6,4},{4,6},{10,8},{8,10},{14,12},{12,14},{3,1},{1,3},... | collective-permute-start | bytes 294920 | tf_op jit(solution)/shard_map/ppermute | solution.py:30
  32.7 1.8 %collective-permute-start.11 = (bf16[400,512]{1,0:T(8,128)(2,1)S(1)}, bf16[400,512]{1,0:T(8,128)(2,1)S(1)}, u32[]{:S(2)}, u32[]{:S(2)}) collective-permute-start(bf16[400,512]{1,0:T(8,128)(2,1)S(1)} %get-tuple-element.59), channel_id=1, source_target_pairs={{1,0},{0,1},{3,2},{2,3},{5,4},{4,5},{7,6},{6,7},{9,8},{8,9},{11,10... | collective-permute-start | bytes 1228808 | tf_op jit(solution)/shard_map/ppermute | solution.py:30

commit v20 on v19

--- a/solution.py
+++ b/solution.py
@@ -504,7 +504,7 @@
         scratch=[pltpu.SMEM(covisible.shape, jnp.int32), pltpu.SemaphoreType.DMA((1 + 7,))],
     )
     if paired and power:
-        everywhere = stacked(everywhere, swapped(everywhere, "blk", 2), FIRST)
+        everywhere = stacked(everywhere, swapped(everywhere, "blk", 2), FIRST // 10)
     queries, special_queries, *state = call(
         functools.partial(first_kernel, images),
         [bf16(pairs, PAIR, 2 * patch_total), bf16(width, heads * special_block), *state_shape],
@@ -537,23 +537,27 @@
             (mask, key_pairs, queries, special_queries, *state),
         )
 
-    def halved(part, gate):
+    def halved(part, gate, step=per_image):
         part = after(part, gate)
-        starts = range(0, part.shape[0], per_image)
-        return [both(part[start : start + per_image]) for start in starts]
+        return [both(part[start : start + step]) for start in range(0, part.shape[0], step)]
 
     stretches = lambda owner: [[image] for image in image_rows(owner)]
     if paired:
-        far = after(crossed(patches, "blk"), state[0])
+        piece = patch_total // 3
+        far = [
+            after(crossed(own[start : start + piece], "blk"), state[0])
+            for start in range(0, patch_total, piece)
+        ]
         near = swapped(patches, "blk", 1)
         if power:
-            everywhere = after(everywhere, far)
+            everywhere = after(everywhere, *far)
             bit = 4
             while 2 * bit < owner_count:
                 everywhere = stacked(everywhere, swapped(everywhere, "blk", bit))
                 bit *= 2
             arrived = swapped(everywhere, "blk", bit)
-        state = prepared(1, halved(far, state[0]), state)
+        parts = [half for part in far for half in halved(part, state[0], piece)]
+        state = prepared(1, parts, state)
         if power:
             real = real_rows * owner_count // 2
             blocks = (real + -real % TILE_ROWS, real)

time: 35.5 us -> 37.7 us (1.062)
  starting transfers between devices: 9.31 us -> 13.3 us
  waiting for transfers between devices: 9.55 us -> 7.78 us
    ppermute x1 -> x3, starting transfers between devices: 5.6 us -> 8.36 us  [crossed(): lax.ppermute(block, axis, [(i, (i + (-1 if i % 2 == 0 else 1)) % count) f...]
    ppermute x11 -> x12, starting transfers between devices: 3.71 us -> 4.92 us  [swapped(): return lax.ppermute(block, axis, [(i ^ bit, i) for i in range(count)])]
    ppermute x1 -> x3, waiting for transfers between devices: 2.05 us -> 0.88 us  [crossed(): lax.ppermute(block, axis, [(i, (i + (-1 if i % 2 == 0 else 1)) % count) f...]
    ppermute x11 -> x12, waiting for transfers between devices: 7.5 us -> 6.91 us  [swapped(): return lax.ppermute(block, axis, [(i ^ bit, i) for i in range(count)])]
  transfers between devices with their start and end apart: 12 -> 15, of which waited for: 7 -> 6; matrix products, arithmetic and copies ran while one was open for 0% -> 0% of each run, Pallas kernels for 36% -> 34%
where the time goes in v20:
time: 37.7 us; the launch traced here: 37.5 us
  Pallas kernels  15.6 us (41%)
  starting transfers between devices  13.3 us (35%)
  waiting for transfers between devices  7.78 us (21%)
  between operations  0.8 us (2%)
    pallas_call x14, Pallas kernels, call(): pl.pallas_call(kernel, out_shape=out_shape, in_specs=in_specs or [VMEM] *...  15.6 us
    ppermute x3, starting transfers between devices, crossed(): lax.ppermute(block, axis, [(i, (i + (-1 if i % 2 == 0 else 1)) % count) f...  8.36 us
    ppermute x12, waiting for transfers between devices, swapped(): return lax.ppermute(block, axis, [(i ^ bit, i) for i in range(count)])  6.91 us
    ppermute x12, starting transfers between devices, swapped(): return lax.ppermute(block, axis, [(i ^ bit, i) for i in range(count)])  4.92 us
    ppermute x3, waiting for transfers between devices, crossed(): lax.ppermute(block, axis, [(i, (i + (-1 if i % 2 == 0 else 1)) % count) f...  0.88 us
  transfers between devices with their start and end apart: 15, of which 6 were waited for; matrix products, arithmetic and copies ran while one was open for 0% of the time, Pallas kernels for 34%

profile of v20, /device:TPU:0, one launch (start us, length us, event | category | flops | bytes accessed | tf_op | source)
XLA Modules:
  0.0 37.5 jit_solution(10573307125310835258)
XLA Ops:
  0.6 0.5 %collective-permute-start.3 = (bf16[384,512]{1,0:T(8,128)(2,1)}, bf16[384,512]{1,0:T(8,128)(2,1)S(1)}, u32[]{:S(2)}, u32[]{:S(2)}) collective-permute-start(bf16[384,512]{1,0:T(8,128)(2,1)} %bitcast.4), channel_id=1, source_target_pairs={{1,0},{0,1},{3,2},{2,3},{5,4},{4,5},{7,6},{6,7},{9,8},{8,9},{11,10... | collective-permute-start | bytes 1179656 | tf_op jit(solution)/shard_map/ppermute | solution.py:30
  1.1 2.6 %collective-permute-start.10 = (bf16[384,512]{1,0:T(8,128)(2,1)}, bf16[384,512]{1,0:T(8,128)(2,1)S(1)}, u32[]{:S(2)}, u32[]{:S(2)}) collective-permute-start(bf16[384,512]{1,0:T(8,128)(2,1)} %bitcast.5), channel_id=1, source_target_pairs={{2,0},{0,2},{6,4},{4,6},{10,8},{8,10},{14,12},{12,14},{3,1},{1,3},... | collective-permute-start | bytes 1179656 | tf_op jit(solution)/shard_map/ppermute | solution.py:30
  3.7 1.1 %shard_map.95 = (bf16[16,512]{1,0:T(8,128)(2,1)S(1)}, bf16[384,512]{1,0:T(8,128)(2,1)S(1)}) custom-call(s32[2]{0:T(128)} %frame_order.1, bf16[5,2,512]{2,1,0:T(2,128)(2,1)} %bitcast.7, bf16[5,1024]{1,0:T(8,128)(2,1)} %role_first.1, bf16[5,1024]{1,0:T(8,128)(2,1)} %role_rest.1, bf16[384,512]{1,0:T(8,128)(2,1)} %bitcast.6), custom_call_target="tpu_custom_call" | custom-call | tf_op jit(solution)/shard_map/pallas_call | solution.py:406
  4.8 0.2 collective-permute-start
  5.1 3.6 %collective-permute-start.2 = (bf16[128,512]{1,0:T(8,128)(2,1)S(1)}, bf16[128,512]{1,0:T(8,128)(2,1)S(1)}, u32[]{:S(2)}, u32[]{:S(2)}) collective-permute-start(bf16[128,512]{1,0:T(8,128)(2,1)S(1)} %get-tuple-element.74), channel_id=1, source_target_pairs={{0,14},{2,4},{4,2},{6,8},{8,6},{10,12},{12,10},{14,0},{1,15},{3,5}... | collective-permute-start | bytes 393224 | tf_op jit(solution)/shard_map/ppermute | solution.py:35
  8.7 1.1 %collective-permute-start.4 = (bf16[128,512]{1,0:T(8,128)(2,1)S(1)}, bf16[128,512]{1,0:T(8,128)(2,1)S(1)}, u32[]{:S(2)}, u32[]{:S(2)}) collective-permute-start(bf16[128,512]{1,0:T(8,128)(2,1)S(1)} %get-tuple-element.73), channel_id=1, source_target_pairs={{0,14},{2,4},{4,2},{6,8},{8,6},{10,12},{12,10},{14,0},{1,15},{3,5}... | collective-permute-start | bytes 393224 | tf_op jit(solution)/shard_map/ppermute | solution.py:35
  9.9 3.6 %collective-permute-start.5 = (bf16[128,512]{1,0:T(8,128)(2,1)S(1)}, bf16[128,512]{1,0:T(8,128)(2,1)S(1)}, u32[]{:S(2)}, u32[]{:S(2)}) collective-permute-start(bf16[128,512]{1,0:T(8,128)(2,1)S(1)} %get-tuple-element.72), channel_id=1, source_target_pairs={{0,14},{2,4},{4,2},{6,8},{8,6},{10,12},{12,10},{14,0},{1,15},{3,5}... | collective-permute-start | bytes 393224 | tf_op jit(solution)/shard_map/ppermute | solution.py:35
  13.5 2.3 %shard_map.96 = (f32[8,512]{1,0:T(8,128)S(1)}, bf16[3,1024,512]{2,1,0:T(8,128)(2,1)S(1)}, bf16[16,1024]{1,0:T(8,128)(2,1)S(1)}, bf16[512,1024]{1,0:T(8,128)(2,1)S(1)}) custom-call(s32[2,16]{1,0:T(2,128)} %covisible.1, bf16[16,512]{1,0:T(8,128)(2,1)S(1)} %get-tuple-element.36.special, bf16[16,512]{1,0:T(8,128)(2,1)S(1)} %collective-permute-done.other_special, ...), custom_call_target="tpu_custom_call" | custom-call | tf_op jit(solution)/shard_map/pallas_call | solution.py:406
  15.8 0.1 collective-permute-start.1
  15.8 3.4 %shard_map.98 = (bf16[4,128,768]{2,1,0:T(8,128)(2,1)S(1)}, bf16[512,128]{1,0:T(8,128)(2,1)S(1)}, f32[8,768]{1,0:T(8,128)S(1)}, f32[8,768]{1,0:T(8,128)S(1)}, f32...) custom-call(f32[8,512]{1,0:T(8,128)S(1)} %get-tuple-element.37.mask, bf16[384,512]{1,0:T(8,128)(2,1)S(1)} %get-tuple-element.39.own, ...), custom_call_target="tpu_custom_call" | custom-call | tf_op jit(solution)/shard_map/pallas_call | solution.py:406
  19.2 0.9 %collective-permute-done.5.refs_2_ = bf16[128,512]{1,0:T(8,128)(2,1)S(1)} collective-permute-done((bf16[128,512]{1,0:T(8,128)(2,1)S(1)}, bf16[128,512]{1,0:T(8,128)(2,1)S(1)}, u32[]{:S(2)}, u32[]{:S(2)}) %collective-permute-start.5) | collective-permute-done | bytes 131104 | tf_op jit(solution)/shard_map/ppermute | solution.py:35
  20.1 0.5 %collective-permute-start.7 = (bf16[128,512]{1,0:T(8,128)(2,1)S(1)}, bf16[128,512]{1,0:T(8,128)(2,1)S(1)}, u32[]{:S(2)}, u32[]{:S(2)}) collective-permute-start(bf16[128,512]{1,0:T(8,128)(2,1)S(1)} %collective-permute-done.4.refs_1_), channel_id=1, source_target_pairs={{1,0},{0,1},{3,2},{2,3},{5,4},{4,5},{7,6},{6,7},{9,8},{8,9},{11,10... | collective-permute-start | bytes 393224 | tf_op jit(solution)/shard_map/ppermute | solution.py:30
  20.6 0.0 collective-permute-start.8
  20.6 0.6 %shard_map.99.sums = f32[2,384,512]{2,1,0:T(8,128)S(1)} custom-call(bf16[128,512]{1,0:T(8,128)(2,1)S(1)} %collective-permute-done.2.refs_0_, bf16[128,512]{1,0:T(8,128)(2,1)S(1)} %collective-permute-done.4.refs_1_, bf16[128,512]{1,0:T(8,128)(2,1)S(1)} %collective-permute-done.5.refs_2_, bf16[3,1024,512]{2,1,0:T(8,128)(2,1)S(1)} %get-tuple-element.40.weights.refs_3_.refs_2_), custom_call_target="tpu_custom_call" | custom-call | tf_op jit(solution)/shard_map/pallas_call | solution.py:406
  21.2 0.2 collective-permute-start.9
  21.4 0.0 collective-permute-done.6.refs_0_
  21.5 0.2 collective-permute-done.7.refs_1_
  21.7 0.3 collective-permute-done.8.refs_2_
  22.0 0.6 %shard_map.100.key_pairs = bf16[384,1024]{1,0:T(8,128)(2,1)S(1)} custom-call(f32[2,384,512]{2,1,0:T(8,128)S(1)} %shard_map.99.sums, bf16[128,512]{1,0:T(8,128)(2,1)S(1)} %collective-permute-done.6.refs_0_, bf16[128,512]{1,0:T(8,128)(2,1)S(1)} %collective-permute-done.7.refs_1_, bf16[128,512]{1,0:T(8,128)(2,1)S(1)} %collective-permute-done.8.refs_2_, ...), custom_call_target="tpu_custom_call" | custom-call | tf_op jit(solution)/shard_map/pallas_call | solution.py:406
  22.6 1.8 %shard_map.101 = (f32[8,768]{1,0:T(8,128)S(1)}, f32[8,768]{1,0:T(8,128)S(1)}, f32[4,64,768]{2,1,0:T(8,128)S(1)}, f32[512,128]{1,0:T(8,128)S(1)}) custom-call(f32[8,512]{1,0:T(8,128)S(1)} %get-tuple-element.37.mask, bf16[384,1024]{1,0:T(8,128)(2,1)S(1)} %shard_map.100.key_pairs, bf16[4,128,768]{2,1,0:T(8,128)(2,1)S(1)} %get-tuple-element.49.queries, ...), custom_call_target="tpu_custom_call" | custom-call | tf_op jit(solution)/shard_map/pallas_call | solution.py:406
  24.4 0.3 collective-permute-start.11
  24.7 0.3 collective-permute-start.12
  25.0 3.1 %collective-permute-done.9.second = bf16[32,1024]{1,0:T(8,128)(2,1)S(1)} collective-permute-done((bf16[32,1024]{1,0:T(8,128)(2,1)S(1)}, bf16[32,1024]{1,0:T(8,128)(2,1)S(1)}, u32[]{:S(2)}, u32[]{:S(2)}) %collective-permute-start.9) | collective-permute-done | bytes 65568 | tf_op jit(solution)/shard_map/ppermute | solution.py:30
  28.1 0.2 collective-permute-start.13
  28.3 0.6 %shard_map.103.sums = f32[2,384,512]{2,1,0:T(8,128)S(1)} custom-call(bf16[192,512]{1,0:T(8,128)(2,1)S(1)} %get-tuple-element.71.refs_0_, bf16[192,512]{1,0:T(8,128)(2,1)S(1)} %get-tuple-element.70.refs_1_, bf16[3,1024,512]{2,1,0:T(8,128)(2,1)S(1)} %get-tuple-element.40.weights.refs_3_.refs_2_), custom_call_target="tpu_custom_call" | custom-call | tf_op jit(solution)/shard_map/pallas_call | solution.py:406
  28.9 0.6 %shard_map.104.key_pairs = bf16[384,1024]{1,0:T(8,128)(2,1)S(1)} custom-call(f32[2,384,512]{2,1,0:T(8,128)S(1)} %shard_map.103.sums, bf16[192,512]{1,0:T(8,128)(2,1)S(1)} %collective-permute-done.11.refs_0_, bf16[192,512]{1,0:T(8,128)(2,1)S(1)} %collective-permute-done.12.refs_1_, bf16[3,1024,512]{2,1,0:T(8,128)(2,1)S(1)} %get-tuple-element.40.weights.refs_3_.refs_2_), custom_call_target="tpu_custom_call" | custom-call | tf_op jit(solution)/shard_map/pallas_call | solution.py:406
  29.4 1.8 %shard_map.105 = (f32[8,768]{1,0:T(8,128)S(1)}, f32[8,768]{1,0:T(8,128)S(1)}, f32[4,64,768]{2,1,0:T(8,128)S(1)}, f32[512,128]{1,0:T(8,128)S(1)}) custom-call(f32[8,512]{1,0:T(8,128)S(1)} %get-tuple-element.37.mask, bf16[384,1024]{1,0:T(8,128)(2,1)S(1)} %shard_map.104.key_pairs, bf16[4,128,768]{2,1,0:T(8,128)(2,1)S(1)} %get-tuple-element.49.queries, ...), custom_call_target="tpu_custom_call" | custom-call | tf_op jit(solution)/shard_map/pallas_call | solution.py:406
  31.3 1.5 %collective-permute-done.13.second = bf16[48,1024]{1,0:T(8,128)(2,1)S(1)} collective-permute-done((bf16[48,1024]{1,0:T(8,128)(2,1)S(1)}, bf16[48,1024]{1,0:T(8,128)(2,1)S(1)}, u32[]{:S(2)}, u32[]{:S(2)}) %collective-permute-start.13) | collective-permute-done | bytes 98336 | tf_op jit(solution)/shard_map/ppermute | solution.py:30
  32.8 2.1 %shard_map.107 = (f32[400,512]{1,0:T(8,128)S(1)}, bf16[400,512]{1,0:T(8,128)(2,1)S(1)}) custom-call(f32[8,512]{1,0:T(8,128)S(1)} %get-tuple-element.37.mask, bf16[96,1024]{1,0:T(8,128)(2,1)S(1)} %shard_map.106.special_pairs, bf16[4,128,768]{2,1,0:T(8,128)(2,1)S(1)} %get-tuple-element.49.queries, bf16[512,128]{1,0:T(8,128)(2,1)S(1)} %get-tuple-element.50.special_queries, ...), custom_call_target="tpu_custom_call" | custom-call | tf_op jit(solution)/shard_map/pallas_call | solution.py:406
  34.9 0.1 collective-permute-start.14
  35.0 1.7 %collective-permute-done.14.received = bf16[400,512]{1,0:T(8,128)(2,1)S(1)} collective-permute-done((bf16[400,512]{1,0:T(8,128)(2,1)S(1)}, bf16[400,512]{1,0:T(8,128)(2,1)S(1)}, u32[]{:S(2)}, u32[]{:S(2)}) %collective-permute-start.14) | collective-permute-done | bytes 409632 | tf_op jit(solution)/shard_map/ppermute | solution.py:30
  36.7 0.8 %shard_map.108 = (bf16[384,512]{1,0:T(8,128)(2,1)}, bf16[5,2,512]{2,1,0:T(2,128)(2,1)}) custom-call(f32[400,512]{1,0:T(8,128)S(1)} %get-tuple-element.66.kept, bf16[400,512]{1,0:T(8,128)(2,1)S(1)} %collective-permute-done.14.received), custom_call_target="tpu_custom_call" | custom-call | tf_op jit(solution)/shard_map/pallas_call | solution.py:406
  (14 shorter events, 0.1 us)
Async XLA Ops:
  0.6 15.1 %collective-permute-start.3 = (bf16[384,512]{1,0:T(8,128)(2,1)}, bf16[384,512]{1,0:T(8,128)(2,1)S(1)}, u32[]{:S(2)}, u32[]{:S(2)}) collective-permute-start(bf16[384,512]{1,0:T(8,128)(2,1)} %bitcast.4), channel_id=1, source_target_pairs={{1,0},{0,1},{3,2},{2,3},{5,4},{4,5},{7,6},{6,7},{9,8},{8,9},{11,10... | collective-permute-start | bytes 1179656 | tf_op jit(solution)/shard_map/ppermute | solution.py:30
  1.1 23.2 %collective-permute-start.10 = (bf16[384,512]{1,0:T(8,128)(2,1)}, bf16[384,512]{1,0:T(8,128)(2,1)S(1)}, u32[]{:S(2)}, u32[]{:S(2)}) collective-permute-start(bf16[384,512]{1,0:T(8,128)(2,1)} %bitcast.5), channel_id=1, source_target_pairs={{2,0},{0,2},{6,4},{4,6},{10,8},{8,10},{14,12},{12,14},{3,1},{1,3},... | collective-permute-start | bytes 1179656 | tf_op jit(solution)/shard_map/ppermute | solution.py:30
  4.8 5.1 %collective-permute-start = (bf16[16,512]{1,0:T(8,128)(2,1)S(1)}, bf16[16,512]{1,0:T(8,128)(2,1)S(1)}, u32[]{:S(2)}, u32[]{:S(2)}) collective-permute-start(bf16[16,512]{1,0:T(8,128)(2,1)S(1)} %get-tuple-element.36.special), channel_id=1, source_target_pairs={{1,0},{0,1},{3,2},{2,3},{5,4},{4,5},{7,6},{6,7},{9,8},{8,9},{11,10... | collective-permute-start | bytes 49160 | tf_op jit(solution)/shard_map/ppermute | solution.py:30
  5.1 14.1 %collective-permute-start.2 = (bf16[128,512]{1,0:T(8,128)(2,1)S(1)}, bf16[128,512]{1,0:T(8,128)(2,1)S(1)}, u32[]{:S(2)}, u32[]{:S(2)}) collective-permute-start(bf16[128,512]{1,0:T(8,128)(2,1)S(1)} %get-tuple-element.74), channel_id=1, source_target_pairs={{0,14},{2,4},{4,2},{6,8},{8,6},{10,12},{12,10},{14,0},{1,15},{3,5}... | collective-permute-start | bytes 393224 | tf_op jit(solution)/shard_map/ppermute | solution.py:35
  8.7 10.5 %collective-permute-start.4 = (bf16[128,512]{1,0:T(8,128)(2,1)S(1)}, bf16[128,512]{1,0:T(8,128)(2,1)S(1)}, u32[]{:S(2)}, u32[]{:S(2)}) collective-permute-start(bf16[128,512]{1,0:T(8,128)(2,1)S(1)} %get-tuple-element.73), channel_id=1, source_target_pairs={{0,14},{2,4},{4,2},{6,8},{8,6},{10,12},{12,10},{14,0},{1,15},{3,5}... | collective-permute-start | bytes 393224 | tf_op jit(solution)/shard_map/ppermute | solution.py:35
  9.9 10.2 %collective-permute-start.5 = (bf16[128,512]{1,0:T(8,128)(2,1)S(1)}, bf16[128,512]{1,0:T(8,128)(2,1)S(1)}, u32[]{:S(2)}, u32[]{:S(2)}) collective-permute-start(bf16[128,512]{1,0:T(8,128)(2,1)S(1)} %get-tuple-element.72), channel_id=1, source_target_pairs={{0,14},{2,4},{4,2},{6,8},{8,6},{10,12},{12,10},{14,0},{1,15},{3,5}... | collective-permute-start | bytes 393224 | tf_op jit(solution)/shard_map/ppermute | solution.py:35
  15.8 4.9 %collective-permute-start.1 = (bf16[16,1024]{1,0:T(8,128)(2,1)S(1)}, bf16[16,1024]{1,0:T(8,128)(2,1)S(1)}, u32[]{:S(2)}, u32[]{:S(2)}) collective-permute-start(bf16[16,1024]{1,0:T(8,128)(2,1)S(1)} %get-tuple-element.38.first), channel_id=1, source_target_pairs={{4,0},{6,2},{0,4},{2,6},{12,8},{14,10},{8,12},{10,14},{5,1},{7,3},... | collective-permute-start | bytes 98312 | tf_op jit(solution)/shard_map/ppermute | solution.py:30
  20.1 1.3 %collective-permute-start.6 = (bf16[128,512]{1,0:T(8,128)(2,1)S(1)}, bf16[128,512]{1,0:T(8,128)(2,1)S(1)}, u32[]{:S(2)}, u32[]{:S(2)}) collective-permute-start(bf16[128,512]{1,0:T(8,128)(2,1)S(1)} %collective-permute-done.2.refs_0_), channel_id=1, source_target_pairs={{1,0},{0,1},{3,2},{2,3},{5,4},{4,5},{7,6},{6,7},{9,8},{8,9},{11,10... | collective-permute-start | bytes 393224 | tf_op jit(solution)/shard_map/ppermute | solution.py:30
  20.1 1.5 %collective-permute-start.7 = (bf16[128,512]{1,0:T(8,128)(2,1)S(1)}, bf16[128,512]{1,0:T(8,128)(2,1)S(1)}, u32[]{:S(2)}, u32[]{:S(2)}) collective-permute-start(bf16[128,512]{1,0:T(8,128)(2,1)S(1)} %collective-permute-done.4.refs_1_), channel_id=1, source_target_pairs={{1,0},{0,1},{3,2},{2,3},{5,4},{4,5},{7,6},{6,7},{9,8},{8,9},{11,10... | collective-permute-start | bytes 393224 | tf_op jit(solution)/shard_map/ppermute | solution.py:30
  20.6 1.3 %collective-permute-start.8 = (bf16[128,512]{1,0:T(8,128)(2,1)S(1)}, bf16[128,512]{1,0:T(8,128)(2,1)S(1)}, u32[]{:S(2)}, u32[]{:S(2)}) collective-permute-start(bf16[128,512]{1,0:T(8,128)(2,1)S(1)} %collective-permute-done.5.refs_2_), channel_id=1, source_target_pairs={{1,0},{0,1},{3,2},{2,3},{5,4},{4,5},{7,6},{6,7},{9,8},{8,9},{11,10... | collective-permute-start | bytes 393224 | tf_op jit(solution)/shard_map/ppermute | solution.py:30
  21.2 6.9 %collective-permute-start.9 = (bf16[32,1024]{1,0:T(8,128)(2,1)S(1)}, bf16[32,1024]{1,0:T(8,128)(2,1)S(1)}, u32[]{:S(2)}, u32[]{:S(2)}) collective-permute-start(bf16[32,1024]{1,0:T(8,128)(2,1)S(1)} %shard_map.97.first), channel_id=1, source_target_pairs={{8,0},{10,2},{12,4},{14,6},{0,8},{2,10},{4,12},{6,14},{9,1},{11,3}... | collective-permute-start | bytes 196616 | tf_op jit(solution)/shard_map/ppermute | solution.py:30
  24.4 4.4 %collective-permute-start.11 = (bf16[192,512]{1,0:T(8,128)(2,1)S(1)}, bf16[192,512]{1,0:T(8,128)(2,1)S(1)}, u32[]{:S(2)}, u32[]{:S(2)}) collective-permute-start(bf16[192,512]{1,0:T(8,128)(2,1)S(1)} %get-tuple-element.71.refs_0_), channel_id=1, source_target_pairs={{1,0},{0,1},{3,2},{2,3},{5,4},{4,5},{7,6},{6,7},{9,8},{8,9},{11,10... | collective-permute-start | bytes 589832 | tf_op jit(solution)/shard_map/ppermute | solution.py:30
  24.7 4.2 %collective-permute-start.12 = (bf16[192,512]{1,0:T(8,128)(2,1)S(1)}, bf16[192,512]{1,0:T(8,128)(2,1)S(1)}, u32[]{:S(2)}, u32[]{:S(2)}) collective-permute-start(bf16[192,512]{1,0:T(8,128)(2,1)S(1)} %get-tuple-element.70.refs_1_), channel_id=1, source_target_pairs={{1,0},{0,1},{3,2},{2,3},{5,4},{4,5},{7,6},{6,7},{9,8},{8,9},{11,10... | collective-permute-start | bytes 589832 | tf_op jit(solution)/shard_map/ppermute | solution.py:30
  28.1 4.7 %collective-permute-start.13 = (bf16[48,1024]{1,0:T(8,128)(2,1)S(1)}, bf16[48,1024]{1,0:T(8,128)(2,1)S(1)}, u32[]{:S(2)}, u32[]{:S(2)}) collective-permute-start(bf16[48,1024]{1,0:T(8,128)(2,1)S(1)} %shard_map.102.first), channel_id=1, source_target_pairs={{2,0},{0,2},{6,4},{4,6},{10,8},{8,10},{14,12},{12,14},{3,1},{1,3},... | collective-permute-start | bytes 294920 | tf_op jit(solution)/shard_map/ppermute | solution.py:30
  34.9 1.8 %collective-permute-start.14 = (bf16[400,512]{1,0:T(8,128)(2,1)S(1)}, bf16[400,512]{1,0:T(8,128)(2,1)S(1)}, u32[]{:S(2)}, u32[]{:S(2)}) collective-permute-start(bf16[400,512]{1,0:T(8,128)(2,1)S(1)} %get-tuple-element.67), channel_id=1, source_target_pairs={{1,0},{0,1},{3,2},{2,3},{5,4},{4,5},{7,6},{6,7},{9,8},{8,9},{11,10... | collective-permute-start | bytes 1228808 | tf_op jit(solution)/shard_map/ppermute | solution.py:30

commit v21 on v18

--- a/solution.py
+++ b/solution.py
@@ -364,7 +364,7 @@
     w_here, kept_out, sent_out = refs[4:]
     masks = [(special_pairs.shape[0], None)]
     pairs, rows = queries.shape[0], queries.shape[2] // 2
-    columns, out, special = [], None, None
+    columns, waiting, out, special = [], [], None, None
     sides = halves(kept_out.shape[1])
     for pair, sub, _, total, weight in attend_all(
         given(special_pairs), masks, lambda pair: queries[pair], lambda: special_queries[...],
@@ -376,18 +376,21 @@
             lane = lax.broadcasted_iota(jnp.int32, share.shape, 1) // TILE_ROWS
             share = jnp.transpose(jnp.where(row == lane, share, 0.0))
             share = sum(share[i * TILE_ROWS : (i + 1) * TILE_ROWS] for i in range(2 * pairs))
-            special = [product(share.astype(jnp.bfloat16), w_here[:, side]) for side in sides]
-            continue
-        columns.append(share)
-        if pair % 2 == 1 and sub == 1:
-            quad = jnp.transpose(jnp.concatenate(columns, axis=0).astype(jnp.bfloat16))
-            features = slice((pair // 2) * QUAD, (pair // 2 + 1) * QUAD)
-            added = [product(quad, w_here[features, side]) for side in sides]
-            out = added if out is None else [before + more for before, more in zip(out, added)]
-            columns = []
-    for place, values in ((slice(0, rows), out), (slice(rows, kept_out.shape[0]), special)):
-        sent_out[place, :] = values[1].astype(jnp.bfloat16)
-        kept_out[place, :] = values[0]
+            special = share.astype(jnp.bfloat16)
+        else:
+            columns.append(share)
+            if pair % 2 == 1 and sub == 1:
+                quad = jnp.transpose(jnp.concatenate(columns, axis=0).astype(jnp.bfloat16))
+                waiting.append((slice((pair // 2) * QUAD, (pair // 2 + 1) * QUAD), quad))
+                columns = []
+        if special is not None:
+            for features, quad in waiting:
+                quad = jnp.concatenate([quad, special[:, features]], axis=0)
+                added = [product(quad, w_here[features, side]) for side in sides]
+                out = added if out is None else [before + more for before, more in zip(out, added)]
+            waiting = []
+    sent_out[...] = out[1].astype(jnp.bfloat16)
+    kept_out[...] = out[0]
 
 
 def end_kernel(images, kept, received, patch_out, special_out):

time: 35.5 us -> 35 us (0.986)
  Pallas kernels: 16.1 us -> 15.5 us
    pallas_call x11, Pallas kernels: 16.1 us -> 15.5 us  [call(): pl.pallas_call(kernel, out_shape=out_shape, in_specs=in_specs or [VMEM] *...]
  transfers between devices with their start and end apart: 12 -> 12, of which waited for: 7 -> 7; matrix products, arithmetic and copies ran while one was open for 0% -> 0% of each run, Pallas kernels for 37% -> 38%
where the time goes in v21:
time: 35 us; the launch traced here: 34.8 us
  Pallas kernels  15.5 us (44%)
  starting transfers between devices  9.25 us (26%)
  waiting for transfers between devices  9.19 us (26%)
  between operations  0.75 us (2%)
    pallas_call x11, Pallas kernels, call(): pl.pallas_call(kernel, out_shape=out_shape, in_specs=in_specs or [VMEM] *...  15.5 us
    ppermute x11, waiting for transfers between devices, swapped(): return lax.ppermute(block, axis, [(i ^ bit, i) for i in range(count)])  7.14 us
    ppermute x1, starting transfers between devices, crossed(): lax.ppermute(block, axis, [(i, (i + (-1 if i % 2 == 0 else 1)) % count) f...  5.6 us
    ppermute x11, starting transfers between devices, swapped(): return lax.ppermute(block, axis, [(i ^ bit, i) for i in range(count)])  3.65 us
    ppermute x1, waiting for transfers between devices, crossed(): lax.ppermute(block, axis, [(i, (i + (-1 if i % 2 == 0 else 1)) % count) f...  2.05 us
  transfers between devices with their start and end apart: 12, of which 7 were waited for; matrix products, arithmetic and copies ran while one was open for 0% of the time, Pallas kernels for 38%

profile of v21, /device:TPU:0, one launch (start us, length us, event | category | flops | bytes accessed | tf_op | source)
XLA Modules:
  0.0 34.8 jit_solution(6524703696142868057)
XLA Ops:
  0.6 0.5 %collective-permute-start.3 = (bf16[384,512]{1,0:T(8,128)(2,1)}, bf16[384,512]{1,0:T(8,128)(2,1)S(1)}, u32[]{:S(2)}, u32[]{:S(2)}) collective-permute-start(bf16[384,512]{1,0:T(8,128)(2,1)} %bitcast.4), channel_id=1, source_target_pairs={{1,0},{0,1},{3,2},{2,3},{5,4},{4,5},{7,6},{6,7},{9,8},{8,9},{11,10... | collective-permute-start | bytes 1179656 | tf_op jit(solution)/shard_map/ppermute | solution.py:30
  1.1 5.6 %collective-permute-start.2 = (bf16[384,512]{1,0:T(8,128)(2,1)}, bf16[384,512]{1,0:T(8,128)(2,1)S(1)}, u32[]{:S(2)}, u32[]{:S(2)}) collective-permute-start(bf16[384,512]{1,0:T(8,128)(2,1)} %bitcast.5), channel_id=1, source_target_pairs={{0,14},{2,4},{4,2},{6,8},{8,6},{10,12},{12,10},{14,0},{1,15},{3,5}... | collective-permute-start | bytes 1179656 | tf_op jit(solution)/shard_map/ppermute | solution.py:35
  6.8 1.1 %shard_map.95 = (bf16[16,512]{1,0:T(8,128)(2,1)S(1)}, bf16[384,512]{1,0:T(8,128)(2,1)S(1)}) custom-call(s32[2]{0:T(128)} %frame_order.1, bf16[5,2,512]{2,1,0:T(2,128)(2,1)} %bitcast.8, bf16[5,1024]{1,0:T(8,128)(2,1)} %role_first.1, bf16[5,1024]{1,0:T(8,128)(2,1)} %role_rest.1, bf16[384,512]{1,0:T(8,128)(2,1)} %bitcast.6), custom_call_target="tpu_custom_call" | custom-call | tf_op jit(solution)/shard_map/pallas_call | solution.py:413
  7.9 0.2 collective-permute-start
  8.1 0.0 collective-permute-start.7
  8.1 1.0 %collective-permute-done.other_special = bf16[16,512]{1,0:T(8,128)(2,1)S(1)} collective-permute-done((bf16[16,512]{1,0:T(8,128)(2,1)S(1)}, bf16[16,512]{1,0:T(8,128)(2,1)S(1)}, u32[]{:S(2)}, u32[]{:S(2)}) %collective-permute-start) | collective-permute-done | bytes 16416 | tf_op jit(solution)/shard_map/ppermute | solution.py:30
  9.1 2.3 %shard_map.96 = (f32[8,512]{1,0:T(8,128)S(1)}, bf16[3,1024,512]{2,1,0:T(8,128)(2,1)S(1)}, bf16[16,1024]{1,0:T(8,128)(2,1)S(1)}, bf16[512,1024]{1,0:T(8,128)(2,1)S(1)}) custom-call(s32[2,16]{1,0:T(2,128)} %covisible.1, bf16[16,512]{1,0:T(8,128)(2,1)S(1)} %get-tuple-element.32.special, bf16[16,512]{1,0:T(8,128)(2,1)S(1)} %collective-permute-done.other_special, ...), custom_call_target="tpu_custom_call" | custom-call | tf_op jit(solution)/shard_map/pallas_call | solution.py:413
  11.4 0.1 collective-permute-start.1
  11.5 0.0 collective-permute-done.3.other
  11.5 3.4 %shard_map.98 = (bf16[4,128,768]{2,1,0:T(8,128)(2,1)S(1)}, bf16[512,128]{1,0:T(8,128)(2,1)S(1)}, f32[8,768]{1,0:T(8,128)S(1)}, f32[8,768]{1,0:T(8,128)S(1)}, f32...) custom-call(f32[8,512]{1,0:T(8,128)S(1)} %get-tuple-element.33.mask, bf16[384,512]{1,0:T(8,128)(2,1)S(1)} %get-tuple-element.35.own, ...), custom_call_target="tpu_custom_call" | custom-call | tf_op jit(solution)/shard_map/pallas_call | solution.py:413
  14.9 2.1 %collective-permute-done.2 = bf16[384,512]{1,0:T(8,128)(2,1)S(1)} collective-permute-done((bf16[384,512]{1,0:T(8,128)(2,1)}, bf16[384,512]{1,0:T(8,128)(2,1)S(1)}, u32[]{:S(2)}, u32[]{:S(2)}) %collective-permute-start.2) | collective-permute-done | bytes 393248 | tf_op jit(solution)/shard_map/ppermute | solution.py:35
  17.0 0.1 collective-permute-start.4
  17.0 0.5 %collective-permute-start.5 = (bf16[192,512]{1,0:T(8,128)(2,1)S(1)}, bf16[192,512]{1,0:T(8,128)(2,1)S(1)}, u32[]{:S(2)}, u32[]{:S(2)}) collective-permute-start(bf16[192,512]{1,0:T(8,128)(2,1)S(1)} %get-tuple-element.64.refs_1_), channel_id=1, source_target_pairs={{1,0},{0,1},{3,2},{2,3},{5,4},{4,5},{7,6},{6,7},{9,8},{8,9},{11,10... | collective-permute-start | bytes 589832 | tf_op jit(solution)/shard_map/ppermute | solution.py:30
  17.5 0.0 collective-permute-done.1.second
  17.6 1.5 %collective-permute-start.6 = (bf16[32,1024]{1,0:T(8,128)(2,1)S(1)}, bf16[32,1024]{1,0:T(8,128)(2,1)S(1)}, u32[]{:S(2)}, u32[]{:S(2)}) collective-permute-start(bf16[32,1024]{1,0:T(8,128)(2,1)S(1)} %shard_map.97.first), channel_id=1, source_target_pairs={{8,0},{10,2},{12,4},{14,6},{0,8},{2,10},{4,12},{6,14},{9,1},{11,3}... | collective-permute-start | bytes 196616 | tf_op jit(solution)/shard_map/ppermute | solution.py:30
  19.1 0.0 collective-permute-done.4.refs_2_
  19.1 0.0 collective-permute-done.5.refs_3_
  19.1 3.4 %shard_map.99 = (f32[8,768]{1,0:T(8,128)S(1)}, f32[8,768]{1,0:T(8,128)S(1)}, f32[4,64,768]{2,1,0:T(8,128)S(1)}, f32[512,128]{1,0:T(8,128)S(1)}) custom-call(f32[8,512]{1,0:T(8,128)S(1)} %get-tuple-element.33.mask, bf16[192,512]{1,0:T(8,128)(2,1)S(1)} %get-tuple-element.65.refs_0_, bf16[192,512]{1,0:T(8,128)(2,1)S(1)} %get-tuple-element.64.refs_1_, ...), custom_call_target="tpu_custom_call" | custom-call | tf_op jit(solution)/shard_map/pallas_call | solution.py:413
  22.5 2.6 %collective-permute-done.7 = bf16[384,512]{1,0:T(8,128)(2,1)S(1)} collective-permute-done((bf16[384,512]{1,0:T(8,128)(2,1)}, bf16[384,512]{1,0:T(8,128)(2,1)S(1)}, u32[]{:S(2)}, u32[]{:S(2)}) %collective-permute-start.7) | collective-permute-done | bytes 393248 | tf_op jit(solution)/shard_map/ppermute | solution.py:30
  25.1 0.1 collective-permute-start.8
  25.2 0.5 %collective-permute-start.9 = (bf16[192,512]{1,0:T(8,128)(2,1)S(1)}, bf16[192,512]{1,0:T(8,128)(2,1)S(1)}, u32[]{:S(2)}, u32[]{:S(2)}) collective-permute-start(bf16[192,512]{1,0:T(8,128)(2,1)S(1)} %get-tuple-element.62.refs_1_), channel_id=1, source_target_pairs={{1,0},{0,1},{3,2},{2,3},{5,4},{4,5},{7,6},{6,7},{9,8},{8,9},{11,10... | collective-permute-start | bytes 589832 | tf_op jit(solution)/shard_map/ppermute | solution.py:30
  25.7 0.0 collective-permute-done.6.second
  25.7 0.1 collective-permute-start.10
  25.8 0.6 %shard_map.101.sums = f32[2,384,512]{2,1,0:T(8,128)S(1)} custom-call(bf16[192,512]{1,0:T(8,128)(2,1)S(1)} %get-tuple-element.63.refs_0_, bf16[192,512]{1,0:T(8,128)(2,1)S(1)} %get-tuple-element.62.refs_1_, bf16[3,1024,512]{2,1,0:T(8,128)(2,1)S(1)} %get-tuple-element.36.weights.refs_4_.refs_2_), custom_call_target="tpu_custom_call" | custom-call | tf_op jit(solution)/shard_map/pallas_call | solution.py:413
  26.4 0.2 collective-permute-done.8.refs_0_
  26.6 0.3 collective-permute-done.9.refs_1_
  26.9 2.4 %shard_map.102 = (f32[8,768]{1,0:T(8,128)S(1)}, f32[8,768]{1,0:T(8,128)S(1)}, f32[4,64,768]{2,1,0:T(8,128)S(1)}, f32[512,128]{1,0:T(8,128)S(1)}) custom-call(f32[8,512]{1,0:T(8,128)S(1)} %get-tuple-element.33.mask, f32[2,384,512]{2,1,0:T(8,128)S(1)} %shard_map.101.sums, bf16[192,512]{1,0:T(8,128)(2,1)S(1)} %collective-permute-done.8.refs_0_, ...), custom_call_target="tpu_custom_call" | custom-call | tf_op jit(solution)/shard_map/pallas_call | solution.py:413
  29.3 1.3 %collective-permute-done.10.second = bf16[48,1024]{1,0:T(8,128)(2,1)S(1)} collective-permute-done((bf16[48,1024]{1,0:T(8,128)(2,1)S(1)}, bf16[48,1024]{1,0:T(8,128)(2,1)S(1)}, u32[]{:S(2)}, u32[]{:S(2)}) %collective-permute-start.10) | collective-permute-done | bytes 98336 | tf_op jit(solution)/shard_map/ppermute | solution.py:30
  30.6 1.5 %shard_map.104 = (f32[400,512]{1,0:T(8,128)S(1)}, bf16[400,512]{1,0:T(8,128)(2,1)S(1)}) custom-call(f32[8,512]{1,0:T(8,128)S(1)} %get-tuple-element.33.mask, bf16[96,1024]{1,0:T(8,128)(2,1)S(1)} %shard_map.103.special_pairs, bf16[4,128,768]{2,1,0:T(8,128)(2,1)S(1)} %get-tuple-element.41.refs_5_.refs_3_.queries, ...), custom_call_target="tpu_custom_call" | custom-call | tf_op jit(solution)/shard_map/pallas_call | solution.py:413
  32.1 0.1 collective-permute-start.11
  32.2 1.7 %collective-permute-done.11.received = bf16[400,512]{1,0:T(8,128)(2,1)S(1)} collective-permute-done((bf16[400,512]{1,0:T(8,128)(2,1)S(1)}, bf16[400,512]{1,0:T(8,128)(2,1)S(1)}, u32[]{:S(2)}, u32[]{:S(2)}) %collective-permute-start.11) | collective-permute-done | bytes 409632 | tf_op jit(solution)/shard_map/ppermute | solution.py:30
  33.9 0.8 %shard_map.105 = (bf16[384,512]{1,0:T(8,128)(2,1)}, bf16[5,2,512]{2,1,0:T(2,128)(2,1)}) custom-call(f32[400,512]{1,0:T(8,128)S(1)} %get-tuple-element.58.kept, bf16[400,512]{1,0:T(8,128)(2,1)S(1)} %collective-permute-done.11.received), custom_call_target="tpu_custom_call" | custom-call | tf_op jit(solution)/shard_map/pallas_call | solution.py:413
  (5 shorter events, 0.1 us)
Async XLA Ops:
  0.6 10.9 %collective-permute-start.3 = (bf16[384,512]{1,0:T(8,128)(2,1)}, bf16[384,512]{1,0:T(8,128)(2,1)S(1)}, u32[]{:S(2)}, u32[]{:S(2)}) collective-permute-start(bf16[384,512]{1,0:T(8,128)(2,1)} %bitcast.4), channel_id=1, source_target_pairs={{1,0},{0,1},{3,2},{2,3},{5,4},{4,5},{7,6},{6,7},{9,8},{8,9},{11,10... | collective-permute-start | bytes 1179656 | tf_op jit(solution)/shard_map/ppermute | solution.py:30
  1.1 15.8 %collective-permute-start.2 = (bf16[384,512]{1,0:T(8,128)(2,1)}, bf16[384,512]{1,0:T(8,128)(2,1)S(1)}, u32[]{:S(2)}, u32[]{:S(2)}) collective-permute-start(bf16[384,512]{1,0:T(8,128)(2,1)} %bitcast.5), channel_id=1, source_target_pairs={{0,14},{2,4},{4,2},{6,8},{8,6},{10,12},{12,10},{14,0},{1,15},{3,5}... | collective-permute-start | bytes 1179656 | tf_op jit(solution)/shard_map/ppermute | solution.py:35
  7.9 1.2 %collective-permute-start = (bf16[16,512]{1,0:T(8,128)(2,1)S(1)}, bf16[16,512]{1,0:T(8,128)(2,1)S(1)}, u32[]{:S(2)}, u32[]{:S(2)}) collective-permute-start(bf16[16,512]{1,0:T(8,128)(2,1)S(1)} %get-tuple-element.32.special), channel_id=1, source_target_pairs={{1,0},{0,1},{3,2},{2,3},{5,4},{4,5},{7,6},{6,7},{9,8},{8,9},{11,10... | collective-permute-start | bytes 49160 | tf_op jit(solution)/shard_map/ppermute | solution.py:30
  8.1 17.0 %collective-permute-start.7 = (bf16[384,512]{1,0:T(8,128)(2,1)}, bf16[384,512]{1,0:T(8,128)(2,1)S(1)}, u32[]{:S(2)}, u32[]{:S(2)}) collective-permute-start(bf16[384,512]{1,0:T(8,128)(2,1)} %bitcast.7), channel_id=1, source_target_pairs={{2,0},{0,2},{6,4},{4,6},{10,8},{8,10},{14,12},{12,14},{3,1},{1,3},... | collective-permute-start | bytes 1179656 | tf_op jit(solution)/shard_map/ppermute | solution.py:30
  11.4 6.1 %collective-permute-start.1 = (bf16[16,1024]{1,0:T(8,128)(2,1)S(1)}, bf16[16,1024]{1,0:T(8,128)(2,1)S(1)}, u32[]{:S(2)}, u32[]{:S(2)}) collective-permute-start(bf16[16,1024]{1,0:T(8,128)(2,1)S(1)} %get-tuple-element.34.first), channel_id=1, source_target_pairs={{4,0},{6,2},{0,4},{2,6},{12,8},{14,10},{8,12},{10,14},{5,1},{7,3},... | collective-permute-start | bytes 98312 | tf_op jit(solution)/shard_map/ppermute | solution.py:30
  17.0 2.1 %collective-permute-start.4 = (bf16[192,512]{1,0:T(8,128)(2,1)S(1)}, bf16[192,512]{1,0:T(8,128)(2,1)S(1)}, u32[]{:S(2)}, u32[]{:S(2)}) collective-permute-start(bf16[192,512]{1,0:T(8,128)(2,1)S(1)} %get-tuple-element.65.refs_0_), channel_id=1, source_target_pairs={{1,0},{0,1},{3,2},{2,3},{5,4},{4,5},{7,6},{6,7},{9,8},{8,9},{11,10... | collective-permute-start | bytes 589832 | tf_op jit(solution)/shard_map/ppermute | solution.py:30
  17.0 2.1 %collective-permute-start.5 = (bf16[192,512]{1,0:T(8,128)(2,1)S(1)}, bf16[192,512]{1,0:T(8,128)(2,1)S(1)}, u32[]{:S(2)}, u32[]{:S(2)}) collective-permute-start(bf16[192,512]{1,0:T(8,128)(2,1)S(1)} %get-tuple-element.64.refs_1_), channel_id=1, source_target_pairs={{1,0},{0,1},{3,2},{2,3},{5,4},{4,5},{7,6},{6,7},{9,8},{8,9},{11,10... | collective-permute-start | bytes 589832 | tf_op jit(solution)/shard_map/ppermute | solution.py:30
  17.6 8.1 %collective-permute-start.6 = (bf16[32,1024]{1,0:T(8,128)(2,1)S(1)}, bf16[32,1024]{1,0:T(8,128)(2,1)S(1)}, u32[]{:S(2)}, u32[]{:S(2)}) collective-permute-start(bf16[32,1024]{1,0:T(8,128)(2,1)S(1)} %shard_map.97.first), channel_id=1, source_target_pairs={{8,0},{10,2},{12,4},{14,6},{0,8},{2,10},{4,12},{6,14},{9,1},{11,3}... | collective-permute-start | bytes 196616 | tf_op jit(solution)/shard_map/ppermute | solution.py:30
  25.1 1.5 %collective-permute-start.8 = (bf16[192,512]{1,0:T(8,128)(2,1)S(1)}, bf16[192,512]{1,0:T(8,128)(2,1)S(1)}, u32[]{:S(2)}, u32[]{:S(2)}) collective-permute-start(bf16[192,512]{1,0:T(8,128)(2,1)S(1)} %get-tuple-element.63.refs_0_), channel_id=1, source_target_pairs={{1,0},{0,1},{3,2},{2,3},{5,4},{4,5},{7,6},{6,7},{9,8},{8,9},{11,10... | collective-permute-start | bytes 589832 | tf_op jit(solution)/shard_map/ppermute | solution.py:30
  25.2 1.7 %collective-permute-start.9 = (bf16[192,512]{1,0:T(8,128)(2,1)S(1)}, bf16[192,512]{1,0:T(8,128)(2,1)S(1)}, u32[]{:S(2)}, u32[]{:S(2)}) collective-permute-start(bf16[192,512]{1,0:T(8,128)(2,1)S(1)} %get-tuple-element.62.refs_1_), channel_id=1, source_target_pairs={{1,0},{0,1},{3,2},{2,3},{5,4},{4,5},{7,6},{6,7},{9,8},{8,9},{11,10... | collective-permute-start | bytes 589832 | tf_op jit(solution)/shard_map/ppermute | solution.py:30
  25.7 4.8 %collective-permute-start.10 = (bf16[48,1024]{1,0:T(8,128)(2,1)S(1)}, bf16[48,1024]{1,0:T(8,128)(2,1)S(1)}, u32[]{:S(2)}, u32[]{:S(2)}) collective-permute-start(bf16[48,1024]{1,0:T(8,128)(2,1)S(1)} %shard_map.100.first), channel_id=1, source_target_pairs={{2,0},{0,2},{6,4},{4,6},{10,8},{8,10},{14,12},{12,14},{3,1},{1,3},... | collective-permute-start | bytes 294920 | tf_op jit(solution)/shard_map/ppermute | solution.py:30
  32.1 1.8 %collective-permute-start.11 = (bf16[400,512]{1,0:T(8,128)(2,1)S(1)}, bf16[400,512]{1,0:T(8,128)(2,1)S(1)}, u32[]{:S(2)}, u32[]{:S(2)}) collective-permute-start(bf16[400,512]{1,0:T(8,128)(2,1)S(1)} %get-tuple-element.59), channel_id=1, source_target_pairs={{1,0},{0,1},{3,2},{2,3},{5,4},{4,5},{7,6},{6,7},{9,8},{8,9},{11,10... | collective-permute-start | bytes 1228808 | tf_op jit(solution)/shard_map/ppermute | solution.py:30

commit v22 on v21

--- a/solution.py
+++ b/solution.py
@@ -342,17 +342,26 @@
     return columns
 
 
-def begun_kernel(stretches, mask, sums, *refs):
+def begun_kernel(stretches, special_real, mask, sums, *refs):
     count = len(stretches)
     other = jnp.concatenate([ref[...] for ref in refs[:count]], axis=0)
     masks = [(rows, mask[i : i + 1, :]) for part in stretches for rows, i in part]
-    weights, queries, special_queries = refs[count : count + 3]
-    state_in, state_out = refs[count + 3 : count + 7], refs[count + 7 :]
+    weights, queries, special_queries, special_pairs = refs[count : count + 4]
+    state_in, state_out = refs[count + 4 : count + 8], refs[count + 8 :]
+    sources = [begun(sums, other, weights)]
+    if special_real is not None:
+        sources.append(given(special_pairs))
+        masks.append((special_pairs.shape[0], None))
     pairs, rows = queries.shape[0], queries.shape[2] // 2
+
+    def joint(which, quad):
+        parts = [source(which, quad).astype(jnp.bfloat16) for source in sources]
+        return jnp.concatenate(parts, axis=0)
+
     state = State(rows, state_out)
     for result in attend_all(
-        begun(sums, other, weights), masks, lambda pair: queries[pair], lambda: special_queries[...],
-        State(rows, state_in), pairs, rows, None,
+        joint, masks, lambda pair: queries[pair], lambda: special_queries[...],
+        State(rows, state_in), pairs, rows, special_real,
     ):
         state.put(*result)
 
@@ -562,12 +571,12 @@
             flops=0,
         )
         state = call(
-            functools.partial(begun_kernel, stretches(2)),
+            functools.partial(begun_kernel, stretches(2), blocks if power else None),
             state_shape,
-            (mask, sums, *[part[1] for part in parts], *fixed, *state),
+            (mask, sums, *[part[1] for part in parts], *fixed, everywhere, *state),
         )
         if power:
-            everywhere = stacked(after(everywhere, state[0]), arrived)
+            everywhere = arrived
     else:
         for i, offset in enumerate(offsets[1:]):
             state = later(stretches(i + 1), halved(shifted(patches, "blk", -offset), state[0]), state)

time: 35 us -> 34.9 us (level)
    pallas_call x11 -> x10, Pallas kernels: 15.5 us -> 15.4 us  [call(): pl.pallas_call(kernel, out_shape=out_shape, in_specs=in_specs or [VMEM] *...]
where the time goes in v22:
time: 34.9 us; the launch traced here: 34.6 us
  Pallas kernels  15.4 us (44%)
  starting transfers between devices  9.25 us (27%)
  waiting for transfers between devices  9.15 us (26%)
  between operations  0.74 us (2%)
    pallas_call x10, Pallas kernels, call(): pl.pallas_call(kernel, out_shape=out_shape, in_specs=in_specs or [VMEM] *...  15.4 us
    ppermute x11, waiting for transfers between devices, swapped(): return lax.ppermute(block, axis, [(i ^ bit, i) for i in range(count)])  7.1 us
    ppermute x1, starting transfers between devices, crossed(): lax.ppermute(block, axis, [(i, (i + (-1 if i % 2 == 0 else 1)) % count) f...  5.6 us
    ppermute x11, starting transfers between devices, swapped(): return lax.ppermute(block, axis, [(i ^ bit, i) for i in range(count)])  3.65 us
    ppermute x1, waiting for transfers between devices, crossed(): lax.ppermute(block, axis, [(i, (i + (-1 if i % 2 == 0 else 1)) % count) f...  2.05 us
  transfers between devices with their start and end apart: 12, of which 7 were waited for; matrix products, arithmetic and copies ran while one was open for 0% of the time, Pallas kernels for 38%

profile of v22, /device:TPU:0, one launch (start us, length us, event | category | flops | bytes accessed | tf_op | source)
XLA Modules:
  0.0 34.6 jit_solution(18046985578802977902)
XLA Ops:
  0.6 0.5 %collective-permute-start.3 = (bf16[384,512]{1,0:T(8,128)(2,1)}, bf16[384,512]{1,0:T(8,128)(2,1)S(1)}, u32[]{:S(2)}, u32[]{:S(2)}) collective-permute-start(bf16[384,512]{1,0:T(8,128)(2,1)} %bitcast.4), channel_id=1, source_target_pairs={{1,0},{0,1},{3,2},{2,3},{5,4},{4,5},{7,6},{6,7},{9,8},{8,9},{11,10... | collective-permute-start | bytes 1179656 | tf_op jit(solution)/shard_map/ppermute | solution.py:30
  1.1 5.6 %collective-permute-start.2 = (bf16[384,512]{1,0:T(8,128)(2,1)}, bf16[384,512]{1,0:T(8,128)(2,1)S(1)}, u32[]{:S(2)}, u32[]{:S(2)}) collective-permute-start(bf16[384,512]{1,0:T(8,128)(2,1)} %bitcast.5), channel_id=1, source_target_pairs={{0,14},{2,4},{4,2},{6,8},{8,6},{10,12},{12,10},{14,0},{1,15},{3,5}... | collective-permute-start | bytes 1179656 | tf_op jit(solution)/shard_map/ppermute | solution.py:35
  6.8 1.1 %shard_map.95 = (bf16[16,512]{1,0:T(8,128)(2,1)S(1)}, bf16[384,512]{1,0:T(8,128)(2,1)S(1)}) custom-call(s32[2]{0:T(128)} %frame_order.1, bf16[5,2,512]{2,1,0:T(2,128)(2,1)} %bitcast.8, bf16[5,1024]{1,0:T(8,128)(2,1)} %role_first.1, bf16[5,1024]{1,0:T(8,128)(2,1)} %role_rest.1, bf16[384,512]{1,0:T(8,128)(2,1)} %bitcast.6), custom_call_target="tpu_custom_call" | custom-call | tf_op jit(solution)/shard_map/pallas_call | solution.py:422
  7.9 0.2 collective-permute-start
  8.1 0.0 collective-permute-start.8
  8.1 1.0 %collective-permute-done.other_special = bf16[16,512]{1,0:T(8,128)(2,1)S(1)} collective-permute-done((bf16[16,512]{1,0:T(8,128)(2,1)S(1)}, bf16[16,512]{1,0:T(8,128)(2,1)S(1)}, u32[]{:S(2)}, u32[]{:S(2)}) %collective-permute-start) | collective-permute-done | bytes 16416 | tf_op jit(solution)/shard_map/ppermute | solution.py:30
  9.1 2.3 %shard_map.96 = (f32[8,512]{1,0:T(8,128)S(1)}, bf16[3,1024,512]{2,1,0:T(8,128)(2,1)S(1)}, bf16[16,1024]{1,0:T(8,128)(2,1)S(1)}, bf16[512,1024]{1,0:T(8,128)(2,1)S(1)}) custom-call(s32[2,16]{1,0:T(2,128)} %covisible.1, bf16[16,512]{1,0:T(8,128)(2,1)S(1)} %get-tuple-element.31.special, bf16[16,512]{1,0:T(8,128)(2,1)S(1)} %collective-permute-done.other_special, ...), custom_call_target="tpu_custom_call" | custom-call | tf_op jit(solution)/shard_map/pallas_call | solution.py:422
  11.4 0.1 collective-permute-start.1
  11.5 0.0 collective-permute-done.3.other
  11.5 3.4 %shard_map.98 = (bf16[4,128,768]{2,1,0:T(8,128)(2,1)S(1)}, bf16[512,128]{1,0:T(8,128)(2,1)S(1)}, f32[8,768]{1,0:T(8,128)S(1)}, f32[8,768]{1,0:T(8,128)S(1)}, f32...) custom-call(f32[8,512]{1,0:T(8,128)S(1)} %get-tuple-element.32.mask, bf16[384,512]{1,0:T(8,128)(2,1)S(1)} %get-tuple-element.34.own, ...), custom_call_target="tpu_custom_call" | custom-call | tf_op jit(solution)/shard_map/pallas_call | solution.py:422
  14.9 2.1 %collective-permute-done.2 = bf16[384,512]{1,0:T(8,128)(2,1)S(1)} collective-permute-done((bf16[384,512]{1,0:T(8,128)(2,1)}, bf16[384,512]{1,0:T(8,128)(2,1)S(1)}, u32[]{:S(2)}, u32[]{:S(2)}) %collective-permute-start.2) | collective-permute-done | bytes 393248 | tf_op jit(solution)/shard_map/ppermute | solution.py:35
  17.0 0.1 collective-permute-start.4
  17.0 0.5 %collective-permute-start.5 = (bf16[192,512]{1,0:T(8,128)(2,1)S(1)}, bf16[192,512]{1,0:T(8,128)(2,1)S(1)}, u32[]{:S(2)}, u32[]{:S(2)}) collective-permute-start(bf16[192,512]{1,0:T(8,128)(2,1)S(1)} %get-tuple-element.62.refs_1_), channel_id=1, source_target_pairs={{1,0},{0,1},{3,2},{2,3},{5,4},{4,5},{7,6},{6,7},{9,8},{8,9},{11,10... | collective-permute-start | bytes 589832 | tf_op jit(solution)/shard_map/ppermute | solution.py:30
  17.5 0.0 collective-permute-done.1.second
  17.6 1.5 %collective-permute-start.6 = (bf16[32,1024]{1,0:T(8,128)(2,1)S(1)}, bf16[32,1024]{1,0:T(8,128)(2,1)S(1)}, u32[]{:S(2)}, u32[]{:S(2)}) collective-permute-start(bf16[32,1024]{1,0:T(8,128)(2,1)S(1)} %shard_map.97.first), channel_id=1, source_target_pairs={{8,0},{10,2},{12,4},{14,6},{0,8},{2,10},{4,12},{6,14},{9,1},{11,3}... | collective-permute-start | bytes 196616 | tf_op jit(solution)/shard_map/ppermute | solution.py:30
  19.1 0.0 collective-permute-done.4.refs_2_
  19.1 0.0 collective-permute-done.5.refs_3_
  19.1 3.4 %shard_map.99 = (f32[8,768]{1,0:T(8,128)S(1)}, f32[8,768]{1,0:T(8,128)S(1)}, f32[4,64,768]{2,1,0:T(8,128)S(1)}, f32[512,128]{1,0:T(8,128)S(1)}) custom-call(f32[8,512]{1,0:T(8,128)S(1)} %get-tuple-element.32.mask, bf16[192,512]{1,0:T(8,128)(2,1)S(1)} %get-tuple-element.63.refs_0_, bf16[192,512]{1,0:T(8,128)(2,1)S(1)} %get-tuple-element.62.refs_1_, ...), custom_call_target="tpu_custom_call" | custom-call | tf_op jit(solution)/shard_map/pallas_call | solution.py:422
  22.5 2.6 %collective-permute-done.8 = bf16[384,512]{1,0:T(8,128)(2,1)S(1)} collective-permute-done((bf16[384,512]{1,0:T(8,128)(2,1)}, bf16[384,512]{1,0:T(8,128)(2,1)S(1)}, u32[]{:S(2)}, u32[]{:S(2)}) %collective-permute-start.8) | collective-permute-done | bytes 393248 | tf_op jit(solution)/shard_map/ppermute | solution.py:30
  25.1 0.1 collective-permute-start.10
  25.2 0.5 %collective-permute-start.9 = (bf16[192,512]{1,0:T(8,128)(2,1)S(1)}, bf16[192,512]{1,0:T(8,128)(2,1)S(1)}, u32[]{:S(2)}, u32[]{:S(2)}) collective-permute-start(bf16[192,512]{1,0:T(8,128)(2,1)S(1)} %get-tuple-element.61.refs_0_), channel_id=1, source_target_pairs={{1,0},{0,1},{3,2},{2,3},{5,4},{4,5},{7,6},{6,7},{9,8},{8,9},{11,10... | collective-permute-start | bytes 589832 | tf_op jit(solution)/shard_map/ppermute | solution.py:30
  25.7 0.0 collective-permute-done.6.second
  25.7 0.1 collective-permute-start.7
  25.8 0.6 %shard_map.101.sums = f32[2,384,512]{2,1,0:T(8,128)S(1)} custom-call(bf16[192,512]{1,0:T(8,128)(2,1)S(1)} %get-tuple-element.61.refs_0_, bf16[192,512]{1,0:T(8,128)(2,1)S(1)} %get-tuple-element.60.refs_1_, bf16[3,1024,512]{2,1,0:T(8,128)(2,1)S(1)} %get-tuple-element.35.weights.refs_4_.refs_2_), custom_call_target="tpu_custom_call" | custom-call | tf_op jit(solution)/shard_map/pallas_call | solution.py:422
  26.4 0.2 collective-permute-done.10.refs_1_
  26.6 0.3 collective-permute-done.9.refs_0_
  26.9 2.4 %shard_map.102 = (f32[8,768]{1,0:T(8,128)S(1)}, f32[8,768]{1,0:T(8,128)S(1)}, f32[4,64,768]{2,1,0:T(8,128)S(1)}, f32[512,128]{1,0:T(8,128)S(1)}) custom-call(f32[8,512]{1,0:T(8,128)S(1)} %get-tuple-element.32.mask, f32[2,384,512]{2,1,0:T(8,128)S(1)} %shard_map.101.sums, bf16[192,512]{1,0:T(8,128)(2,1)S(1)} %collective-permute-done.9.refs_0_, ...), custom_call_target="tpu_custom_call" | custom-call | tf_op jit(solution)/shard_map/pallas_call | solution.py:422
  29.4 1.2 %collective-permute-done.7.special_pairs = bf16[48,1024]{1,0:T(8,128)(2,1)S(1)} collective-permute-done((bf16[48,1024]{1,0:T(8,128)(2,1)S(1)}, bf16[48,1024]{1,0:T(8,128)(2,1)S(1)}, u32[]{:S(2)}, u32[]{:S(2)}) %collective-permute-start.7) | collective-permute-done | bytes 98336 | tf_op jit(solution)/shard_map/ppermute | solution.py:30
  30.6 1.4 %shard_map.103 = (f32[400,512]{1,0:T(8,128)S(1)}, bf16[400,512]{1,0:T(8,128)(2,1)S(1)}) custom-call(f32[8,512]{1,0:T(8,128)S(1)} %get-tuple-element.32.mask, bf16[48,1024]{1,0:T(8,128)(2,1)S(1)} %collective-permute-done.7.special_pairs, bf16[4,128,768]{2,1,0:T(8,128)(2,1)S(1)} %get-tuple-element.40.refs_5_.refs_3_.queries, ...), custom_call_target="tpu_custom_call" | custom-call | tf_op jit(solution)/shard_map/pallas_call | solution.py:422
  32.0 0.1 collective-permute-start.11
  32.1 1.7 %collective-permute-done.11.received = bf16[400,512]{1,0:T(8,128)(2,1)S(1)} collective-permute-done((bf16[400,512]{1,0:T(8,128)(2,1)S(1)}, bf16[400,512]{1,0:T(8,128)(2,1)S(1)}, u32[]{:S(2)}, u32[]{:S(2)}) %collective-permute-start.11) | collective-permute-done | bytes 409632 | tf_op jit(solution)/shard_map/ppermute | solution.py:30
  33.8 0.8 %shard_map.104 = (bf16[384,512]{1,0:T(8,128)(2,1)}, bf16[5,2,512]{2,1,0:T(2,128)(2,1)}) custom-call(f32[400,512]{1,0:T(8,128)S(1)} %get-tuple-element.56.kept, bf16[400,512]{1,0:T(8,128)(2,1)S(1)} %collective-permute-done.11.received), custom_call_target="tpu_custom_call" | custom-call | tf_op jit(solution)/shard_map/pallas_call | solution.py:422
  (4 shorter events, 0.1 us)
Async XLA Ops:
  0.6 10.9 %collective-permute-start.3 = (bf16[384,512]{1,0:T(8,128)(2,1)}, bf16[384,512]{1,0:T(8,128)(2,1)S(1)}, u32[]{:S(2)}, u32[]{:S(2)}) collective-permute-start(bf16[384,512]{1,0:T(8,128)(2,1)} %bitcast.4), channel_id=1, source_target_pairs={{1,0},{0,1},{3,2},{2,3},{5,4},{4,5},{7,6},{6,7},{9,8},{8,9},{11,10... | collective-permute-start | bytes 1179656 | tf_op jit(solution)/shard_map/ppermute | solution.py:30
  1.1 15.8 %collective-permute-start.2 = (bf16[384,512]{1,0:T(8,128)(2,1)}, bf16[384,512]{1,0:T(8,128)(2,1)S(1)}, u32[]{:S(2)}, u32[]{:S(2)}) collective-permute-start(bf16[384,512]{1,0:T(8,128)(2,1)} %bitcast.5), channel_id=1, source_target_pairs={{0,14},{2,4},{4,2},{6,8},{8,6},{10,12},{12,10},{14,0},{1,15},{3,5}... | collective-permute-start | bytes 1179656 | tf_op jit(solution)/shard_map/ppermute | solution.py:35
  7.9 1.2 %collective-permute-start = (bf16[16,512]{1,0:T(8,128)(2,1)S(1)}, bf16[16,512]{1,0:T(8,128)(2,1)S(1)}, u32[]{:S(2)}, u32[]{:S(2)}) collective-permute-start(bf16[16,512]{1,0:T(8,128)(2,1)S(1)} %get-tuple-element.31.special), channel_id=1, source_target_pairs={{1,0},{0,1},{3,2},{2,3},{5,4},{4,5},{7,6},{6,7},{9,8},{8,9},{11,10... | collective-permute-start | bytes 49160 | tf_op jit(solution)/shard_map/ppermute | solution.py:30
  8.1 17.0 %collective-permute-start.8 = (bf16[384,512]{1,0:T(8,128)(2,1)}, bf16[384,512]{1,0:T(8,128)(2,1)S(1)}, u32[]{:S(2)}, u32[]{:S(2)}) collective-permute-start(bf16[384,512]{1,0:T(8,128)(2,1)} %bitcast.7), channel_id=1, source_target_pairs={{2,0},{0,2},{6,4},{4,6},{10,8},{8,10},{14,12},{12,14},{3,1},{1,3},... | collective-permute-start | bytes 1179656 | tf_op jit(solution)/shard_map/ppermute | solution.py:30
  11.4 6.1 %collective-permute-start.1 = (bf16[16,1024]{1,0:T(8,128)(2,1)S(1)}, bf16[16,1024]{1,0:T(8,128)(2,1)S(1)}, u32[]{:S(2)}, u32[]{:S(2)}) collective-permute-start(bf16[16,1024]{1,0:T(8,128)(2,1)S(1)} %get-tuple-element.33.first), channel_id=1, source_target_pairs={{4,0},{6,2},{0,4},{2,6},{12,8},{14,10},{8,12},{10,14},{5,1},{7,3},... | collective-permute-start | bytes 98312 | tf_op jit(solution)/shard_map/ppermute | solution.py:30
  17.0 2.1 %collective-permute-start.4 = (bf16[192,512]{1,0:T(8,128)(2,1)S(1)}, bf16[192,512]{1,0:T(8,128)(2,1)S(1)}, u32[]{:S(2)}, u32[]{:S(2)}) collective-permute-start(bf16[192,512]{1,0:T(8,128)(2,1)S(1)} %get-tuple-element.63.refs_0_), channel_id=1, source_target_pairs={{1,0},{0,1},{3,2},{2,3},{5,4},{4,5},{7,6},{6,7},{9,8},{8,9},{11,10... | collective-permute-start | bytes 589832 | tf_op jit(solution)/shard_map/ppermute | solution.py:30
  17.0 2.1 %collective-permute-start.5 = (bf16[192,512]{1,0:T(8,128)(2,1)S(1)}, bf16[192,512]{1,0:T(8,128)(2,1)S(1)}, u32[]{:S(2)}, u32[]{:S(2)}) collective-permute-start(bf16[192,512]{1,0:T(8,128)(2,1)S(1)} %get-tuple-element.62.refs_1_), channel_id=1, source_target_pairs={{1,0},{0,1},{3,2},{2,3},{5,4},{4,5},{7,6},{6,7},{9,8},{8,9},{11,10... | collective-permute-start | bytes 589832 | tf_op jit(solution)/shard_map/ppermute | solution.py:30
  17.6 8.1 %collective-permute-start.6 = (bf16[32,1024]{1,0:T(8,128)(2,1)S(1)}, bf16[32,1024]{1,0:T(8,128)(2,1)S(1)}, u32[]{:S(2)}, u32[]{:S(2)}) collective-permute-start(bf16[32,1024]{1,0:T(8,128)(2,1)S(1)} %shard_map.97.first), channel_id=1, source_target_pairs={{8,0},{10,2},{12,4},{14,6},{0,8},{2,10},{4,12},{6,14},{9,1},{11,3}... | collective-permute-start | bytes 196616 | tf_op jit(solution)/shard_map/ppermute | solution.py:30
  25.1 1.5 %collective-permute-start.10 = (bf16[192,512]{1,0:T(8,128)(2,1)S(1)}, bf16[192,512]{1,0:T(8,128)(2,1)S(1)}, u32[]{:S(2)}, u32[]{:S(2)}) collective-permute-start(bf16[192,512]{1,0:T(8,128)(2,1)S(1)} %get-tuple-element.60.refs_1_), channel_id=1, source_target_pairs={{1,0},{0,1},{3,2},{2,3},{5,4},{4,5},{7,6},{6,7},{9,8},{8,9},{11,10... | collective-permute-start | bytes 589832 | tf_op jit(solution)/shard_map/ppermute | solution.py:30
  25.2 1.7 %collective-permute-start.9 = (bf16[192,512]{1,0:T(8,128)(2,1)S(1)}, bf16[192,512]{1,0:T(8,128)(2,1)S(1)}, u32[]{:S(2)}, u32[]{:S(2)}) collective-permute-start(bf16[192,512]{1,0:T(8,128)(2,1)S(1)} %get-tuple-element.61.refs_0_), channel_id=1, source_target_pairs={{1,0},{0,1},{3,2},{2,3},{5,4},{4,5},{7,6},{6,7},{9,8},{8,9},{11,10... | collective-permute-start | bytes 589832 | tf_op jit(solution)/shard_map/ppermute | solution.py:30
  25.7 4.8 %collective-permute-start.7 = (bf16[48,1024]{1,0:T(8,128)(2,1)S(1)}, bf16[48,1024]{1,0:T(8,128)(2,1)S(1)}, u32[]{:S(2)}, u32[]{:S(2)}) collective-permute-start(bf16[48,1024]{1,0:T(8,128)(2,1)S(1)} %shard_map.100.refs_5_), channel_id=1, source_target_pairs={{2,0},{0,2},{6,4},{4,6},{10,8},{8,10},{14,12},{12,14},{3,1},{1,3},... | collective-permute-start | bytes 294920 | tf_op jit(solution)/shard_map/ppermute | solution.py:30
  32.0 1.8 %collective-permute-start.11 = (bf16[400,512]{1,0:T(8,128)(2,1)S(1)}, bf16[400,512]{1,0:T(8,128)(2,1)S(1)}, u32[]{:S(2)}, u32[]{:S(2)}) collective-permute-start(bf16[400,512]{1,0:T(8,128)(2,1)S(1)} %get-tuple-element.57), channel_id=1, source_target_pairs={{1,0},{0,1},{3,2},{2,3},{5,4},{4,5},{7,6},{6,7},{9,8},{8,9},{11,10... | collective-permute-start | bytes 1228808 | tf_op jit(solution)/shard_map/ppermute | solution.py:30

commit v23 on v22

--- a/solution.py
+++ b/solution.py
@@ -563,7 +563,7 @@
                 flops=FIRST,
             )
             arrived = swapped(everywhere, "blk", 1)
-        parts = halved(near, state[0])
+        parts = [both(after(near, state[0]))]
         (sums,) = call(
             functools.partial(half_kernel, len(parts)),
             [f32(2, patch_total, width)],
@@ -571,7 +571,7 @@
             flops=0,
         )
         state = call(
-            functools.partial(begun_kernel, stretches(2), blocks if power else None),
+            functools.partial(begun_kernel, [image_rows(2)], blocks if power else None),
             state_shape,
             (mask, sums, *[part[1] for part in parts], *fixed, everywhere, *state),
         )

time: 34.9 us -> 34.7 us (level)
  starting transfers between devices: 9.25 us -> 8.73 us
  waiting for transfers between devices: 9.15 us -> 9.52 us
    ppermute x11 -> x10, starting transfers between devices: 3.65 us -> 3.13 us  [swapped(): return lax.ppermute(block, axis, [(i ^ bit, i) for i in range(count)])]
    ppermute x11 -> x10, waiting for transfers between devices: 7.1 us -> 7.47 us  [swapped(): return lax.ppermute(block, axis, [(i ^ bit, i) for i in range(count)])]
  transfers between devices with their start and end apart: 12 -> 11, of which waited for: 7 -> 6; matrix products, arithmetic and copies ran while one was open for 0% -> 0% of each run, Pallas kernels for 38% -> 38%
where the time goes in v23:
time: 34.7 us; the launch traced here: 34.5 us
  Pallas kernels  15.4 us (44%)
  waiting for transfers between devices  9.52 us (27%)
  starting transfers between devices  8.73 us (25%)
  between operations  0.74 us (2%)
    pallas_call x10, Pallas kernels, call(): pl.pallas_call(kernel, out_shape=out_shape, in_specs=in_specs or [VMEM] *...  15.4 us
    ppermute x10, waiting for transfers between devices, swapped(): return lax.ppermute(block, axis, [(i ^ bit, i) for i in range(count)])  7.47 us
    ppermute x1, starting transfers between devices, crossed(): lax.ppermute(block, axis, [(i, (i + (-1 if i % 2 == 0 else 1)) % count) f...  5.6 us
    ppermute x10, starting transfers between devices, swapped(): return lax.ppermute(block, axis, [(i ^ bit, i) for i in range(count)])  3.13 us
    ppermute x1, waiting for transfers between devices, crossed(): lax.ppermute(block, axis, [(i, (i + (-1 if i % 2 == 0 else 1)) % count) f...  2.05 us
  transfers between devices with their start and end apart: 11, of which 6 were waited for; matrix products, arithmetic and copies ran while one was open for 0% of the time, Pallas kernels for 38%

profile of v23, /device:TPU:0, one launch (start us, length us, event | category | flops | bytes accessed | tf_op | source)
XLA Modules:
  0.0 34.5 jit_solution(5106922441637545726)
XLA Ops:
  0.6 0.5 %collective-permute-start.3 = (bf16[384,512]{1,0:T(8,128)(2,1)}, bf16[384,512]{1,0:T(8,128)(2,1)S(1)}, u32[]{:S(2)}, u32[]{:S(2)}) collective-permute-start(bf16[384,512]{1,0:T(8,128)(2,1)} %bitcast.4), channel_id=1, source_target_pairs={{1,0},{0,1},{3,2},{2,3},{5,4},{4,5},{7,6},{6,7},{9,8},{8,9},{11,10... | collective-permute-start | bytes 1179656 | tf_op jit(solution)/shard_map/ppermute | solution.py:30
  1.1 5.6 %collective-permute-start.2 = (bf16[384,512]{1,0:T(8,128)(2,1)}, bf16[384,512]{1,0:T(8,128)(2,1)S(1)}, u32[]{:S(2)}, u32[]{:S(2)}) collective-permute-start(bf16[384,512]{1,0:T(8,128)(2,1)} %bitcast.5), channel_id=1, source_target_pairs={{0,14},{2,4},{4,2},{6,8},{8,6},{10,12},{12,10},{14,0},{1,15},{3,5}... | collective-permute-start | bytes 1179656 | tf_op jit(solution)/shard_map/ppermute | solution.py:35
  6.8 1.1 %shard_map.95 = (bf16[16,512]{1,0:T(8,128)(2,1)S(1)}, bf16[384,512]{1,0:T(8,128)(2,1)S(1)}) custom-call(s32[2]{0:T(128)} %frame_order.1, bf16[5,2,512]{2,1,0:T(2,128)(2,1)} %bitcast.8, bf16[5,1024]{1,0:T(8,128)(2,1)} %role_first.1, bf16[5,1024]{1,0:T(8,128)(2,1)} %role_rest.1, bf16[384,512]{1,0:T(8,128)(2,1)} %bitcast.6), custom_call_target="tpu_custom_call" | custom-call | tf_op jit(solution)/shard_map/pallas_call | solution.py:422
  7.9 0.2 collective-permute-start
  8.1 0.0 collective-permute-start.8
  8.1 1.0 %collective-permute-done.other_special = bf16[16,512]{1,0:T(8,128)(2,1)S(1)} collective-permute-done((bf16[16,512]{1,0:T(8,128)(2,1)S(1)}, bf16[16,512]{1,0:T(8,128)(2,1)S(1)}, u32[]{:S(2)}, u32[]{:S(2)}) %collective-permute-start) | collective-permute-done | bytes 16416 | tf_op jit(solution)/shard_map/ppermute | solution.py:30
  9.1 2.3 %shard_map.96 = (f32[8,512]{1,0:T(8,128)S(1)}, bf16[3,1024,512]{2,1,0:T(8,128)(2,1)S(1)}, bf16[16,1024]{1,0:T(8,128)(2,1)S(1)}, bf16[512,1024]{1,0:T(8,128)(2,1)S(1)}) custom-call(s32[2,16]{1,0:T(2,128)} %covisible.1, bf16[16,512]{1,0:T(8,128)(2,1)S(1)} %get-tuple-element.31.special, bf16[16,512]{1,0:T(8,128)(2,1)S(1)} %collective-permute-done.other_special, ...), custom_call_target="tpu_custom_call" | custom-call | tf_op jit(solution)/shard_map/pallas_call | solution.py:422
  11.4 0.1 collective-permute-start.1
  11.5 0.0 collective-permute-done.3.other
  11.5 3.4 %shard_map.98 = (bf16[4,128,768]{2,1,0:T(8,128)(2,1)S(1)}, bf16[512,128]{1,0:T(8,128)(2,1)S(1)}, f32[8,768]{1,0:T(8,128)S(1)}, f32[8,768]{1,0:T(8,128)S(1)}, f32...) custom-call(f32[8,512]{1,0:T(8,128)S(1)} %get-tuple-element.32.mask, bf16[384,512]{1,0:T(8,128)(2,1)S(1)} %get-tuple-element.34.own, ...), custom_call_target="tpu_custom_call" | custom-call | tf_op jit(solution)/shard_map/pallas_call | solution.py:422
  14.9 2.1 %collective-permute-done.2 = bf16[384,512]{1,0:T(8,128)(2,1)S(1)} collective-permute-done((bf16[384,512]{1,0:T(8,128)(2,1)}, bf16[384,512]{1,0:T(8,128)(2,1)S(1)}, u32[]{:S(2)}, u32[]{:S(2)}) %collective-permute-start.2) | collective-permute-done | bytes 393248 | tf_op jit(solution)/shard_map/ppermute | solution.py:35
  17.0 0.1 collective-permute-start.4
  17.0 0.5 %collective-permute-start.5 = (bf16[192,512]{1,0:T(8,128)(2,1)S(1)}, bf16[192,512]{1,0:T(8,128)(2,1)S(1)}, u32[]{:S(2)}, u32[]{:S(2)}) collective-permute-start(bf16[192,512]{1,0:T(8,128)(2,1)S(1)} %get-tuple-element.60.refs_1_), channel_id=1, source_target_pairs={{1,0},{0,1},{3,2},{2,3},{5,4},{4,5},{7,6},{6,7},{9,8},{8,9},{11,10... | collective-permute-start | bytes 589832 | tf_op jit(solution)/shard_map/ppermute | solution.py:30
  17.5 0.0 collective-permute-done.1.second
  17.6 1.5 %collective-permute-start.6 = (bf16[32,1024]{1,0:T(8,128)(2,1)S(1)}, bf16[32,1024]{1,0:T(8,128)(2,1)S(1)}, u32[]{:S(2)}, u32[]{:S(2)}) collective-permute-start(bf16[32,1024]{1,0:T(8,128)(2,1)S(1)} %shard_map.97.first), channel_id=1, source_target_pairs={{8,0},{10,2},{12,4},{14,6},{0,8},{2,10},{4,12},{6,14},{9,1},{11,3}... | collective-permute-start | bytes 196616 | tf_op jit(solution)/shard_map/ppermute | solution.py:30
  19.1 0.0 collective-permute-done.4.refs_2_
  19.1 0.0 collective-permute-done.5.refs_3_
  19.1 3.4 %shard_map.99 = (f32[8,768]{1,0:T(8,128)S(1)}, f32[8,768]{1,0:T(8,128)S(1)}, f32[4,64,768]{2,1,0:T(8,128)S(1)}, f32[512,128]{1,0:T(8,128)S(1)}) custom-call(f32[8,512]{1,0:T(8,128)S(1)} %get-tuple-element.32.mask, bf16[192,512]{1,0:T(8,128)(2,1)S(1)} %get-tuple-element.61.refs_0_, bf16[192,512]{1,0:T(8,128)(2,1)S(1)} %get-tuple-element.60.refs_1_, ...), custom_call_target="tpu_custom_call" | custom-call | tf_op jit(solution)/shard_map/pallas_call | solution.py:422
  22.5 2.6 %collective-permute-done.8.refs_0_ = bf16[384,512]{1,0:T(8,128)(2,1)S(1)} collective-permute-done((bf16[384,512]{1,0:T(8,128)(2,1)}, bf16[384,512]{1,0:T(8,128)(2,1)S(1)}, u32[]{:S(2)}, u32[]{:S(2)}) %collective-permute-start.8) | collective-permute-done | bytes 393248 | tf_op jit(solution)/shard_map/ppermute | solution.py:30
  25.1 0.1 collective-permute-start.9
  25.2 0.0 collective-permute-done.6.second
  25.2 0.1 collective-permute-start.7
  25.3 0.6 %shard_map.101.sums = f32[2,384,512]{2,1,0:T(8,128)S(1)} custom-call(bf16[384,512]{1,0:T(8,128)(2,1)S(1)} %collective-permute-done.8.refs_0_, bf16[3,1024,512]{2,1,0:T(8,128)(2,1)S(1)} %get-tuple-element.35.weights.refs_4_.refs_1_), custom_call_target="tpu_custom_call" | custom-call | tf_op jit(solution)/shard_map/pallas_call | solution.py:422
  25.8 1.0 %collective-permute-done.9.refs_0_ = bf16[384,512]{1,0:T(8,128)(2,1)S(1)} collective-permute-done((bf16[384,512]{1,0:T(8,128)(2,1)S(1)}, bf16[384,512]{1,0:T(8,128)(2,1)S(1)}, u32[]{:S(2)}, u32[]{:S(2)}) %collective-permute-start.9) | collective-permute-done | bytes 393248 | tf_op jit(solution)/shard_map/ppermute | solution.py:30
  26.8 2.4 %shard_map.102 = (f32[8,768]{1,0:T(8,128)S(1)}, f32[8,768]{1,0:T(8,128)S(1)}, f32[4,64,768]{2,1,0:T(8,128)S(1)}, f32[512,128]{1,0:T(8,128)S(1)}) custom-call(f32[8,512]{1,0:T(8,128)S(1)} %get-tuple-element.32.mask, f32[2,384,512]{2,1,0:T(8,128)S(1)} %shard_map.101.sums, bf16[384,512]{1,0:T(8,128)(2,1)S(1)} %collective-permute-done.9.refs_0_, ...), custom_call_target="tpu_custom_call" | custom-call | tf_op jit(solution)/shard_map/pallas_call | solution.py:422
  29.3 1.1 %collective-permute-done.7.special_pairs = bf16[48,1024]{1,0:T(8,128)(2,1)S(1)} collective-permute-done((bf16[48,1024]{1,0:T(8,128)(2,1)S(1)}, bf16[48,1024]{1,0:T(8,128)(2,1)S(1)}, u32[]{:S(2)}, u32[]{:S(2)}) %collective-permute-start.7) | collective-permute-done | bytes 98336 | tf_op jit(solution)/shard_map/ppermute | solution.py:30
  30.4 1.4 %shard_map.103 = (f32[400,512]{1,0:T(8,128)S(1)}, bf16[400,512]{1,0:T(8,128)(2,1)S(1)}) custom-call(f32[8,512]{1,0:T(8,128)S(1)} %get-tuple-element.32.mask, bf16[48,1024]{1,0:T(8,128)(2,1)S(1)} %collective-permute-done.7.special_pairs, bf16[4,128,768]{2,1,0:T(8,128)(2,1)S(1)} %get-tuple-element.40.refs_5_.refs_2_.queries, ...), custom_call_target="tpu_custom_call" | custom-call | tf_op jit(solution)/shard_map/pallas_call | solution.py:422
  31.8 0.1 collective-permute-start.10
  31.9 1.7 %collective-permute-done.10.received = bf16[400,512]{1,0:T(8,128)(2,1)S(1)} collective-permute-done((bf16[400,512]{1,0:T(8,128)(2,1)S(1)}, bf16[400,512]{1,0:T(8,128)(2,1)S(1)}, u32[]{:S(2)}, u32[]{:S(2)}) %collective-permute-start.10) | collective-permute-done | bytes 409632 | tf_op jit(solution)/shard_map/ppermute | solution.py:30
  33.6 0.8 %shard_map.104 = (bf16[384,512]{1,0:T(8,128)(2,1)}, bf16[5,2,512]{2,1,0:T(2,128)(2,1)}) custom-call(f32[400,512]{1,0:T(8,128)S(1)} %get-tuple-element.56.kept, bf16[400,512]{1,0:T(8,128)(2,1)S(1)} %collective-permute-done.10.received), custom_call_target="tpu_custom_call" | custom-call | tf_op jit(solution)/shard_map/pallas_call | solution.py:422
  (3 shorter events, 0.1 us)
Async XLA Ops:
  0.6 10.9 %collective-permute-start.3 = (bf16[384,512]{1,0:T(8,128)(2,1)}, bf16[384,512]{1,0:T(8,128)(2,1)S(1)}, u32[]{:S(2)}, u32[]{:S(2)}) collective-permute-start(bf16[384,512]{1,0:T(8,128)(2,1)} %bitcast.4), channel_id=1, source_target_pairs={{1,0},{0,1},{3,2},{2,3},{5,4},{4,5},{7,6},{6,7},{9,8},{8,9},{11,10... | collective-permute-start | bytes 1179656 | tf_op jit(solution)/shard_map/ppermute | solution.py:30
  1.1 15.8 %collective-permute-start.2 = (bf16[384,512]{1,0:T(8,128)(2,1)}, bf16[384,512]{1,0:T(8,128)(2,1)S(1)}, u32[]{:S(2)}, u32[]{:S(2)}) collective-permute-start(bf16[384,512]{1,0:T(8,128)(2,1)} %bitcast.5), channel_id=1, source_target_pairs={{0,14},{2,4},{4,2},{6,8},{8,6},{10,12},{12,10},{14,0},{1,15},{3,5}... | collective-permute-start | bytes 1179656 | tf_op jit(solution)/shard_map/ppermute | solution.py:35
  7.9 1.2 %collective-permute-start = (bf16[16,512]{1,0:T(8,128)(2,1)S(1)}, bf16[16,512]{1,0:T(8,128)(2,1)S(1)}, u32[]{:S(2)}, u32[]{:S(2)}) collective-permute-start(bf16[16,512]{1,0:T(8,128)(2,1)S(1)} %get-tuple-element.31.special), channel_id=1, source_target_pairs={{1,0},{0,1},{3,2},{2,3},{5,4},{4,5},{7,6},{6,7},{9,8},{8,9},{11,10... | collective-permute-start | bytes 49160 | tf_op jit(solution)/shard_map/ppermute | solution.py:30
  8.1 17.0 %collective-permute-start.8 = (bf16[384,512]{1,0:T(8,128)(2,1)}, bf16[384,512]{1,0:T(8,128)(2,1)S(1)}, u32[]{:S(2)}, u32[]{:S(2)}) collective-permute-start(bf16[384,512]{1,0:T(8,128)(2,1)} %bitcast.7), channel_id=1, source_target_pairs={{2,0},{0,2},{6,4},{4,6},{10,8},{8,10},{14,12},{12,14},{3,1},{1,3},... | collective-permute-start | bytes 1179656 | tf_op jit(solution)/shard_map/ppermute | solution.py:30
  11.4 6.1 %collective-permute-start.1 = (bf16[16,1024]{1,0:T(8,128)(2,1)S(1)}, bf16[16,1024]{1,0:T(8,128)(2,1)S(1)}, u32[]{:S(2)}, u32[]{:S(2)}) collective-permute-start(bf16[16,1024]{1,0:T(8,128)(2,1)S(1)} %get-tuple-element.33.first), channel_id=1, source_target_pairs={{4,0},{6,2},{0,4},{2,6},{12,8},{14,10},{8,12},{10,14},{5,1},{7,3},... | collective-permute-start | bytes 98312 | tf_op jit(solution)/shard_map/ppermute | solution.py:30
  17.0 2.1 %collective-permute-start.4 = (bf16[192,512]{1,0:T(8,128)(2,1)S(1)}, bf16[192,512]{1,0:T(8,128)(2,1)S(1)}, u32[]{:S(2)}, u32[]{:S(2)}) collective-permute-start(bf16[192,512]{1,0:T(8,128)(2,1)S(1)} %get-tuple-element.61.refs_0_), channel_id=1, source_target_pairs={{1,0},{0,1},{3,2},{2,3},{5,4},{4,5},{7,6},{6,7},{9,8},{8,9},{11,10... | collective-permute-start | bytes 589832 | tf_op jit(solution)/shard_map/ppermute | solution.py:30
  17.0 2.1 %collective-permute-start.5 = (bf16[192,512]{1,0:T(8,128)(2,1)S(1)}, bf16[192,512]{1,0:T(8,128)(2,1)S(1)}, u32[]{:S(2)}, u32[]{:S(2)}) collective-permute-start(bf16[192,512]{1,0:T(8,128)(2,1)S(1)} %get-tuple-element.60.refs_1_), channel_id=1, source_target_pairs={{1,0},{0,1},{3,2},{2,3},{5,4},{4,5},{7,6},{6,7},{9,8},{8,9},{11,10... | collective-permute-start | bytes 589832 | tf_op jit(solution)/shard_map/ppermute | solution.py:30
  17.6 7.6 %collective-permute-start.6 = (bf16[32,1024]{1,0:T(8,128)(2,1)S(1)}, bf16[32,1024]{1,0:T(8,128)(2,1)S(1)}, u32[]{:S(2)}, u32[]{:S(2)}) collective-permute-start(bf16[32,1024]{1,0:T(8,128)(2,1)S(1)} %shard_map.97.first), channel_id=1, source_target_pairs={{8,0},{10,2},{12,4},{14,6},{0,8},{2,10},{4,12},{6,14},{9,1},{11,3}... | collective-permute-start | bytes 196616 | tf_op jit(solution)/shard_map/ppermute | solution.py:30
  25.1 1.7 %collective-permute-start.9 = (bf16[384,512]{1,0:T(8,128)(2,1)S(1)}, bf16[384,512]{1,0:T(8,128)(2,1)S(1)}, u32[]{:S(2)}, u32[]{:S(2)}) collective-permute-start(bf16[384,512]{1,0:T(8,128)(2,1)S(1)} %collective-permute-done.8.refs_0_), channel_id=1, source_target_pairs={{1,0},{0,1},{3,2},{2,3},{5,4},{4,5},{7,6},{6,7},{9,8},{8,9},{11,10... | collective-permute-start | bytes 1179656 | tf_op jit(solution)/shard_map/ppermute | solution.py:30
  25.2 5.2 %collective-permute-start.7 = (bf16[48,1024]{1,0:T(8,128)(2,1)S(1)}, bf16[48,1024]{1,0:T(8,128)(2,1)S(1)}, u32[]{:S(2)}, u32[]{:S(2)}) collective-permute-start(bf16[48,1024]{1,0:T(8,128)(2,1)S(1)} %shard_map.100.refs_4_), channel_id=1, source_target_pairs={{2,0},{0,2},{6,4},{4,6},{10,8},{8,10},{14,12},{12,14},{3,1},{1,3},... | collective-permute-start | bytes 294920 | tf_op jit(solution)/shard_map/ppermute | solution.py:30
  31.8 1.8 %collective-permute-start.10 = (bf16[400,512]{1,0:T(8,128)(2,1)S(1)}, bf16[400,512]{1,0:T(8,128)(2,1)S(1)}, u32[]{:S(2)}, u32[]{:S(2)}) collective-permute-start(bf16[400,512]{1,0:T(8,128)(2,1)S(1)} %get-tuple-element.57), channel_id=1, source_target_pairs={{1,0},{0,1},{3,2},{2,3},{5,4},{4,5},{7,6},{6,7},{9,8},{8,9},{11,10... | collective-permute-start | bytes 1228808 | tf_op jit(solution)/shard_map/ppermute | solution.py:30

commit v24 on v22

--- a/solution.py
+++ b/solution.py
@@ -537,11 +537,9 @@
 
     image_rows = lambda owner: [(per_image, owner * images + b) for b in range(images)]
     def halved(part, gate):
-        part = after(part, gate)
-        starts = range(0, part.shape[0], per_image)
-        return [both(part[start : start + per_image]) for start in starts]
-
-    stretches = lambda owner: [[image] for image in image_rows(owner)]
+        return [both(after(part, gate))]
+
+    stretches = lambda owner: [image_rows(owner)]
     if paired:
         far = after(crossed(patches, "blk"), state[0])
         near = swapped(patches, "blk", 1)

time: 34.9 us -> 34.7 us (level)
  starting transfers between devices: 9.25 us -> 8.78 us
  waiting for transfers between devices: 9.15 us -> 9.59 us
    ppermute x11 -> x9, waiting for transfers between devices: 7.1 us -> 7.63 us  [swapped(): return lax.ppermute(block, axis, [(i ^ bit, i) for i in range(count)])]
    ppermute x11 -> x9, starting transfers between devices: 3.65 us -> 3.18 us  [swapped(): return lax.ppermute(block, axis, [(i ^ bit, i) for i in range(count)])]
  transfers between devices with their start and end apart: 12 -> 10, of which waited for: 7 -> 6; matrix products, arithmetic and copies ran while one was open for 0% -> 0% of each run, Pallas kernels for 38% -> 38%
where the time goes in v24:
time: 34.7 us; the launch traced here: 34.6 us
  Pallas kernels  15.4 us (44%)
  waiting for transfers between devices  9.59 us (28%)
  starting transfers between devices  8.78 us (25%)
  between operations  0.75 us (2%)
    pallas_call x10, Pallas kernels, call(): pl.pallas_call(kernel, out_shape=out_shape, in_specs=in_specs or [VMEM] *...  15.4 us
    ppermute x9, waiting for transfers between devices, swapped(): return lax.ppermute(block, axis, [(i ^ bit, i) for i in range(count)])  7.63 us
    ppermute x1, starting transfers between devices, crossed(): lax.ppermute(block, axis, [(i, (i + (-1 if i % 2 == 0 else 1)) % count) f...  5.6 us
    ppermute x9, starting transfers between devices, swapped(): return lax.ppermute(block, axis, [(i ^ bit, i) for i in range(count)])  3.18 us
    ppermute x1, waiting for transfers between devices, crossed(): lax.ppermute(block, axis, [(i, (i + (-1 if i % 2 == 0 else 1)) % count) f...  1.95 us
  transfers between devices with their start and end apart: 10, of which 6 were waited for; matrix products, arithmetic and copies ran while one was open for 0% of the time, Pallas kernels for 38%

profile of v24, /device:TPU:0, one launch (start us, length us, event | category | flops | bytes accessed | tf_op | source)
XLA Modules:
  0.0 34.6 jit_solution(16663755488519921253)
XLA Ops:
  0.6 0.0 copy-start
  0.6 0.5 %collective-permute-start.3 = (bf16[384,512]{1,0:T(8,128)(2,1)}, bf16[384,512]{1,0:T(8,128)(2,1)S(1)}, u32[]{:S(2)}, u32[]{:S(2)}) collective-permute-start(bf16[384,512]{1,0:T(8,128)(2,1)} %bitcast.4), channel_id=1, source_target_pairs={{1,0},{0,1},{3,2},{2,3},{5,4},{4,5},{7,6},{6,7},{9,8},{8,9},{11,10... | collective-permute-start | bytes 1179656 | tf_op jit(solution)/shard_map/ppermute | solution.py:30
  1.2 5.6 %collective-permute-start.2 = (bf16[384,512]{1,0:T(8,128)(2,1)}, bf16[384,512]{1,0:T(8,128)(2,1)S(1)}, u32[]{:S(2)}, u32[]{:S(2)}) collective-permute-start(bf16[384,512]{1,0:T(8,128)(2,1)} %bitcast.5), channel_id=1, source_target_pairs={{0,14},{2,4},{4,2},{6,8},{8,6},{10,12},{12,10},{14,0},{1,15},{3,5}... | collective-permute-start | bytes 1179656 | tf_op jit(solution)/shard_map/ppermute | solution.py:35
  6.8 1.1 %shard_map.95 = (bf16[16,512]{1,0:T(8,128)(2,1)S(1)}, bf16[384,512]{1,0:T(8,128)(2,1)S(1)}) custom-call(s32[2]{0:T(128)} %frame_order.1, bf16[5,2,512]{2,1,0:T(2,128)(2,1)} %bitcast.8, bf16[5,1024]{1,0:T(8,128)(2,1)} %role_first.1, bf16[5,1024]{1,0:T(8,128)(2,1)} %role_rest.1, bf16[384,512]{1,0:T(8,128)(2,1)} %bitcast.6), custom_call_target="tpu_custom_call" | custom-call | tf_op jit(solution)/shard_map/pallas_call | solution.py:422
  7.9 0.2 collective-permute-start
  8.1 1.0 %collective-permute-done.other_special = bf16[16,512]{1,0:T(8,128)(2,1)S(1)} collective-permute-done((bf16[16,512]{1,0:T(8,128)(2,1)S(1)}, bf16[16,512]{1,0:T(8,128)(2,1)S(1)}, u32[]{:S(2)}, u32[]{:S(2)}) %collective-permute-start) | collective-permute-done | bytes 16416 | tf_op jit(solution)/shard_map/ppermute | solution.py:30
  9.1 2.3 %shard_map.96 = (f32[8,512]{1,0:T(8,128)S(1)}, bf16[3,1024,512]{2,1,0:T(8,128)(2,1)S(1)}, bf16[16,1024]{1,0:T(8,128)(2,1)S(1)}, bf16[512,1024]{1,0:T(8,128)(2,1)S(1)}) custom-call(s32[2,16]{1,0:T(2,128)} %covisible.1, bf16[16,512]{1,0:T(8,128)(2,1)S(1)} %get-tuple-element.31.special, bf16[16,512]{1,0:T(8,128)(2,1)S(1)} %collective-permute-done.other_special, ...), custom_call_target="tpu_custom_call" | custom-call | tf_op jit(solution)/shard_map/pallas_call | solution.py:422
  11.4 0.1 collective-permute-start.1
  11.5 0.0 copy-done
  11.5 0.1 collective-permute-start.7
  11.6 0.0 collective-permute-done.3.other
  11.6 3.4 %shard_map.98 = (bf16[4,128,768]{2,1,0:T(8,128)(2,1)S(1)}, bf16[512,128]{1,0:T(8,128)(2,1)S(1)}, f32[8,768]{1,0:T(8,128)S(1)}, f32[8,768]{1,0:T(8,128)S(1)}, f32...) custom-call(f32[8,512]{1,0:T(8,128)S(1)} %get-tuple-element.32.mask, bf16[384,512]{1,0:T(8,128)(2,1)S(1)} %get-tuple-element.34.own, ...), custom_call_target="tpu_custom_call" | custom-call | tf_op jit(solution)/shard_map/pallas_call | solution.py:422
  15.0 2.0 %collective-permute-done.2.refs_0_ = bf16[384,512]{1,0:T(8,128)(2,1)S(1)} collective-permute-done((bf16[384,512]{1,0:T(8,128)(2,1)}, bf16[384,512]{1,0:T(8,128)(2,1)S(1)}, u32[]{:S(2)}, u32[]{:S(2)}) %collective-permute-start.2) | collective-permute-done | bytes 393248 | tf_op jit(solution)/shard_map/ppermute | solution.py:35
  16.9 0.0 collective-permute-start.4
  16.9 0.0 collective-permute-done.1.second
  17.0 2.1 %collective-permute-start.5 = (bf16[32,1024]{1,0:T(8,128)(2,1)S(1)}, bf16[32,1024]{1,0:T(8,128)(2,1)S(1)}, u32[]{:S(2)}, u32[]{:S(2)}) collective-permute-start(bf16[32,1024]{1,0:T(8,128)(2,1)S(1)} %shard_map.97.first), channel_id=1, source_target_pairs={{8,0},{10,2},{12,4},{14,6},{0,8},{2,10},{4,12},{6,14},{9,1},{11,3}... | collective-permute-start | bytes 196616 | tf_op jit(solution)/shard_map/ppermute | solution.py:30
  19.1 0.0 collective-permute-done.4.refs_1_
  19.1 3.4 %shard_map.99 = (f32[8,768]{1,0:T(8,128)S(1)}, f32[8,768]{1,0:T(8,128)S(1)}, f32[4,64,768]{2,1,0:T(8,128)S(1)}, f32[512,128]{1,0:T(8,128)S(1)}) custom-call(f32[8,512]{1,0:T(8,128)S(1)} %get-tuple-element.32.mask, bf16[384,512]{1,0:T(8,128)(2,1)S(1)} %collective-permute-done.2.refs_0_, bf16[384,512]{1,0:T(8,128)(2,1)S(1)} %collective-permute-done.4.refs_1_, ...), custom_call_target="tpu_custom_call" | custom-call | tf_op jit(solution)/shard_map/pallas_call | solution.py:422
  22.5 2.7 %collective-permute-done.7.refs_0_ = bf16[384,512]{1,0:T(8,128)(2,1)S(1)} collective-permute-done((bf16[384,512]{1,0:T(8,128)(2,1)S(1)}, bf16[384,512]{1,0:T(8,128)(2,1)S(1)}, u32[]{:S(2)}, u32[]{:S(2)}) %collective-permute-start.7) | collective-permute-done | bytes 393248 | tf_op jit(solution)/shard_map/ppermute | solution.py:30
  25.2 0.0 collective-permute-start.8
  25.2 0.0 collective-permute-done.5.second
  25.3 0.1 collective-permute-start.6
  25.4 0.6 %shard_map.101.sums = f32[2,384,512]{2,1,0:T(8,128)S(1)} custom-call(bf16[384,512]{1,0:T(8,128)(2,1)S(1)} %collective-permute-done.7.refs_0_, bf16[3,1024,512]{2,1,0:T(8,128)(2,1)S(1)} %get-tuple-element.35.weights.refs_2_.refs_1_), custom_call_target="tpu_custom_call" | custom-call | tf_op jit(solution)/shard_map/pallas_call | solution.py:422
  25.9 1.0 %collective-permute-done.8.refs_0_ = bf16[384,512]{1,0:T(8,128)(2,1)S(1)} collective-permute-done((bf16[384,512]{1,0:T(8,128)(2,1)S(1)}, bf16[384,512]{1,0:T(8,128)(2,1)S(1)}, u32[]{:S(2)}, u32[]{:S(2)}) %collective-permute-start.8) | collective-permute-done | bytes 393248 | tf_op jit(solution)/shard_map/ppermute | solution.py:30
  26.9 2.4 %shard_map.102 = (f32[8,768]{1,0:T(8,128)S(1)}, f32[8,768]{1,0:T(8,128)S(1)}, f32[4,64,768]{2,1,0:T(8,128)S(1)}, f32[512,128]{1,0:T(8,128)S(1)}) custom-call(f32[8,512]{1,0:T(8,128)S(1)} %get-tuple-element.32.mask, f32[2,384,512]{2,1,0:T(8,128)S(1)} %shard_map.101.sums, bf16[384,512]{1,0:T(8,128)(2,1)S(1)} %collective-permute-done.8.refs_0_, ...), custom_call_target="tpu_custom_call" | custom-call | tf_op jit(solution)/shard_map/pallas_call | solution.py:422
  29.4 1.1 %collective-permute-done.6.special_pairs = bf16[48,1024]{1,0:T(8,128)(2,1)S(1)} collective-permute-done((bf16[48,1024]{1,0:T(8,128)(2,1)S(1)}, bf16[48,1024]{1,0:T(8,128)(2,1)S(1)}, u32[]{:S(2)}, u32[]{:S(2)}) %collective-permute-start.6) | collective-permute-done | bytes 98336 | tf_op jit(solution)/shard_map/ppermute | solution.py:30
  30.5 1.4 %shard_map.103 = (f32[400,512]{1,0:T(8,128)S(1)}, bf16[400,512]{1,0:T(8,128)(2,1)S(1)}) custom-call(f32[8,512]{1,0:T(8,128)S(1)} %get-tuple-element.32.mask, bf16[48,1024]{1,0:T(8,128)(2,1)S(1)} %collective-permute-done.6.special_pairs, bf16[4,128,768]{2,1,0:T(8,128)(2,1)S(1)} %get-tuple-element.40.refs_3_.refs_2_.queries, ...), custom_call_target="tpu_custom_call" | custom-call | tf_op jit(solution)/shard_map/pallas_call | solution.py:422
  31.9 0.1 collective-permute-start.9
  32.0 1.7 %collective-permute-done.9.received = bf16[400,512]{1,0:T(8,128)(2,1)S(1)} collective-permute-done((bf16[400,512]{1,0:T(8,128)(2,1)S(1)}, bf16[400,512]{1,0:T(8,128)(2,1)S(1)}, u32[]{:S(2)}, u32[]{:S(2)}) %collective-permute-start.9) | collective-permute-done | bytes 409632 | tf_op jit(solution)/shard_map/ppermute | solution.py:30
  33.8 0.8 %shard_map.104 = (bf16[384,512]{1,0:T(8,128)(2,1)}, bf16[5,2,512]{2,1,0:T(2,128)(2,1)}) custom-call(f32[400,512]{1,0:T(8,128)S(1)} %get-tuple-element.56.kept, bf16[400,512]{1,0:T(8,128)(2,1)S(1)} %collective-permute-done.9.received), custom_call_target="tpu_custom_call" | custom-call | tf_op jit(solution)/shard_map/pallas_call | solution.py:422
  (2 shorter events, 0.0 us)
Async XLA Ops:
  0.6 10.9 %copy-start = (bf16[2,192,512]{2,1,0:T(8,128)(2,1)S(1)}, bf16[2,192,512]{2,1,0:T(8,128)(2,1)}, u32[]{:S(2)}) copy-start(bf16[2,192,512]{2,1,0:T(8,128)(2,1)} %param.8) | copy-start | bytes 1179652
  0.6 11.0 %collective-permute-start.3 = (bf16[384,512]{1,0:T(8,128)(2,1)}, bf16[384,512]{1,0:T(8,128)(2,1)S(1)}, u32[]{:S(2)}, u32[]{:S(2)}) collective-permute-start(bf16[384,512]{1,0:T(8,128)(2,1)} %bitcast.4), channel_id=1, source_target_pairs={{1,0},{0,1},{3,2},{2,3},{5,4},{4,5},{7,6},{6,7},{9,8},{8,9},{11,10... | collective-permute-start | bytes 1179656 | tf_op jit(solution)/shard_map/ppermute | solution.py:30
  1.2 15.8 %collective-permute-start.2 = (bf16[384,512]{1,0:T(8,128)(2,1)}, bf16[384,512]{1,0:T(8,128)(2,1)S(1)}, u32[]{:S(2)}, u32[]{:S(2)}) collective-permute-start(bf16[384,512]{1,0:T(8,128)(2,1)} %bitcast.5), channel_id=1, source_target_pairs={{0,14},{2,4},{4,2},{6,8},{8,6},{10,12},{12,10},{14,0},{1,15},{3,5}... | collective-permute-start | bytes 1179656 | tf_op jit(solution)/shard_map/ppermute | solution.py:35
  7.9 1.2 %collective-permute-start = (bf16[16,512]{1,0:T(8,128)(2,1)S(1)}, bf16[16,512]{1,0:T(8,128)(2,1)S(1)}, u32[]{:S(2)}, u32[]{:S(2)}) collective-permute-start(bf16[16,512]{1,0:T(8,128)(2,1)S(1)} %get-tuple-element.31.special), channel_id=1, source_target_pairs={{1,0},{0,1},{3,2},{2,3},{5,4},{4,5},{7,6},{6,7},{9,8},{8,9},{11,10... | collective-permute-start | bytes 49160 | tf_op jit(solution)/shard_map/ppermute | solution.py:30
  11.4 5.5 %collective-permute-start.1 = (bf16[16,1024]{1,0:T(8,128)(2,1)S(1)}, bf16[16,1024]{1,0:T(8,128)(2,1)S(1)}, u32[]{:S(2)}, u32[]{:S(2)}) collective-permute-start(bf16[16,1024]{1,0:T(8,128)(2,1)S(1)} %get-tuple-element.33.first), channel_id=1, source_target_pairs={{4,0},{6,2},{0,4},{2,6},{12,8},{14,10},{8,12},{10,14},{5,1},{7,3},... | collective-permute-start | bytes 98312 | tf_op jit(solution)/shard_map/ppermute | solution.py:30
  11.5 13.7 %collective-permute-start.7 = (bf16[384,512]{1,0:T(8,128)(2,1)S(1)}, bf16[384,512]{1,0:T(8,128)(2,1)S(1)}, u32[]{:S(2)}, u32[]{:S(2)}) collective-permute-start(bf16[384,512]{1,0:T(8,128)(2,1)S(1)} %bitcast.7), channel_id=1, source_target_pairs={{2,0},{0,2},{6,4},{4,6},{10,8},{8,10},{14,12},{12,14},{3,1},{1,3},... | collective-permute-start | bytes 1179656 | tf_op jit(solution)/shard_map/ppermute | solution.py:30
  16.9 2.1 %collective-permute-start.4 = (bf16[384,512]{1,0:T(8,128)(2,1)S(1)}, bf16[384,512]{1,0:T(8,128)(2,1)S(1)}, u32[]{:S(2)}, u32[]{:S(2)}) collective-permute-start(bf16[384,512]{1,0:T(8,128)(2,1)S(1)} %collective-permute-done.2.refs_0_), channel_id=1, source_target_pairs={{1,0},{0,1},{3,2},{2,3},{5,4},{4,5},{7,6},{6,7},{9,8},{8,9},{11,10... | collective-permute-start | bytes 1179656 | tf_op jit(solution)/shard_map/ppermute | solution.py:30
  17.0 8.3 %collective-permute-start.5 = (bf16[32,1024]{1,0:T(8,128)(2,1)S(1)}, bf16[32,1024]{1,0:T(8,128)(2,1)S(1)}, u32[]{:S(2)}, u32[]{:S(2)}) collective-permute-start(bf16[32,1024]{1,0:T(8,128)(2,1)S(1)} %shard_map.97.first), channel_id=1, source_target_pairs={{8,0},{10,2},{12,4},{14,6},{0,8},{2,10},{4,12},{6,14},{9,1},{11,3}... | collective-permute-start | bytes 196616 | tf_op jit(solution)/shard_map/ppermute | solution.py:30
  25.2 1.7 %collective-permute-start.8 = (bf16[384,512]{1,0:T(8,128)(2,1)S(1)}, bf16[384,512]{1,0:T(8,128)(2,1)S(1)}, u32[]{:S(2)}, u32[]{:S(2)}) collective-permute-start(bf16[384,512]{1,0:T(8,128)(2,1)S(1)} %collective-permute-done.7.refs_0_), channel_id=1, source_target_pairs={{1,0},{0,1},{3,2},{2,3},{5,4},{4,5},{7,6},{6,7},{9,8},{8,9},{11,10... | collective-permute-start | bytes 1179656 | tf_op jit(solution)/shard_map/ppermute | solution.py:30
  25.3 5.2 %collective-permute-start.6 = (bf16[48,1024]{1,0:T(8,128)(2,1)S(1)}, bf16[48,1024]{1,0:T(8,128)(2,1)S(1)}, u32[]{:S(2)}, u32[]{:S(2)}) collective-permute-start(bf16[48,1024]{1,0:T(8,128)(2,1)S(1)} %shard_map.100.refs_4_), channel_id=1, source_target_pairs={{2,0},{0,2},{6,4},{4,6},{10,8},{8,10},{14,12},{12,14},{3,1},{1,3},... | collective-permute-start | bytes 294920 | tf_op jit(solution)/shard_map/ppermute | solution.py:30
  31.9 1.8 %collective-permute-start.9 = (bf16[400,512]{1,0:T(8,128)(2,1)S(1)}, bf16[400,512]{1,0:T(8,128)(2,1)S(1)}, u32[]{:S(2)}, u32[]{:S(2)}) collective-permute-start(bf16[400,512]{1,0:T(8,128)(2,1)S(1)} %get-tuple-element.57), channel_id=1, source_target_pairs={{1,0},{0,1},{3,2},{2,3},{5,4},{4,5},{7,6},{6,7},{9,8},{8,9},{11,10... | collective-permute-start | bytes 1228808 | tf_op jit(solution)/shard_map/ppermute | solution.py:30
